TPU v7x, 32 devices: a whole 2x2x4 slice. The times are simulated.
32 devices in a mesh: fsdp: 4 (over z), ctx: 4 (over y, x), tp: 2 (over core).
Axes of the slice: x: 2, y: 2, z: 4, core: 2. Of those that a mesh axis runs over, the one named last changes fastest.
Arguments:
- tokens: bfloat16 [2, 2048, 1792], P(None, ('fsdp', 'ctx')), may hold values from -6 to 6
- cotangent: bfloat16 [2, 2048, 1792], P(None, ('fsdp', 'ctx')), may hold values from -6 to 6
- attn_in: bfloat16 [3, 1792, 1792], P(None, 'fsdp', 'tp'), may hold values from -0.125 to 0.125
- attn_out: bfloat16 [1792, 1792], P('tp', 'fsdp'), may hold values from -1 to 1
- gate_up: bfloat16 [2, 1792, 4864], P(None, 'fsdp', 'tp'), may hold values from -0.125 to 0.125
- down_proj: bfloat16 [4864, 1792], P('tp', 'fsdp'), may hold values from -0.078125 to 0.078125
- conv_weight: bfloat16 [2, 3, 896], P('tp', None, 'fsdp'), may hold values from -3 to 3
- norm_gains: bfloat16 [2, 1792], P(None, 'fsdp'), may hold values from 0.5 to 1.5
- deal_order: int32 [2, 2048], P(None, ('fsdp', 'ctx')), may hold values from 0 to 2047, as said below
- lengths: int32 [2, 4, 3], P(None, 'fsdp'), may hold values from 1 to 416, 512 in all within a row
Outputs:
- activations: bfloat16 [2, 2048, 1792], P(None, ('fsdp', 'ctx'))
- input_grad: bfloat16 [2, 2048, 1792], P(None, ('fsdp', 'ctx'))
- grad_attn_in: float32 [3, 1792, 1792], P(None, 'fsdp', 'tp')
- grad_attn_out: float32 [1792, 1792], P('tp', 'fsdp')
- grad_gate_up: float32 [2, 1792, 4864], P(None, 'fsdp', 'tp')
- grad_down: float32 [4864, 1792], P('tp', 'fsdp')
- grad_conv: float32 [2, 3, 896], P('tp', None, 'fsdp')
- grad_gains: float32 [2, 1792], P(None, 'fsdp')
Inputs may be any that keep to these rules, and one draw needn't show every extreme that they name: Each row of deal_order is a permutation of the 2048 tokens; the 128 rows that each device of fsdp and ctx holds in the dealt layout take exactly 8 tokens from each device's block of 128 rows of the given order.
All inputs are finite; a program needn't handle non-finite values.
Results may differ from a plain program's by a relative error of at most 0.014.
Values may be sent and summed in bfloat16 or wider, within the bound.
No kernel may reach another device: no remote copies, remote signals or barrier semaphores. Data moves between devices by JAX's collectives and lax.ppermute only.
A program may use at most 320 MiB of HBM per device.

v0:
```python
import math

import jax
import jax.numpy as jnp
from jax import lax
from jax.sharding import PartitionSpec as P

HEAD = 64
WINDOW = 64
CONV = 3
BATCHES = 2


epsilon = 1e-06
masked_score = -1e30


def passed_along(value, axis, steps):
    count = lax.axis_size(axis)
    initial, last = (max(0, -steps), min(count, count - steps))
    return lax.ppermute(value, axis, [(source, source + steps) for source in range(initial, last)])


def rms_scale(values, gain):
    return values * lax.rsqrt(jnp.mean(values * values, axis=-1, keepdims=True) + epsilon) * gain


def head_sum(partial_sum):
    return lax.psum(partial_sum, "tp")


def conv_gate(values_ext, conv_rows, seg_ext):
    length = values_ext.shape[0] - (CONV - 1)
    own_seg = seg_ext[CONV - 1 :]
    conv_mix = jnp.zeros((length, values_ext.shape[1]), jnp.float32)
    for lag_step in range(CONV):
        offset = CONV - 1 - lag_step
        earlier = values_ext[offset : offset + length]
        same_seq = seg_ext[offset : offset + length] == own_seg
        conv_mix = conv_mix + jnp.where(same_seq[:, None], earlier * conv_rows[lag_step], 0.0)
    return values_ext[CONV - 1 :] * jax.nn.silu(conv_mix)


def window_scores(queries, key_rows, allowed):
    heads_q = queries.reshape(queries.shape[0], -1, HEAD)
    heads_k = key_rows.reshape(key_rows.shape[0], -1, HEAD)
    scaling = 1.0 / math.sqrt(HEAD)
    scores = (
        jnp.einsum("qhd,khd->hqk", heads_q, heads_k, preferred_element_type=jnp.float32) * scaling
    )
    return jnp.where(allowed[None], scores, masked_score)


def attend_forward(queries, key_rows, values, allowed):
    scores = window_scores(queries, key_rows, allowed)
    row_max = jnp.max(scores, axis=-1, keepdims=True)
    weights = jnp.exp(scores - row_max)
    row_total = jnp.sum(weights, axis=-1, keepdims=True)
    weights_low = (weights / row_total).astype(jnp.bfloat16)
    heads_v = values.reshape(values.shape[0], -1, HEAD)
    blended = jnp.einsum("hqk,khd->qhd", weights_low, heads_v, preferred_element_type=jnp.float32)
    return (blended.reshape(queries.shape).astype(jnp.bfloat16), row_max + jnp.log(row_total))


def attend_backward(queries, key_rows, values, allowed, log_total, grad_blended):
    scores = window_scores(queries, key_rows, allowed)
    weights = jnp.exp(scores - log_total)
    weights_low = weights.astype(jnp.bfloat16)
    heads_q = queries.reshape(queries.shape[0], -1, HEAD)
    heads_k = key_rows.reshape(key_rows.shape[0], -1, HEAD)
    heads_v = values.reshape(values.shape[0], -1, HEAD)
    heads_g = grad_blended.reshape(grad_blended.shape[0], -1, HEAD)
    grad_weights = jnp.einsum("qhd,khd->hqk", heads_g, heads_v, preferred_element_type=jnp.float32)
    grad_values = jnp.einsum(
        "hqk,qhd->khd", weights_low, heads_g, preferred_element_type=jnp.float32
    )
    inner_sum = jnp.sum(weights * grad_weights, axis=-1, keepdims=True)
    grad_scores = (weights * (grad_weights - inner_sum)).astype(jnp.bfloat16)
    scaling = 1.0 / math.sqrt(HEAD)
    grad_queries = (
        jnp.einsum("hqk,khd->qhd", grad_scores, heads_k, preferred_element_type=jnp.float32)
        * scaling
    )
    grad_keys = (
        jnp.einsum("hqk,qhd->khd", grad_scores, heads_q, preferred_element_type=jnp.float32)
        * scaling
    )
    return (
        grad_queries.reshape(queries.shape),
        grad_keys.reshape(key_rows.shape),
        grad_values.reshape(values.shape),
    )


def layer_pass(dealt_rows, grad_dealt, gathered, seg_ext, places, rim_width):
    attn_w, out_w, gate_w, down_w, conv_w, gain_w = gathered
    tok_rows = dealt_rows.shape[0]
    conv_rows = conv_w[0].astype(jnp.float32)
    gain_rows = gain_w.astype(jnp.float32)
    seg_query = seg_ext[rim_width:]
    seg_key = seg_ext[CONV - 1 :]
    pos_query = places[rim_width:]
    pos_key = places[CONV - 1 :]
    allowed = (
        (seg_key[None, :] == seg_query[:, None])
        & (pos_key[None, :] <= pos_query[:, None])
        & (pos_key[None, :] > pos_query[:, None] - WINDOW)
    )
    inputs = dealt_rows.astype(jnp.float32)
    normed, norm_pull = jax.vjp(rms_scale, inputs, gain_rows[0])
    hidden = normed.astype(jnp.bfloat16)
    projected = jnp.einsum(
        "td,cde->cte", hidden, attn_w, preferred_element_type=jnp.float32
    ).astype(jnp.bfloat16)
    rim_rows = passed_along(projected[1:, tok_rows - rim_width :], "ctx", 1)
    key_ext = jnp.concatenate([rim_rows[0], projected[1]])
    value_ext = jnp.concatenate([rim_rows[1], projected[2]]).astype(jnp.float32)

    def gate_values(values_in, conv_in):
        return conv_gate(values_in, conv_in, seg_ext)

    gated_vals, gate_pull = jax.vjp(gate_values, value_ext, conv_rows)
    gated_low = gated_vals.astype(jnp.bfloat16)
    key_rows = key_ext[CONV - 1 :]
    attended, log_total = attend_forward(projected[0], key_rows, gated_low, allowed)
    resid = inputs + head_sum(jnp.dot(attended, out_w, preferred_element_type=jnp.float32))
    normed_two, norm_two_pull = jax.vjp(rms_scale, resid, gain_rows[1])
    hidden_two = normed_two.astype(jnp.bfloat16)
    gate_up_out = jnp.einsum("td,cdf->ctf", hidden_two, gate_w, preferred_element_type=jnp.float32)
    sigmoid_gate = jax.nn.sigmoid(gate_up_out[0])
    silu_gate = gate_up_out[0] * sigmoid_gate
    inner_act = (silu_gate * gate_up_out[1]).astype(jnp.bfloat16)
    result = resid + head_sum(jnp.dot(inner_act, down_w, preferred_element_type=jnp.float32))
    grad_down = jnp.einsum("tf,td->fd", inner_act, grad_dealt, preferred_element_type=jnp.float32)
    grad_inner = jnp.einsum("td,fd->tf", grad_dealt, down_w, preferred_element_type=jnp.float32)
    grad_gate = (
        grad_inner * gate_up_out[1] * sigmoid_gate * (1.0 + gate_up_out[0] * (1.0 - sigmoid_gate))
    )
    grad_upper = grad_inner * silu_gate
    grad_pair = jnp.stack([grad_gate, grad_upper]).astype(jnp.bfloat16)
    grad_gate_up = jnp.einsum(
        "td,ctf->cdf", hidden_two, grad_pair, preferred_element_type=jnp.float32
    )
    grad_hidden_two = head_sum(
        jnp.einsum("ctf,cdf->td", grad_pair, gate_w, preferred_element_type=jnp.float32)
    )
    grad_resid_norm, grad_gain_two = norm_two_pull(grad_hidden_two)
    grad_resid = grad_dealt.astype(jnp.float32) + grad_resid_norm
    grad_branch = grad_resid.astype(jnp.bfloat16)
    grad_attn_out = jnp.einsum(
        "te,td->ed", attended, grad_branch, preferred_element_type=jnp.float32
    )
    grad_attended = jnp.einsum(
        "td,ed->te", grad_branch, out_w, preferred_element_type=jnp.float32
    ).astype(jnp.bfloat16)
    grad_queries, grad_keys, grad_gated = attend_backward(
        projected[0], key_rows, gated_low, allowed, log_total, grad_attended
    )
    grad_value_ext, grad_conv = gate_pull(grad_gated)
    grad_key_ext = jnp.concatenate(
        [jnp.zeros((CONV - 1, grad_keys.shape[1]), jnp.float32), grad_keys]
    )
    returned = passed_along(
        jnp.stack([grad_key_ext[:rim_width], grad_value_ext[:rim_width]]).astype(jnp.bfloat16),
        "ctx",
        -1,
    ).astype(jnp.float32)
    grad_kv = jnp.stack([grad_key_ext[rim_width:], grad_value_ext[rim_width:]])
    grad_kv = grad_kv.at[:, tok_rows - rim_width :].add(returned)
    grad_proj = jnp.concatenate([grad_queries[None], grad_kv]).astype(jnp.bfloat16)
    grad_attn_in = jnp.einsum("td,cte->cde", hidden, grad_proj, preferred_element_type=jnp.float32)
    grad_hidden = head_sum(
        jnp.einsum("cte,cde->td", grad_proj, attn_w, preferred_element_type=jnp.float32)
    )
    grad_input_norm, grad_gain_one = norm_pull(grad_hidden)
    grad_input = grad_resid + grad_input_norm
    grad_set = (
        grad_attn_in,
        grad_attn_out,
        grad_gate_up,
        grad_down,
        grad_conv[None],
        jnp.stack([grad_gain_one, grad_gain_two]),
    )
    return (result, grad_input, grad_set)


def per_device(
    tokens,
    cotangent,
    attn_in,
    attn_out,
    gate_up,
    down_proj,
    conv_weight,
    norm_gains,
    deal_order,
    lengths,
):
    tok_rows = tokens.shape[1]
    workers = lax.axis_size(("fsdp", "ctx"))
    slots_each = tok_rows // workers
    rim_width = WINDOW + CONV - 2
    position = lax.axis_index("ctx") * tok_rows
    places = position - rim_width + jnp.arange(tok_rows + rim_width, dtype=jnp.int32)
    summed = None
    activations = []
    input_grads = []
    for batch_index in range(BATCHES):
        gathered = (
            lax.all_gather(attn_in, "fsdp", axis=1, tiled=True),
            lax.all_gather(attn_out, "fsdp", axis=1, tiled=True),
            lax.all_gather(gate_up, "fsdp", axis=1, tiled=True),
            lax.all_gather(down_proj, "fsdp", axis=1, tiled=True),
            lax.all_gather(conv_weight, "fsdp", axis=2, tiled=True),
            lax.all_gather(norm_gains, "fsdp", axis=1, tiled=True),
        )
        wanted = deal_order[batch_index]
        source = wanted // tok_rows
        arrange = jnp.argsort(source, stable=True)
        asking = (wanted - source * tok_rows)[arrange].reshape(workers, slots_each)
        asked_rows = lax.all_to_all(
            asking, ("fsdp", "ctx"), split_axis=0, concat_axis=0, tiled=True
        ).reshape(-1)
        sent_x = tokens[batch_index][asked_rows].reshape(workers, slots_each, -1)
        sent_grad = cotangent[batch_index][asked_rows].reshape(workers, slots_each, -1)
        got_x, got_grad = (
            lax.all_to_all(sent_x, ("fsdp", "ctx"), split_axis=0, concat_axis=0, tiled=True),
            lax.all_to_all(sent_grad, ("fsdp", "ctx"), split_axis=0, concat_axis=0, tiled=True),
        )
        undo_order = jnp.argsort(arrange)
        dealt_rows = got_x.reshape(tok_rows, -1)[undo_order]
        grad_dealt = got_grad.reshape(tok_rows, -1)[undo_order]
        seq_ends = jnp.cumsum(lengths[batch_index, 0])
        seg_count = jnp.sum((places[:, None] >= seq_ends[None, :]).astype(jnp.int32), axis=1)
        seg_ext = jnp.where(places >= 0, seg_count, -1)
        result, grad_input, grad_set = layer_pass(
            dealt_rows, grad_dealt, gathered, seg_ext, places, rim_width
        )
        summed = grad_set if summed is None else jax.tree.map(jnp.add, summed, grad_set)
        send_y = result.astype(jnp.bfloat16)[arrange].reshape(workers, slots_each, -1)
        send_dx = grad_input.astype(jnp.bfloat16)[arrange].reshape(workers, slots_each, -1)
        home_y, home_dx = (
            lax.all_to_all(send_y, ("fsdp", "ctx"), split_axis=0, concat_axis=0, tiled=True),
            lax.all_to_all(send_dx, ("fsdp", "ctx"), split_axis=0, concat_axis=0, tiled=True),
        )
        activations.append(
            jnp.zeros_like(tokens[batch_index]).at[asked_rows].set(home_y.reshape(tok_rows, -1))
        )
        input_grads.append(
            jnp.zeros_like(tokens[batch_index]).at[asked_rows].set(home_dx.reshape(tok_rows, -1))
        )
    shares = (
        lax.psum_scatter(summed[0], ("fsdp", "ctx"), scatter_dimension=1, tiled=True),
        lax.psum_scatter(summed[1], ("fsdp", "ctx"), scatter_dimension=1, tiled=True),
        lax.psum_scatter(summed[2], ("fsdp", "ctx"), scatter_dimension=1, tiled=True),
        lax.psum_scatter(summed[3], ("fsdp", "ctx"), scatter_dimension=1, tiled=True),
        lax.psum_scatter(summed[4], ("fsdp", "ctx"), scatter_dimension=2, tiled=True),
        lax.psum_scatter(summed[5], ("fsdp", "ctx"), scatter_dimension=1, tiled=True),
    )
    final_grads = (
        lax.all_gather(shares[0].astype(jnp.bfloat16), "ctx", axis=1, tiled=True).astype(
            jnp.float32
        ),
        lax.all_gather(shares[1].astype(jnp.bfloat16), "ctx", axis=1, tiled=True).astype(
            jnp.float32
        ),
        lax.all_gather(shares[2].astype(jnp.bfloat16), "ctx", axis=1, tiled=True).astype(
            jnp.float32
        ),
        lax.all_gather(shares[3].astype(jnp.bfloat16), "ctx", axis=1, tiled=True).astype(
            jnp.float32
        ),
        lax.all_gather(shares[4].astype(jnp.bfloat16), "ctx", axis=2, tiled=True).astype(
            jnp.float32
        ),
        lax.all_gather(shares[5].astype(jnp.bfloat16), "ctx", axis=1, tiled=True).astype(
            jnp.float32
        ),
    )
    return (
        jnp.stack(activations),
        jnp.stack(input_grads),
        final_grads[0],
        final_grads[1],
        final_grads[2],
        final_grads[3],
        final_grads[4],
        final_grads[5],
    )


def solution(mesh):
    return jax.shard_map(
        per_device,
        mesh=mesh,
        in_specs=(
            P(None, ("fsdp", "ctx"), None),
            P(None, ("fsdp", "ctx"), None),
            P(None, "fsdp", "tp"),
            P("tp", "fsdp"),
            P(None, "fsdp", "tp"),
            P("tp", "fsdp"),
            P("tp", None, "fsdp"),
            P(None, "fsdp"),
            P(None, ("fsdp", "ctx")),
            P(None, "fsdp", None),
        ),
        out_specs=(
            P(None, ("fsdp", "ctx"), None),
            P(None, ("fsdp", "ctx"), None),
            P(None, "fsdp", "tp"),
            P("tp", "fsdp"),
            P(None, "fsdp", "tp"),
            P("tp", "fsdp"),
            P("tp", None, "fsdp"),
            P(None, "fsdp"),
        ),
        check_vma=False,
    )
```

profile of v0, /device:TPU:0, one launch (start us, length us, event | category | flops | bytes accessed | tf_op | source)
XLA Modules:
  0.0 3156.9 jit_solution(6694999277793042578)
XLA Ops:
  12.5 8.3 all-to-all-start
  26.7 13.1 all-gather
  45.1 9.2 all-to-all-start.3
  57.2 4.3 all-to-all-done.3
  61.5 7.9 all-to-all-start.1
  72.2 16.4 all-to-all-done.1
  88.6 9.6 all-to-all-start.4
  98.8 42.4 %all_gather.44 = bf16[1,3,896]{1,0,2:T(2,128)(2,1)S(1)} all-gather(bf16[1,3,224]{1,0,2:T(2,128)(2,1)S(1)} %copy.197), channel_id=1, replica_groups=mesh['fsdp'=4,'ctx'=4,'tp'=2] {'fsdp'}, dimensions={2}, use_global_device_ids=true | all-gather | bytes 6720 | tf_op jit(solution)/shard_map/all_gather | solution.py:215
  141.8 9.3 slice_reduce_fusion.2
  153.5 55.9 %all-gather.10.cloned.1.call-done = bf16[3,1792,896]{2,1,0:T(8,128)(2,1)} async-done(((bf16[3,448,896]{2,1,0:T(8,128)(2,1)}), bf16[3,1792,896]{2,1,0:T(8,128)(2,1)}) %all-gather.10.cloned.1.call-update) | async-done | bytes 9633808 | tf_op jit(solution)/shard_map/all_gather | solution.py:211
  209.4 5.5 fusion.4
  214.9 3.9 collective-permute-start
  220.6 3.4 collective-permute-start.1
  225.2 4.4 collective-permute-done.1
  237.3 36.5 %all-gather.12.cloned.1.call-done = bf16[896,1792]{0,1:T(8,128)(2,1)} async-done(((bf16[896,448]{0,1:T(8,128)(2,1)}), bf16[896,1792]{0,1:T(8,128)(2,1)}) %all-gather.12.cloned.1.call-update) | async-done | bytes 3211280 | tf_op jit(solution)/shard_map/all_gather | solution.py:212
  273.8 4.1 fusion.110
  286.4 4.3 all-to-all-start.8
  293.8 10.8 all-to-all-done.8
  304.7 4.2 all-to-all-start.6
  309.1 3.3 gather_fusion.12
  312.4 22.0 all-to-all-done.6
  341.1 260.6 %all-gather.14.cloned.1.call-done = bf16[2,1792,2432]{2,1,0:T(8,128)(2,1)} async-done(((bf16[2,448,2432]{2,1,0:T(8,128)(2,1)}), bf16[2,1792,2432]{2,1,0:T(8,128)(2,1)}) %all-gather.14.cloned.1.call-update) | async-done | bytes 17432592 | tf_op jit(solution)/shard_map/all_gather | solution.py:213
  601.7 10.3 convolution_bitcast_fusion
  612.1 3.3 copy-done
  615.6 4.0 convolution_bitcast_fusion.1
  619.7 137.6 %all-gather.16.cloned.1.call-done = bf16[2432,1792]{0,1:T(8,128)(2,1)} async-done(((bf16[2432,448]{0,1:T(8,128)(2,1)}), bf16[2432,1792]{0,1:T(8,128)(2,1)}) %all-gather.16.cloned.1.call-update) | async-done | bytes 8716304 | tf_op jit(solution)/shard_map/all_gather | solution.py:214
  757.3 7.4 fusion.48
  768.4 13.3 convolution_bitcast_fusion.3
  781.7 12.9 convolution_bitcast_fusion.5
  794.8 7.1 fusion.113
  801.9 6.9 fusion.111
  808.8 5.1 all-reduce.29.cloned.1.call-done
  814.0 3.2 multiply_reduce_fusion.3
  860.8 4.0 collective-permute-done.3
  872.6 7.5 convolution_bitcast_fusion.2
  880.1 7.4 convolution_bitcast_fusion.4
  888.5 3.5 fusion.114
  892.1 9.7 convolution_add_fusion
  903.8 10.9 fusion.65
  914.7 15.7 add_bitcast_fusion.1
  930.5 31.4 copy.231
  961.9 18.1 copy.238
  981.2 15.1 fusion.32
  996.3 26.4 add_bitcast_fusion
  1022.8 53.1 %copy.222 = f32[2,1792,2432]{2,0,1:T(2,128)} copy(f32[2,1792,2432]{1,2,0:T(8,128)} %add_bitcast_fusion) | data formatting | bytes 69730304 | tf_op jit(solution)/shard_map/add | solution.py:240
  1076.1 1707.9 %all-reduce.32 = (bf16[2,1792,2432]{2,0,1:T(2,128)(2,1)}, bf16[1,3,896]{2,0,1:T(2,128)(2,1)S(1)}) all-reduce(f32[2,1792,2432]{2,0,1:T(2,128)} %copy.222, f32[1,3,896]{2,0,1:T(1,128)S(1)} %add.312), channel_id=4, replica_groups=mesh['fsdp'=4,'ctx'=4,'tp'=2] {'fsdp','ctx'}, use_global_device_ids=true, to_apply=%region_36.37.clone | all-reduce | flops 8718976 | bytes 52313856
  2792.9 3.8 convolution_add_fusion.1
  2802.0 10.1 all-to-all-start.5
  2817.6 10.2 all-to-all-done.5
  2827.8 3.8 all-to-all-start.2
  2835.8 10.5 all-to-all-done.2
  2846.2 3.7 all-to-all-start.9
  2851.8 12.3 all-to-all-done.9
  2864.1 3.9 all-to-all-start.7
  2868.9 9.2 all_gather.52
  2879.7 8.2 all-gather.1
  2897.2 27.4 all-gather.20.cloned.1.call-done
  2924.6 6.3 copy.225
  2930.9 134.8 %reduce-scatter.10.cloned.1.call-done = f32[896,112]{0,1:T(8,128)} async-done(((f32[896,1792]{0,1:T(8,128)}), f32[896,112]{0,1:T(8,128)}) %reduce-scatter.10.cloned.1.call-update) | async-done | bytes 401424 | tf_op jit(solution)/shard_map/reduce_scatter | solution.py:255
  3066.8 10.4 all_gather.49
  3078.4 27.2 all-gather.22.cloned.1.call-done
  3105.6 4.0 convert_element_type.228
  3109.6 36.4 %all-gather.18.cloned.1.call-done = bf16[3,448,896]{2,1,0:T(8,128)(2,1)} async-done(((bf16[3,112,896]{2,1,0:T(8,128)(2,1)}), bf16[3,448,896]{2,1,0:T(8,128)(2,1)}) %all-gather.18.cloned.1.call-update) | async-done | bytes 2408464 | tf_op jit(solution)/shard_map/all_gather | solution.py:262
  3146.0 4.2 convert_element_type.222
  (399 shorter events, 151.8 us)
Async XLA Ops:
  7.2 16.9 copy-start.58
  7.2 202.2 %all-gather.10.cloned.1.call-start = ((), (), s32[]{:S(2)}) async-start(), calls=%async_computation.14 | async-start | bytes 12042240 | tf_op jit(solution)/shard_map/all_gather | solution.py:211
  10.5 13.6 copy-start.75
  11.8 15.0 copy-start.78
  12.5 32.6 %all-to-all-start = ((s32[16,1,8]{2,1,0:T(1,128)}), s32[16,1,8]{2,1,0:T(1,128)S(1)}, u32[]{:S(2)}, u32[]{:S(2)}) async-start(s32[16,1,8]{2,1,0:T(1,128)} %bitcast.1), calls=%async_computation | async-start | bytes 16384 | tf_op jit(solution)/shard_map/all_to_all | solution.py:222
  20.8 21.8 copy-start.80
  20.8 253.0 %all-gather.12.cloned.1.call-start = ((), (), s32[]{:S(2)}) async-start(), calls=%async_computation.15 | async-start | bytes 4014080 | tf_op jit(solution)/shard_map/all_gather | solution.py:212
  45.1 16.5 all-to-all-start.3
  61.5 27.0 all-to-all-start.1
  70.4 28.2 copy-start.77
  88.6 63.7 %all-to-all-start.4 = ((bf16[16,8,1792]{2,1,0:T(8,128)(2,1)}), bf16[16,8,1792]{2,1,0:T(8,128)(2,1)S(1)}, u32[]{:S(2)}, u32[]{:S(2)}) async-start(bf16[16,8,1792]{2,1,0:T(8,128)(2,1)} %bitcast.33), calls=%async_computation.4 | async-start | bytes 917504 | tf_op jit(solution)/shard_map/all_to_all | solution.py:228
  98.2 239.4 %all-reduce.31.cloned.1.call-start = ((), (), s32[]{:S(2)}) async-start(), calls=%async_computation.27 | async-start | bytes 3670016 | tf_op jit(solution)/shard_map/psum | solution.py:29
  152.1 57.3 %copy-start.20 = (bf16[128,1792]{1,0:T(8,128)(2,1)}, bf16[128,1792]{1,0:T(8,128)(2,1)S(1)}, u32[]{:S(2)}) copy-start(bf16[128,1792]{1,0:T(8,128)(2,1)S(1)} %gather_fusion.2) | copy-start | bytes 1376260
  153.3 65.6 %copy-start.18 = (bf16[128,1792]{1,0:T(8,128)(2,1)}, bf16[128,1792]{1,0:T(8,128)(2,1)S(1)}, u32[]{:S(2)}) copy-start(bf16[128,1792]{1,0:T(8,128)(2,1)S(1)} %gather_fusion.6) | copy-start | bytes 1376260
  153.4 61.4 %copy-start.85 = (f32[128]{0:T(128)}, f32[128]{0:T(128)S(1)}, u32[]{:S(2)}) copy-start(f32[128]{0:T(128)S(1)} %fusion.30) | copy-start | bytes 1540
  209.4 9.5 copy-start.1
  214.9 9.5 collective-permute-start
  220.6 9.0 collective-permute-start.1
  224.4 9.8 copy-start.48
  273.8 4.1 copy-start.61
  279.9 321.9 %all-gather.14.cloned.1.call-start = ((), (), s32[]{:S(2)}) async-start(), calls=%async_computation.16 | async-start | bytes 21790720 | tf_op jit(solution)/shard_map/all_gather | solution.py:213
  280.5 476.8 %all-gather.16.cloned.1.call-start = ((), (), s32[]{:S(2)}) async-start(), calls=%async_computation.17 | async-start | bytes 10895360 | tf_op jit(solution)/shard_map/all_gather | solution.py:214
  286.4 18.3 all-to-all-start.8
  304.7 29.7 all-to-all-start.6
  308.9 505.0 %all-reduce.29.cloned.1.call-start = ((), (), s32[]{:S(2)}) async-start(), calls=%async_computation.26 | async-start | bytes 3670016 | tf_op jit(solution)/shard_map/psum | solution.py:29
  601.7 13.6 copy-start
  601.7 13.9 copy-start.3
  757.3 7.4 copy-start.8
  757.3 8.2 copy-start.26
  757.3 8.2 copy-start.33
  794.7 1989.4 %all-reduce.27.cloned.1.call-start = ((), (), s32[]{:S(2)}) async-start(), calls=%async_computation.25 | async-start | bytes 7340032 | tf_op jit(solution)/shard_map/psum | solution.py:29
  794.8 7.1 copy-start.43
  854.2 10.6 collective-permute-start.3
  859.2 11.3 collective-permute-start.2
  860.6 19.5 copy-start.46
  868.4 11.7 copy-start.29
  872.5 7.6 copy-start.31
  887.5 4.5 copy-start.28
  887.5 4.5 copy-start.41
  887.5 1909.3 %reduce-scatter.12.cloned.1.call-start = ((), (), s32[]{:S(2)}) async-start(), calls=%async_computation.21 | async-start | bytes 18522112 | tf_op jit(solution)/shard_map/reduce_scatter | solution.py:257
  901.8 1910.4 %reduce-scatter.14.cloned.1.call-start = ((), (), s32[]{:S(2)}) async-start(), calls=%async_computation.23 | async-start | bytes 20471808
  903.8 10.9 copy-start.19
  903.8 10.9 copy-start.30
  980.0 16.3 copy-start.7
  980.0 1898.7 %reduce-scatter.16.cloned.1.call-start = ((), (), s32[]{:S(2)}) async-start(), calls=%async_computation.24 | async-start | bytes 974848
  1022.8 53.2 %copy-start.71 = (f32[896]{0:T(1024)S(1)}, f32[896]{0:T(1024)}, u32[]{:S(2)}) copy-start(f32[896]{0:T(1024)} %get-tuple-element.104) | copy-start | bytes 10756
  1022.8 53.2 %copy-start.70 = (f32[896]{0:T(1024)S(1)}, f32[896]{0:T(1024)}, u32[]{:S(2)}) copy-start(f32[896]{0:T(1024)} %get-tuple-element.105) | copy-start | bytes 10756
  1022.8 53.2 %copy-start.69 = (f32[896]{0:T(1024)S(1)}, f32[896]{0:T(1024)}, u32[]{:S(2)}) copy-start(f32[896]{0:T(1024)} %get-tuple-element.103) | copy-start | bytes 10756
  1022.8 53.2 %copy-start.74 = (f32[896]{0:T(1024)S(1)}, f32[896]{0:T(1024)}, u32[]{:S(2)}) copy-start(f32[896]{0:T(1024)} %get-tuple-element.101) | copy-start | bytes 10756
  1022.8 53.2 %copy-start.73 = (f32[896]{0:T(1024)S(1)}, f32[896]{0:T(1024)}, u32[]{:S(2)}) copy-start(f32[896]{0:T(1024)} %get-tuple-element.102) | copy-start | bytes 10756
  1022.8 53.2 %copy-start.72 = (f32[896]{0:T(1024)S(1)}, f32[896]{0:T(1024)}, u32[]{:S(2)}) copy-start(f32[896]{0:T(1024)} %get-tuple-element.100) | copy-start | bytes 10756
  1022.8 53.3 %copy-start.68 = (f32[1792]{0:T(1024)S(1)}, f32[1792]{0:T(1024)}, u32[]{:S(2)}) copy-start(f32[1792]{0:T(1024)} %get-tuple-element.98) | copy-start | bytes 21508
  1022.8 53.3 %copy-start.67 = (f32[1792]{0:T(1024)S(1)}, f32[1792]{0:T(1024)}, u32[]{:S(2)}) copy-start(f32[1792]{0:T(1024)} %get-tuple-element.181) | copy-start | bytes 21508
  2787.4 137.2 %all-gather.20.cloned.1.call-start = ((), (), s32[]{:S(2)}) async-start(), calls=%async_computation.20 | async-start | bytes 5447680 | tf_op jit(solution)/shard_map/all_gather | solution.py:268
  2790.5 275.2 %reduce-scatter.10.cloned.1.call-start = ((), (), s32[]{:S(2)}) async-start(), calls=%async_computation.19 | async-start | bytes 6823936 | tf_op jit(solution)/shard_map/reduce_scatter | solution.py:255
  2796.7 308.9 %all-gather.22.cloned.1.call-start = ((), (), s32[]{:S(2)}) async-start(), calls=%async_computation.22 | async-start | bytes 2723840 | tf_op jit(solution)/shard_map/all_gather | solution.py:271
  2802.0 25.8 all-to-all-start.5
  2812.1 333.8 %all-gather.18.cloned.1.call-start = ((), (), s32[]{:S(2)}) async-start(), calls=%async_computation.18 | async-start | bytes 3010560 | tf_op jit(solution)/shard_map/all_gather | solution.py:262
  2815.8 15.9 copy-start.84
  2815.8 15.9 copy-start.86
  2817.6 14.1 copy-start.23
  2827.8 18.4 all-to-all-start.2
  2846.2 17.8 all-to-all-start.9
  2864.1 29.6 all-to-all-start.7
  (52 other events, 105.5 us)
Sparse Core Ops, SparseCore 0:
  9.6 199.7 all-gather.9
  210.9 62.7 all-gather.11
  280.0 19.4 all-reduce.30
  301.1 300.6 all-gather.13
  603.2 154.0 all-gather.15
  794.8 19.1 all-reduce.28
  887.6 25.8 all-reduce.26
  916.0 595.0 reduce-scatter.11
  1516.9 486.5 reduce-scatter.13
  2787.6 84.0 reduce-scatter.15
  2874.2 50.3 all-gather.19
  2926.9 138.7 reduce-scatter.9
  3068.3 37.3 all-gather.21
  3108.1 37.8 all-gather.17
where the time goes:
time: 3170 us; the launch traced here: 3160 us
  blocking collectives  1790 us (56%)
  waiting for transfers between devices  821 us (26%)
  matrix products  199 us (6%)
  local copies, waits for them, and re-layouts  196 us (6%)
  starting transfers between devices  76 us (2%)
  other arithmetic  56.1 us (2%)
    unnamed x1, blocking collectives  1710 us
    all_gather x1, waiting for transfers between devices, per_device(): lax.all_gather(gate_up, 'fsdp', axis=1, tiled=True)  261 us
    all_gather x1, waiting for transfers between devices, per_device(): lax.all_gather(down_proj, 'fsdp', axis=1, tiled=True)  138 us
    reduce_scatter x1, waiting for transfers between devices, per_device(): lax.psum_scatter(summed[1], ('fsdp', 'ctx'), scatter_dimension=1, tiled=T...  135 us
    unnamed x185, local copies, waits for them, and re-layouts  72.4 us
  transfers between devices with their start and end apart: 28, of which 19 were waited for; matrix products, arithmetic and copies ran while one was open for 11% of the time, Pallas kernels for 0%

commit v1 on v0

v1 whole, which is shorter than its diff:
```python
import math

import jax
import jax.numpy as jnp
from jax import lax
from jax.experimental import pallas as pl
from jax.experimental.pallas import tpu as pltpu
from jax.sharding import PartitionSpec as P

HEAD = 64
WINDOW = 64
CONV = 3
BATCHES = 2
BLOCK = 128
HEADS_EACH = 4

epsilon = 1e-06
masked_score = -1e30
f32 = jnp.float32
bf16 = jnp.bfloat16


def flipped(value, sizes, step):
    n_fsdp, n_ctx, n_tp = sizes
    pairs = []
    for f in range(n_fsdp):
        for c in range(n_ctx):
            for t in range(n_tp):
                if step == 2:
                    other = (c, t ^ 1)
                else:
                    other = (c ^ (1 if t == step else 2), t)
                pairs.append(((f * n_ctx + c) * n_tp + t, (f * n_ctx + other[0]) * n_tp + other[1]))
    return lax.ppermute(value, ("fsdp", "ctx", "tp"), pairs)


def plane_gather(own, sizes):
    one = flipped(own, sizes, 0)
    two = flipped(own, sizes, 1)
    three = flipped(one, sizes, 1)
    mine = [own, one, two, three]
    return jnp.concatenate(mine + [flipped(block, sizes, 2) for block in mine])


def plane_scatter(kept, sent, sizes):
    total = kept + flipped(sent.astype(bf16), sizes, 2).astype(f32)
    for step in (1, 0):
        half = total.shape[0] // 2
        total = total[:half] + flipped(total[half:].astype(bf16), sizes, step).astype(f32)
    return total


def product(left, right, dims, out_type=f32):
    return lax.dot_general(left, right, (dims, ((), ())), preferred_element_type=f32).astype(out_type)


NN = ((1,), (0,))
NT = ((1,), (1,))
TN = ((0,), (0,))


def seg_of(places, ends):
    return (places >= ends[0]).astype(jnp.int32) + (places >= ends[1]).astype(jnp.int32)


def conv_terms(values, conv, ends):
    rows = values.shape[0]
    places = lax.broadcasted_iota(jnp.int32, values.shape, 0)
    own_seg = seg_of(places, ends)
    shifted = [values]
    for lag in range(1, CONV):
        same = (places >= lag) & (seg_of(places - lag, ends) == own_seg)
        shifted.append(jnp.where(same, pltpu.roll(values, lag, 0), 0.0))
    mix = shifted[0] * conv[0:1]
    for lag in range(1, CONV):
        mix = mix + shifted[lag] * conv[lag : lag + 1]
    return shifted, mix


def block_mask(block, first, span, ends):
    query = block * BLOCK + lax.broadcasted_iota(jnp.int32, (BLOCK, span), 0)
    key = first * BLOCK + lax.broadcasted_iota(jnp.int32, (BLOCK, span), 1)
    return (seg_of(query, ends) == seg_of(key, ends)) & (key <= query) & (key > query - WINDOW)


def head_lanes(tile, head):
    lanes = lax.broadcasted_iota(jnp.int32, tile.shape, 1)
    return (lanes >= head * HEAD) & (lanes < (head + 1) * HEAD)


def window_weights(query, keys, allowed):
    scores = product(query, keys, NT) * (1.0 / math.sqrt(HEAD))
    scores = jnp.where(allowed, scores, masked_score)
    weights = jnp.exp(scores - jnp.max(scores, axis=-1, keepdims=True))
    return weights / jnp.sum(weights, axis=-1, keepdims=True)


def ends_of(lengths_ref, batch):
    first = lengths_ref[batch, 0]
    return (first, first + lengths_ref[batch, 1])


def attend_forward_kernel(lengths_ref, qkv_ref, conv_ref, out_ref, gated_ref):
    width = HEADS_EACH * HEAD
    group = qkv_ref.shape[0] // BATCHES
    conv = conv_ref[...]
    for batch in range(BATCHES):
        ends = ends_of(lengths_ref, batch)
        base = batch * group
        values = qkv_ref[base : base + group, 2 * width :].astype(f32)
        _, mix = conv_terms(values, conv, ends)
        gated_ref[...] = (values * (mix * jax.nn.sigmoid(mix))).astype(bf16)
        for block in range(group // BLOCK):
            first = max(block - 1, 0)
            span = (block + 1 - first) * BLOCK
            allowed = block_mask(block, first, span, ends)
            rows = slice(base + block * BLOCK, base + (block + 1) * BLOCK)
            for pair in range(width // 128):
                lanes = slice(pair * 128, (pair + 1) * 128)
                query = qkv_ref[rows, lanes]
                keys = qkv_ref[
                    base + first * BLOCK : base + first * BLOCK + span,
                    width + pair * 128 : width + (pair + 1) * 128,
                ]
                gated = gated_ref[first * BLOCK : first * BLOCK + span, lanes]
                blended = []
                for head in range(2):
                    chosen = jnp.where(head_lanes(query, head), query, jnp.zeros_like(query))
                    weights = window_weights(chosen, keys, allowed).astype(bf16)
                    blended.append(product(weights, gated, NN))
                merged = jnp.where(head_lanes(blended[0], 0), blended[0], blended[1])
                out_ref[rows, lanes] = merged.astype(bf16)


def attend_backward_kernel(
    lengths_ref, qkv_ref, grad_ref, conv_ref, out_ref, grad_conv_ref, gated_ref, keys_sum, gated_sum
):
    width = HEADS_EACH * HEAD
    group = qkv_ref.shape[0] // BATCHES
    conv = conv_ref[...]
    scaling = 1.0 / math.sqrt(HEAD)
    conv_sums = [jnp.zeros((1, width), f32) for _ in range(CONV)]
    for batch in range(BATCHES):
        ends = ends_of(lengths_ref, batch)
        base = batch * group
        values = qkv_ref[base : base + group, 2 * width :].astype(f32)
        shifted, mix = conv_terms(values, conv, ends)
        sigmoid = jax.nn.sigmoid(mix)
        gated_ref[...] = (values * (mix * sigmoid)).astype(bf16)
        keys_sum[...] = jnp.zeros_like(keys_sum)
        gated_sum[...] = jnp.zeros_like(gated_sum)
        for block in range(group // BLOCK):
            first = max(block - 1, 0)
            span = (block + 1 - first) * BLOCK
            allowed = block_mask(block, first, span, ends)
            rows = slice(base + block * BLOCK, base + (block + 1) * BLOCK)
            local = slice(first * BLOCK, first * BLOCK + span)
            for pair in range(width // 128):
                lanes = slice(pair * 128, (pair + 1) * 128)
                query = qkv_ref[rows, lanes]
                grad = grad_ref[rows, lanes]
                keys = qkv_ref[
                    base + first * BLOCK : base + first * BLOCK + span,
                    width + pair * 128 : width + (pair + 1) * 128,
                ]
                gated = gated_ref[local, lanes]
                grad_queries = []
                grad_keys = None
                grad_gated = None
                for head in range(2):
                    mine = head_lanes(query, head)
                    chosen = jnp.where(mine, query, jnp.zeros_like(query))
                    chosen_grad = jnp.where(mine, grad, jnp.zeros_like(grad))
                    weights = window_weights(chosen, keys, allowed)
                    grad_weights = product(chosen_grad, gated, NT)
                    inner = jnp.sum(weights * grad_weights, axis=-1, keepdims=True)
                    grad_scores = (weights * (grad_weights - inner)).astype(bf16)
                    grad_queries.append(product(grad_scores, keys, NN))
                    more_keys = product(grad_scores, chosen, TN)
                    more_gated = product(weights.astype(bf16), chosen_grad, TN)
                    grad_keys = more_keys if grad_keys is None else grad_keys + more_keys
                    grad_gated = more_gated if grad_gated is None else grad_gated + more_gated
                merged = jnp.where(head_lanes(grad_queries[0], 0), grad_queries[0], grad_queries[1])
                out_ref[rows, lanes] = (merged * scaling).astype(bf16)
                keys_sum[local, lanes] += grad_keys
                gated_sum[local, lanes] += grad_gated
        out_ref[base : base + group, width : 2 * width] = (keys_sum[...] * scaling).astype(bf16)
        grad_gated = gated_sum[...]
        grad_mix = grad_gated * values * (sigmoid * (1.0 + mix * (1.0 - sigmoid)))
        grad_values = grad_gated * (mix * sigmoid) + grad_mix * conv[0:1]
        places = lax.broadcasted_iota(jnp.int32, values.shape, 0)
        own_seg = seg_of(places, ends)
        conv_sums[0] = conv_sums[0] + jnp.sum(grad_mix * shifted[0], axis=0, keepdims=True)
        for lag in range(1, CONV):
            same = (places < group - lag) & (seg_of(places + lag, ends) == own_seg)
            later = jnp.where(same, pltpu.roll(grad_mix, group - lag, 0), 0.0)
            grad_values = grad_values + later * conv[lag : lag + 1]
            conv_sums[lag] = conv_sums[lag] + jnp.sum(grad_mix * shifted[lag], axis=0, keepdims=True)
        out_ref[base : base + group, 2 * width :] = grad_values.astype(bf16)
    for lag in range(CONV):
        grad_conv_ref[lag : lag + 1, :] = conv_sums[lag]


VMEM = pl.BlockSpec(memory_space=pltpu.VMEM)
SMEM = pl.BlockSpec(memory_space=pltpu.SMEM)


def attend_forward(lengths, qkv, conv):
    rows, width = qkv.shape[0], HEADS_EACH * HEAD
    return pl.pallas_call(
        attend_forward_kernel,
        out_shape=jax.ShapeDtypeStruct((rows, width), bf16),
        in_specs=[SMEM, VMEM, VMEM],
        out_specs=VMEM,
        scratch_shapes=[pltpu.VMEM((rows // BATCHES, width), bf16)],
        compiler_params=pltpu.CompilerParams(vmem_limit_bytes=32 * 1024 * 1024),
        name="attend_forward",
    )(lengths, qkv, conv)


def attend_backward(lengths, qkv, grad, conv):
    rows, width = qkv.shape[0], HEADS_EACH * HEAD
    group = rows // BATCHES
    return pl.pallas_call(
        attend_backward_kernel,
        out_shape=(
            jax.ShapeDtypeStruct((rows, 3 * width), bf16),
            jax.ShapeDtypeStruct((CONV, width), f32),
        ),
        in_specs=[SMEM, VMEM, VMEM, VMEM],
        out_specs=(VMEM, VMEM),
        scratch_shapes=[
            pltpu.VMEM((group, width), bf16),
            pltpu.VMEM((group, width), f32),
            pltpu.VMEM((group, width), f32),
        ],
        compiler_params=pltpu.CompilerParams(vmem_limit_bytes=32 * 1024 * 1024),
        name="attend_backward",
    )(lengths, qkv, grad, conv)


def part_of(total, each, index):
    start = jnp.minimum(index * each, total - each)
    return start, index * each - start


def joined(parts, total, each, axis):
    pieces = []
    for index, part in enumerate(parts):
        shared = index * each - min(index * each, total - each)
        pieces.append(lax.slice_in_dim(part, shared, each, axis=axis))
    return jnp.concatenate(pieces, axis=axis)


def per_device(
    tokens,
    cotangent,
    attn_in,
    attn_out,
    gate_up,
    down_proj,
    conv_weight,
    norm_gains,
    deal_order,
    lengths,
):
    sizes = tuple(lax.axis_size(axis) for axis in ("fsdp", "ctx", "tp"))
    n_fsdp, n_ctx, n_tp = sizes
    workers = n_fsdp * n_ctx
    f, c, t = (lax.axis_index(axis) for axis in ("fsdp", "ctx", "tp"))
    me = f * n_ctx + c
    tok_rows, d_model = tokens.shape[1:]
    d_own = attn_in.shape[1]
    heads_all = attn_in.shape[2]
    width = HEADS_EACH * HEAD
    ff_all = gate_up.shape[2]
    ff = -(-ff_all // (n_ctx * 128)) * 128
    from_each = tok_rows // n_fsdp
    half = from_each // n_tp
    group = n_ctx * tok_rows
    plane = BATCHES * group

    start, shared = part_of(heads_all, width, c)
    sliced = lax.dynamic_slice_in_dim(attn_in, start, width, 2)
    out_part = lax.dynamic_slice_in_dim(attn_out, start, width, 0)
    out_part = jnp.where(jnp.arange(width)[:, None] >= shared, out_part, jnp.zeros_like(out_part))
    attn_own = jnp.concatenate([sliced[0], sliced[1], sliced[2], out_part.T], axis=1)
    ff_start, ff_shared = part_of(ff_all, ff, c)
    sliced = lax.dynamic_slice_in_dim(gate_up, ff_start, ff, 2)
    down_part = lax.dynamic_slice_in_dim(down_proj, ff_start, ff, 0)
    down_part = jnp.where(jnp.arange(ff)[:, None] >= ff_shared, down_part, jnp.zeros_like(down_part))
    mlp_own = jnp.concatenate([sliced[0], sliced[1], down_part.T], axis=1)
    attn_w = lax.all_gather(attn_own, "fsdp", axis=0, tiled=True)
    mlp_w = lax.all_gather(mlp_own, "fsdp", axis=0, tiled=True)
    qkv_w, out_w = attn_w[:, : 3 * width], attn_w[:, 3 * width :]
    gate_w, down_w = mlp_w[:, : 2 * ff], mlp_w[:, 2 * ff :]

    small = jnp.concatenate(
        [
            deal_order.reshape(-1).astype(f32),
            norm_gains.reshape(-1).astype(f32),
            conv_weight.reshape(-1).astype(f32),
        ]
    )
    small = lax.all_to_all(
        jnp.broadcast_to(small[None], (workers,) + small.shape),
        ("fsdp", "ctx"),
        split_axis=0,
        concat_axis=0,
        tiled=True,
    )
    n_order, n_gain = deal_order.size, norm_gains.size
    orders = small[:, :n_order].astype(jnp.int32).reshape(workers, BATCHES, tok_rows)
    by_fsdp = small.reshape(n_fsdp, n_ctx, -1)[:, 0]
    gains = by_fsdp[:, n_order : n_order + n_gain].reshape(n_fsdp, 2, -1)
    gains = jnp.transpose(gains, (1, 0, 2)).reshape(2, 1, d_model)
    conv = by_fsdp[:, n_order + n_gain :].reshape(n_fsdp, CONV, -1)
    conv = jnp.transpose(conv, (1, 0, 2)).reshape(CONV, heads_all)
    conv = lax.dynamic_slice_in_dim(conv, start, width, 1)

    given = me * tok_rows + jnp.arange(tok_rows, dtype=jnp.int32)
    by_batch = jnp.transpose(orders, (1, 0, 2)).reshape(BATCHES, -1)
    planes = jnp.arange(workers * tok_rows, dtype=jnp.int32) // group
    to_plane = jnp.sum(
        jnp.where(by_batch[:, None, :] == given[None, :, None], planes[None, None, :], 0), axis=2
    )
    earlier = jnp.arange(tok_rows)[None, :] < jnp.arange(tok_rows)[:, None]
    slot = jnp.sum(
        ((to_plane[:, None, :] == to_plane[:, :, None]) & earlier[None]).astype(jnp.int32), axis=2
    )
    place = ((slot // half) * n_fsdp + to_plane) * (BATCHES * half) + slot % half
    place = place + jnp.arange(BATCHES, dtype=jnp.int32)[:, None] * half
    place = place.reshape(-1)
    sent_rows = BATCHES * tok_rows // n_tp
    wire = t * sent_rows + jnp.arange(sent_rows, dtype=jnp.int32)
    choose = (place[None, :] == wire[:, None]).astype(bf16)
    both = jnp.concatenate([wire, (1 - t) * sent_rows + jnp.arange(sent_rows, dtype=jnp.int32)])
    undo = (place[:, None] == both[None, :]).astype(bf16)

    def to_planes(rows):
        picked = product(choose, rows.reshape(-1, d_model), NN, bf16)
        return lax.all_to_all(picked, "fsdp", split_axis=0, concat_axis=0, tiled=True)

    def to_given(rows):
        home = lax.all_to_all(rows, "fsdp", split_axis=0, concat_axis=0, tiled=True)
        pair = jnp.concatenate([home, flipped(home, sizes, 2)])
        return product(undo, pair, NN, bf16).reshape(BATCHES, tok_rows, d_model)

    own_x = to_planes(tokens).astype(f32)
    own_g = to_planes(cotangent)

    dealt = lax.dynamic_slice_in_dim(orders, f * n_ctx, n_ctx, 0)
    dealt = jnp.transpose(dealt, (1, 0, 2)).reshape(BATCHES, group)
    giver = dealt // tok_rows
    rank = jnp.sum(
        (
            (giver[:, None, :] == giver[:, :, None]) & (dealt[:, None, :] < dealt[:, :, None])
        ).astype(jnp.int32),
        axis=2,
    )
    core = rank // half
    away = (giver % n_ctx) ^ c
    swapped = jnp.where(core == 0, away, (away % 2) * 2 + away // 2)
    block = jnp.where(core == t, 0, n_ctx) + swapped
    arrival = block * (plane // (n_ctx * n_tp)) + (giver // n_ctx) * (BATCHES * half)
    arrival = arrival + jnp.arange(BATCHES, dtype=jnp.int32)[:, None] * half + rank % half
    deal = (arrival.reshape(-1)[:, None] == jnp.arange(plane, dtype=jnp.int32)[None, :]).astype(bf16)

    first_scale = lax.rsqrt(jnp.mean(own_x * own_x, axis=-1, keepdims=True) + epsilon)
    hidden = plane_gather((own_x * first_scale * gains[0]).astype(bf16), sizes)
    own_lengths = lengths[:, 0]
    qkv = product(deal, product(hidden, qkv_w, NN, bf16), NN, bf16)
    attended = product(deal, attend_forward(own_lengths, qkv, conv), TN, bf16)
    kept = plane // 2
    branch = plane_scatter(
        product(attended[:kept], out_w, NT), product(attended[kept:], out_w, NT, bf16), sizes
    )
    resid = own_x + branch

    second_scale = lax.rsqrt(jnp.mean(resid * resid, axis=-1, keepdims=True) + epsilon)
    hidden_two = plane_gather((resid * second_scale * gains[1]).astype(bf16), sizes)
    grad_dealt = plane_gather(own_g, sizes)
    grad_inner = product(grad_dealt, down_w, NN)
    gate_up_out = product(hidden_two, gate_w, NN)
    gate_act, upper = gate_up_out[:, :ff], gate_up_out[:, ff:]
    sigmoid = jax.nn.sigmoid(gate_act)
    silu = gate_act * sigmoid
    inner = (silu * upper).astype(bf16)
    grad_gate = grad_inner * upper * (sigmoid * (1.0 + gate_act * (1.0 - sigmoid)))
    grad_pair = jnp.concatenate([grad_gate, grad_inner * silu], axis=1).astype(bf16)
    grad_two = plane_scatter(
        product(grad_pair[:kept], gate_w, NT), product(grad_pair[kept:], gate_w, NT, bf16), sizes
    )
    grad_mlp = jnp.concatenate(
        [product(hidden_two, grad_pair, TN, bf16), product(grad_dealt, inner, TN, bf16)], axis=1
    )
    grad_mlp = lax.psum_scatter(grad_mlp, "fsdp", scatter_dimension=0, tiled=True)
    lifted = plane_scatter(
        product(inner[:kept], down_w, NT), product(inner[kept:], down_w, NT, bf16), sizes
    )
    activations = to_given((resid + lifted).astype(bf16))

    normed = resid * second_scale
    scaled = grad_two * gains[1]
    grad_resid = own_g.astype(f32) + second_scale * (
        scaled - normed * jnp.mean(scaled * normed, axis=-1, keepdims=True)
    )
    grad_gain_two = jnp.sum(grad_two * normed, axis=0)

    grad_branch = plane_gather(grad_resid.astype(bf16), sizes)
    grad_attended = product(deal, product(grad_branch, out_w, NN, bf16), NN, bf16)
    grad_proj, grad_conv = attend_backward(own_lengths, qkv, grad_attended, conv)
    grad_proj = product(deal, grad_proj, TN, bf16)
    grad_hidden = plane_scatter(
        product(grad_proj[:kept], qkv_w, NT), product(grad_proj[kept:], qkv_w, NT, bf16), sizes
    )
    grad_attn = jnp.concatenate(
        [product(hidden, grad_proj, TN, bf16), product(grad_branch, attended, TN, bf16)], axis=1
    )
    grad_attn = lax.psum_scatter(grad_attn, "fsdp", scatter_dimension=0, tiled=True)

    normed = own_x * first_scale
    scaled = grad_hidden * gains[0]
    grad_x = grad_resid + first_scale * (
        scaled - normed * jnp.mean(scaled * normed, axis=-1, keepdims=True)
    )
    grad_gain_one = jnp.sum(grad_hidden * normed, axis=0)
    input_grad = to_given(grad_x.astype(bf16))

    placed = lax.dynamic_update_slice(jnp.zeros((CONV, heads_all), f32), grad_conv, (0, start))
    placed = jnp.where(jnp.arange(heads_all)[None, :] >= start + shared, placed, 0.0)
    sums = jnp.concatenate([placed.reshape(-1), grad_gain_one, grad_gain_two])
    sums = lax.psum(sums, ("fsdp", "ctx"))
    grad_conv = sums[: CONV * heads_all].reshape(CONV, heads_all)
    grad_conv = lax.dynamic_slice_in_dim(grad_conv, f * (heads_all // n_fsdp), heads_all // n_fsdp, 1)
    gain_sums = sums[CONV * heads_all :]
    gain_sums = gain_sums + flipped(gain_sums, sizes, 2)
    grad_gains = lax.dynamic_slice_in_dim(gain_sums.reshape(2, d_model), f * d_own, d_own, 1)

    grad_mlp = lax.all_gather(grad_mlp, "ctx", axis=0).astype(f32)
    grad_attn = lax.all_gather(grad_attn, "ctx", axis=0).astype(f32)
    in_parts = [jnp.stack([grad_attn[k][:, i * width : (i + 1) * width] for i in range(3)]) for k in range(n_ctx)]
    gate_parts = [jnp.stack([grad_mlp[k][:, i * ff : (i + 1) * ff] for i in range(2)]) for k in range(n_ctx)]
    out_parts = [grad_attn[k][:, 3 * width :].T for k in range(n_ctx)]
    down_parts = [grad_mlp[k][:, 2 * ff :].T for k in range(n_ctx)]
    return (
        activations,
        input_grad,
        joined(in_parts, heads_all, width, 2),
        joined(out_parts, heads_all, width, 0),
        joined(gate_parts, ff_all, ff, 2),
        joined(down_parts, ff_all, ff, 0),
        grad_conv[None],
        grad_gains,
    )


def solution(mesh):
    return jax.shard_map(
        per_device,
        mesh=mesh,
        in_specs=(
            P(None, ("fsdp", "ctx"), None),
            P(None, ("fsdp", "ctx"), None),
            P(None, "fsdp", "tp"),
            P("tp", "fsdp"),
            P(None, "fsdp", "tp"),
            P("tp", "fsdp"),
            P("tp", None, "fsdp"),
            P(None, "fsdp"),
            P(None, ("fsdp", "ctx")),
            P(None, "fsdp", None),
        ),
        out_specs=(
            P(None, ("fsdp", "ctx"), None),
            P(None, ("fsdp", "ctx"), None),
            P(None, "fsdp", "tp"),
            P("tp", "fsdp"),
            P(None, "fsdp", "tp"),
            P("tp", "fsdp"),
            P("tp", None, "fsdp"),
            P(None, "fsdp"),
        ),
        check_vma=False,
    )
```

time: 3170 us -> 739 us (0.23)
  blocking collectives: 1790 us -> 74.9 us
  waiting for transfers between devices: 821 us -> 395 us
  local copies, waits for them, and re-layouts: 196 us -> 53.7 us
  matrix products: 199 us -> 73.1 us
    unnamed x1 -> x0, blocking collectives: 1710 us -> none
    all_gather x7 -> x4, waiting for transfers between devices: 582 us -> 36.7 us  [the longest x1 24 us: per_device(): mlp_w = lax.all_gather(mlp_own, 'fsdp', axis=0, tiled=True)]
    ppermute x4 -> x43, waiting for transfers between devices: 10.4 us -> 142 us  [flipped(): return lax.ppermute(value, ('fsdp', 'ctx', 'tp'), pairs)]
    dot_general x36 -> x22, matrix products: 199 us -> 73.1 us  [product(): lax.dot_general(left, right, (dims, ((), ())), preferred_element_type=f32)]
    all_gather x5 -> x0, blocking collectives: 83.3 us -> none  [the longest x1 42.4 us: per_device(): lax.all_gather(conv_weight, 'fsdp', axis=2, tiled=True)]
    psum x0 -> x1, blocking collectives: none -> 74.9 us  [per_device(): sums = lax.psum(sums, ('fsdp', 'ctx'))]
    add x2 -> x0, local copies, waits for them, and re-layouts: 53.1 us -> none  [per_device(): jax.tree.map(jnp.add, summed, grad_set)]
    unnamed x185 -> x100, local copies, waits for them, and re-layouts: 72.4 us -> 32.6 us
  transfers between devices with their start and end apart: 28 -> 54, of which waited for: 19 -> 27; matrix products, arithmetic and copies ran while one was open for 11% -> 13% of each run, Pallas kernels for 0% -> 1%
where the time goes in v1:
time: 739 us; the launch traced here: 735 us
  waiting for transfers between devices  395 us (53%)
  blocking collectives  74.9 us (10%)
  matrix products  73.1 us (10%)
  starting transfers between devices  56.3 us (8%)
  local copies, waits for them, and re-layouts  53.7 us (7%)
  other arithmetic  47.1 us (6%)
  Pallas kernels  19.9 us (3%)
  between operations  15.3 us (2%)
    ppermute x43, waiting for transfers between devices, flipped(): return lax.ppermute(value, ('fsdp', 'ctx', 'tp'), pairs)  142 us
    reduce_scatter x1, waiting for transfers between devices, per_device(): lax.psum_scatter(grad_mlp, 'fsdp', scatter_dimension=0, tiled=True)  123 us
    psum x1, blocking collectives, per_device(): sums = lax.psum(sums, ('fsdp', 'ctx'))  74.9 us
    dot_general x22, matrix products, product(): lax.dot_general(left, right, (dims, ((), ())), preferred_element_type=f32)  73.1 us
    all_to_all x2, waiting for transfers between devices, to_planes(): lax.all_to_all(picked, 'fsdp', split_axis=0, concat_axis=0, tiled=True)  44.6 us
    reduce_scatter x1, waiting for transfers between devices, per_device(): lax.psum_scatter(grad_attn, 'fsdp', scatter_dimension=0, tiled=True)  35.8 us
    unnamed x100, local copies, waits for them, and re-layouts  32.6 us
    ppermute x43, starting transfers between devices, flipped(): return lax.ppermute(value, ('fsdp', 'ctx', 'tp'), pairs)  28.8 us
  transfers between devices with their start and end apart: 54, of which 27 were waited for; matrix products, arithmetic and copies ran while one was open for 13% of the time, Pallas kernels for 1%

profile of v1, /device:TPU:0, one launch (start us, length us, event | category | flops | bytes accessed | tf_op | source)
XLA Modules:
  0.0 735.1 jit_solution(17055292141680886229)
XLA Ops:
  12.0 8.2 %all-to-all-start = ((f32[16,1,1824]{2,1,0:T(1,128)}), f32[16,1,1824]{2,1,0:T(1,128)S(1)}, u32[]{:S(2)}, u32[]{:S(2)}) async-start(f32[16,1,1824]{2,1,0:T(1,128)} %broadcast_in_dim.48), calls=%async_computation | async-start | bytes 245760 | tf_op jit(solution)/shard_map/all_to_all | solution.py:305
  20.3 1.9 dynamic-slice_bitcast_fusion.1
  23.7 4.3 all-to-all-done
  29.8 5.3 all-to-all-start.1
  37.5 20.8 %all-to-all-done.1 = bf16[4,32,1792]{2,1,0:T(8,128)(2,1)S(1)} async-done(((bf16[4,32,1792]{2,1,0:T(8,128)(2,1)}), bf16[4,32,1792]{2,1,0:T(8,128)(2,1)S(1)}, u32[]{:S(2)}, u32[]{:S(2)}) %all-to-all-start.1) | async-done | bytes 458784 | tf_op jit(solution)/shard_map/all_to_all | solution.py:342
  63.3 7.6 %collective-permute-done = bf16[128,1792]{1,0:T(8,128)(2,1)S(1)} collective-permute-done((bf16[128,1792]{1,0:T(8,128)(2,1)S(1)}, bf16[128,1792]{1,0:T(8,128)(2,1)S(1)}, u32[]{:S(2)}, u32[]{:S(2)}) %collective-permute-start) | collective-permute-done | bytes 458784 | tf_op jit(solution)/shard_map/ppermute | solution.py:34
  73.6 5.7 collective-permute-done.2
  83.3 12.7 %all-gather.7.cloned.1.call-done = bf16[1792,1024]{1,0:T(8,128)(2,1)} async-done(((bf16[448,1024]{1,0:T(8,128)(2,1)}), bf16[1792,1024]{1,0:T(8,128)(2,1)}) %all-gather.7.cloned.1.call-update) | async-done | bytes 3670032 | tf_op jit(solution)/shard_map/all_gather | solution.py:293
  96.0 7.5 %fusion.39.qkv_ref = bf16[1024,768]{1,0:T(8,128)(2,1)S(1)} fusion(s32[1024]{0:T(1024)S(1)} %fusion.107, bf16[1024,1792]{1,0:T(8,128)(2,1)} %constant_dynamic-update-slice_fusion, bf16[1792,1024]{1,0:T(8,128)(2,1)} %all-gather.7.cloned.1.call-done), kind=kOutput, calls=%fused_computation.73 | convolution fusion | flops 4431806464 | bytes 7999488 | tf_op jit(solution)/shard_map/dot_general | solution.py:54
  103.6 5.8 attend_forward.1
  110.8 3.3 convolution_convert_fusion.3
  115.2 3.5 all-to-all-start.3
  119.4 23.8 %all-to-all-done.3 = bf16[4,32,1792]{2,1,0:T(8,128)(2,1)S(1)} async-done(((bf16[4,32,1792]{2,1,0:T(8,128)(2,1)}), bf16[4,32,1792]{2,1,0:T(8,128)(2,1)S(1)}, u32[]{:S(2)}, u32[]{:S(2)}) %all-to-all-start.3) | async-done | bytes 458784 | tf_op jit(solution)/shard_map/all_to_all | solution.py:342
  146.3 2.5 convert_add_fusion.3
  149.5 8.7 %collective-permute-done.21 = bf16[128,1792]{1,0:T(8,128)(2,1)S(1)} collective-permute-done((bf16[128,1792]{1,0:T(8,128)(2,1)S(1)}, bf16[128,1792]{1,0:T(8,128)(2,1)S(1)}, u32[]{:S(2)}, u32[]{:S(2)}) %collective-permute-start.21) | collective-permute-done | bytes 458784 | tf_op jit(solution)/shard_map/ppermute | solution.py:34
  160.1 11.4 %collective-permute-done.23 = bf16[128,1792]{1,0:T(8,128)(2,1)S(1)} collective-permute-done((bf16[128,1792]{1,0:T(8,128)(2,1)S(1)}, bf16[128,1792]{1,0:T(8,128)(2,1)S(1)}, u32[]{:S(2)}, u32[]{:S(2)}) %collective-permute-start.23) | collective-permute-done | bytes 458784 | tf_op jit(solution)/shard_map/ppermute | solution.py:34
  173.0 7.3 collective-permute-done.9
  184.3 9.4 %collective-permute-done.10 = bf16[128,1792]{1,0:T(8,128)(2,1)S(1)} collective-permute-done((bf16[128,1792]{1,0:T(8,128)(2,1)S(1)}, bf16[128,1792]{1,0:T(8,128)(2,1)S(1)}, u32[]{:S(2)}, u32[]{:S(2)}) %collective-permute-start.10) | collective-permute-done | bytes 458784 | tf_op jit(solution)/shard_map/ppermute | solution.py:34
  197.5 5.4 collective-permute-done.12
  207.0 24.0 %all-gather.9.cloned.1.call-done = bf16[1792,1920]{1,0:T(8,128)(2,1)} async-done(((bf16[448,1920]{1,0:T(8,128)(2,1)}), bf16[1792,1920]{1,0:T(8,128)(2,1)}) %all-gather.9.cloned.1.call-update) | async-done | bytes 6881296 | tf_op jit(solution)/shard_map/all_gather | solution.py:294
  230.9 8.5 %fusion.10 = f32[1024,1280]{1,0:T(8,128)S(1)} fusion(bf16[1024,1792]{1,0:T(8,128)(2,1)} %constant_dynamic-update-slice_fusion.8, bf16[1792,1920]{1,0:T(8,128)(2,1)} %all-gather.9.cloned.1.call-done), kind=kOutput, calls=%fused_computation.24 | convolution fusion | flops 4697620480 | bytes 13500416 | tf_op jit(solution)/shard_map/dot_general | solution.py:54
  239.4 3.7 multiply_convert_fusion
  243.2 2.6 fusion.14
  245.9 1.6 convolution_convert_fusion.5
  249.6 2.7 convert_add_fusion.1
  256.4 9.6 %collective-permute-done.29 = bf16[256,1792]{1,0:T(8,128)(2,1)S(1)} collective-permute-done((bf16[256,1792]{1,0:T(8,128)(2,1)S(1)}, bf16[256,1792]{1,0:T(8,128)(2,1)S(1)}, u32[]{:S(2)}, u32[]{:S(2)}) %collective-permute-start.29) | collective-permute-done | bytes 917536 | tf_op jit(solution)/shard_map/ppermute | solution.py:34
  267.7 13.0 %collective-permute-done.18 = bf16[256,1792]{1,0:T(8,128)(2,1)S(1)} collective-permute-done((bf16[256,1792]{1,0:T(8,128)(2,1)S(1)}, bf16[256,1792]{1,0:T(8,128)(2,1)S(1)}, u32[]{:S(2)}, u32[]{:S(2)}) %collective-permute-start.18) | collective-permute-done | bytes 917536 | tf_op jit(solution)/shard_map/ppermute | solution.py:34
  282.8 6.6 collective-permute-done.19
  293.9 9.0 %collective-permute-done.31 = bf16[128,1792]{1,0:T(8,128)(2,1)S(1)} collective-permute-done((bf16[128,1792]{1,0:T(8,128)(2,1)S(1)}, bf16[128,1792]{1,0:T(8,128)(2,1)S(1)}, u32[]{:S(2)}, u32[]{:S(2)}) %collective-permute-start.31) | collective-permute-done | bytes 458784 | tf_op jit(solution)/shard_map/ppermute | solution.py:34
  304.7 6.7 collective-permute-done.33
  313.2 1.8 copy-done.18
  315.0 2.1 convolution_convert_fusion.8
  317.2 4.9 fusion.46.grad_ref
  322.1 14.1 %attend_backward.1 = (bf16[1024,768]{1,0:T(8,128)(2,1)S(1)}, f32[3,256]{1,0:T(4,128)S(1)}) custom-call(s32[2,3]{1,0:T(2,128)S(1)} %bitcast.175, bf16[1024,768]{1,0:T(8,128)(2,1)S(1)} %fusion.39.qkv_ref, bf16[1024,256]{1,0:T(8,128)(2,1)S(1)} %fusion.46.grad_ref, f32[3,256]{1,0:T(4,128)S(1)} %constant_dynamic-slice_fusion.2.conv_ref), custom_call_target="tpu_custom_call" | custom-call | tf_op jit(solution)/shard_map/attend_backward/pallas_call | solution.py:224
  336.2 2.4 fusion.40
  339.7 3.3 convolution_convert_fusion.1
  343.0 2.1 pad_maximum_fusion.2
  345.1 5.9 copy.52
  352.3 6.3 convolution_convert_fusion.2
  358.6 7.4 %convolution_convert_fusion = bf16[1792,1280]{0,1:T(8,128)(2,1)S(1)} fusion(bf16[1024,1792]{1,0:T(8,128)(2,1)} %constant_dynamic-update-slice_fusion.8, bf16[1024,640]{1,0:T(8,128)(2,1)S(1)} %copy-done.31, bf16[1024,640]{1,0:T(8,128)(2,1)S(1)} %copy-done.33), kind=kOutput, calls=%fused_computation.3 | convolution fusion | flops 4705157120 | bytes 10878976 | tf_op jit(solution)/shard_map/dot_general | solution.py:54
  366.0 5.0 pad_maximum_fusion
  371.0 9.9 %copy.54 = bf16[1792,1920]{1,0:T(8,128)(2,1)} copy(bf16[1792,1920]{0,1:T(8,128)(2,1)} %pad_maximum_fusion) | data formatting | bytes 13762560
  381.1 35.8 %reduce-scatter.7.cloned.1.call-done = bf16[448,1024]{1,0:T(8,128)(2,1)} async-done(((bf16[1792,1024]{1,0:T(8,128)(2,1)}), bf16[448,1024]{1,0:T(8,128)(2,1)}) %reduce-scatter.7.cloned.1.call-update) | async-done | bytes 917520 | tf_op jit(solution)/shard_map/reduce_scatter | solution.py:420
  417.0 122.8 %reduce-scatter.9.cloned.1.call-done = bf16[448,1920]{1,0:T(8,128)(2,1)} async-done(((bf16[1792,1920]{1,0:T(8,128)(2,1)}), bf16[448,1920]{1,0:T(8,128)(2,1)}) %reduce-scatter.9.cloned.1.call-update) | async-done | bytes 1720336 | tf_op jit(solution)/shard_map/reduce_scatter | solution.py:397
  539.8 3.6 convolution_convert_fusion.4
  543.5 3.8 collective-permute-done.38
  547.2 1.6 convert_add_fusion
  548.9 1.8 copy-done.12
  552.3 4.2 all-to-all-start.2
  556.6 16.2 %collective-permute-done.39 = bf16[256,1792]{1,0:T(8,128)(2,1)} collective-permute-done((bf16[256,1792]{1,0:T(8,128)(2,1)S(1)}, bf16[256,1792]{1,0:T(8,128)(2,1)}, u32[]{:S(2)}, u32[]{:S(2)}) %collective-permute-start.39) | collective-permute-done | bytes 917536 | tf_op jit(solution)/shard_map/ppermute | solution.py:34
  572.8 2.3 slice_add_fusion
  575.9 1.6 collective-permute-start.40
  577.7 16.7 %collective-permute-done.40 = bf16[128,1792]{1,0:T(8,128)(2,1)S(1)} collective-permute-done((bf16[128,1792]{1,0:T(8,128)(2,1)}, bf16[128,1792]{1,0:T(8,128)(2,1)S(1)}, u32[]{:S(2)}, u32[]{:S(2)}) %collective-permute-start.40) | collective-permute-done | bytes 458784 | tf_op jit(solution)/shard_map/ppermute | solution.py:34
  594.8 2.3 fusion.65
  597.1 4.8 all-to-all-start.4
  601.9 2.5 convolution_convert_fusion.7
  604.8 8.9 %all-to-all-done.4 = bf16[4,32,1792]{2,1,0:T(8,128)(2,1)S(1)} async-done(((bf16[4,32,1792]{2,1,0:T(8,128)(2,1)}), bf16[4,32,1792]{2,1,0:T(8,128)(2,1)S(1)}, u32[]{:S(2)}, u32[]{:S(2)}) %all-to-all-start.4) | async-done | bytes 458784 | tf_op jit(solution)/shard_map/all_to_all | solution.py:345
  613.6 74.9 %psum.7 = f32[6272]{0:T(1024)S(1)} all-reduce(f32[6272]{0:T(1024)S(1)} %pad_maximum_fusion.8), channel_id=1, replica_groups=mesh['fsdp'=4,'ctx'=4,'tp'=2] {'fsdp','ctx'}, use_global_device_ids=true, to_apply=%region_11.12 | all-reduce | flops 6272 | bytes 50176 | tf_op jit(solution)/shard_map/psum | solution.py:433
  691.8 2.9 convert_element_type.219
  696.9 2.6 fusion.1
  699.5 8.8 %convert_element_type.220 = f32[1792,1920]{1,0:T(8,128)} convert(bf16[1792,1920]{1,0:T(8,128)(2,1)} %all-gather.13.cloned.1.call-done) | non-fusion elementwise | flops 3440640 | bytes 20643840 | tf_op jit(solution)/shard_map/convert_element_type | solution.py:440
  708.3 9.3 %slice_bitcast_fusion.3 = (f32[640,448]{0,1:T(8,128)}, f32[640,448]{0,1:T(8,128)}, f32[640,448]{0,1:T(8,128)}, f32[640,448]{0,1:T(8,128)}, f32[1,448,640]{2,1,0:...) fusion(f32[1792,1920]{1,0:T(8,128)} %convert_element_type.220), kind=kLoop, calls=%fused_computation.84 | loop fusion | bytes 27525120 | tf_op jit(solution)/shard_map/transpose | solution.py:445
  718.9 4.6 pad_maximum_fusion.1
  724.4 3.7 fusion
  (274 shorter events, 75.6 us)
Async XLA Ops:
  7.2 21.5 %copy-start = (bf16[2,128,1792]{2,1,0:T(8,128)(2,1)S(1)}, bf16[2,128,1792]{2,1,0:T(8,128)(2,1)}, u32[]{:S(2)}) copy-start(bf16[2,128,1792]{2,1,0:T(8,128)(2,1)} %param.10) | copy-start | bytes 2752516
  7.2 88.8 %all-gather.7.cloned.1.call-start = ((), (), s32[]{:S(2)}) async-start(), calls=%async_computation.7 | async-start | bytes 4587520 | tf_op jit(solution)/shard_map/all_gather | solution.py:293
  12.0 16.0 %all-to-all-start = ((f32[16,1,1824]{2,1,0:T(1,128)}), f32[16,1,1824]{2,1,0:T(1,128)S(1)}, u32[]{:S(2)}, u32[]{:S(2)}) async-start(f32[16,1,1824]{2,1,0:T(1,128)} %broadcast_in_dim.48), calls=%async_computation | async-start | bytes 245760 | tf_op jit(solution)/shard_map/all_to_all | solution.py:305
  29.8 28.6 %all-to-all-start.1 = ((bf16[4,32,1792]{2,1,0:T(8,128)(2,1)}), bf16[4,32,1792]{2,1,0:T(8,128)(2,1)S(1)}, u32[]{:S(2)}, u32[]{:S(2)}) async-start(bf16[4,32,1792]{2,1,0:T(8,128)(2,1)} %bitcast.7), calls=%async_computation.1 | async-start | bytes 917504 | tf_op jit(solution)/shard_map/all_to_all | solution.py:342
  35.1 195.9 %all-gather.9.cloned.1.call-start = ((), (), s32[]{:S(2)}) async-start(), calls=%async_computation.8 | async-start | bytes 8601600 | tf_op jit(solution)/shard_map/all_gather | solution.py:294
  59.5 12.0 %collective-permute-start.1 = (bf16[128,1792]{1,0:T(8,128)(2,1)S(1)}, bf16[128,1792]{1,0:T(8,128)(2,1)S(1)}, u32[]{:S(2)}, u32[]{:S(2)}) collective-permute-start(bf16[128,1792]{1,0:T(8,128)(2,1)S(1)} %get-tuple-element.89), channel_id=1, source_target_pairs={{0,4},{1,3},{2,6},{3,1},{4,0},{5,7},{6,2},{7,5},{8,12},{9,11},{10,... | collective-permute-start | bytes 1376264 | tf_op jit(solution)/shard_map/ppermute | solution.py:34
  60.8 10.0 %collective-permute-start = (bf16[128,1792]{1,0:T(8,128)(2,1)S(1)}, bf16[128,1792]{1,0:T(8,128)(2,1)S(1)}, u32[]{:S(2)}, u32[]{:S(2)}) collective-permute-start(bf16[128,1792]{1,0:T(8,128)(2,1)S(1)} %get-tuple-element.89), channel_id=1, source_target_pairs={{0,2},{1,5},{2,0},{3,7},{4,6},{5,1},{6,4},{7,3},{8,10},{9,13},{10,... | collective-permute-start | bytes 1376264 | tf_op jit(solution)/shard_map/ppermute | solution.py:34
  63.2 16.9 %collective-permute-start.3 = (bf16[128,1792]{1,0:T(8,128)(2,1)S(1)}, bf16[128,1792]{1,0:T(8,128)(2,1)S(1)}, u32[]{:S(2)}, u32[]{:S(2)}) collective-permute-start(bf16[128,1792]{1,0:T(8,128)(2,1)S(1)} %get-tuple-element.89), channel_id=1, source_target_pairs={{0,1},{1,0},{2,3},{3,2},{4,5},{5,4},{6,7},{7,6},{8,9},{9,8},{10,11... | collective-permute-start | bytes 1376264 | tf_op jit(solution)/shard_map/ppermute | solution.py:34
  70.8 10.1 %collective-permute-start.4 = (bf16[128,1792]{1,0:T(8,128)(2,1)S(1)}, bf16[128,1792]{1,0:T(8,128)(2,1)S(1)}, u32[]{:S(2)}, u32[]{:S(2)}) collective-permute-start(bf16[128,1792]{1,0:T(8,128)(2,1)S(1)} %collective-permute-done), channel_id=1, source_target_pairs={{0,1},{1,0},{2,3},{3,2},{4,5},{5,4},{6,7},{7,6},{8,9},{9,8},{10,11... | collective-permute-start | bytes 1376264 | tf_op jit(solution)/shard_map/ppermute | solution.py:34
  70.8 8.5 %collective-permute-start.2 = (bf16[128,1792]{1,0:T(8,128)(2,1)S(1)}, bf16[128,1792]{1,0:T(8,128)(2,1)S(1)}, u32[]{:S(2)}, u32[]{:S(2)}) collective-permute-start(bf16[128,1792]{1,0:T(8,128)(2,1)S(1)} %collective-permute-done), channel_id=1, source_target_pairs={{0,4},{1,3},{2,6},{3,1},{4,0},{5,7},{6,2},{7,5},{8,12},{9,11},{10,... | collective-permute-start | bytes 1376264 | tf_op jit(solution)/shard_map/ppermute | solution.py:34
  71.5 10.2 %collective-permute-start.5 = (bf16[128,1792]{1,0:T(8,128)(2,1)S(1)}, bf16[128,1792]{1,0:T(8,128)(2,1)S(1)}, u32[]{:S(2)}, u32[]{:S(2)}) collective-permute-start(bf16[128,1792]{1,0:T(8,128)(2,1)S(1)} %collective-permute-done.1), channel_id=1, source_target_pairs={{0,1},{1,0},{2,3},{3,2},{4,5},{5,4},{6,7},{7,6},{8,9},{9,8},{10,11... | collective-permute-start | bytes 1376264 | tf_op jit(solution)/shard_map/ppermute | solution.py:34
  79.3 3.2 collective-permute-start.6
  83.3 20.2 %copy-start.2 = (s32[2,1,3]{2,1,0:T(1,128)S(1)}, s32[2,1,3]{2,1,0:T(1,128)}, u32[]{:S(2)}) copy-start(s32[2,1,3]{2,1,0:T(1,128)} %param.19) | copy-start | bytes 76
  110.8 38.0 %copy-start.16 = (bf16[1024,256]{1,0:T(8,128)(2,1)}, bf16[1024,256]{1,0:T(8,128)(2,1)S(1)}, u32[]{:S(2)}) copy-start(bf16[1024,256]{1,0:T(8,128)(2,1)S(1)} %fusion.45) | copy-start | bytes 1572868
  114.1 32.2 %collective-permute-start.7 = (bf16[512,1792]{1,0:T(8,128)(2,1)}, bf16[512,1792]{1,0:T(8,128)(2,1)}, u32[]{:S(2)}, u32[]{:S(2)}) collective-permute-start(bf16[512,1792]{1,0:T(8,128)(2,1)} %convolution_convert_fusion.3), channel_id=1, source_target_pairs={{0,1},{1,0},{2,3},{3,2},{4,5},{5,4},{6,7},{7,6},{8,9},{9,8},{10,11... | collective-permute-start | bytes 5505032 | tf_op jit(solution)/shard_map/ppermute | solution.py:34
  115.2 27.9 %all-to-all-start.3 = ((bf16[4,32,1792]{2,1,0:T(8,128)(2,1)}), bf16[4,32,1792]{2,1,0:T(8,128)(2,1)S(1)}, u32[]{:S(2)}, u32[]{:S(2)}) async-start(bf16[4,32,1792]{2,1,0:T(8,128)(2,1)} %bitcast.27), calls=%async_computation.3 | async-start | bytes 917504 | tf_op jit(solution)/shard_map/all_to_all | solution.py:342
  118.7 298.2 %reduce-scatter.7.cloned.1.call-start = ((), (), s32[]{:S(2)}) async-start(), calls=%async_computation.11 | async-start | bytes 4587520 | tf_op jit(solution)/shard_map/reduce_scatter | solution.py:420
  143.2 29.8 %collective-permute-start.24 = (bf16[128,1792]{1,0:T(8,128)(2,1)S(1)}, bf16[128,1792]{1,0:T(8,128)(2,1)S(1)}, u32[]{:S(2)}, u32[]{:S(2)}) collective-permute-start(bf16[128,1792]{1,0:T(8,128)(2,1)S(1)} %bitcast.176), channel_id=1, source_target_pairs={{0,1},{1,0},{2,3},{3,2},{4,5},{5,4},{6,7},{7,6},{8,9},{9,8},{10,11... | collective-permute-start | bytes 1376264 | tf_op jit(solution)/shard_map/ppermute | solution.py:34
  143.3 15.6 %collective-permute-start.22 = (bf16[128,1792]{1,0:T(8,128)(2,1)S(1)}, bf16[128,1792]{1,0:T(8,128)(2,1)S(1)}, u32[]{:S(2)}, u32[]{:S(2)}) collective-permute-start(bf16[128,1792]{1,0:T(8,128)(2,1)S(1)} %bitcast.177), channel_id=1, source_target_pairs={{0,4},{1,3},{2,6},{3,1},{4,0},{5,7},{6,2},{7,5},{8,12},{9,11},{10,... | collective-permute-start | bytes 1376264 | tf_op jit(solution)/shard_map/ppermute | solution.py:34
  144.8 13.5 %collective-permute-start.21 = (bf16[128,1792]{1,0:T(8,128)(2,1)S(1)}, bf16[128,1792]{1,0:T(8,128)(2,1)S(1)}, u32[]{:S(2)}, u32[]{:S(2)}) collective-permute-start(bf16[128,1792]{1,0:T(8,128)(2,1)S(1)} %bitcast.178), channel_id=1, source_target_pairs={{0,2},{1,5},{2,0},{3,7},{4,6},{5,1},{6,4},{7,3},{8,10},{9,13},{10,... | collective-permute-start | bytes 1376264 | tf_op jit(solution)/shard_map/ppermute | solution.py:34
  148.9 22.6 %collective-permute-start.8 = (bf16[256,1792]{1,0:T(8,128)(2,1)S(1)}, bf16[256,1792]{1,0:T(8,128)(2,1)S(1)}, u32[]{:S(2)}, u32[]{:S(2)}) collective-permute-start(bf16[256,1792]{1,0:T(8,128)(2,1)S(1)} %slice.625), channel_id=1, source_target_pairs={{0,4},{1,3},{2,6},{3,1},{4,0},{5,7},{6,2},{7,5},{8,12},{9,11},{10,... | collective-permute-start | bytes 2752520 | tf_op jit(solution)/shard_map/ppermute | solution.py:34
  158.3 14.7 %collective-permute-start.25 = (bf16[128,1792]{1,0:T(8,128)(2,1)S(1)}, bf16[128,1792]{1,0:T(8,128)(2,1)S(1)}, u32[]{:S(2)}, u32[]{:S(2)}) collective-permute-start(bf16[128,1792]{1,0:T(8,128)(2,1)S(1)} %collective-permute-done.21), channel_id=1, source_target_pairs={{0,1},{1,0},{2,3},{3,2},{4,5},{5,4},{6,7},{7,6},{8,9},{9,8},{10,11... | collective-permute-start | bytes 1376264 | tf_op jit(solution)/shard_map/ppermute | solution.py:34
  158.3 13.2 %collective-permute-start.23 = (bf16[128,1792]{1,0:T(8,128)(2,1)S(1)}, bf16[128,1792]{1,0:T(8,128)(2,1)S(1)}, u32[]{:S(2)}, u32[]{:S(2)}) collective-permute-start(bf16[128,1792]{1,0:T(8,128)(2,1)S(1)} %collective-permute-done.21), channel_id=1, source_target_pairs={{0,4},{1,3},{2,6},{3,1},{4,0},{5,7},{6,2},{7,5},{8,12},{9,11},{10,... | collective-permute-start | bytes 1376264 | tf_op jit(solution)/shard_map/ppermute | solution.py:34
  159.0 25.2 %collective-permute-start.26 = (bf16[128,1792]{1,0:T(8,128)(2,1)S(1)}, bf16[128,1792]{1,0:T(8,128)(2,1)S(1)}, u32[]{:S(2)}, u32[]{:S(2)}) collective-permute-start(bf16[128,1792]{1,0:T(8,128)(2,1)S(1)} %collective-permute-done.22), channel_id=1, source_target_pairs={{0,1},{1,0},{2,3},{3,2},{4,5},{5,4},{6,7},{7,6},{8,9},{9,8},{10,11... | collective-permute-start | bytes 1376264 | tf_op jit(solution)/shard_map/ppermute | solution.py:34
  171.5 12.7 %collective-permute-start.27 = (bf16[128,1792]{1,0:T(8,128)(2,1)S(1)}, bf16[128,1792]{1,0:T(8,128)(2,1)S(1)}, u32[]{:S(2)}, u32[]{:S(2)}) collective-permute-start(bf16[128,1792]{1,0:T(8,128)(2,1)S(1)} %collective-permute-done.23), channel_id=1, source_target_pairs={{0,1},{1,0},{2,3},{3,2},{4,5},{5,4},{6,7},{7,6},{8,9},{9,8},{10,11... | collective-permute-start | bytes 1376264 | tf_op jit(solution)/shard_map/ppermute | solution.py:34
  171.7 8.5 %collective-permute-start.9 = (bf16[128,1792]{1,0:T(8,128)(2,1)S(1)}, bf16[128,1792]{1,0:T(8,128)(2,1)S(1)}, u32[]{:S(2)}, u32[]{:S(2)}) collective-permute-start(bf16[128,1792]{1,0:T(8,128)(2,1)S(1)} %slice.629), channel_id=1, source_target_pairs={{0,2},{1,5},{2,0},{3,7},{4,6},{5,1},{6,4},{7,3},{8,10},{9,13},{10,... | collective-permute-start | bytes 1376264 | tf_op jit(solution)/shard_map/ppermute | solution.py:34
  181.5 14.4 %collective-permute-start.11 = (bf16[128,1792]{1,0:T(8,128)(2,1)S(1)}, bf16[128,1792]{1,0:T(8,128)(2,1)S(1)}, u32[]{:S(2)}, u32[]{:S(2)}) collective-permute-start(bf16[128,1792]{1,0:T(8,128)(2,1)S(1)} %get-tuple-element.45), channel_id=1, source_target_pairs={{0,4},{1,3},{2,6},{3,1},{4,0},{5,7},{6,2},{7,5},{8,12},{9,11},{10,... | collective-permute-start | bytes 1376264 | tf_op jit(solution)/shard_map/ppermute | solution.py:34
  183.0 10.7 %collective-permute-start.10 = (bf16[128,1792]{1,0:T(8,128)(2,1)S(1)}, bf16[128,1792]{1,0:T(8,128)(2,1)S(1)}, u32[]{:S(2)}, u32[]{:S(2)}) collective-permute-start(bf16[128,1792]{1,0:T(8,128)(2,1)S(1)} %get-tuple-element.45), channel_id=1, source_target_pairs={{0,2},{1,5},{2,0},{3,7},{4,6},{5,1},{6,4},{7,3},{8,10},{9,13},{10,... | collective-permute-start | bytes 1376264 | tf_op jit(solution)/shard_map/ppermute | solution.py:34
  184.2 21.9 %copy-start.19 = (bf16[1024,1792]{1,0:T(8,128)(2,1)}, bf16[1024,1792]{1,0:T(8,128)(2,1)S(1)}, u32[]{:S(2)}) copy-start(bf16[1024,1792]{1,0:T(8,128)(2,1)S(1)} %constant_dynamic-update-slice_fusion.16) | copy-start | bytes 11010052
  184.2 19.5 %collective-permute-start.13 = (bf16[128,1792]{1,0:T(8,128)(2,1)S(1)}, bf16[128,1792]{1,0:T(8,128)(2,1)S(1)}, u32[]{:S(2)}, u32[]{:S(2)}) collective-permute-start(bf16[128,1792]{1,0:T(8,128)(2,1)S(1)} %get-tuple-element.45), channel_id=1, source_target_pairs={{0,1},{1,0},{2,3},{3,2},{4,5},{5,4},{6,7},{7,6},{8,9},{9,8},{10,11... | collective-permute-start | bytes 1376264 | tf_op jit(solution)/shard_map/ppermute | solution.py:34
  193.7 10.9 %collective-permute-start.14 = (bf16[128,1792]{1,0:T(8,128)(2,1)S(1)}, bf16[128,1792]{1,0:T(8,128)(2,1)S(1)}, u32[]{:S(2)}, u32[]{:S(2)}) collective-permute-start(bf16[128,1792]{1,0:T(8,128)(2,1)S(1)} %collective-permute-done.10), channel_id=1, source_target_pairs={{0,1},{1,0},{2,3},{3,2},{4,5},{5,4},{6,7},{7,6},{8,9},{9,8},{10,11... | collective-permute-start | bytes 1376264 | tf_op jit(solution)/shard_map/ppermute | solution.py:34
  194.5 8.5 %collective-permute-start.12 = (bf16[128,1792]{1,0:T(8,128)(2,1)S(1)}, bf16[128,1792]{1,0:T(8,128)(2,1)S(1)}, u32[]{:S(2)}, u32[]{:S(2)}) collective-permute-start(bf16[128,1792]{1,0:T(8,128)(2,1)S(1)} %collective-permute-done.10), channel_id=1, source_target_pairs={{0,4},{1,3},{2,6},{3,1},{4,0},{5,7},{6,2},{7,5},{8,12},{9,11},{10,... | collective-permute-start | bytes 1376264 | tf_op jit(solution)/shard_map/ppermute | solution.py:34
  195.9 9.4 %collective-permute-start.15 = (bf16[128,1792]{1,0:T(8,128)(2,1)S(1)}, bf16[128,1792]{1,0:T(8,128)(2,1)S(1)}, u32[]{:S(2)}, u32[]{:S(2)}) collective-permute-start(bf16[128,1792]{1,0:T(8,128)(2,1)S(1)} %collective-permute-done.11), channel_id=1, source_target_pairs={{0,1},{1,0},{2,3},{3,2},{4,5},{5,4},{6,7},{7,6},{8,9},{9,8},{10,11... | collective-permute-start | bytes 1376264 | tf_op jit(solution)/shard_map/ppermute | solution.py:34
  203.0 3.2 collective-permute-start.16
  230.9 8.5 %copy-start.25 = (bf16[1792,1920]{1,0:T(8,128)(2,1)S(1)}, bf16[1792,1920]{1,0:T(8,128)(2,1)}, u32[]{:S(2)}) copy-start(bf16[1792,1920]{1,0:T(8,128)(2,1)} %all-gather.9.cloned.1.call-done) | copy-start | bytes 20643844
  243.2 10.8 %copy-start.26 = (bf16[1024,640]{1,0:T(8,128)(2,1)}, bf16[1024,640]{1,0:T(8,128)(2,1)S(1)}, u32[]{:S(2)}) copy-start(bf16[1024,640]{1,0:T(8,128)(2,1)S(1)} %get-tuple-element.80) | copy-start | bytes 3932164
  245.8 3.9 collective-permute-start.28
  247.5 6.5 collective-permute-start.17
  252.5 13.5 %collective-permute-start.29 = (bf16[256,1792]{1,0:T(8,128)(2,1)S(1)}, bf16[256,1792]{1,0:T(8,128)(2,1)S(1)}, u32[]{:S(2)}, u32[]{:S(2)}) collective-permute-start(bf16[256,1792]{1,0:T(8,128)(2,1)S(1)} %slice.623), channel_id=1, source_target_pairs={{0,4},{1,3},{2,6},{3,1},{4,0},{5,7},{6,2},{7,5},{8,12},{9,11},{10,... | collective-permute-start | bytes 2752520 | tf_op jit(solution)/shard_map/ppermute | solution.py:34
  255.7 24.9 %collective-permute-start.18 = (bf16[256,1792]{1,0:T(8,128)(2,1)S(1)}, bf16[256,1792]{1,0:T(8,128)(2,1)S(1)}, u32[]{:S(2)}, u32[]{:S(2)}) collective-permute-start(bf16[256,1792]{1,0:T(8,128)(2,1)S(1)} %slice.624), channel_id=1, source_target_pairs={{0,4},{1,3},{2,6},{3,1},{4,0},{5,7},{6,2},{7,5},{8,12},{9,11},{10,... | collective-permute-start | bytes 2752520 | tf_op jit(solution)/shard_map/ppermute | solution.py:34
  266.1 23.3 %copy-start.11 = (bf16[4,32,1792]{2,1,0:T(8,128)(2,1)S(1)}, bf16[4,32,1792]{2,1,0:T(8,128)(2,1)}, u32[]{:S(2)}) copy-start(bf16[4,32,1792]{2,1,0:T(8,128)(2,1)} %copy-done.10) | copy-start | bytes 1376260
  266.2 16.3 %collective-permute-start.30 = (bf16[128,1792]{1,0:T(8,128)(2,1)S(1)}, bf16[128,1792]{1,0:T(8,128)(2,1)S(1)}, u32[]{:S(2)}, u32[]{:S(2)}) collective-permute-start(bf16[128,1792]{1,0:T(8,128)(2,1)S(1)} %slice.627), channel_id=1, source_target_pairs={{0,2},{1,5},{2,0},{3,7},{4,6},{5,1},{6,4},{7,3},{8,10},{9,13},{10,... | collective-permute-start | bytes 1376264 | tf_op jit(solution)/shard_map/ppermute | solution.py:34
  280.9 8.5 %collective-permute-start.19 = (bf16[128,1792]{1,0:T(8,128)(2,1)S(1)}, bf16[128,1792]{1,0:T(8,128)(2,1)S(1)}, u32[]{:S(2)}, u32[]{:S(2)}) collective-permute-start(bf16[128,1792]{1,0:T(8,128)(2,1)S(1)} %slice.628), channel_id=1, source_target_pairs={{0,2},{1,5},{2,0},{3,7},{4,6},{5,1},{6,4},{7,3},{8,10},{9,13},{10,... | collective-permute-start | bytes 1376264 | tf_op jit(solution)/shard_map/ppermute | solution.py:34
  290.7 20.9 %copy-start.3 = (f32[128,1792]{1,0:T(8,128)}, f32[128,1792]{1,0:T(8,128)S(1)}, u32[]{:S(2)}) copy-start(f32[128,1792]{1,0:T(8,128)S(1)} %get-tuple-element.86) | copy-start | bytes 2752516
  290.8 24.3 %copy-start.17 = (bf16[1024,256]{1,0:T(8,128)(2,1)S(1)}, bf16[1024,256]{1,0:T(8,128)(2,1)}, u32[]{:S(2)}) copy-start(bf16[1024,256]{1,0:T(8,128)(2,1)} %copy-done.16) | copy-start | bytes 1572868
  290.8 12.1 %collective-permute-start.31 = (bf16[128,1792]{1,0:T(8,128)(2,1)S(1)}, bf16[128,1792]{1,0:T(8,128)(2,1)S(1)}, u32[]{:S(2)}, u32[]{:S(2)}) collective-permute-start(bf16[128,1792]{1,0:T(8,128)(2,1)S(1)} %get-tuple-element.43), channel_id=1, source_target_pairs={{0,2},{1,5},{2,0},{3,7},{4,6},{5,1},{6,4},{7,3},{8,10},{9,13},{10,... | collective-permute-start | bytes 1376264 | tf_op jit(solution)/shard_map/ppermute | solution.py:34
  292.3 11.2 %collective-permute-start.32 = (bf16[128,1792]{1,0:T(8,128)(2,1)S(1)}, bf16[128,1792]{1,0:T(8,128)(2,1)S(1)}, u32[]{:S(2)}, u32[]{:S(2)}) collective-permute-start(bf16[128,1792]{1,0:T(8,128)(2,1)S(1)} %get-tuple-element.43), channel_id=1, source_target_pairs={{0,4},{1,3},{2,6},{3,1},{4,0},{5,7},{6,2},{7,5},{8,12},{9,11},{10,... | collective-permute-start | bytes 1376264 | tf_op jit(solution)/shard_map/ppermute | solution.py:34
  293.9 17.6 %collective-permute-start.34 = (bf16[128,1792]{1,0:T(8,128)(2,1)S(1)}, bf16[128,1792]{1,0:T(8,128)(2,1)S(1)}, u32[]{:S(2)}, u32[]{:S(2)}) collective-permute-start(bf16[128,1792]{1,0:T(8,128)(2,1)S(1)} %get-tuple-element.43), channel_id=1, source_target_pairs={{0,1},{1,0},{2,3},{3,2},{4,5},{5,4},{6,7},{7,6},{8,9},{9,8},{10,11... | collective-permute-start | bytes 1376264 | tf_op jit(solution)/shard_map/ppermute | solution.py:34
  302.9 8.6 %collective-permute-start.35 = (bf16[128,1792]{1,0:T(8,128)(2,1)S(1)}, bf16[128,1792]{1,0:T(8,128)(2,1)S(1)}, u32[]{:S(2)}, u32[]{:S(2)}) collective-permute-start(bf16[128,1792]{1,0:T(8,128)(2,1)S(1)} %collective-permute-done.31), channel_id=1, source_target_pairs={{0,1},{1,0},{2,3},{3,2},{4,5},{5,4},{6,7},{7,6},{8,9},{9,8},{10,11... | collective-permute-start | bytes 1376264 | tf_op jit(solution)/shard_map/ppermute | solution.py:34
  302.9 8.5 %collective-permute-start.33 = (bf16[128,1792]{1,0:T(8,128)(2,1)S(1)}, bf16[128,1792]{1,0:T(8,128)(2,1)S(1)}, u32[]{:S(2)}, u32[]{:S(2)}) collective-permute-start(bf16[128,1792]{1,0:T(8,128)(2,1)S(1)} %collective-permute-done.31), channel_id=1, source_target_pairs={{0,4},{1,3},{2,6},{3,1},{4,0},{5,7},{6,2},{7,5},{8,12},{9,11},{10,... | collective-permute-start | bytes 1376264 | tf_op jit(solution)/shard_map/ppermute | solution.py:34
  303.5 8.0 %collective-permute-start.36 = (bf16[128,1792]{1,0:T(8,128)(2,1)S(1)}, bf16[128,1792]{1,0:T(8,128)(2,1)S(1)}, u32[]{:S(2)}, u32[]{:S(2)}) collective-permute-start(bf16[128,1792]{1,0:T(8,128)(2,1)S(1)} %collective-permute-done.32), channel_id=1, source_target_pairs={{0,1},{1,0},{2,3},{3,2},{4,5},{5,4},{6,7},{7,6},{8,9},{9,8},{10,11... | collective-permute-start | bytes 1376264 | tf_op jit(solution)/shard_map/ppermute | solution.py:34
  311.4 1.8 collective-permute-start.37
  351.1 188.7 %reduce-scatter.9.cloned.1.call-start = ((), (), s32[]{:S(2)}) async-start(), calls=%async_computation.12 | async-start | bytes 8601600 | tf_op jit(solution)/shard_map/reduce_scatter | solution.py:397
  381.0 158.8 %copy-start.29 = (bf16[1024,768]{1,0:T(8,128)(2,1)S(1)}, bf16[1024,768]{1,0:T(8,128)(2,1)}, u32[]{:S(2)}) copy-start(bf16[1024,768]{1,0:T(8,128)(2,1)} %copy-done.28) | copy-start | bytes 4718596
  381.0 310.8 %all-gather.11.cloned.1.call-start = ((), (), s32[]{:S(2)}) async-start(), calls=%async_computation.9 | async-start | bytes 4587520 | tf_op jit(solution)/shard_map/all_gather | solution.py:441
  416.9 282.6 %all-gather.13.cloned.1.call-start = ((), (), s32[]{:S(2)}) async-start(), calls=%async_computation.10 | async-start | bytes 8601600 | tf_op jit(solution)/shard_map/all_gather | solution.py:440
  543.4 3.9 collective-permute-start.38
  550.8 22.0 %collective-permute-start.39 = (bf16[256,1792]{1,0:T(8,128)(2,1)S(1)}, bf16[256,1792]{1,0:T(8,128)(2,1)}, u32[]{:S(2)}, u32[]{:S(2)}) collective-permute-start(bf16[256,1792]{1,0:T(8,128)(2,1)S(1)} %slice.622), channel_id=1, source_target_pairs={{0,4},{1,3},{2,6},{3,1},{4,0},{5,7},{6,2},{7,5},{8,12},{9,11},{10,... | collective-permute-start | bytes 2752520 | tf_op jit(solution)/shard_map/ppermute | solution.py:34
  552.3 25.3 %all-to-all-start.2 = ((bf16[4,32,1792]{2,1,0:T(8,128)(2,1)}), bf16[4,32,1792]{2,1,0:T(8,128)(2,1)}, u32[]{:S(2)}, u32[]{:S(2)}) async-start(bf16[4,32,1792]{2,1,0:T(8,128)(2,1)} %bitcast.23), calls=%async_computation.2 | async-start | bytes 917504 | tf_op jit(solution)/shard_map/all_to_all | solution.py:345
  575.9 18.5 %collective-permute-start.40 = (bf16[128,1792]{1,0:T(8,128)(2,1)}, bf16[128,1792]{1,0:T(8,128)(2,1)S(1)}, u32[]{:S(2)}, u32[]{:S(2)}) collective-permute-start(bf16[128,1792]{1,0:T(8,128)(2,1)} %slice.626), channel_id=1, source_target_pairs={{0,2},{1,5},{2,0},{3,7},{4,6},{5,1},{6,4},{7,3},{8,10},{9,13},{10,... | collective-permute-start | bytes 1376264 | tf_op jit(solution)/shard_map/ppermute | solution.py:34
  577.6 24.3 %collective-permute-start.20 = (bf16[128,1792]{1,0:T(8,128)(2,1)}, bf16[128,1792]{1,0:T(8,128)(2,1)}, u32[]{:S(2)}, u32[]{:S(2)}) collective-permute-start(bf16[128,1792]{1,0:T(8,128)(2,1)} %bitcast.24), channel_id=1, source_target_pairs={{0,1},{1,0},{2,3},{3,2},{4,5},{5,4},{6,7},{7,6},{8,9},{9,8},{10,11... | collective-permute-start | bytes 1376264 | tf_op jit(solution)/shard_map/ppermute | solution.py:34
  597.1 16.5 %all-to-all-start.4 = ((bf16[4,32,1792]{2,1,0:T(8,128)(2,1)}), bf16[4,32,1792]{2,1,0:T(8,128)(2,1)S(1)}, u32[]{:S(2)}, u32[]{:S(2)}) async-start(bf16[4,32,1792]{2,1,0:T(8,128)(2,1)} %bitcast.29), calls=%async_computation.4 | async-start | bytes 917504 | tf_op jit(solution)/shard_map/all_to_all | solution.py:345
  613.6 76.8 %collective-permute-start.41 = (bf16[128,1792]{1,0:T(8,128)(2,1)S(1)}, bf16[128,1792]{1,0:T(8,128)(2,1)S(1)}, u32[]{:S(2)}, u32[]{:S(2)}) collective-permute-start(bf16[128,1792]{1,0:T(8,128)(2,1)S(1)} %bitcast.181), channel_id=1, source_target_pairs={{0,1},{1,0},{2,3},{3,2},{4,5},{5,4},{6,7},{7,6},{8,9},{9,8},{10,11... | collective-permute-start | bytes 1376264 | tf_op jit(solution)/shard_map/ppermute | solution.py:34
  688.5 1.2 collective-permute-start.42
  (24 other events, 109.7 us)
Sparse Core Ops, SparseCore 0:
  11.2 84.7 all-gather.6
  97.6 133.3 all-gather.8
  351.2 65.6 reduce-scatter.6
  419.1 120.6 reduce-scatter.8
  541.6 58.5 all-gather.10
  602.0 76.9 all-gather.12

commit v2 on v1

--- a/solution.py
+++ b/solution.py
@@ -1,3 +1,4 @@
+import functools
 import math
 
 import jax
@@ -48,6 +49,27 @@
         half = total.shape[0] // 2
         total = total[:half] + flipped(total[half:].astype(bf16), sizes, step).astype(f32)
     return total
+
+
+def after(value, *others):
+    return lax.optimization_barrier((value,) + others)[0]
+
+
+def z_shifted(value, sizes, steps):
+    n = sizes[0]
+    return lax.ppermute(value, "fsdp", [(i, (i + steps) % n) for i in range(n)])
+
+
+def z_exchange(blocks, sizes):
+    got = [blocks[0]] + [z_shifted(blocks[k], sizes, k) for k in range(1, sizes[0])]
+    return jnp.concatenate(got)
+
+
+def ctx_shares(own, sizes, core):
+    one = flipped(own, sizes, 0)
+    two = flipped(own, sizes, 1)
+    three = flipped(one, sizes, 1)
+    return [own, jnp.where(core == 0, one, two), jnp.where(core == 0, two, one), three]
 
 
 def product(left, right, dims, out_type=f32):
@@ -201,6 +223,76 @@
         grad_conv_ref[lag : lag + 1, :] = conv_sums[lag]
 
 
+def weight_grad_kernel(*refs):
+    out_ref = refs[-1]
+    at = 0
+    for left_ref, right_ref in zip(refs[:-1:2], refs[1:-1:2]):
+        width = right_ref.shape[1]
+        out_ref[:, at : at + width] = product(left_ref[...], right_ref[...], TN, bf16)
+        at += width
+
+
+def weight_grad(*pairs, step=256):
+    rows, d_model = pairs[0][0].shape
+    width = sum(right.shape[1] for _, right in pairs)
+    specs = []
+    for left, right in pairs:
+        specs.append(pl.BlockSpec((rows, step), lambda i: (0, i)))
+        specs.append(pl.BlockSpec((rows, right.shape[1]), lambda i: (0, 0)))
+    return pl.pallas_call(
+        weight_grad_kernel,
+        grid=(d_model // step,),
+        out_shape=jax.ShapeDtypeStruct((d_model, width), bf16),
+        in_specs=specs,
+        out_specs=pl.BlockSpec((step, width), lambda i: (i, 0)),
+        compiler_params=pltpu.CompilerParams(vmem_limit_bytes=40 * 1024 * 1024),
+        cost_estimate=pl.CostEstimate(
+            flops=2 * rows * d_model * width,
+            bytes_accessed=2 * (rows * d_model * len(pairs) + (rows + d_model) * width),
+            transcendentals=0,
+        ),
+        name="weight_grad",
+    )(*[operand for pair in pairs for operand in pair])
+
+
+def placed_kernel(each, total, counts, index_ref, *refs):
+    n_parts = len(refs) - len(counts)
+    outs = refs[n_parts:]
+    for piece in range(n_parts):
+        start = min(piece * each, total - each)
+        shared = piece * each - start
+        for k in range(n_parts):
+
+            @pl.when((index_ref[0] ^ k) == piece)
+            def _():
+                at = 0
+                for out, count in zip(outs, counts):
+                    for i in range(count):
+                        part = refs[k][:, at + shared : at + each].astype(f32)
+                        at += each
+                        out[i, :, start + shared : start + each] = part
+
+
+def placed(parts, index, each, total, counts, steps):
+    rows = parts[0].shape[0]
+    block = rows // steps
+    out_shape = [jax.ShapeDtypeStruct((count, rows, total), f32) for count in counts]
+    out_specs = [pl.BlockSpec((count, block, total), lambda i: (0, i, 0)) for count in counts]
+    width = parts[0].shape[1]
+    return pl.pallas_call(
+        functools.partial(placed_kernel, each, total, counts),
+        grid=(steps,),
+        out_shape=out_shape,
+        in_specs=[SMEM] + [pl.BlockSpec((block, width), lambda i: (i, 0))] * len(parts),
+        out_specs=out_specs,
+        compiler_params=pltpu.CompilerParams(vmem_limit_bytes=40 * 1024 * 1024),
+        cost_estimate=pl.CostEstimate(
+            flops=0, bytes_accessed=rows * width * len(parts) * 6, transcendentals=0
+        ),
+        name="placed",
+    )(index.reshape(1).astype(jnp.int32), *parts)
+
+
 VMEM = pl.BlockSpec(memory_space=pltpu.VMEM)
 SMEM = pl.BlockSpec(memory_space=pltpu.SMEM)
 
@@ -244,12 +336,12 @@
     return start, index * each - start
 
 
-def joined(parts, total, each, axis):
+def joined(parts, total, each):
     pieces = []
     for index, part in enumerate(parts):
-        shared = index * each - min(index * each, total - each)
-        pieces.append(lax.slice_in_dim(part, shared, each, axis=axis))
-    return jnp.concatenate(pieces, axis=axis)
+        start = min(index * each, total - each)
+        pieces.append(part[:, index * each - start :])
+    return jnp.concatenate(pieces, axis=1)
 
 
 def per_device(
@@ -291,9 +383,9 @@
     down_part = jnp.where(jnp.arange(ff)[:, None] >= ff_shared, down_part, jnp.zeros_like(down_part))
     mlp_own = jnp.concatenate([sliced[0], sliced[1], down_part.T], axis=1)
     attn_w = lax.all_gather(attn_own, "fsdp", axis=0, tiled=True)
-    mlp_w = lax.all_gather(mlp_own, "fsdp", axis=0, tiled=True)
+    mlp_w = lax.all_gather(after(mlp_own, attn_own), "fsdp", axis=0, tiled=True)
+    gate_w, down_w = mlp_w[:, : 2 * ff], mlp_w[:, 2 * ff :]
     qkv_w, out_w = attn_w[:, : 3 * width], attn_w[:, 3 * width :]
-    gate_w, down_w = mlp_w[:, : 2 * ff], mlp_w[:, 2 * ff :]
 
     small = jnp.concatenate(
         [
@@ -302,6 +394,7 @@
             conv_weight.reshape(-1).astype(f32),
         ]
     )
+    small = after(small, attn_own)
     small = lax.all_to_all(
         jnp.broadcast_to(small[None], (workers,) + small.shape),
         ("fsdp", "ctx"),
@@ -328,7 +421,7 @@
     slot = jnp.sum(
         ((to_plane[:, None, :] == to_plane[:, :, None]) & earlier[None]).astype(jnp.int32), axis=2
     )
-    place = ((slot // half) * n_fsdp + to_plane) * (BATCHES * half) + slot % half
+    place = ((slot // half) * n_fsdp + (to_plane - f) % n_fsdp) * (BATCHES * half) + slot % half
     place = place + jnp.arange(BATCHES, dtype=jnp.int32)[:, None] * half
     place = place.reshape(-1)
     sent_rows = BATCHES * tok_rows // n_tp
@@ -339,15 +432,17 @@
 
     def to_planes(rows):
         picked = product(choose, rows.reshape(-1, d_model), NN, bf16)
-        return lax.all_to_all(picked, "fsdp", split_axis=0, concat_axis=0, tiled=True)
+        return z_exchange(jnp.split(picked, n_fsdp), sizes)
 
     def to_given(rows):
-        home = lax.all_to_all(rows, "fsdp", split_axis=0, concat_axis=0, tiled=True)
+        blocks = jnp.split(rows, n_fsdp)
+        home = jnp.concatenate(
+            [blocks[0]] + [z_shifted(blocks[k], sizes, n_fsdp - k) for k in range(1, n_fsdp)]
+        )
         pair = jnp.concatenate([home, flipped(home, sizes, 2)])
         return product(undo, pair, NN, bf16).reshape(BATCHES, tok_rows, d_model)
 
     own_x = to_planes(tokens).astype(f32)
-    own_g = to_planes(cotangent)
 
     dealt = lax.dynamic_slice_in_dim(orders, f * n_ctx, n_ctx, 0)
     dealt = jnp.transpose(dealt, (1, 0, 2)).reshape(BATCHES, group)
@@ -362,24 +457,27 @@
     away = (giver % n_ctx) ^ c
     swapped = jnp.where(core == 0, away, (away % 2) * 2 + away // 2)
     block = jnp.where(core == t, 0, n_ctx) + swapped
-    arrival = block * (plane // (n_ctx * n_tp)) + (giver // n_ctx) * (BATCHES * half)
+    arrival = block * (plane // (n_ctx * n_tp)) + (f - giver // n_ctx) % n_fsdp * (BATCHES * half)
     arrival = arrival + jnp.arange(BATCHES, dtype=jnp.int32)[:, None] * half + rank % half
     deal = (arrival.reshape(-1)[:, None] == jnp.arange(plane, dtype=jnp.int32)[None, :]).astype(bf16)
 
     first_scale = lax.rsqrt(jnp.mean(own_x * own_x, axis=-1, keepdims=True) + epsilon)
     hidden = plane_gather((own_x * first_scale * gains[0]).astype(bf16), sizes)
     own_lengths = lengths[:, 0]
+    own_g = to_planes(after(cotangent, hidden))
     qkv = product(deal, product(hidden, qkv_w, NN, bf16), NN, bf16)
+    grad_dealt = plane_gather(after(own_g, qkv), sizes)
     attended = product(deal, attend_forward(own_lengths, qkv, conv), TN, bf16)
     kept = plane // 2
     branch = plane_scatter(
-        product(attended[:kept], out_w, NT), product(attended[kept:], out_w, NT, bf16), sizes
+        product(attended[:kept], out_w, NT),
+        product(attended[kept:], out_w, NT, bf16),
+        sizes,
     )
     resid = own_x + branch
 
     second_scale = lax.rsqrt(jnp.mean(resid * resid, axis=-1, keepdims=True) + epsilon)
     hidden_two = plane_gather((resid * second_scale * gains[1]).astype(bf16), sizes)
-    grad_dealt = plane_gather(own_g, sizes)
     grad_inner = product(grad_dealt, down_w, NN)
     gate_up_out = product(hidden_two, gate_w, NN)
     gate_act, upper = gate_up_out[:, :ff], gate_up_out[:, ff:]
@@ -388,68 +486,85 @@
     inner = (silu * upper).astype(bf16)
     grad_gate = grad_inner * upper * (sigmoid * (1.0 + gate_act * (1.0 - sigmoid)))
     grad_pair = jnp.concatenate([grad_gate, grad_inner * silu], axis=1).astype(bf16)
+    grad_mlp_w = weight_grad((hidden_two, grad_pair), (grad_dealt, inner))
+    grad_mlp = lax.psum_scatter(grad_mlp_w, "fsdp", scatter_dimension=0, tiled=True)
+    grad_pair = after(grad_pair, grad_mlp_w)
     grad_two = plane_scatter(
-        product(grad_pair[:kept], gate_w, NT), product(grad_pair[kept:], gate_w, NT, bf16), sizes
-    )
-    grad_mlp = jnp.concatenate(
-        [product(hidden_two, grad_pair, TN, bf16), product(grad_dealt, inner, TN, bf16)], axis=1
-    )
-    grad_mlp = lax.psum_scatter(grad_mlp, "fsdp", scatter_dimension=0, tiled=True)
+        product(grad_pair[:kept], gate_w, NT),
+        product(grad_pair[kept:], gate_w, NT, bf16),
+        sizes,
+    )
     lifted = plane_scatter(
-        product(inner[:kept], down_w, NT), product(inner[kept:], down_w, NT, bf16), sizes
-    )
-    activations = to_given((resid + lifted).astype(bf16))
-
+        product(inner[:kept], down_w, NT),
+        product(inner[kept:], down_w, NT, bf16),
+        sizes,
+    )
     normed = resid * second_scale
     scaled = grad_two * gains[1]
     grad_resid = own_g.astype(f32) + second_scale * (
         scaled - normed * jnp.mean(scaled * normed, axis=-1, keepdims=True)
     )
-    grad_gain_two = jnp.sum(grad_two * normed, axis=0)
-
-    grad_branch = plane_gather(grad_resid.astype(bf16), sizes)
+
+    grad_branch = plane_gather(
+        after(grad_resid.astype(bf16), lifted), sizes
+    )
     grad_attended = product(deal, product(grad_branch, out_w, NN, bf16), NN, bf16)
     grad_proj, grad_conv = attend_backward(own_lengths, qkv, grad_attended, conv)
     grad_proj = product(deal, grad_proj, TN, bf16)
+    grad_attn_w = weight_grad((hidden, grad_proj), (grad_branch, attended))
+    grad_attn = lax.psum_scatter(grad_attn_w, "fsdp", scatter_dimension=0, tiled=True)
+    grad_proj = after(grad_proj, grad_attn_w)
     grad_hidden = plane_scatter(
         product(grad_proj[:kept], qkv_w, NT), product(grad_proj[kept:], qkv_w, NT, bf16), sizes
     )
-    grad_attn = jnp.concatenate(
-        [product(hidden, grad_proj, TN, bf16), product(grad_branch, attended, TN, bf16)], axis=1
-    )
-    grad_attn = lax.psum_scatter(grad_attn, "fsdp", scatter_dimension=0, tiled=True)
-
     normed = own_x * first_scale
     scaled = grad_hidden * gains[0]
     grad_x = grad_resid + first_scale * (
         scaled - normed * jnp.mean(scaled * normed, axis=-1, keepdims=True)
     )
-    grad_gain_one = jnp.sum(grad_hidden * normed, axis=0)
     input_grad = to_given(grad_x.astype(bf16))
 
-    placed = lax.dynamic_update_slice(jnp.zeros((CONV, heads_all), f32), grad_conv, (0, start))
-    placed = jnp.where(jnp.arange(heads_all)[None, :] >= start + shared, placed, 0.0)
-    sums = jnp.concatenate([placed.reshape(-1), grad_gain_one, grad_gain_two])
-    sums = lax.psum(sums, ("fsdp", "ctx"))
-    grad_conv = sums[: CONV * heads_all].reshape(CONV, heads_all)
-    grad_conv = lax.dynamic_slice_in_dim(grad_conv, f * (heads_all // n_fsdp), heads_all // n_fsdp, 1)
-    gain_sums = sums[CONV * heads_all :]
-    gain_sums = gain_sums + flipped(gain_sums, sizes, 2)
-    grad_gains = lax.dynamic_slice_in_dim(gain_sums.reshape(2, d_model), f * d_own, d_own, 1)
-
-    grad_mlp = lax.all_gather(grad_mlp, "ctx", axis=0).astype(f32)
-    grad_attn = lax.all_gather(grad_attn, "ctx", axis=0).astype(f32)
-    in_parts = [jnp.stack([grad_attn[k][:, i * width : (i + 1) * width] for i in range(3)]) for k in range(n_ctx)]
-    gate_parts = [jnp.stack([grad_mlp[k][:, i * ff : (i + 1) * ff] for i in range(2)]) for k in range(n_ctx)]
-    out_parts = [grad_attn[k][:, 3 * width :].T for k in range(n_ctx)]
-    down_parts = [grad_mlp[k][:, 2 * ff :].T for k in range(n_ctx)]
+    activations = to_given((resid + lifted).astype(bf16))
+
+    if n_fsdp > 4:
+        taps = lax.psum(grad_conv, "fsdp")
+    else:
+        taps = sum([z_shifted(grad_conv, sizes, k) for k in range(1, n_fsdp)], grad_conv)
+
+    steps = 4 if d_own % 64 == 0 else 1
+    grad_gate_up, grad_down = placed(
+        ctx_shares(grad_mlp, sizes, t), c, ff, ff_all, (2, 1), steps
+    )
+
+    def gain_part(own, grad, each, skipped):
+        columns = own.shape[1]
+        counted = (jnp.arange(columns) % each) >= skipped
+        terms = own.astype(f32) * grad[:, :columns].astype(f32)
+        return jnp.sum(jnp.where(counted[None, :], terms, 0.0), axis=1)
+
+    grad_attn, taps = after((grad_attn, taps), grad_down)
+    sums = jnp.stack(
+        [
+            gain_part(attn_own[:, : 3 * width], grad_attn, width, shared),
+            gain_part(mlp_own[:, : 2 * ff], grad_mlp, ff, ff_shared),
+        ]
+    )
+    for step in (2, 0, 1):
+        sums = sums + flipped(sums, sizes, step)
+    grad_gains = sums / norm_gains.astype(f32)
+    taps = ctx_shares(taps, sizes, t)
+    taps = lax.switch(c, [lambda k=k: joined([taps[k ^ p] for p in range(n_ctx)], heads_all, width) for k in range(n_ctx)])
+    grad_conv = lax.dynamic_slice_in_dim(taps, f * (heads_all // n_fsdp), heads_all // n_fsdp, 1)
+    grad_attn_in, grad_attn_out = placed(
+        ctx_shares(grad_attn, sizes, t), c, width, heads_all, (3, 1), steps
+    )
     return (
         activations,
         input_grad,
-        joined(in_parts, heads_all, width, 2),
-        joined(out_parts, heads_all, width, 0),
-        joined(gate_parts, ff_all, ff, 2),
-        joined(down_parts, ff_all, ff, 0),
+        grad_attn_in,
+        grad_attn_out[0].T,
+        grad_gate_up,
+        grad_down[0].T,
         grad_conv[None],
         grad_gains,
     )

time: 739 us -> 519 us (0.70)
  waiting for transfers between devices: 395 us -> 256 us
  blocking collectives: 74.9 us -> 0 us
  Pallas kernels: 19.9 us -> 47.8 us
  other arithmetic: 47.1 us -> 22.4 us
  local copies, waits for them, and re-layouts: 53.7 us -> 42.8 us
    reduce_scatter x2, waiting for transfers between devices: 159 us -> 0.01 us  [the longest x1 0.01 us: per_device(): lax.psum_scatter(grad_mlp_w, 'fsdp', scatter_dimension=0, tiled=True)]
    psum x1 -> x0, blocking collectives: 74.9 us -> none  [per_device(): sums = lax.psum(sums, ('fsdp', 'ctx'))]
    all_to_all x4 -> x0, waiting for transfers between devices: 53.5 us -> none  [the longest x2 44.6 us: to_planes(): lax.all_to_all(picked, 'fsdp', split_axis=0, concat_axis=0, tiled=True)]
    ppermute x0 -> x15, waiting for transfers between devices: none -> 44.6 us  [z_shifted(): return lax.ppermute(value, 'fsdp', [(i, (i + steps) % n) for i in range(n)])]
    pallas_call x0 -> x4, Pallas kernels: none -> 27.7 us  [the longest x2 19.4 us: weight_grad(): pl.pallas_call(weight_grad_kernel, grid=(d_model // step,), out_shape=jax...]
    ppermute x43 -> x54, waiting for transfers between devices: 142 us -> 163 us  [flipped(): return lax.ppermute(value, ('fsdp', 'ctx', 'tp'), pairs)]
    concatenate x7 -> x5, other arithmetic: 19.2 us -> 0.3 us  [the longest x1 0.19 us: per_device(): jnp.concatenate([grad_gate, grad_inner * silu], axis=1).astype(bf16)]
    all_to_all x4 -> x0, starting transfers between devices: 17.8 us -> none  [the longest x2 9.01 us: to_given(): home = lax.all_to_all(rows, 'fsdp', split_axis=0, concat_axis=0, tiled=True)]
  transfers between devices with their start and end apart: 54 -> 74, of which waited for: 27 -> 29; matrix products, arithmetic and copies ran while one was open for 13% -> 21% of each run, Pallas kernels for 1% -> 6%
where the time goes in v2:
time: 519 us; the launch traced here: 515 us
  waiting for transfers between devices  256 us (49%)
  matrix products  68.2 us (13%)
  starting transfers between devices  63.2 us (12%)
  Pallas kernels  47.8 us (9%)
  local copies, waits for them, and re-layouts  42.8 us (8%)
  other arithmetic  22.4 us (4%)
  between operations  15 us (3%)
    ppermute x54, waiting for transfers between devices, flipped(): return lax.ppermute(value, ('fsdp', 'ctx', 'tp'), pairs)  163 us
    dot_general x18, matrix products, product(): lax.dot_general(left, right, (dims, ((), ())), preferred_element_type=f32)  68.2 us
    ppermute x15, waiting for transfers between devices, z_shifted(): return lax.ppermute(value, 'fsdp', [(i, (i + steps) % n) for i in range(n)])  44.6 us
    ppermute x54, starting transfers between devices, flipped(): return lax.ppermute(value, ('fsdp', 'ctx', 'tp'), pairs)  37 us
    all_gather x1, waiting for transfers between devices, per_device(): mlp_w = lax.all_gather(after(mlp_own, attn_own), 'fsdp', axis=0, tiled=True)  32 us
    unnamed x121, local copies, waits for them, and re-layouts  30.2 us
    pallas_call x2, Pallas kernels, weight_grad(): pl.pallas_call(weight_grad_kernel, grid=(d_model // step,), out_shape=jax...  19.4 us
    ppermute x15, starting transfers between devices, z_shifted(): return lax.ppermute(value, 'fsdp', [(i, (i + steps) % n) for i in range(n)])  17.6 us
  transfers between devices with their start and end apart: 74, of which 29 were waited for; matrix products, arithmetic and copies ran while one was open for 21% of the time, Pallas kernels for 6%

profile of v2, /device:TPU:0, one launch (start us, length us, event | category | flops | bytes accessed | tf_op | source)
XLA Modules:
  0.0 514.8 jit_solution(10136359879149993283)
XLA Ops:
  12.8 8.2 %all-to-all-start = ((f32[16,1,1824]{2,1,0:T(1,128)}), f32[16,1,1824]{2,1,0:T(1,128)S(1)}, u32[]{:S(2)}, u32[]{:S(2)}) async-start(f32[16,1,1824]{2,1,0:T(1,128)} %broadcast_in_dim.62), calls=%async_computation | async-start | bytes 245760 | tf_op jit(solution)/shard_map/all_to_all | solution.py:398
  21.2 1.9 dynamic-slice_bitcast_fusion.1
  23.1 1.8 select_bitcast_fusion
  26.5 2.4 all-to-all-done
  30.4 4.1 collective-permute-start.2
  35.8 4.8 collective-permute-done.2
  40.7 16.8 %collective-permute-done.1 = bf16[32,1792]{1,0:T(8,128)(2,1)S(1)} collective-permute-done((bf16[32,1792]{1,0:T(8,128)(2,1)S(1)}, bf16[32,1792]{1,0:T(8,128)(2,1)S(1)}, u32[]{:S(2)}, u32[]{:S(2)}) %collective-permute-start.1) | collective-permute-done | bytes 114720 | tf_op jit(solution)/shard_map/ppermute | solution.py:60
  61.2 9.7 %collective-permute-done.3 = bf16[128,1792]{1,0:T(8,128)(2,1)S(1)} collective-permute-done((bf16[128,1792]{1,0:T(8,128)(2,1)}, bf16[128,1792]{1,0:T(8,128)(2,1)S(1)}, u32[]{:S(2)}, u32[]{:S(2)}) %collective-permute-start.3) | collective-permute-done | bytes 458784 | tf_op jit(solution)/shard_map/ppermute | solution.py:35
  73.3 6.1 %collective-permute-done.5 = bf16[128,1792]{1,0:T(8,128)(2,1)S(1)} collective-permute-done((bf16[128,1792]{1,0:T(8,128)(2,1)S(1)}, bf16[128,1792]{1,0:T(8,128)(2,1)S(1)}, u32[]{:S(2)}, u32[]{:S(2)}) %collective-permute-start.5) | collective-permute-done | bytes 458784 | tf_op jit(solution)/shard_map/ppermute | solution.py:35
  83.4 13.5 %all-gather.3.cloned.1.call-done = bf16[1792,1024]{1,0:T(8,128)(2,1)} async-done(((bf16[448,1024]{1,0:T(8,128)(2,1)}), bf16[1792,1024]{1,0:T(8,128)(2,1)}) %all-gather.3.cloned.1.call-update) | async-done | bytes 3670032 | tf_op jit(solution)/shard_map/all_gather | solution.py:385
  96.9 7.5 %fusion.37.qkv_ref = bf16[1024,768]{1,0:T(8,128)(2,1)S(1)} fusion(s32[1024]{0:T(1024)S(1)} %fusion.98, bf16[1024,1792]{1,0:T(8,128)(2,1)} %constant_dynamic-update-slice_fusion.refs_0_, bf16[1792,1024]{1,0:T(8,128)(2,1)} %all-gather.3.cloned.1.call-done), kind=kOutput, calls=%fused_computation.62 | convolution fusion | flops 4431806464 | bytes 7999488 | tf_op jit(solution)/shard_map/dot_general | solution.py:76
  104.4 5.8 %attend_forward.1 = bf16[1024,256]{1,0:T(8,128)(2,1)S(1)} custom-call(s32[2,3]{1,0:T(2,128)S(1)} %bitcast.84, bf16[1024,768]{1,0:T(8,128)(2,1)S(1)} %fusion.37.qkv_ref, f32[3,256]{1,0:T(4,128)S(1)} %constant_dynamic-slice_fusion.1.conv_ref), custom_call_target="tpu_custom_call" | custom-call | tf_op jit(solution)/shard_map/attend_forward/pallas_call | solution.py:302
  111.7 3.1 convolution_convert_fusion
  118.1 8.5 %collective-permute-done.29 = bf16[32,1792]{1,0:T(8,128)(2,1)S(1)} collective-permute-done((bf16[32,1792]{1,0:T(8,128)(2,1)}, bf16[32,1792]{1,0:T(8,128)(2,1)S(1)}, u32[]{:S(2)}, u32[]{:S(2)}) %collective-permute-start.29) | collective-permute-done | bytes 114720 | tf_op jit(solution)/shard_map/ppermute | solution.py:60
  126.7 9.7 %collective-permute-done.28 = bf16[32,1792]{1,0:T(8,128)(2,1)S(1)} collective-permute-done((bf16[32,1792]{1,0:T(8,128)(2,1)}, bf16[32,1792]{1,0:T(8,128)(2,1)S(1)}, u32[]{:S(2)}, u32[]{:S(2)}) %collective-permute-start.28) | collective-permute-done | bytes 114720 | tf_op jit(solution)/shard_map/ppermute | solution.py:60
  139.4 2.5 convert_add_fusion.3
  143.5 6.2 %collective-permute-done.30 = bf16[128,1792]{1,0:T(8,128)(2,1)S(1)} collective-permute-done((bf16[128,1792]{1,0:T(8,128)(2,1)S(1)}, bf16[128,1792]{1,0:T(8,128)(2,1)S(1)}, u32[]{:S(2)}, u32[]{:S(2)}) %collective-permute-start.30) | collective-permute-done | bytes 458784 | tf_op jit(solution)/shard_map/ppermute | solution.py:35
  149.7 1.6 collective-permute-start.32
  153.5 10.0 %collective-permute-done.32 = bf16[128,1792]{1,0:T(8,128)(2,1)S(1)} collective-permute-done((bf16[128,1792]{1,0:T(8,128)(2,1)S(1)}, bf16[128,1792]{1,0:T(8,128)(2,1)S(1)}, u32[]{:S(2)}, u32[]{:S(2)}) %collective-permute-start.32) | collective-permute-done | bytes 458784 | tf_op jit(solution)/shard_map/ppermute | solution.py:35
  169.0 5.3 %collective-permute-done.12 = bf16[128,1792]{1,0:T(8,128)(2,1)S(1)} collective-permute-done((bf16[128,1792]{1,0:T(8,128)(2,1)S(1)}, bf16[128,1792]{1,0:T(8,128)(2,1)S(1)}, u32[]{:S(2)}, u32[]{:S(2)}) %collective-permute-start.12) | collective-permute-done | bytes 458784 | tf_op jit(solution)/shard_map/ppermute | solution.py:35
  179.4 8.5 %collective-permute-done.13 = bf16[128,1792]{1,0:T(8,128)(2,1)S(1)} collective-permute-done((bf16[128,1792]{1,0:T(8,128)(2,1)S(1)}, bf16[128,1792]{1,0:T(8,128)(2,1)S(1)}, u32[]{:S(2)}, u32[]{:S(2)}) %collective-permute-start.13) | collective-permute-done | bytes 458784 | tf_op jit(solution)/shard_map/ppermute | solution.py:35
  187.8 1.8 collective-permute-start.15
  191.7 4.6 collective-permute-done.15
  200.3 32.0 %all-gather.5.cloned.1.call-done = bf16[1792,1920]{1,0:T(8,128)(2,1)} async-done(((bf16[448,1920]{1,0:T(8,128)(2,1)}), bf16[1792,1920]{1,0:T(8,128)(2,1)}) %all-gather.5.cloned.1.call-update) | async-done | bytes 6881296 | tf_op jit(solution)/shard_map/all_gather | solution.py:386
  232.3 8.3 %fusion.8 = f32[1024,1280]{1,0:T(8,128)S(1)} fusion(bf16[1024,1792]{1,0:T(8,128)(2,1)} %constant_dynamic-update-slice_fusion.8.refs_0_, bf16[1792,1920]{1,0:T(8,128)(2,1)} %all-gather.5.cloned.1.call-done), kind=kOutput, calls=%fused_computation.17 | convolution fusion | flops 4697620480 | bytes 13500416 | tf_op jit(solution)/shard_map/dot_general | solution.py:76
  240.6 6.4 %multiply_convert_fusion.1 = (bf16[1024,640]{1,0:T(8,128)(2,1)S(1)}, bf16[1024,640]{1,0:T(8,128)(2,1)S(1)}, bf16[1024,640]{1,0:T(8,128)(2,1)S(1)}) fusion(f32[1024,1280]{1,0:T(8,128)S(1)} %fusion.8, bf16[1024,1792]{1,0:T(8,128)(2,1)} %constant_dynamic-update-slice_fusion.21.refs_2_, bf16[1792,1920]{1,0:T(8,128)(2,1)} %all-gather.5.cloned.1.call-done), kind=kOutput, calls=%fused_computation.25 | convolution fusion | flops 2358640640 | bytes 15138816 | tf_op jit(solution)/shard_map/dot_general | solution.py:76
  248.0 12.0 %weight_grad.2 = bf16[1792,1920]{1,0:T(8,128)(2,1)} custom-call(bf16[1024,1792]{1,0:T(8,128)(2,1)} %constant_dynamic-update-slice_fusion.8.refs_0_, bf16[1024,1280]{1,0:T(8,128)(2,1)S(1)} %pad_maximum_fusion.4.refs_1_, bf16[1024,1792]{1,0:T(8,128)(2,1)} %constant_dynamic-update-slice_fusion.21.refs_2_, bf16[1024,640]{1,0:T(8,128)(2,1)S(1)} %get-tuple-element.107.refs_3_), custom_call_target="tpu_custom_call" | custom-call | flops 7046430720 | bytes 18153472 | tf_op jit(solution)/shard_map/weight_grad/pallas_call | solution.py:242
  261.9 5.4 %fusion.12 = bf16[512,1792]{1,0:T(8,128)(2,1)S(1)} fusion(bf16[1792,1920]{1,0:T(8,128)(2,1)} %all-gather.5.cloned.1.call-done, bf16[1024,1280]{1,0:T(8,128)(2,1)} %copy-done.5), kind=kOutput, calls=%fused_computation.20 | convolution fusion | flops 2349727744 | bytes 7733248 | tf_op jit(solution)/shard_map/dot_general | solution.py:76
  267.4 3.5 convolution_convert_fusion.2
  271.6 4.9 convert_add_fusion.1
  276.6 1.6 collective-permute-start.38
  278.2 3.4 convert_add_fusion.2
  282.2 7.9 %collective-permute-done.38 = bf16[256,1792]{1,0:T(8,128)(2,1)S(1)} collective-permute-done((bf16[256,1792]{1,0:T(8,128)(2,1)S(1)}, bf16[256,1792]{1,0:T(8,128)(2,1)S(1)}, u32[]{:S(2)}, u32[]{:S(2)}) %collective-permute-start.38) | collective-permute-done | bytes 917536 | tf_op jit(solution)/shard_map/ppermute | solution.py:35
  290.4 1.6 collective-permute-start.39
  292.0 12.8 %collective-permute-done.21 = bf16[256,1792]{1,0:T(8,128)(2,1)S(1)} collective-permute-done((bf16[256,1792]{1,0:T(8,128)(2,1)S(1)}, bf16[256,1792]{1,0:T(8,128)(2,1)S(1)}, u32[]{:S(2)}, u32[]{:S(2)}) %collective-permute-start.21) | collective-permute-done | bytes 917536 | tf_op jit(solution)/shard_map/ppermute | solution.py:35
  306.9 6.6 %collective-permute-done.22 = bf16[128,1792]{1,0:T(8,128)(2,1)S(1)} collective-permute-done((bf16[128,1792]{1,0:T(8,128)(2,1)S(1)}, bf16[128,1792]{1,0:T(8,128)(2,1)S(1)}, u32[]{:S(2)}, u32[]{:S(2)}) %collective-permute-start.22) | collective-permute-done | bytes 458784 | tf_op jit(solution)/shard_map/ppermute | solution.py:35
  318.9 9.6 %collective-permute-done.40 = bf16[128,1792]{1,0:T(8,128)(2,1)S(1)} collective-permute-done((bf16[128,1792]{1,0:T(8,128)(2,1)S(1)}, bf16[128,1792]{1,0:T(8,128)(2,1)S(1)}, u32[]{:S(2)}, u32[]{:S(2)}) %collective-permute-start.40) | collective-permute-done | bytes 458784 | tf_op jit(solution)/shard_map/ppermute | solution.py:35
  330.6 6.4 %collective-permute-done.42 = bf16[128,1792]{1,0:T(8,128)(2,1)S(1)} collective-permute-done((bf16[128,1792]{1,0:T(8,128)(2,1)S(1)}, bf16[128,1792]{1,0:T(8,128)(2,1)S(1)}, u32[]{:S(2)}, u32[]{:S(2)}) %collective-permute-start.42) | collective-permute-done | bytes 458784 | tf_op jit(solution)/shard_map/ppermute | solution.py:35
  341.0 4.9 fusion.42.grad_ref
  345.9 14.3 %attend_backward.1 = (bf16[1024,768]{1,0:T(8,128)(2,1)S(1)}, f32[3,256]{1,0:T(4,128)S(1)}) custom-call(s32[2,3]{1,0:T(2,128)S(1)} %bitcast.85, bf16[1024,768]{1,0:T(8,128)(2,1)S(1)} %fusion.37.qkv_ref, bf16[1024,256]{1,0:T(8,128)(2,1)S(1)} %fusion.42.grad_ref, f32[3,256]{1,0:T(4,128)S(1)} %constant_dynamic-slice_fusion.1.conv_ref), custom_call_target="tpu_custom_call" | custom-call | tf_op jit(solution)/shard_map/attend_backward/pallas_call | solution.py:316
  360.2 2.4 fusion.38.refs_1_
  362.6 7.3 %weight_grad.3 = bf16[1792,1024]{1,0:T(8,128)(2,1)S(1)} custom-call(bf16[1024,1792]{1,0:T(8,128)(2,1)S(1)} %copy-done.7, bf16[1024,768]{1,0:T(8,128)(2,1)S(1)} %fusion.38.refs_1_, bf16[1024,1792]{1,0:T(8,128)(2,1)} %constant_dynamic-update-slice_fusion.29.refs_2_, bf16[1024,256]{1,0:T(8,128)(2,1)S(1)} %fusion.41.refs_3_), custom_call_target="tpu_custom_call" | custom-call | flops 3758096384 | bytes 13107200 | tf_op jit(solution)/shard_map/weight_grad/pallas_call | solution.py:242
  369.9 1.8 copy-done.3
  371.8 4.6 convolution_convert_fusion.1
  380.7 4.0 convert_add_fusion
  385.0 4.8 collective-permute-done.24
  392.0 6.2 %collective-permute-done.48 = bf16[256,1792]{1,0:T(8,128)(2,1)S(1)} collective-permute-done((bf16[256,1792]{1,0:T(8,128)(2,1)S(1)}, bf16[256,1792]{1,0:T(8,128)(2,1)S(1)}, u32[]{:S(2)}, u32[]{:S(2)}) %collective-permute-start.48) | collective-permute-done | bytes 917536 | tf_op jit(solution)/shard_map/ppermute | solution.py:35
  403.3 2.8 convolution_convert_fusion.4
  406.1 2.2 collective-permute-start.56
  410.8 1.6 fusion.47
  414.2 2.3 collective-permute-start.50
  417.4 23.9 %collective-permute-done.57 = bf16[448,1920]{1,0:T(8,128)(2,1)S(1)} collective-permute-done((bf16[448,1920]{1,0:T(8,128)(2,1)}, bf16[448,1920]{1,0:T(8,128)(2,1)S(1)}, u32[]{:S(2)}, u32[]{:S(2)}) %collective-permute-start.57) | collective-permute-done | bytes 1720352 | tf_op jit(solution)/shard_map/ppermute | solution.py:35
  441.6 1.7 collective-permute-done.53
  445.0 18.3 %collective-permute-done.59.refs_3_ = bf16[448,1920]{1,0:T(8,128)(2,1)S(1)} collective-permute-done((bf16[448,1920]{1,0:T(8,128)(2,1)S(1)}, bf16[448,1920]{1,0:T(8,128)(2,1)S(1)}, u32[]{:S(2)}, u32[]{:S(2)}) %collective-permute-start.59) | collective-permute-done | bytes 1720352 | tf_op jit(solution)/shard_map/ppermute | solution.py:35
  463.3 5.1 placed.2
  472.0 1.6 select_reduce_fusion.2
  474.1 2.6 convolution_convert_fusion.3
  477.0 1.7 collective-permute-start.65
  478.7 5.9 %collective-permute-done.63 = f32[3,256]{1,0:T(4,128)S(1)} collective-permute-done((f32[3,256]{1,0:T(4,128)S(1)}, f32[3,256]{1,0:T(4,128)S(1)}, u32[]{:S(2)}, u32[]{:S(2)}) %collective-permute-start.63) | collective-permute-done | bytes 3104 | tf_op jit(solution)/shard_map/ppermute | solution.py:35
  484.7 1.6 collective-permute-start.67
  486.3 2.0 collective-permute-start.62
  488.3 3.7 collective-permute-done.65
  493.2 8.7 %collective-permute-done.68 = f32[2,448]{1,0:T(2,128)S(1)} collective-permute-done((f32[2,448]{1,0:T(2,128)S(1)}, f32[2,448]{1,0:T(2,128)S(1)}, u32[]{:S(2)}, u32[]{:S(2)}) %collective-permute-start.68) | collective-permute-done | bytes 3616 | tf_op jit(solution)/shard_map/ppermute | solution.py:35
  504.8 3.3 placed.3
  (331 shorter events, 93.6 us)
Async XLA Ops:
  7.2 89.7 %all-gather.3.cloned.1.call-start = ((), (), s32[]{:S(2)}) async-start(), calls=%async_computation.3 | async-start | bytes 4587520 | tf_op jit(solution)/shard_map/all_gather | solution.py:385
  12.8 16.0 %all-to-all-start = ((f32[16,1,1824]{2,1,0:T(1,128)}), f32[16,1,1824]{2,1,0:T(1,128)S(1)}, u32[]{:S(2)}, u32[]{:S(2)}) async-start(f32[16,1,1824]{2,1,0:T(1,128)} %broadcast_in_dim.62), calls=%async_computation | async-start | bytes 245760 | tf_op jit(solution)/shard_map/all_to_all | solution.py:398
  21.1 211.2 %all-gather.5.cloned.1.call-start = ((), (), s32[]{:S(2)}) async-start(), calls=%async_computation.4 | async-start | bytes 8601600 | tf_op jit(solution)/shard_map/all_gather | solution.py:386
  26.3 376.5 %reduce-scatter.5.cloned.1.call-start = ((), (), s32[]{:S(2)}) async-start(), calls=%async_computation.6 | async-start | bytes 8601600 | tf_op jit(solution)/shard_map/reduce_scatter | solution.py:490
  30.4 10.3 %collective-permute-start.2 = (bf16[32,1792]{1,0:T(8,128)(2,1)S(1)}, bf16[32,1792]{1,0:T(8,128)(2,1)S(1)}, u32[]{:S(2)}, u32[]{:S(2)}) collective-permute-start(bf16[32,1792]{1,0:T(8,128)(2,1)S(1)} %get-tuple-element.134), channel_id=1, source_target_pairs={{0,24},{8,0},{16,8},{24,16},{1,25},{9,1},{17,9},{25,17},{2,26},{10... | collective-permute-start | bytes 344072 | tf_op jit(solution)/shard_map/ppermute | solution.py:60
  34.5 22.9 %collective-permute-start.1 = (bf16[32,1792]{1,0:T(8,128)(2,1)S(1)}, bf16[32,1792]{1,0:T(8,128)(2,1)S(1)}, u32[]{:S(2)}, u32[]{:S(2)}) collective-permute-start(bf16[32,1792]{1,0:T(8,128)(2,1)S(1)} %get-tuple-element.135), channel_id=1, source_target_pairs={{0,16},{8,24},{16,0},{24,8},{1,17},{9,25},{17,1},{25,9},{2,18},{10... | collective-permute-start | bytes 344072 | tf_op jit(solution)/shard_map/ppermute | solution.py:60
  34.5 22.9 %collective-permute-start = (bf16[32,1792]{1,0:T(8,128)(2,1)S(1)}, bf16[32,1792]{1,0:T(8,128)(2,1)S(1)}, u32[]{:S(2)}, u32[]{:S(2)}) collective-permute-start(bf16[32,1792]{1,0:T(8,128)(2,1)S(1)} %get-tuple-element.136), channel_id=1, source_target_pairs={{0,8},{8,16},{16,24},{24,0},{1,9},{9,17},{17,25},{25,1},{2,10},{10... | collective-permute-start | bytes 344072 | tf_op jit(solution)/shard_map/ppermute | solution.py:60
  58.7 12.1 %collective-permute-start.3 = (bf16[128,1792]{1,0:T(8,128)(2,1)}, bf16[128,1792]{1,0:T(8,128)(2,1)S(1)}, u32[]{:S(2)}, u32[]{:S(2)}) collective-permute-start(bf16[128,1792]{1,0:T(8,128)(2,1)} %get-tuple-element.102), channel_id=1, source_target_pairs={{0,2},{1,5},{2,0},{3,7},{4,6},{5,1},{6,4},{7,3},{8,10},{9,13},{10,... | collective-permute-start | bytes 1376264 | tf_op jit(solution)/shard_map/ppermute | solution.py:35
  60.1 11.1 %collective-permute-start.4 = (bf16[128,1792]{1,0:T(8,128)(2,1)}, bf16[128,1792]{1,0:T(8,128)(2,1)S(1)}, u32[]{:S(2)}, u32[]{:S(2)}) collective-permute-start(bf16[128,1792]{1,0:T(8,128)(2,1)} %get-tuple-element.102), channel_id=1, source_target_pairs={{0,4},{1,3},{2,6},{3,1},{4,0},{5,7},{6,2},{7,5},{8,12},{9,11},{10,... | collective-permute-start | bytes 1376264 | tf_op jit(solution)/shard_map/ppermute | solution.py:35
  61.1 19.1 %collective-permute-start.6 = (bf16[128,1792]{1,0:T(8,128)(2,1)}, bf16[128,1792]{1,0:T(8,128)(2,1)S(1)}, u32[]{:S(2)}, u32[]{:S(2)}) collective-permute-start(bf16[128,1792]{1,0:T(8,128)(2,1)} %get-tuple-element.102), channel_id=1, source_target_pairs={{0,1},{1,0},{2,3},{3,2},{4,5},{5,4},{6,7},{7,6},{8,9},{9,8},{10,11... | collective-permute-start | bytes 1376264 | tf_op jit(solution)/shard_map/ppermute | solution.py:35
  70.9 8.5 %collective-permute-start.5 = (bf16[128,1792]{1,0:T(8,128)(2,1)S(1)}, bf16[128,1792]{1,0:T(8,128)(2,1)S(1)}, u32[]{:S(2)}, u32[]{:S(2)}) collective-permute-start(bf16[128,1792]{1,0:T(8,128)(2,1)S(1)} %collective-permute-done.3), channel_id=1, source_target_pairs={{0,4},{1,3},{2,6},{3,1},{4,0},{5,7},{6,2},{7,5},{8,12},{9,11},{10,... | collective-permute-start | bytes 1376264 | tf_op jit(solution)/shard_map/ppermute | solution.py:35
  71.2 9.8 %collective-permute-start.7 = (bf16[128,1792]{1,0:T(8,128)(2,1)S(1)}, bf16[128,1792]{1,0:T(8,128)(2,1)S(1)}, u32[]{:S(2)}, u32[]{:S(2)}) collective-permute-start(bf16[128,1792]{1,0:T(8,128)(2,1)S(1)} %collective-permute-done.3), channel_id=1, source_target_pairs={{0,1},{1,0},{2,3},{3,2},{4,5},{5,4},{6,7},{7,6},{8,9},{9,8},{10,11... | collective-permute-start | bytes 1376264 | tf_op jit(solution)/shard_map/ppermute | solution.py:35
  71.2 10.6 %collective-permute-start.8 = (bf16[128,1792]{1,0:T(8,128)(2,1)S(1)}, bf16[128,1792]{1,0:T(8,128)(2,1)S(1)}, u32[]{:S(2)}, u32[]{:S(2)}) collective-permute-start(bf16[128,1792]{1,0:T(8,128)(2,1)S(1)} %collective-permute-done.4), channel_id=1, source_target_pairs={{0,1},{1,0},{2,3},{3,2},{4,5},{5,4},{6,7},{7,6},{8,9},{9,8},{10,11... | collective-permute-start | bytes 1376264 | tf_op jit(solution)/shard_map/ppermute | solution.py:35
  114.8 24.7 %collective-permute-start.10 = (bf16[512,1792]{1,0:T(8,128)(2,1)}, bf16[512,1792]{1,0:T(8,128)(2,1)}, u32[]{:S(2)}, u32[]{:S(2)}) collective-permute-start(bf16[512,1792]{1,0:T(8,128)(2,1)} %convolution_convert_fusion), channel_id=1, source_target_pairs={{0,1},{1,0},{2,3},{3,2},{4,5},{5,4},{6,7},{7,6},{8,9},{9,8},{10,11... | collective-permute-start | bytes 5505032 | tf_op jit(solution)/shard_map/ppermute | solution.py:35
  115.9 10.8 %collective-permute-start.29 = (bf16[32,1792]{1,0:T(8,128)(2,1)}, bf16[32,1792]{1,0:T(8,128)(2,1)S(1)}, u32[]{:S(2)}, u32[]{:S(2)}) collective-permute-start(bf16[32,1792]{1,0:T(8,128)(2,1)} %get-tuple-element.125), channel_id=1, source_target_pairs={{0,24},{8,0},{16,8},{24,16},{1,25},{9,1},{17,9},{25,17},{2,26},{10... | collective-permute-start | bytes 344072 | tf_op jit(solution)/shard_map/ppermute | solution.py:60
  116.8 19.6 %collective-permute-start.28 = (bf16[32,1792]{1,0:T(8,128)(2,1)}, bf16[32,1792]{1,0:T(8,128)(2,1)S(1)}, u32[]{:S(2)}, u32[]{:S(2)}) collective-permute-start(bf16[32,1792]{1,0:T(8,128)(2,1)} %get-tuple-element.126), channel_id=1, source_target_pairs={{0,16},{8,24},{16,0},{24,8},{1,17},{9,25},{17,1},{25,9},{2,18},{10... | collective-permute-start | bytes 344072 | tf_op jit(solution)/shard_map/ppermute | solution.py:60
  116.8 19.6 %collective-permute-start.27 = (bf16[32,1792]{1,0:T(8,128)(2,1)}, bf16[32,1792]{1,0:T(8,128)(2,1)S(1)}, u32[]{:S(2)}, u32[]{:S(2)}) collective-permute-start(bf16[32,1792]{1,0:T(8,128)(2,1)} %get-tuple-element.127), channel_id=1, source_target_pairs={{0,8},{8,16},{16,24},{24,0},{1,9},{9,17},{17,25},{25,1},{2,10},{10... | collective-permute-start | bytes 344072 | tf_op jit(solution)/shard_map/ppermute | solution.py:60
  136.4 13.3 %collective-permute-start.30 = (bf16[128,1792]{1,0:T(8,128)(2,1)S(1)}, bf16[128,1792]{1,0:T(8,128)(2,1)S(1)}, u32[]{:S(2)}, u32[]{:S(2)}) collective-permute-start(bf16[128,1792]{1,0:T(8,128)(2,1)S(1)} %pad_maximum_fusion.9), channel_id=1, source_target_pairs={{0,2},{1,5},{2,0},{3,7},{4,6},{5,1},{6,4},{7,3},{8,10},{9,13},{10,... | collective-permute-start | bytes 1376264 | tf_op jit(solution)/shard_map/ppermute | solution.py:35
  138.0 13.4 %collective-permute-start.31 = (bf16[128,1792]{1,0:T(8,128)(2,1)S(1)}, bf16[128,1792]{1,0:T(8,128)(2,1)S(1)}, u32[]{:S(2)}, u32[]{:S(2)}) collective-permute-start(bf16[128,1792]{1,0:T(8,128)(2,1)S(1)} %pad_maximum_fusion.9), channel_id=1, source_target_pairs={{0,4},{1,3},{2,6},{3,1},{4,0},{5,7},{6,2},{7,5},{8,12},{9,11},{10,... | collective-permute-start | bytes 1376264 | tf_op jit(solution)/shard_map/ppermute | solution.py:35
  139.4 28.0 %collective-permute-start.33 = (bf16[128,1792]{1,0:T(8,128)(2,1)S(1)}, bf16[128,1792]{1,0:T(8,128)(2,1)S(1)}, u32[]{:S(2)}, u32[]{:S(2)}) collective-permute-start(bf16[128,1792]{1,0:T(8,128)(2,1)S(1)} %pad_maximum_fusion.9), channel_id=1, source_target_pairs={{0,1},{1,0},{2,3},{3,2},{4,5},{5,4},{6,7},{7,6},{8,9},{9,8},{10,11... | collective-permute-start | bytes 1376264 | tf_op jit(solution)/shard_map/ppermute | solution.py:35
  142.1 23.5 %collective-permute-start.11 = (bf16[256,1792]{1,0:T(8,128)(2,1)S(1)}, bf16[256,1792]{1,0:T(8,128)(2,1)S(1)}, u32[]{:S(2)}, u32[]{:S(2)}) collective-permute-start(bf16[256,1792]{1,0:T(8,128)(2,1)S(1)} %slice.334), channel_id=1, source_target_pairs={{0,4},{1,3},{2,6},{3,1},{4,0},{5,7},{6,2},{7,5},{8,12},{9,11},{10,... | collective-permute-start | bytes 2752520 | tf_op jit(solution)/shard_map/ppermute | solution.py:35
  149.7 13.9 %collective-permute-start.32 = (bf16[128,1792]{1,0:T(8,128)(2,1)S(1)}, bf16[128,1792]{1,0:T(8,128)(2,1)S(1)}, u32[]{:S(2)}, u32[]{:S(2)}) collective-permute-start(bf16[128,1792]{1,0:T(8,128)(2,1)S(1)} %collective-permute-done.30), channel_id=1, source_target_pairs={{0,4},{1,3},{2,6},{3,1},{4,0},{5,7},{6,2},{7,5},{8,12},{9,11},{10,... | collective-permute-start | bytes 1376264 | tf_op jit(solution)/shard_map/ppermute | solution.py:35
  151.3 16.9 %collective-permute-start.34 = (bf16[128,1792]{1,0:T(8,128)(2,1)S(1)}, bf16[128,1792]{1,0:T(8,128)(2,1)S(1)}, u32[]{:S(2)}, u32[]{:S(2)}) collective-permute-start(bf16[128,1792]{1,0:T(8,128)(2,1)S(1)} %collective-permute-done.30), channel_id=1, source_target_pairs={{0,1},{1,0},{2,3},{3,2},{4,5},{5,4},{6,7},{7,6},{8,9},{9,8},{10,11... | collective-permute-start | bytes 1376264 | tf_op jit(solution)/shard_map/ppermute | solution.py:35
  151.3 26.4 %collective-permute-start.35 = (bf16[128,1792]{1,0:T(8,128)(2,1)S(1)}, bf16[128,1792]{1,0:T(8,128)(2,1)S(1)}, u32[]{:S(2)}, u32[]{:S(2)}) collective-permute-start(bf16[128,1792]{1,0:T(8,128)(2,1)S(1)} %collective-permute-done.31), channel_id=1, source_target_pairs={{0,1},{1,0},{2,3},{3,2},{4,5},{5,4},{6,7},{7,6},{8,9},{9,8},{10,11... | collective-permute-start | bytes 1376264 | tf_op jit(solution)/shard_map/ppermute | solution.py:35
  163.5 15.0 %collective-permute-start.36 = (bf16[128,1792]{1,0:T(8,128)(2,1)S(1)}, bf16[128,1792]{1,0:T(8,128)(2,1)S(1)}, u32[]{:S(2)}, u32[]{:S(2)}) collective-permute-start(bf16[128,1792]{1,0:T(8,128)(2,1)S(1)} %collective-permute-done.32), channel_id=1, source_target_pairs={{0,1},{1,0},{2,3},{3,2},{4,5},{5,4},{6,7},{7,6},{8,9},{9,8},{10,11... | collective-permute-start | bytes 1376264 | tf_op jit(solution)/shard_map/ppermute | solution.py:35
  165.8 8.5 %collective-permute-start.12 = (bf16[128,1792]{1,0:T(8,128)(2,1)S(1)}, bf16[128,1792]{1,0:T(8,128)(2,1)S(1)}, u32[]{:S(2)}, u32[]{:S(2)}) collective-permute-start(bf16[128,1792]{1,0:T(8,128)(2,1)S(1)} %slice.338), channel_id=1, source_target_pairs={{0,2},{1,5},{2,0},{3,7},{4,6},{5,1},{6,4},{7,3},{8,10},{9,13},{10,... | collective-permute-start | bytes 1376264 | tf_op jit(solution)/shard_map/ppermute | solution.py:35
  175.6 12.2 %collective-permute-start.13 = (bf16[128,1792]{1,0:T(8,128)(2,1)S(1)}, bf16[128,1792]{1,0:T(8,128)(2,1)S(1)}, u32[]{:S(2)}, u32[]{:S(2)}) collective-permute-start(bf16[128,1792]{1,0:T(8,128)(2,1)S(1)} %get-tuple-element.98), channel_id=1, source_target_pairs={{0,2},{1,5},{2,0},{3,7},{4,6},{5,1},{6,4},{7,3},{8,10},{9,13},{10,... | collective-permute-start | bytes 1376264 | tf_op jit(solution)/shard_map/ppermute | solution.py:35
  177.1 12.5 %collective-permute-start.14 = (bf16[128,1792]{1,0:T(8,128)(2,1)S(1)}, bf16[128,1792]{1,0:T(8,128)(2,1)S(1)}, u32[]{:S(2)}, u32[]{:S(2)}) collective-permute-start(bf16[128,1792]{1,0:T(8,128)(2,1)S(1)} %get-tuple-element.98), channel_id=1, source_target_pairs={{0,4},{1,3},{2,6},{3,1},{4,0},{5,7},{6,2},{7,5},{8,12},{9,11},{10,... | collective-permute-start | bytes 1376264 | tf_op jit(solution)/shard_map/ppermute | solution.py:35
  179.4 17.7 %collective-permute-start.16 = (bf16[128,1792]{1,0:T(8,128)(2,1)S(1)}, bf16[128,1792]{1,0:T(8,128)(2,1)S(1)}, u32[]{:S(2)}, u32[]{:S(2)}) collective-permute-start(bf16[128,1792]{1,0:T(8,128)(2,1)S(1)} %get-tuple-element.98), channel_id=1, source_target_pairs={{0,1},{1,0},{2,3},{3,2},{4,5},{5,4},{6,7},{7,6},{8,9},{9,8},{10,11... | collective-permute-start | bytes 1376264 | tf_op jit(solution)/shard_map/ppermute | solution.py:35
  187.8 8.5 %collective-permute-start.15 = (bf16[128,1792]{1,0:T(8,128)(2,1)S(1)}, bf16[128,1792]{1,0:T(8,128)(2,1)S(1)}, u32[]{:S(2)}, u32[]{:S(2)}) collective-permute-start(bf16[128,1792]{1,0:T(8,128)(2,1)S(1)} %collective-permute-done.13), channel_id=1, source_target_pairs={{0,4},{1,3},{2,6},{3,1},{4,0},{5,7},{6,2},{7,5},{8,12},{9,11},{10,... | collective-permute-start | bytes 1376264 | tf_op jit(solution)/shard_map/ppermute | solution.py:35
  189.6 8.3 %collective-permute-start.17 = (bf16[128,1792]{1,0:T(8,128)(2,1)S(1)}, bf16[128,1792]{1,0:T(8,128)(2,1)S(1)}, u32[]{:S(2)}, u32[]{:S(2)}) collective-permute-start(bf16[128,1792]{1,0:T(8,128)(2,1)S(1)} %collective-permute-done.13), channel_id=1, source_target_pairs={{0,1},{1,0},{2,3},{3,2},{4,5},{5,4},{6,7},{7,6},{8,9},{9,8},{10,11... | collective-permute-start | bytes 1376264 | tf_op jit(solution)/shard_map/ppermute | solution.py:35
  189.6 9.1 %collective-permute-start.18 = (bf16[128,1792]{1,0:T(8,128)(2,1)S(1)}, bf16[128,1792]{1,0:T(8,128)(2,1)S(1)}, u32[]{:S(2)}, u32[]{:S(2)}) collective-permute-start(bf16[128,1792]{1,0:T(8,128)(2,1)S(1)} %collective-permute-done.14), channel_id=1, source_target_pairs={{0,1},{1,0},{2,3},{3,2},{4,5},{5,4},{6,7},{7,6},{8,9},{9,8},{10,11... | collective-permute-start | bytes 1376264 | tf_op jit(solution)/shard_map/ppermute | solution.py:35
  261.6 206.8 %reduce-scatter.3.cloned.1.call-start = ((), (), s32[]{:S(2)}) async-start(), calls=%async_computation.5 | async-start | bytes 4587520 | tf_op jit(solution)/shard_map/reduce_scatter | solution.py:515
  270.8 7.4 %collective-permute-start.20 = (bf16[512,1792]{1,0:T(8,128)(2,1)S(1)}, bf16[512,1792]{1,0:T(8,128)(2,1)S(1)}, u32[]{:S(2)}, u32[]{:S(2)}) collective-permute-start(bf16[512,1792]{1,0:T(8,128)(2,1)S(1)} %convolution_convert_fusion.2), channel_id=1, source_target_pairs={{0,1},{1,0},{2,3},{3,2},{4,5},{5,4},{6,7},{7,6},{8,9},{9,8},{10,11... | collective-permute-start | bytes 5505032 | tf_op jit(solution)/shard_map/ppermute | solution.py:35
  276.6 13.5 %collective-permute-start.38 = (bf16[256,1792]{1,0:T(8,128)(2,1)S(1)}, bf16[256,1792]{1,0:T(8,128)(2,1)S(1)}, u32[]{:S(2)}, u32[]{:S(2)}) collective-permute-start(bf16[256,1792]{1,0:T(8,128)(2,1)S(1)} %slice.332), channel_id=1, source_target_pairs={{0,4},{1,3},{2,6},{3,1},{4,0},{5,7},{6,2},{7,5},{8,12},{9,11},{10,... | collective-permute-start | bytes 2752520 | tf_op jit(solution)/shard_map/ppermute | solution.py:35
  281.8 23.0 %collective-permute-start.21 = (bf16[256,1792]{1,0:T(8,128)(2,1)S(1)}, bf16[256,1792]{1,0:T(8,128)(2,1)S(1)}, u32[]{:S(2)}, u32[]{:S(2)}) collective-permute-start(bf16[256,1792]{1,0:T(8,128)(2,1)S(1)} %slice.333), channel_id=1, source_target_pairs={{0,4},{1,3},{2,6},{3,1},{4,0},{5,7},{6,2},{7,5},{8,12},{9,11},{10,... | collective-permute-start | bytes 2752520 | tf_op jit(solution)/shard_map/ppermute | solution.py:35
  290.4 16.3 %collective-permute-start.39 = (bf16[128,1792]{1,0:T(8,128)(2,1)S(1)}, bf16[128,1792]{1,0:T(8,128)(2,1)S(1)}, u32[]{:S(2)}, u32[]{:S(2)}) collective-permute-start(bf16[128,1792]{1,0:T(8,128)(2,1)S(1)} %slice.336), channel_id=1, source_target_pairs={{0,2},{1,5},{2,0},{3,7},{4,6},{5,1},{6,4},{7,3},{8,10},{9,13},{10,... | collective-permute-start | bytes 1376264 | tf_op jit(solution)/shard_map/ppermute | solution.py:35
  305.0 8.5 %collective-permute-start.22 = (bf16[128,1792]{1,0:T(8,128)(2,1)S(1)}, bf16[128,1792]{1,0:T(8,128)(2,1)S(1)}, u32[]{:S(2)}, u32[]{:S(2)}) collective-permute-start(bf16[128,1792]{1,0:T(8,128)(2,1)S(1)} %slice.337), channel_id=1, source_target_pairs={{0,2},{1,5},{2,0},{3,7},{4,6},{5,1},{6,4},{7,3},{8,10},{9,13},{10,... | collective-permute-start | bytes 1376264 | tf_op jit(solution)/shard_map/ppermute | solution.py:35
  315.1 13.4 %collective-permute-start.40 = (bf16[128,1792]{1,0:T(8,128)(2,1)S(1)}, bf16[128,1792]{1,0:T(8,128)(2,1)S(1)}, u32[]{:S(2)}, u32[]{:S(2)}) collective-permute-start(bf16[128,1792]{1,0:T(8,128)(2,1)S(1)} %get-tuple-element.81), channel_id=1, source_target_pairs={{0,2},{1,5},{2,0},{3,7},{4,6},{5,1},{6,4},{7,3},{8,10},{9,13},{10,... | collective-permute-start | bytes 1376264 | tf_op jit(solution)/shard_map/ppermute | solution.py:35
  316.7 11.9 %collective-permute-start.41 = (bf16[128,1792]{1,0:T(8,128)(2,1)S(1)}, bf16[128,1792]{1,0:T(8,128)(2,1)S(1)}, u32[]{:S(2)}, u32[]{:S(2)}) collective-permute-start(bf16[128,1792]{1,0:T(8,128)(2,1)S(1)} %get-tuple-element.81), channel_id=1, source_target_pairs={{0,4},{1,3},{2,6},{3,1},{4,0},{5,7},{6,2},{7,5},{8,12},{9,11},{10,... | collective-permute-start | bytes 1376264 | tf_op jit(solution)/shard_map/ppermute | solution.py:35
  318.1 19.7 %collective-permute-start.43 = (bf16[128,1792]{1,0:T(8,128)(2,1)S(1)}, bf16[128,1792]{1,0:T(8,128)(2,1)S(1)}, u32[]{:S(2)}, u32[]{:S(2)}) collective-permute-start(bf16[128,1792]{1,0:T(8,128)(2,1)S(1)} %get-tuple-element.81), channel_id=1, source_target_pairs={{0,1},{1,0},{2,3},{3,2},{4,5},{5,4},{6,7},{7,6},{8,9},{9,8},{10,11... | collective-permute-start | bytes 1376264 | tf_op jit(solution)/shard_map/ppermute | solution.py:35
  328.5 8.5 %collective-permute-start.42 = (bf16[128,1792]{1,0:T(8,128)(2,1)S(1)}, bf16[128,1792]{1,0:T(8,128)(2,1)S(1)}, u32[]{:S(2)}, u32[]{:S(2)}) collective-permute-start(bf16[128,1792]{1,0:T(8,128)(2,1)S(1)} %collective-permute-done.40), channel_id=1, source_target_pairs={{0,4},{1,3},{2,6},{3,1},{4,0},{5,7},{6,2},{7,5},{8,12},{9,11},{10,... | collective-permute-start | bytes 1376264 | tf_op jit(solution)/shard_map/ppermute | solution.py:35
  328.5 10.1 %collective-permute-start.44 = (bf16[128,1792]{1,0:T(8,128)(2,1)S(1)}, bf16[128,1792]{1,0:T(8,128)(2,1)S(1)}, u32[]{:S(2)}, u32[]{:S(2)}) collective-permute-start(bf16[128,1792]{1,0:T(8,128)(2,1)S(1)} %collective-permute-done.40), channel_id=1, source_target_pairs={{0,1},{1,0},{2,3},{3,2},{4,5},{5,4},{6,7},{7,6},{8,9},{9,8},{10,11... | collective-permute-start | bytes 1376264 | tf_op jit(solution)/shard_map/ppermute | solution.py:35
  328.5 10.9 %collective-permute-start.45 = (bf16[128,1792]{1,0:T(8,128)(2,1)S(1)}, bf16[128,1792]{1,0:T(8,128)(2,1)S(1)}, u32[]{:S(2)}, u32[]{:S(2)}) collective-permute-start(bf16[128,1792]{1,0:T(8,128)(2,1)S(1)} %collective-permute-done.41), channel_id=1, source_target_pairs={{0,1},{1,0},{2,3},{3,2},{4,5},{5,4},{6,7},{7,6},{8,9},{9,8},{10,11... | collective-permute-start | bytes 1376264 | tf_op jit(solution)/shard_map/ppermute | solution.py:35
  378.9 10.9 %collective-permute-start.24 = (bf16[32,1792]{1,0:T(8,128)(2,1)S(1)}, bf16[32,1792]{1,0:T(8,128)(2,1)S(1)}, u32[]{:S(2)}, u32[]{:S(2)}) collective-permute-start(bf16[32,1792]{1,0:T(8,128)(2,1)S(1)} %get-tuple-element.131), channel_id=1, source_target_pairs={{0,16},{8,24},{16,0},{24,8},{1,17},{9,25},{17,1},{25,9},{2,18},{10... | collective-permute-start | bytes 344072 | tf_op jit(solution)/shard_map/ppermute | solution.py:60
  378.9 10.9 %collective-permute-start.25 = (bf16[32,1792]{1,0:T(8,128)(2,1)S(1)}, bf16[32,1792]{1,0:T(8,128)(2,1)S(1)}, u32[]{:S(2)}, u32[]{:S(2)}) collective-permute-start(bf16[32,1792]{1,0:T(8,128)(2,1)S(1)} %get-tuple-element.130), channel_id=1, source_target_pairs={{0,8},{8,16},{16,24},{24,0},{1,9},{9,17},{17,25},{25,1},{2,10},{10... | collective-permute-start | bytes 344072 | tf_op jit(solution)/shard_map/ppermute | solution.py:60
  384.7 13.5 %collective-permute-start.48 = (bf16[256,1792]{1,0:T(8,128)(2,1)S(1)}, bf16[256,1792]{1,0:T(8,128)(2,1)S(1)}, u32[]{:S(2)}, u32[]{:S(2)}) collective-permute-start(bf16[256,1792]{1,0:T(8,128)(2,1)S(1)} %slice.331), channel_id=1, source_target_pairs={{0,4},{1,3},{2,6},{3,1},{4,0},{5,7},{6,2},{7,5},{8,12},{9,11},{10,... | collective-permute-start | bytes 2752520 | tf_op jit(solution)/shard_map/ppermute | solution.py:35
  389.9 12.1 %collective-permute-start.26 = (bf16[128,1792]{1,0:T(8,128)(2,1)S(1)}, bf16[128,1792]{1,0:T(8,128)(2,1)S(1)}, u32[]{:S(2)}, u32[]{:S(2)}) collective-permute-start(bf16[128,1792]{1,0:T(8,128)(2,1)S(1)} %pad_maximum_fusion.8), channel_id=1, source_target_pairs={{0,1},{1,0},{2,3},{3,2},{4,5},{5,4},{6,7},{7,6},{8,9},{9,8},{10,11... | collective-permute-start | bytes 1376264 | tf_op jit(solution)/shard_map/ppermute | solution.py:35
  400.4 10.4 %collective-permute-start.49 = (bf16[128,1792]{1,0:T(8,128)(2,1)}, bf16[128,1792]{1,0:T(8,128)(2,1)}, u32[]{:S(2)}, u32[]{:S(2)}) collective-permute-start(bf16[128,1792]{1,0:T(8,128)(2,1)} %slice.335), channel_id=1, source_target_pairs={{0,2},{1,5},{2,0},{3,7},{4,6},{5,1},{6,4},{7,3},{8,10},{9,13},{10,... | collective-permute-start | bytes 1376264 | tf_op jit(solution)/shard_map/ppermute | solution.py:35
  402.8 38.5 %collective-permute-start.57 = (bf16[448,1920]{1,0:T(8,128)(2,1)}, bf16[448,1920]{1,0:T(8,128)(2,1)S(1)}, u32[]{:S(2)}, u32[]{:S(2)}) collective-permute-start(bf16[448,1920]{1,0:T(8,128)(2,1)} %reduce-scatter.5.cloned.1.call-done.refs_0_), channel_id=1, source_target_pairs={{0,2},{1,5},{2,0},{3,7},{4,6},{5,1},{6,4},{7,3},{8,10},{9,13},{10,... | collective-permute-start | bytes 5160968 | tf_op jit(solution)/shard_map/ppermute | solution.py:35
  406.1 8.1 %collective-permute-start.56 = (f32[3,256]{1,0:T(4,128)S(1)}, f32[3,256]{1,0:T(4,128)S(1)}, u32[]{:S(2)}, u32[]{:S(2)}) collective-permute-start(f32[3,256]{1,0:T(4,128)S(1)} %get-tuple-element.84), channel_id=1, source_target_pairs={{0,24},{8,0},{16,8},{24,16},{1,25},{9,1},{17,9},{25,17},{2,26},{10... | collective-permute-start | bytes 9224 | tf_op jit(solution)/shard_map/ppermute | solution.py:60
  408.2 8.3 %collective-permute-start.55 = (f32[3,256]{1,0:T(4,128)S(1)}, f32[3,256]{1,0:T(4,128)S(1)}, u32[]{:S(2)}, u32[]{:S(2)}) collective-permute-start(f32[3,256]{1,0:T(4,128)S(1)} %get-tuple-element.84), channel_id=1, source_target_pairs={{0,16},{8,24},{16,0},{24,8},{1,17},{9,25},{17,1},{25,9},{2,18},{10... | collective-permute-start | bytes 9224 | tf_op jit(solution)/shard_map/ppermute | solution.py:60
  413.9 30.8 %collective-permute-start.58 = (bf16[448,1920]{1,0:T(8,128)(2,1)S(1)}, bf16[448,1920]{1,0:T(8,128)(2,1)S(1)}, u32[]{:S(2)}, u32[]{:S(2)}) collective-permute-start(bf16[448,1920]{1,0:T(8,128)(2,1)S(1)} %copy-done.2), channel_id=1, source_target_pairs={{0,4},{1,3},{2,6},{3,1},{4,0},{5,7},{6,2},{7,5},{8,12},{9,11},{10,... | collective-permute-start | bytes 5160968 | tf_op jit(solution)/shard_map/ppermute | solution.py:35
  414.2 27.2 %collective-permute-start.50 = (bf16[32,1792]{1,0:T(8,128)(2,1)S(1)}, bf16[32,1792]{1,0:T(8,128)(2,1)S(1)}, u32[]{:S(2)}, u32[]{:S(2)}) collective-permute-start(bf16[32,1792]{1,0:T(8,128)(2,1)S(1)} %get-tuple-element.123), channel_id=1, source_target_pairs={{0,24},{8,0},{16,8},{24,16},{1,25},{9,1},{17,9},{25,17},{2,26},{10... | collective-permute-start | bytes 344072 | tf_op jit(solution)/shard_map/ppermute | solution.py:60
  416.5 24.9 %collective-permute-start.51 = (bf16[32,1792]{1,0:T(8,128)(2,1)S(1)}, bf16[32,1792]{1,0:T(8,128)(2,1)S(1)}, u32[]{:S(2)}, u32[]{:S(2)}) collective-permute-start(bf16[32,1792]{1,0:T(8,128)(2,1)S(1)} %get-tuple-element.122), channel_id=1, source_target_pairs={{0,16},{8,24},{16,0},{24,8},{1,17},{9,25},{17,1},{25,9},{2,18},{10... | collective-permute-start | bytes 344072 | tf_op jit(solution)/shard_map/ppermute | solution.py:60
  416.5 24.8 %collective-permute-start.52 = (bf16[32,1792]{1,0:T(8,128)(2,1)S(1)}, bf16[32,1792]{1,0:T(8,128)(2,1)S(1)}, u32[]{:S(2)}, u32[]{:S(2)}) collective-permute-start(bf16[32,1792]{1,0:T(8,128)(2,1)S(1)} %get-tuple-element.121), channel_id=1, source_target_pairs={{0,8},{8,16},{16,24},{24,0},{1,9},{9,17},{17,25},{25,1},{2,10},{10... | collective-permute-start | bytes 344072 | tf_op jit(solution)/shard_map/ppermute | solution.py:60
  441.3 22.0 %collective-permute-start.59 = (bf16[448,1920]{1,0:T(8,128)(2,1)S(1)}, bf16[448,1920]{1,0:T(8,128)(2,1)S(1)}, u32[]{:S(2)}, u32[]{:S(2)}) collective-permute-start(bf16[448,1920]{1,0:T(8,128)(2,1)S(1)} %collective-permute-done.57), channel_id=1, source_target_pairs={{0,4},{1,3},{2,6},{3,1},{4,0},{5,7},{6,2},{7,5},{8,12},{9,11},{10,... | collective-permute-start | bytes 5160968 | tf_op jit(solution)/shard_map/ppermute | solution.py:35
  468.4 17.9 %collective-permute-start.60 = (bf16[448,1024]{1,0:T(8,128)(2,1)}, bf16[448,1024]{1,0:T(8,128)(2,1)}, u32[]{:S(2)}, u32[]{:S(2)}) collective-permute-start(bf16[448,1024]{1,0:T(8,128)(2,1)} %reduce-scatter.3.cloned.1.call-done.refs_0_), channel_id=1, source_target_pairs={{0,2},{1,5},{2,0},{3,7},{4,6},{5,1},{6,4},{7,3},{8,10},{9,13},{10,... | collective-permute-start | bytes 2752520 | tf_op jit(solution)/shard_map/ppermute | solution.py:35
  471.5 13.2 %collective-permute-start.63 = (f32[3,256]{1,0:T(4,128)S(1)}, f32[3,256]{1,0:T(4,128)S(1)}, u32[]{:S(2)}, u32[]{:S(2)}) collective-permute-start(f32[3,256]{1,0:T(4,128)S(1)} %add_add_fusion), channel_id=1, source_target_pairs={{0,2},{1,5},{2,0},{3,7},{4,6},{5,1},{6,4},{7,3},{8,10},{9,13},{10,... | collective-permute-start | bytes 9224 | tf_op jit(solution)/shard_map/ppermute | solution.py:35
  473.7 11.0 %collective-permute-start.66 = (f32[2,448]{1,0:T(2,128)S(1)}, f32[2,448]{1,0:T(2,128)S(1)}, u32[]{:S(2)}, u32[]{:S(2)}) collective-permute-start(f32[2,448]{1,0:T(2,128)S(1)} %pad_maximum_fusion.12), channel_id=1, source_target_pairs={{0,1},{1,0},{2,3},{3,2},{4,5},{5,4},{6,7},{7,6},{8,9},{9,8},{10,11... | collective-permute-start | bytes 10760 | tf_op jit(solution)/shard_map/ppermute | solution.py:35
  476.7 26.6 %collective-permute-start.61 = (bf16[448,1024]{1,0:T(8,128)(2,1)S(1)}, bf16[448,1024]{1,0:T(8,128)(2,1)}, u32[]{:S(2)}, u32[]{:S(2)}) collective-permute-start(bf16[448,1024]{1,0:T(8,128)(2,1)S(1)} %copy-done.4), channel_id=1, source_target_pairs={{0,4},{1,3},{2,6},{3,1},{4,0},{5,7},{6,2},{7,5},{8,12},{9,11},{10,... | collective-permute-start | bytes 2752520 | tf_op jit(solution)/shard_map/ppermute | solution.py:35
  477.0 15.0 %collective-permute-start.65 = (f32[3,256]{1,0:T(4,128)S(1)}, f32[3,256]{1,0:T(4,128)S(1)}, u32[]{:S(2)}, u32[]{:S(2)}) collective-permute-start(f32[3,256]{1,0:T(4,128)S(1)} %add_add_fusion), channel_id=1, source_target_pairs={{0,4},{1,3},{2,6},{3,1},{4,0},{5,7},{6,2},{7,5},{8,12},{9,11},{10,... | collective-permute-start | bytes 9224 | tf_op jit(solution)/shard_map/ppermute | solution.py:35
  486.3 18.5 %collective-permute-start.62 = (bf16[448,1024]{1,0:T(8,128)(2,1)}, bf16[448,1024]{1,0:T(8,128)(2,1)S(1)}, u32[]{:S(2)}, u32[]{:S(2)}) collective-permute-start(bf16[448,1024]{1,0:T(8,128)(2,1)} %collective-permute-done.60), channel_id=1, source_target_pairs={{0,4},{1,3},{2,6},{3,1},{4,0},{5,7},{6,2},{7,5},{8,12},{9,11},{10,... | collective-permute-start | bytes 2752520 | tf_op jit(solution)/shard_map/ppermute | solution.py:35
  492.1 9.8 %collective-permute-start.68 = (f32[2,448]{1,0:T(2,128)S(1)}, f32[2,448]{1,0:T(2,128)S(1)}, u32[]{:S(2)}, u32[]{:S(2)}) collective-permute-start(f32[2,448]{1,0:T(2,128)S(1)} %fusion.133), channel_id=1, source_target_pairs={{0,4},{1,3},{2,6},{3,1},{4,0},{5,7},{6,2},{7,5},{8,12},{9,11},{10,... | collective-permute-start | bytes 10760 | tf_op jit(solution)/shard_map/ppermute | solution.py:35
  (52 other events, 628.8 us)
Sparse Core Ops, SparseCore 0:
  12.0 84.7 all-gather.2
  99.0 133.2 all-gather.4
  261.7 118.4 reduce-scatter.4
  383.0 78.6 reduce-scatter.2

commit v3 on v2

--- a/solution.py
+++ b/solution.py
@@ -35,9 +35,12 @@
     return lax.ppermute(value, ("fsdp", "ctx", "tp"), pairs)
 
 
-def plane_gather(own, sizes):
-    one = flipped(own, sizes, 0)
-    two = flipped(own, sizes, 1)
+def near_shares(own, sizes):
+    return flipped(own, sizes, 0), flipped(own, sizes, 1)
+
+
+def plane_gather(own, sizes, near=None):
+    one, two = near or near_shares(own, sizes)
     three = flipped(one, sizes, 1)
     mine = [own, one, two, three]
     return jnp.concatenate(mine + [flipped(block, sizes, 2) for block in mine])
@@ -55,6 +58,15 @@
     return lax.optimization_barrier((value,) + others)[0]
 
 
+def stage(*values):
+    return lax.optimization_barrier(values)
+
+
+def added(part, got):
+    half = part.shape[0] // 2
+    return part[:half] + got[:half].astype(f32), (part[half:] + got[half:].astype(f32)).astype(bf16)
+
+
 def z_shifted(value, sizes, steps):
     n = sizes[0]
     return lax.ppermute(value, "fsdp", [(i, (i + steps) % n) for i in range(n)])
@@ -65,9 +77,8 @@
     return jnp.concatenate(got)
 
 
-def ctx_shares(own, sizes, core):
-    one = flipped(own, sizes, 0)
-    two = flipped(own, sizes, 1)
+def ctx_shares(own, sizes, core, near=None):
+    one, two = near or near_shares(own, sizes)
     three = flipped(one, sizes, 1)
     return [own, jnp.where(core == 0, one, two), jnp.where(core == 0, two, one), three]
 
@@ -223,24 +234,30 @@
         grad_conv_ref[lag : lag + 1, :] = conv_sums[lag]
 
 
-def weight_grad_kernel(*refs):
+def weight_grad_kernel(turned, *refs):
     out_ref = refs[-1]
     at = 0
-    for left_ref, right_ref in zip(refs[:-1:2], refs[1:-1:2]):
+    for is_turned, left_ref, right_ref in zip(turned, refs[:-1:2], refs[1:-1:2]):
         width = right_ref.shape[1]
-        out_ref[:, at : at + width] = product(left_ref[...], right_ref[...], TN, bf16)
+        dims = NN if is_turned else TN
+        out_ref[:, at : at + width] = product(left_ref[...], right_ref[...], dims, bf16)
         at += width
 
 
 def weight_grad(*pairs, step=256):
-    rows, d_model = pairs[0][0].shape
+    rows = pairs[0][1].shape[0]
+    turned = tuple(left.shape[1] == rows for left, _ in pairs)
+    d_model = pairs[0][0].shape[0 if turned[0] else 1]
     width = sum(right.shape[1] for _, right in pairs)
     specs = []
-    for left, right in pairs:
-        specs.append(pl.BlockSpec((rows, step), lambda i: (0, i)))
+    for is_turned, (left, right) in zip(turned, pairs):
+        if is_turned:
+            specs.append(pl.BlockSpec((step, rows), lambda i: (i, 0)))
+        else:
+            specs.append(pl.BlockSpec((rows, step), lambda i: (0, i)))
         specs.append(pl.BlockSpec((rows, right.shape[1]), lambda i: (0, 0)))
     return pl.pallas_call(
-        weight_grad_kernel,
+        functools.partial(weight_grad_kernel, turned),
         grid=(d_model // step,),
         out_shape=jax.ShapeDtypeStruct((d_model, width), bf16),
         in_specs=specs,
@@ -253,6 +270,48 @@
         ),
         name="weight_grad",
     )(*[operand for pair in pairs for operand in pair])
+
+
+def feed_forward_kernel(hidden_ref, grad_ref, weight_ref, inner_ref, pair_ref):
+    ff = inner_ref.shape[1]
+    both = product(hidden_ref[...], weight_ref[:, : 2 * ff], NN)
+    grad_inner = product(grad_ref[...], weight_ref[:, 2 * ff :], NN)
+    gate_act, upper = both[:, :ff], both[:, ff:]
+    sigmoid = jax.nn.sigmoid(gate_act)
+    silu = gate_act * sigmoid
+    inner_ref[...] = (silu * upper).astype(bf16)
+    grad_gate = grad_inner * upper * (sigmoid * (1.0 + gate_act * (1.0 - sigmoid)))
+    pair_ref[:, :ff] = grad_gate.astype(bf16)
+    pair_ref[:, ff:] = (grad_inner * silu).astype(bf16)
+
+
+def feed_forward(hidden, grad, weight, step=256):
+    rows, d_model = hidden.shape
+    ff = weight.shape[1] // 3
+    return pl.pallas_call(
+        feed_forward_kernel,
+        grid=(rows // step,),
+        out_shape=(
+            jax.ShapeDtypeStruct((rows, ff), bf16),
+            jax.ShapeDtypeStruct((rows, 2 * ff), bf16),
+        ),
+        in_specs=[
+            pl.BlockSpec((step, d_model), lambda i: (i, 0)),
+            pl.BlockSpec((step, d_model), lambda i: (i, 0)),
+            pl.BlockSpec((d_model, 3 * ff), lambda i: (0, 0)),
+        ],
+        out_specs=(
+            pl.BlockSpec((step, ff), lambda i: (i, 0)),
+            pl.BlockSpec((step, 2 * ff), lambda i: (i, 0)),
+        ),
+        compiler_params=pltpu.CompilerParams(vmem_limit_bytes=48 * 1024 * 1024),
+        cost_estimate=pl.CostEstimate(
+            flops=6 * rows * d_model * ff,
+            bytes_accessed=2 * (2 * rows * d_model + 3 * (d_model + rows) * ff),
+            transcendentals=rows * ff,
+        ),
+        name="feed_forward",
+    )(hidden, grad, weight)
 
 
 def placed_kernel(each, total, counts, index_ref, *refs):
@@ -293,6 +352,33 @@
     )(index.reshape(1).astype(jnp.int32), *parts)
 
 
+def at_home_kernel(undo_ref, *refs):
+    *blocks, first_ref, second_ref, rows = refs
+    each = blocks[0].shape[0]
+    for k, block in enumerate(blocks):
+        rows[k * each : (k + 1) * each, :] = block[...]
+    d_model = first_ref.shape[2]
+    for batch in range(first_ref.shape[0]):
+        undo = undo_ref[batch * first_ref.shape[1] : (batch + 1) * first_ref.shape[1], :]
+        first_ref[batch] = product(undo, rows[:, :d_model], NN, bf16)
+        second_ref[batch] = product(undo, rows[:, d_model:], NN, bf16)
+
+
+def at_home(undo, blocks, batches, d_model):
+    rows = undo.shape[0]
+    out = jax.ShapeDtypeStruct((batches, rows // batches, d_model), bf16)
+    return pl.pallas_call(
+        at_home_kernel,
+        out_shape=(out, out),
+        in_specs=[VMEM] * (1 + len(blocks)),
+        out_specs=(VMEM, VMEM),
+        scratch_shapes=[pltpu.VMEM((rows, 2 * d_model), bf16)],
+        compiler_params=pltpu.CompilerParams(vmem_limit_bytes=32 * 1024 * 1024),
+        cost_estimate=pl.CostEstimate(flops=0, bytes_accessed=10_000_000, transcendentals=0),
+        name="at_home",
+    )(undo, *blocks)
+
+
 VMEM = pl.BlockSpec(memory_space=pltpu.VMEM)
 SMEM = pl.BlockSpec(memory_space=pltpu.SMEM)
 
@@ -306,6 +392,7 @@
         out_specs=VMEM,
         scratch_shapes=[pltpu.VMEM((rows // BATCHES, width), bf16)],
         compiler_params=pltpu.CompilerParams(vmem_limit_bytes=32 * 1024 * 1024),
+        cost_estimate=pl.CostEstimate(flops=0, bytes_accessed=20_000_000, transcendentals=0),
         name="attend_forward",
     )(lengths, qkv, conv)
 
@@ -327,6 +414,7 @@
             pltpu.VMEM((group, width), f32),
         ],
         compiler_params=pltpu.CompilerParams(vmem_limit_bytes=32 * 1024 * 1024),
+        cost_estimate=pl.CostEstimate(flops=0, bytes_accessed=50_000_000, transcendentals=0),
         name="attend_backward",
     )(lengths, qkv, grad, conv)
 
@@ -334,14 +422,6 @@
 def part_of(total, each, index):
     start = jnp.minimum(index * each, total - each)
     return start, index * each - start
-
-
-def joined(parts, total, each):
-    pieces = []
-    for index, part in enumerate(parts):
-        start = min(index * each, total - each)
-        pieces.append(part[:, index * each - start :])
-    return jnp.concatenate(pieces, axis=1)
 
 
 def per_device(
@@ -434,13 +514,9 @@
         picked = product(choose, rows.reshape(-1, d_model), NN, bf16)
         return z_exchange(jnp.split(picked, n_fsdp), sizes)
 
-    def to_given(rows):
+    def to_home(rows):
         blocks = jnp.split(rows, n_fsdp)
-        home = jnp.concatenate(
-            [blocks[0]] + [z_shifted(blocks[k], sizes, n_fsdp - k) for k in range(1, n_fsdp)]
-        )
-        pair = jnp.concatenate([home, flipped(home, sizes, 2)])
-        return product(undo, pair, NN, bf16).reshape(BATCHES, tok_rows, d_model)
+        return [blocks[0]] + [z_shifted(blocks[k], sizes, n_fsdp - k) for k in range(1, n_fsdp)]
 
     own_x = to_planes(tokens).astype(f32)
 
@@ -478,63 +554,88 @@
 
     second_scale = lax.rsqrt(jnp.mean(resid * resid, axis=-1, keepdims=True) + epsilon)
     hidden_two = plane_gather((resid * second_scale * gains[1]).astype(bf16), sizes)
-    grad_inner = product(grad_dealt, down_w, NN)
-    gate_up_out = product(hidden_two, gate_w, NN)
-    gate_act, upper = gate_up_out[:, :ff], gate_up_out[:, ff:]
-    sigmoid = jax.nn.sigmoid(gate_act)
-    silu = gate_act * sigmoid
-    inner = (silu * upper).astype(bf16)
-    grad_gate = grad_inner * upper * (sigmoid * (1.0 + gate_act * (1.0 - sigmoid)))
-    grad_pair = jnp.concatenate([grad_gate, grad_inner * silu], axis=1).astype(bf16)
-    grad_mlp_w = weight_grad((hidden_two, grad_pair), (grad_dealt, inner))
+    hidden_two_turned, grad_dealt_turned = after((hidden_two.T, grad_dealt.T))
+    inner, grad_pair = feed_forward(
+        after(hidden_two, hidden_two_turned, grad_dealt_turned), grad_dealt, mlp_w
+    )
+    grad_mlp_w = weight_grad((hidden_two_turned, grad_pair), (grad_dealt_turned, inner))
+    grad_mlp_w, grad_pair, inner = stage(grad_mlp_w, grad_pair, inner)
     grad_mlp = lax.psum_scatter(grad_mlp_w, "fsdp", scatter_dimension=0, tiled=True)
-    grad_pair = after(grad_pair, grad_mlp_w)
-    grad_two = plane_scatter(
-        product(grad_pair[:kept], gate_w, NT),
-        product(grad_pair[kept:], gate_w, NT, bf16),
-        sizes,
-    )
-    lifted = plane_scatter(
-        product(inner[:kept], down_w, NT),
-        product(inner[kept:], down_w, NT, bf16),
-        sizes,
-    )
+
+    sent = product(grad_pair[kept:], gate_w, NT, bf16)
+    sent, grad_pair = stage(sent, grad_pair)
+
+    got = flipped(sent, sizes, 2)
+    part = product(grad_pair[:kept], gate_w, NT)
+    got, part = stage(got, part)
+    part, sent = added(part, got)
+    part, sent, inner = stage(part, sent, inner)
+
+    got = flipped(sent, sizes, 1)
+    lift_sent = product(inner[kept:], down_w, NT, bf16)
+    lift = product(inner[:kept], down_w, NT)
+    got, part, lift_sent, lift = stage(got, part, lift_sent, lift)
+    part, sent = added(part, got)
+    part, sent, lift_sent, lift = stage(part, sent, lift_sent, lift)
+
+    got = flipped(sent, sizes, 0)
+    lift_got = flipped(lift_sent, sizes, 2)
+    grad_two = part + got.astype(f32)
     normed = resid * second_scale
     scaled = grad_two * gains[1]
     grad_resid = own_g.astype(f32) + second_scale * (
         scaled - normed * jnp.mean(scaled * normed, axis=-1, keepdims=True)
     )
-
-    grad_branch = plane_gather(
-        after(grad_resid.astype(bf16), lifted), sizes
-    )
+    grad_own = grad_resid.astype(bf16)
+    lift, lift_sent = added(lift, lift_got)
+    grad_own, lift, lift_sent = stage(grad_own, lift, lift_sent)
+
+    near = near_shares(grad_own, sizes)
+    grad_own, near = stage(grad_own, near)
+    grad_branch = plane_gather(grad_own, sizes, near)
+    grad_branch, lift_sent = stage(grad_branch, lift_sent)
+
+    lift_got = flipped(lift_sent, sizes, 1)
     grad_attended = product(deal, product(grad_branch, out_w, NN, bf16), NN, bf16)
     grad_proj, grad_conv = attend_backward(own_lengths, qkv, grad_attended, conv)
+    lift_got, lift, grad_proj = stage(lift_got, lift, grad_proj)
+    lift, lift_sent = added(lift, lift_got)
+    lift, lift_sent, grad_proj = stage(lift, lift_sent, grad_proj)
+
+    lift_got = flipped(lift_sent, sizes, 0)
     grad_proj = product(deal, grad_proj, TN, bf16)
+    sent = product(grad_proj[kept:], qkv_w, NT, bf16)
+    lift_got, grad_proj, sent = stage(lift_got, grad_proj, sent)
+    result = (resid + (lift + lift_got.astype(f32))).astype(bf16)
+
+    got = flipped(sent, sizes, 2)
+    part = product(grad_proj[:kept], qkv_w, NT)
+    got, part = stage(got, part)
+    part, sent = added(part, got)
+    part, sent, grad_proj = stage(part, sent, grad_proj)
+
+    got = flipped(sent, sizes, 1)
     grad_attn_w = weight_grad((hidden, grad_proj), (grad_branch, attended))
+    got, part, grad_attn_w = stage(got, part, grad_attn_w)
     grad_attn = lax.psum_scatter(grad_attn_w, "fsdp", scatter_dimension=0, tiled=True)
-    grad_proj = after(grad_proj, grad_attn_w)
-    grad_hidden = plane_scatter(
-        product(grad_proj[:kept], qkv_w, NT), product(grad_proj[kept:], qkv_w, NT, bf16), sizes
-    )
+    part, sent = added(part, got)
+
+    grad_hidden = part + flipped(sent, sizes, 0).astype(f32)
     normed = own_x * first_scale
     scaled = grad_hidden * gains[0]
     grad_x = grad_resid + first_scale * (
         scaled - normed * jnp.mean(scaled * normed, axis=-1, keepdims=True)
     )
-    input_grad = to_given(grad_x.astype(bf16))
-
-    activations = to_given((resid + lifted).astype(bf16))
-
+    grad_x = grad_x.astype(bf16)
+
+    spread = lax.dynamic_update_slice(jnp.zeros((CONV, heads_all), f32), grad_conv, (0, start))
+    taps = jnp.where(jnp.arange(heads_all)[None, :] >= start + shared, spread, 0.0)
     if n_fsdp > 4:
-        taps = lax.psum(grad_conv, "fsdp")
+        taps = lax.psum(taps, "fsdp")
     else:
-        taps = sum([z_shifted(grad_conv, sizes, k) for k in range(1, n_fsdp)], grad_conv)
+        taps = sum([z_shifted(taps, sizes, k) for k in range(1, n_fsdp)], taps)
 
     steps = 4 if d_own % 64 == 0 else 1
-    grad_gate_up, grad_down = placed(
-        ctx_shares(grad_mlp, sizes, t), c, ff, ff_all, (2, 1), steps
-    )
 
     def gain_part(own, grad, each, skipped):
         columns = own.shape[1]
@@ -542,21 +643,37 @@
         terms = own.astype(f32) * grad[:, :columns].astype(f32)
         return jnp.sum(jnp.where(counted[None, :], terms, 0.0), axis=1)
 
-    grad_attn, taps = after((grad_attn, taps), grad_down)
-    sums = jnp.stack(
-        [
-            gain_part(attn_own[:, : 3 * width], grad_attn, width, shared),
-            gain_part(mlp_own[:, : 2 * ff], grad_mlp, ff, ff_shared),
-        ]
-    )
-    for step in (2, 0, 1):
-        sums = sums + flipped(sums, sizes, step)
-    grad_gains = sums / norm_gains.astype(f32)
-    taps = ctx_shares(taps, sizes, t)
-    taps = lax.switch(c, [lambda k=k: joined([taps[k ^ p] for p in range(n_ctx)], heads_all, width) for k in range(n_ctx)])
-    grad_conv = lax.dynamic_slice_in_dim(taps, f * (heads_all // n_fsdp), heads_all // n_fsdp, 1)
+    mlp_shares = ctx_shares(after(grad_mlp, grad_x), sizes, t)
+    gain_two = gain_part(mlp_own[:, : 2 * ff], grad_mlp, ff, ff_shared)
+    rows_back = jnp.concatenate([result, grad_x], axis=1)
+    grad_gate_up, grad_down = placed(mlp_shares, c, ff, ff_all, (2, 1), steps)
+    grad_attn, rows_back, grad_gate_up, grad_down, gain_two, taps = stage(
+        grad_attn, rows_back, grad_gate_up, grad_down, gain_two, taps
+    )
+
+    near = near_shares(grad_attn, sizes)
+    home = to_home(rows_back)
+    gain_one = gain_part(attn_own[:, : 3 * width], grad_attn, width, shared)
+    gains_grad = jnp.stack([gain_one, gain_two])
+    gains_grad = gains_grad + flipped(gains_grad, sizes, 2)
+    near, gains_grad = stage(near, gains_grad)
+
+    attn_shares = ctx_shares(grad_attn, sizes, t, near)
+    small = jnp.concatenate([gains_grad.reshape(-1), taps.reshape(-1)])
+    for step in (0, 1):
+        small = small + flipped(small, sizes, step)
+    activations, input_grad = at_home(
+        undo, home + [flipped(block, sizes, 2) for block in home], BATCHES, d_model
+    )
+    grad_gains = small[: gains_grad.size].reshape(2, -1) / norm_gains.astype(f32)
+    grad_conv = lax.dynamic_slice_in_dim(
+        small[gains_grad.size :].reshape(CONV, heads_all),
+        f * (heads_all // n_fsdp),
+        heads_all // n_fsdp,
+        1,
+    )
     grad_attn_in, grad_attn_out = placed(
-        ctx_shares(grad_attn, sizes, t), c, width, heads_all, (3, 1), steps
+        attn_shares, c, width, heads_all, (3, 1), steps
     )
     return (
         activations,

time: 519 us -> 511 us (0.985)
  matrix products: 68.2 us -> 44.2 us
  waiting for transfers between devices: 256 us -> 240 us
  other arithmetic: 22.4 us -> 35.8 us
  Pallas kernels: 47.8 us -> 59.4 us
    dot_general x18 -> x14, matrix products: 68.2 us -> 44.2 us  [product(): lax.dot_general(left, right, (dims, ((), ())), preferred_element_type=f32)]
    ppermute x54 -> x53, waiting for transfers between devices: 163 us -> 147 us  [flipped(): return lax.ppermute(value, ('fsdp', 'ctx', 'tp'), pairs)]
    convert_element_type x2 -> x10, other arithmetic: 2.94 us -> 15.1 us  [the longest x6 10.1 us: added(): (part[half:] + got[half:].astype(f32)).astype(bf16)]
    optimization_barrier x0 -> x2, local copies, waits for them, and re-layouts: none -> 11.9 us  [after(): return lax.optimization_barrier((value,) + others)[0]]
    pallas_call x2 -> x4, Pallas kernels: 19.4 us -> 29.8 us  [the longest x2 15.8 us: weight_grad(): pl.pallas_call(functools.partial(weight_grad_kernel, turned), grid=(d_mod...]
    all_gather x1, waiting for transfers between devices: 32 us -> 22.1 us  [per_device(): mlp_w = lax.all_gather(after(mlp_own, attn_own), 'fsdp', axis=0, tiled=True)]
    all_gather x1, waiting for transfers between devices: 13.5 us -> 22.8 us  [per_device(): attn_w = lax.all_gather(attn_own, 'fsdp', axis=0, tiled=True)]
    unnamed x121 -> x146, local copies, waits for them, and re-layouts: 30.2 us -> 23.1 us
  transfers between devices with their start and end apart: 74 -> 70, of which waited for: 29 -> 33; matrix products, arithmetic and copies ran while one was open for 21% -> 21% of each run, Pallas kernels for 6% -> 6%
where the time goes in v3:
time: 511 us; the launch traced here: 507 us
  waiting for transfers between devices  240 us (47%)
  starting transfers between devices  68.2 us (13%)
  Pallas kernels  59.4 us (12%)
  matrix products  44.2 us (9%)
  local copies, waits for them, and re-layouts  44 us (9%)
  other arithmetic  35.8 us (7%)
  between operations  15.2 us (3%)
    ppermute x53, waiting for transfers between devices, flipped(): return lax.ppermute(value, ('fsdp', 'ctx', 'tp'), pairs)  147 us
    ppermute x12, waiting for transfers between devices, z_shifted(): return lax.ppermute(value, 'fsdp', [(i, (i + steps) % n) for i in range(n)])  46 us
    dot_general x14, matrix products, product(): lax.dot_general(left, right, (dims, ((), ())), preferred_element_type=f32)  44.2 us
    ppermute x53, starting transfers between devices, flipped(): return lax.ppermute(value, ('fsdp', 'ctx', 'tp'), pairs)  41.5 us
    unnamed x146, local copies, waits for them, and re-layouts  23.1 us
    all_gather x1, waiting for transfers between devices, per_device(): attn_w = lax.all_gather(attn_own, 'fsdp', axis=0, tiled=True)  22.8 us
    all_gather x1, waiting for transfers between devices, per_device(): mlp_w = lax.all_gather(after(mlp_own, attn_own), 'fsdp', axis=0, tiled=True)  22.1 us
    ppermute x12, starting transfers between devices, z_shifted(): return lax.ppermute(value, 'fsdp', [(i, (i + steps) % n) for i in range(n)])  18.1 us
  transfers between devices with their start and end apart: 70, of which 33 were waited for; matrix products, arithmetic and copies ran while one was open for 21% of the time, Pallas kernels for 6%

profile of v3, /device:TPU:0, one launch (start us, length us, event | category | flops | bytes accessed | tf_op | source)
XLA Modules:
  0.0 507.1 jit_solution(3962184597771107683)
XLA Ops:
  12.1 8.2 %all-to-all-start = ((f32[16,1,1824]{2,1,0:T(1,128)}), f32[16,1,1824]{2,1,0:T(1,128)S(1)}, u32[]{:S(2)}, u32[]{:S(2)}) async-start(f32[16,1,1824]{2,1,0:T(1,128)} %broadcast_in_dim.111), calls=%async_computation | async-start | bytes 245760 | tf_op jit(solution)/shard_map/all_to_all | solution.py:478
  20.4 1.9 dynamic-slice_bitcast_fusion.1
  22.4 1.8 select_bitcast_fusion
  26.3 1.8 all-to-all-done
  29.9 3.9 collective-permute-start.1
  35.8 3.9 collective-permute-done
  39.7 6.8 %collective-permute-done.1 = bf16[32,1792]{1,0:T(8,128)(2,1)S(1)} collective-permute-done((bf16[32,1792]{1,0:T(8,128)(2,1)S(1)}, bf16[32,1792]{1,0:T(8,128)(2,1)S(1)}, u32[]{:S(2)}, u32[]{:S(2)}) %collective-permute-start.1) | collective-permute-done | bytes 114720 | tf_op jit(solution)/shard_map/ppermute | solution.py:72
  51.6 9.2 %collective-permute-done.3 = bf16[128,1792]{1,0:T(8,128)(2,1)S(1)} collective-permute-done((bf16[128,1792]{1,0:T(8,128)(2,1)S(1)}, bf16[128,1792]{1,0:T(8,128)(2,1)S(1)}, u32[]{:S(2)}, u32[]{:S(2)}) %collective-permute-start.3) | collective-permute-done | bytes 458784 | tf_op jit(solution)/shard_map/ppermute | solution.py:35
  64.1 5.2 %collective-permute-done.5 = bf16[128,1792]{1,0:T(8,128)(2,1)S(1)} collective-permute-done((bf16[128,1792]{1,0:T(8,128)(2,1)S(1)}, bf16[128,1792]{1,0:T(8,128)(2,1)S(1)}, u32[]{:S(2)}, u32[]{:S(2)}) %collective-permute-start.5) | collective-permute-done | bytes 458784 | tf_op jit(solution)/shard_map/ppermute | solution.py:35
  73.3 22.8 %all-gather.3.cloned.1.call-done = bf16[1792,1024]{1,0:T(8,128)(2,1)} async-done(((bf16[448,1024]{1,0:T(8,128)(2,1)}), bf16[1792,1024]{1,0:T(8,128)(2,1)}) %all-gather.3.cloned.1.call-update) | async-done | bytes 3670032 | tf_op jit(solution)/shard_map/all_gather | solution.py:465
  96.0 7.5 %fusion.26.qkv_ref = bf16[1024,768]{1,0:T(8,128)(2,1)S(1)} fusion(s32[1024]{0:T(1024)S(1)} %fusion.79, bf16[1024,1792]{1,0:T(8,128)(2,1)} %constant_dynamic-update-slice_fusion.refs_0_, bf16[1792,1024]{1,0:T(8,128)(2,1)} %all-gather.3.cloned.1.call-done), kind=kOutput, calls=%fused_computation.43 | convolution fusion | flops 4431806464 | bytes 7999488 | tf_op jit(solution)/shard_map/dot_general | solution.py:87
  103.6 5.8 %attend_forward.1 = bf16[1024,256]{1,0:T(8,128)(2,1)S(1)} custom-call(s32[2,3]{1,0:T(2,128)S(1)} %bitcast.80, bf16[1024,768]{1,0:T(8,128)(2,1)S(1)} %fusion.26.qkv_ref, f32[3,256]{1,0:T(4,128)S(1)} %constant_dynamic-slice_fusion.1.conv_ref), custom_call_target="tpu_custom_call" | custom-call | bytes 20000000 | tf_op jit(solution)/shard_map/attend_forward/pallas_call | solution.py:388
  110.9 3.1 convolution_convert_fusion
  116.0 2.8 collective-permute-start.12
  118.9 5.8 %collective-permute-done.10 = bf16[32,1792]{1,0:T(8,128)(2,1)S(1)} collective-permute-done((bf16[32,1792]{1,0:T(8,128)(2,1)S(1)}, bf16[32,1792]{1,0:T(8,128)(2,1)S(1)}, u32[]{:S(2)}, u32[]{:S(2)}) %collective-permute-start.10) | collective-permute-done | bytes 114720 | tf_op jit(solution)/shard_map/ppermute | solution.py:72
  124.7 8.7 %collective-permute-done.11 = bf16[32,1792]{1,0:T(8,128)(2,1)S(1)} collective-permute-done((bf16[32,1792]{1,0:T(8,128)(2,1)S(1)}, bf16[32,1792]{1,0:T(8,128)(2,1)S(1)}, u32[]{:S(2)}, u32[]{:S(2)}) %collective-permute-start.11) | collective-permute-done | bytes 114720 | tf_op jit(solution)/shard_map/ppermute | solution.py:72
  136.5 2.5 convert_add_fusion
  140.5 6.4 %collective-permute-done.23 = bf16[128,1792]{1,0:T(8,128)(2,1)S(1)} collective-permute-done((bf16[128,1792]{1,0:T(8,128)(2,1)S(1)}, bf16[128,1792]{1,0:T(8,128)(2,1)S(1)}, u32[]{:S(2)}, u32[]{:S(2)}) %collective-permute-start.23) | collective-permute-done | bytes 458784 | tf_op jit(solution)/shard_map/ppermute | solution.py:35
  150.5 9.7 %collective-permute-done.25 = bf16[128,1792]{1,0:T(8,128)(2,1)S(1)} collective-permute-done((bf16[128,1792]{1,0:T(8,128)(2,1)S(1)}, bf16[128,1792]{1,0:T(8,128)(2,1)S(1)}, u32[]{:S(2)}, u32[]{:S(2)}) %collective-permute-start.25) | collective-permute-done | bytes 458784 | tf_op jit(solution)/shard_map/ppermute | solution.py:35
  165.8 5.4 %collective-permute-done.15 = bf16[128,1792]{1,0:T(8,128)(2,1)S(1)} collective-permute-done((bf16[128,1792]{1,0:T(8,128)(2,1)S(1)}, bf16[128,1792]{1,0:T(8,128)(2,1)S(1)}, u32[]{:S(2)}, u32[]{:S(2)}) %collective-permute-start.15) | collective-permute-done | bytes 458784 | tf_op jit(solution)/shard_map/ppermute | solution.py:35
  176.1 8.4 %collective-permute-done.16 = bf16[128,1792]{1,0:T(8,128)(2,1)S(1)} collective-permute-done((bf16[128,1792]{1,0:T(8,128)(2,1)S(1)}, bf16[128,1792]{1,0:T(8,128)(2,1)S(1)}, u32[]{:S(2)}, u32[]{:S(2)}) %collective-permute-start.16) | collective-permute-done | bytes 458784 | tf_op jit(solution)/shard_map/ppermute | solution.py:35
  184.6 1.8 collective-permute-start.18
  188.4 4.6 collective-permute-done.18
  197.0 6.0 %copy.33.refs_0_ = bf16[1792,1024]{1,0:T(8,128)(2,1)} copy(bf16[1792,1024]{0,1:T(8,128)(2,1)} %bitcast.19) | data formatting | bytes 7340032 | tf_op jit(solution)/shard_map/optimization_barrier | solution.py:58
  203.0 5.9 %copy.34.refs_2_ = bf16[1792,1024]{1,0:T(8,128)(2,1)} copy(bf16[1792,1024]{0,1:T(8,128)(2,1)} %bitcast.20) | data formatting | bytes 7340032 | tf_op jit(solution)/shard_map/optimization_barrier | solution.py:58
  208.9 22.1 %all-gather.5.cloned.1.call-done.weight_ref = bf16[1792,1920]{1,0:T(8,128)(2,1)} async-done(((bf16[448,1920]{1,0:T(8,128)(2,1)}), bf16[1792,1920]{1,0:T(8,128)(2,1)}) %all-gather.5.cloned.1.call-update) | async-done | bytes 6881296 | tf_op jit(solution)/shard_map/all_gather | solution.py:466
  231.1 12.2 %feed_forward.1 = (bf16[1024,640]{1,0:T(8,128)(2,1)S(1)}, bf16[1024,1280]{1,0:T(8,128)(2,1)S(1)}) custom-call(bf16[1024,1792]{1,0:T(8,128)(2,1)} %constant_dynamic-update-slice_fusion.8.hidden_ref, bf16[1024,1792]{1,0:T(8,128)(2,1)} %constant_dynamic-update-slice_fusion.16.grad_ref, bf16[1792,1920]{1,0:T(8,128)(2,1)} %all-gather.5.cloned.1.call-done.weight_ref), custom_call_target="tpu_custom_call" | custom-call | flops 7046430720 | bytes 18153472 | tf_op jit(solution)/shard_map/feed_forward/pallas_call | solution.py:291
  243.4 9.8 %weight_grad.2 = bf16[1792,1920]{1,0:T(8,128)(2,1)} custom-call(bf16[1792,1024]{1,0:T(8,128)(2,1)S(1)} %copy-done.4, bf16[1024,1280]{1,0:T(8,128)(2,1)S(1)} %get-tuple-element.89.refs_1_, bf16[1792,1024]{1,0:T(8,128)(2,1)S(1)} %copy-done.5, bf16[1024,640]{1,0:T(8,128)(2,1)S(1)} %get-tuple-element.95.refs_3_), custom_call_target="tpu_custom_call" | custom-call | flops 7046430720 | bytes 18153472 | tf_op jit(solution)/shard_map/weight_grad/pallas_call | solution.py:259
  255.7 6.5 %fusion.8 = bf16[512,1792]{1,0:T(8,128)(2,1)} fusion(bf16[1792,1920]{1,0:T(8,128)(2,1)} %all-gather.5.cloned.1.call-done.weight_ref, bf16[1024,1280]{1,0:T(8,128)(2,1)} %copy-done.13), kind=kOutput, calls=%fused_computation.11 | convolution fusion | flops 2349727744 | bytes 7733248 | tf_op jit(solution)/shard_map/dot_general | solution.py:87
  262.6 5.3 %fusion.4 = f32[512,1792]{1,0:T(8,128)S(1)} fusion(bf16[1792,1920]{1,0:T(8,128)(2,1)} %all-gather.5.cloned.1.call-done.weight_ref, bf16[1024,1280]{1,0:T(8,128)(2,1)} %copy-done.13), kind=kOutput, calls=%fused_computation.5 | convolution fusion | flops 2348810240 | bytes 9568256 | tf_op jit(solution)/shard_map/dot_general | solution.py:87
  267.9 2.1 add_convert_fusion.2
  270.0 1.7 collective-permute-start.31
  271.7 3.3 convolution_convert_fusion.2
  274.9 3.3 fusion.20
  278.2 5.2 %collective-permute-done.31 = bf16[256,1792]{1,0:T(8,128)(2,1)S(1)} collective-permute-done((bf16[256,1792]{1,0:T(8,128)(2,1)S(1)}, bf16[256,1792]{1,0:T(8,128)(2,1)S(1)}, u32[]{:S(2)}, u32[]{:S(2)}) %collective-permute-start.31) | collective-permute-done | bytes 917536 | tf_op jit(solution)/shard_map/ppermute | solution.py:35
  285.3 6.9 %collective-permute-done.32 = bf16[128,1792]{1,0:T(8,128)(2,1)S(1)} collective-permute-done((bf16[128,1792]{1,0:T(8,128)(2,1)S(1)}, bf16[128,1792]{1,0:T(8,128)(2,1)S(1)}, u32[]{:S(2)}, u32[]{:S(2)}) %collective-permute-start.32) | collective-permute-done | bytes 458784 | tf_op jit(solution)/shard_map/ppermute | solution.py:35
  293.9 1.9 add_convert_fusion.1
  298.8 10.2 %collective-permute-done.34 = bf16[128,1792]{1,0:T(8,128)(2,1)S(1)} collective-permute-done((bf16[128,1792]{1,0:T(8,128)(2,1)S(1)}, bf16[128,1792]{1,0:T(8,128)(2,1)S(1)}, u32[]{:S(2)}, u32[]{:S(2)}) %collective-permute-start.34) | collective-permute-done | bytes 458784 | tf_op jit(solution)/shard_map/ppermute | solution.py:35
  311.2 6.4 %collective-permute-done.36 = bf16[128,1792]{1,0:T(8,128)(2,1)S(1)} collective-permute-done((bf16[128,1792]{1,0:T(8,128)(2,1)S(1)}, bf16[128,1792]{1,0:T(8,128)(2,1)S(1)}, u32[]{:S(2)}, u32[]{:S(2)}) %collective-permute-start.36) | collective-permute-done | bytes 458784 | tf_op jit(solution)/shard_map/ppermute | solution.py:35
  319.4 1.8 copy-done.7
  321.8 5.1 fusion.31.grad_ref
  326.8 14.1 %attend_backward.1 = (bf16[1024,768]{1,0:T(8,128)(2,1)S(1)}, f32[3,256]{1,0:T(4,128)S(1)}) custom-call(s32[2,3]{1,0:T(2,128)S(1)} %bitcast.81, bf16[1024,768]{1,0:T(8,128)(2,1)S(1)} %fusion.26.qkv_ref, bf16[1024,256]{1,0:T(8,128)(2,1)S(1)} %fusion.31.grad_ref, f32[3,256]{1,0:T(4,128)S(1)} %constant_dynamic-slice_fusion.1.conv_ref), custom_call_target="tpu_custom_call" | custom-call | bytes 50000000 | tf_op jit(solution)/shard_map/attend_backward/pallas_call | solution.py:403
  340.9 2.9 add_convert_fusion.5
  345.4 2.4 fusion.27.refs_1_
  349.4 2.9 collective-permute-done.42
  354.0 2.1 collective-permute-done.43
  356.1 1.9 add_convert_fusion
  359.4 6.0 %weight_grad.3 = bf16[1792,1024]{1,0:T(8,128)(2,1)S(1)} custom-call(bf16[1024,1792]{1,0:T(8,128)(2,1)S(1)} %copy-done.9, bf16[1024,768]{1,0:T(8,128)(2,1)S(1)} %fusion.27.refs_1_, bf16[1024,1792]{1,0:T(8,128)(2,1)S(1)} %copy-done.8, bf16[1024,256]{1,0:T(8,128)(2,1)S(1)} %fusion.30.refs_3_), custom_call_target="tpu_custom_call" | custom-call | flops 3758096384 | bytes 13107200 | tf_op jit(solution)/shard_map/weight_grad/pallas_call | solution.py:259
  365.4 1.8 copy-done.3
  367.2 4.4 collective-permute-done.44
  374.5 6.9 %collective-permute-done.45 = bf16[128,1792]{1,0:T(8,128)(2,1)S(1)} collective-permute-done((bf16[128,1792]{1,0:T(8,128)(2,1)S(1)}, bf16[128,1792]{1,0:T(8,128)(2,1)S(1)}, u32[]{:S(2)}, u32[]{:S(2)}) %collective-permute-start.45) | collective-permute-done | bytes 458784 | tf_op jit(solution)/shard_map/ppermute | solution.py:35
  382.9 2.2 fusion.40
  389.2 3.3 collective-permute-start.51
  393.3 4.0 collective-permute-done.51
  397.3 28.6 %collective-permute-done.46 = bf16[448,1920]{1,0:T(8,128)(2,1)} collective-permute-done((bf16[448,1920]{1,0:T(8,128)(2,1)}, bf16[448,1920]{1,0:T(8,128)(2,1)}, u32[]{:S(2)}, u32[]{:S(2)}) %collective-permute-start.46) | collective-permute-done | bytes 1720352 | tf_op jit(solution)/shard_map/ppermute | solution.py:35
  430.8 2.3 broadcast_select_fusion
  433.2 14.9 %collective-permute-done.48.refs_3_ = bf16[448,1920]{1,0:T(8,128)(2,1)S(1)} collective-permute-done((bf16[448,1920]{1,0:T(8,128)(2,1)}, bf16[448,1920]{1,0:T(8,128)(2,1)S(1)}, u32[]{:S(2)}, u32[]{:S(2)}) %collective-permute-start.48) | collective-permute-done | bytes 1720352 | tf_op jit(solution)/shard_map/ppermute | solution.py:35
  448.1 5.1 %placed.2 = (f32[2,448,2432]{2,1,0:T(8,128)}, f32[1,448,2432]{2,1,0:T(8,128)}) custom-call(s32[1]{0:T(128)} %bitcast.24.index_ref, bf16[448,1920]{1,0:T(8,128)(2,1)S(1)} %copy-done.2, bf16[448,1920]{1,0:T(8,128)(2,1)S(1)} %get-tuple-element.169.refs_1_, bf16[448,1920]{1,0:T(8,128)(2,1)S(1)} %get-tuple-element.168.refs_2_, ...), custom_call_target="tpu_custom_call" | custom-call | bytes 20643840 | tf_op jit(solution)/shard_map/placed/pallas_call | solution.py:341
  456.1 2.7 collective-permute-start.52
  462.4 2.5 collective-permute-done.52.refs_1_
  464.9 13.7 %collective-permute-done.53.refs_2_ = bf16[32,3584]{1,0:T(8,128)(2,1)S(1)} collective-permute-done((bf16[32,3584]{1,0:T(8,128)(2,1)S(1)}, bf16[32,3584]{1,0:T(8,128)(2,1)S(1)}, u32[]{:S(2)}, u32[]{:S(2)}) %collective-permute-start.53) | collective-permute-done | bytes 229408 | tf_op jit(solution)/shard_map/ppermute | solution.py:72
  480.8 1.8 at_home.1
  486.9 6.1 %collective-permute-done.64 = f32[3584]{0:T(1024)S(1)} collective-permute-done((f32[3584]{0:T(1024)S(1)}, f32[3584]{0:T(1024)S(1)}, u32[]{:S(2)}, u32[]{:S(2)}) %collective-permute-start.64) | collective-permute-done | bytes 14368 | tf_op jit(solution)/shard_map/ppermute | solution.py:35
  495.6 4.7 placed.3
  (352 shorter events, 101.0 us)
Async XLA Ops:
  7.2 88.8 %all-gather.3.cloned.1.call-start = ((), (), s32[]{:S(2)}) async-start(), calls=%async_computation.3 | async-start | bytes 4587520 | tf_op jit(solution)/shard_map/all_gather | solution.py:465
  12.1 16.0 %all-to-all-start = ((f32[16,1,1824]{2,1,0:T(1,128)}), f32[16,1,1824]{2,1,0:T(1,128)S(1)}, u32[]{:S(2)}, u32[]{:S(2)}) async-start(f32[16,1,1824]{2,1,0:T(1,128)} %broadcast_in_dim.111), calls=%async_computation | async-start | bytes 245760 | tf_op jit(solution)/shard_map/all_to_all | solution.py:478
  20.3 210.8 %all-gather.5.cloned.1.call-start = ((), (), s32[]{:S(2)}) async-start(), calls=%async_computation.4 | async-start | bytes 8601600 | tf_op jit(solution)/shard_map/all_gather | solution.py:466
  25.6 359.5 %reduce-scatter.5.cloned.1.call-start = ((), (), s32[]{:S(2)}) async-start(), calls=%async_computation.6 | async-start | bytes 8601600 | tf_op jit(solution)/shard_map/reduce_scatter | solution.py:563
  29.2 10.5 %collective-permute-start = (bf16[32,1792]{1,0:T(8,128)(2,1)S(1)}, bf16[32,1792]{1,0:T(8,128)(2,1)S(1)}, u32[]{:S(2)}, u32[]{:S(2)}) collective-permute-start(bf16[32,1792]{1,0:T(8,128)(2,1)S(1)} %get-tuple-element.190), channel_id=1, source_target_pairs={{0,8},{8,16},{16,24},{24,0},{1,9},{9,17},{17,25},{25,1},{2,10},{10... | collective-permute-start | bytes 344072 | tf_op jit(solution)/shard_map/ppermute | solution.py:72
  29.9 16.6 %collective-permute-start.1 = (bf16[32,1792]{1,0:T(8,128)(2,1)S(1)}, bf16[32,1792]{1,0:T(8,128)(2,1)S(1)}, u32[]{:S(2)}, u32[]{:S(2)}) collective-permute-start(bf16[32,1792]{1,0:T(8,128)(2,1)S(1)} %get-tuple-element.189), channel_id=1, source_target_pairs={{0,16},{8,24},{16,0},{24,8},{1,17},{9,25},{17,1},{25,9},{2,18},{10... | collective-permute-start | bytes 344072 | tf_op jit(solution)/shard_map/ppermute | solution.py:72
  33.9 12.7 %collective-permute-start.2 = (bf16[32,1792]{1,0:T(8,128)(2,1)S(1)}, bf16[32,1792]{1,0:T(8,128)(2,1)S(1)}, u32[]{:S(2)}, u32[]{:S(2)}) collective-permute-start(bf16[32,1792]{1,0:T(8,128)(2,1)S(1)} %get-tuple-element.188), channel_id=1, source_target_pairs={{0,24},{8,0},{16,8},{24,16},{1,25},{9,1},{17,9},{25,17},{2,26},{10... | collective-permute-start | bytes 344072 | tf_op jit(solution)/shard_map/ppermute | solution.py:72
  47.7 13.1 %collective-permute-start.3 = (bf16[128,1792]{1,0:T(8,128)(2,1)S(1)}, bf16[128,1792]{1,0:T(8,128)(2,1)S(1)}, u32[]{:S(2)}, u32[]{:S(2)}) collective-permute-start(bf16[128,1792]{1,0:T(8,128)(2,1)S(1)} %get-tuple-element.157), channel_id=1, source_target_pairs={{0,2},{1,5},{2,0},{3,7},{4,6},{5,1},{6,4},{7,3},{8,10},{9,13},{10,... | collective-permute-start | bytes 1376264 | tf_op jit(solution)/shard_map/ppermute | solution.py:35
  49.1 12.9 %collective-permute-start.4 = (bf16[128,1792]{1,0:T(8,128)(2,1)S(1)}, bf16[128,1792]{1,0:T(8,128)(2,1)S(1)}, u32[]{:S(2)}, u32[]{:S(2)}) collective-permute-start(bf16[128,1792]{1,0:T(8,128)(2,1)S(1)} %get-tuple-element.157), channel_id=1, source_target_pairs={{0,4},{1,3},{2,6},{3,1},{4,0},{5,7},{6,2},{7,5},{8,12},{9,11},{10,... | collective-permute-start | bytes 1376264 | tf_op jit(solution)/shard_map/ppermute | solution.py:35
  51.5 18.6 %collective-permute-start.6 = (bf16[128,1792]{1,0:T(8,128)(2,1)S(1)}, bf16[128,1792]{1,0:T(8,128)(2,1)S(1)}, u32[]{:S(2)}, u32[]{:S(2)}) collective-permute-start(bf16[128,1792]{1,0:T(8,128)(2,1)S(1)} %get-tuple-element.157), channel_id=1, source_target_pairs={{0,1},{1,0},{2,3},{3,2},{4,5},{5,4},{6,7},{7,6},{8,9},{9,8},{10,11... | collective-permute-start | bytes 1376264 | tf_op jit(solution)/shard_map/ppermute | solution.py:35
  60.8 8.5 %collective-permute-start.5 = (bf16[128,1792]{1,0:T(8,128)(2,1)S(1)}, bf16[128,1792]{1,0:T(8,128)(2,1)S(1)}, u32[]{:S(2)}, u32[]{:S(2)}) collective-permute-start(bf16[128,1792]{1,0:T(8,128)(2,1)S(1)} %collective-permute-done.3), channel_id=1, source_target_pairs={{0,4},{1,3},{2,6},{3,1},{4,0},{5,7},{6,2},{7,5},{8,12},{9,11},{10,... | collective-permute-start | bytes 1376264 | tf_op jit(solution)/shard_map/ppermute | solution.py:35
  62.0 8.9 %collective-permute-start.7 = (bf16[128,1792]{1,0:T(8,128)(2,1)S(1)}, bf16[128,1792]{1,0:T(8,128)(2,1)S(1)}, u32[]{:S(2)}, u32[]{:S(2)}) collective-permute-start(bf16[128,1792]{1,0:T(8,128)(2,1)S(1)} %collective-permute-done.3), channel_id=1, source_target_pairs={{0,1},{1,0},{2,3},{3,2},{4,5},{5,4},{6,7},{7,6},{8,9},{9,8},{10,11... | collective-permute-start | bytes 1376264 | tf_op jit(solution)/shard_map/ppermute | solution.py:35
  62.0 9.7 %collective-permute-start.8 = (bf16[128,1792]{1,0:T(8,128)(2,1)S(1)}, bf16[128,1792]{1,0:T(8,128)(2,1)S(1)}, u32[]{:S(2)}, u32[]{:S(2)}) collective-permute-start(bf16[128,1792]{1,0:T(8,128)(2,1)S(1)} %collective-permute-done.4), channel_id=1, source_target_pairs={{0,1},{1,0},{2,3},{3,2},{4,5},{5,4},{6,7},{7,6},{8,9},{9,8},{10,11... | collective-permute-start | bytes 1376264 | tf_op jit(solution)/shard_map/ppermute | solution.py:35
  69.3 3.2 collective-permute-start.9
  113.9 22.5 %collective-permute-start.13 = (bf16[512,1792]{1,0:T(8,128)(2,1)}, bf16[512,1792]{1,0:T(8,128)(2,1)}, u32[]{:S(2)}, u32[]{:S(2)}) collective-permute-start(bf16[512,1792]{1,0:T(8,128)(2,1)} %convolution_convert_fusion), channel_id=1, source_target_pairs={{0,1},{1,0},{2,3},{3,2},{4,5},{5,4},{6,7},{7,6},{8,9},{9,8},{10,11... | collective-permute-start | bytes 5505032 | tf_op jit(solution)/shard_map/ppermute | solution.py:35
  114.4 10.3 %collective-permute-start.10 = (bf16[32,1792]{1,0:T(8,128)(2,1)S(1)}, bf16[32,1792]{1,0:T(8,128)(2,1)S(1)}, u32[]{:S(2)}, u32[]{:S(2)}) collective-permute-start(bf16[32,1792]{1,0:T(8,128)(2,1)S(1)} %get-tuple-element.186), channel_id=1, source_target_pairs={{0,8},{8,16},{16,24},{24,0},{1,9},{9,17},{17,25},{25,1},{2,10},{10... | collective-permute-start | bytes 344072 | tf_op jit(solution)/shard_map/ppermute | solution.py:72
  114.5 18.9 %collective-permute-start.11 = (bf16[32,1792]{1,0:T(8,128)(2,1)S(1)}, bf16[32,1792]{1,0:T(8,128)(2,1)S(1)}, u32[]{:S(2)}, u32[]{:S(2)}) collective-permute-start(bf16[32,1792]{1,0:T(8,128)(2,1)S(1)} %get-tuple-element.185), channel_id=1, source_target_pairs={{0,16},{8,24},{16,0},{24,8},{1,17},{9,25},{17,1},{25,9},{2,18},{10... | collective-permute-start | bytes 344072 | tf_op jit(solution)/shard_map/ppermute | solution.py:72
  116.0 17.4 %collective-permute-start.12 = (bf16[32,1792]{1,0:T(8,128)(2,1)S(1)}, bf16[32,1792]{1,0:T(8,128)(2,1)S(1)}, u32[]{:S(2)}, u32[]{:S(2)}) collective-permute-start(bf16[32,1792]{1,0:T(8,128)(2,1)S(1)} %get-tuple-element.184), channel_id=1, source_target_pairs={{0,24},{8,0},{16,8},{24,16},{1,25},{9,1},{17,9},{25,17},{2,26},{10... | collective-permute-start | bytes 344072 | tf_op jit(solution)/shard_map/ppermute | solution.py:72
  133.4 13.5 %collective-permute-start.23 = (bf16[128,1792]{1,0:T(8,128)(2,1)S(1)}, bf16[128,1792]{1,0:T(8,128)(2,1)S(1)}, u32[]{:S(2)}, u32[]{:S(2)}) collective-permute-start(bf16[128,1792]{1,0:T(8,128)(2,1)S(1)} %pad_maximum_fusion.4), channel_id=1, source_target_pairs={{0,2},{1,5},{2,0},{3,7},{4,6},{5,1},{6,4},{7,3},{8,10},{9,13},{10,... | collective-permute-start | bytes 1376264 | tf_op jit(solution)/shard_map/ppermute | solution.py:35
  134.9 13.5 %collective-permute-start.24 = (bf16[128,1792]{1,0:T(8,128)(2,1)S(1)}, bf16[128,1792]{1,0:T(8,128)(2,1)S(1)}, u32[]{:S(2)}, u32[]{:S(2)}) collective-permute-start(bf16[128,1792]{1,0:T(8,128)(2,1)S(1)} %pad_maximum_fusion.4), channel_id=1, source_target_pairs={{0,4},{1,3},{2,6},{3,1},{4,0},{5,7},{6,2},{7,5},{8,12},{9,11},{10,... | collective-permute-start | bytes 1376264 | tf_op jit(solution)/shard_map/ppermute | solution.py:35
  136.4 27.8 %collective-permute-start.26 = (bf16[128,1792]{1,0:T(8,128)(2,1)S(1)}, bf16[128,1792]{1,0:T(8,128)(2,1)S(1)}, u32[]{:S(2)}, u32[]{:S(2)}) collective-permute-start(bf16[128,1792]{1,0:T(8,128)(2,1)S(1)} %pad_maximum_fusion.4), channel_id=1, source_target_pairs={{0,1},{1,0},{2,3},{3,2},{4,5},{5,4},{6,7},{7,6},{8,9},{9,8},{10,11... | collective-permute-start | bytes 1376264 | tf_op jit(solution)/shard_map/ppermute | solution.py:35
  139.1 23.4 %collective-permute-start.14 = (bf16[256,1792]{1,0:T(8,128)(2,1)S(1)}, bf16[256,1792]{1,0:T(8,128)(2,1)S(1)}, u32[]{:S(2)}, u32[]{:S(2)}) collective-permute-start(bf16[256,1792]{1,0:T(8,128)(2,1)S(1)} %slice.362), channel_id=1, source_target_pairs={{0,4},{1,3},{2,6},{3,1},{4,0},{5,7},{6,2},{7,5},{8,12},{9,11},{10,... | collective-permute-start | bytes 2752520 | tf_op jit(solution)/shard_map/ppermute | solution.py:35
  146.9 13.3 %collective-permute-start.25 = (bf16[128,1792]{1,0:T(8,128)(2,1)S(1)}, bf16[128,1792]{1,0:T(8,128)(2,1)S(1)}, u32[]{:S(2)}, u32[]{:S(2)}) collective-permute-start(bf16[128,1792]{1,0:T(8,128)(2,1)S(1)} %collective-permute-done.23), channel_id=1, source_target_pairs={{0,4},{1,3},{2,6},{3,1},{4,0},{5,7},{6,2},{7,5},{8,12},{9,11},{10,... | collective-permute-start | bytes 1376264 | tf_op jit(solution)/shard_map/ppermute | solution.py:35
  148.4 16.7 %collective-permute-start.27 = (bf16[128,1792]{1,0:T(8,128)(2,1)S(1)}, bf16[128,1792]{1,0:T(8,128)(2,1)S(1)}, u32[]{:S(2)}, u32[]{:S(2)}) collective-permute-start(bf16[128,1792]{1,0:T(8,128)(2,1)S(1)} %collective-permute-done.23), channel_id=1, source_target_pairs={{0,1},{1,0},{2,3},{3,2},{4,5},{5,4},{6,7},{7,6},{8,9},{9,8},{10,11... | collective-permute-start | bytes 1376264 | tf_op jit(solution)/shard_map/ppermute | solution.py:35
  148.4 26.1 %collective-permute-start.28 = (bf16[128,1792]{1,0:T(8,128)(2,1)S(1)}, bf16[128,1792]{1,0:T(8,128)(2,1)S(1)}, u32[]{:S(2)}, u32[]{:S(2)}) collective-permute-start(bf16[128,1792]{1,0:T(8,128)(2,1)S(1)} %collective-permute-done.24), channel_id=1, source_target_pairs={{0,1},{1,0},{2,3},{3,2},{4,5},{5,4},{6,7},{7,6},{8,9},{9,8},{10,11... | collective-permute-start | bytes 1376264 | tf_op jit(solution)/shard_map/ppermute | solution.py:35
  160.2 15.1 %collective-permute-start.29 = (bf16[128,1792]{1,0:T(8,128)(2,1)S(1)}, bf16[128,1792]{1,0:T(8,128)(2,1)S(1)}, u32[]{:S(2)}, u32[]{:S(2)}) collective-permute-start(bf16[128,1792]{1,0:T(8,128)(2,1)S(1)} %collective-permute-done.25), channel_id=1, source_target_pairs={{0,1},{1,0},{2,3},{3,2},{4,5},{5,4},{6,7},{7,6},{8,9},{9,8},{10,11... | collective-permute-start | bytes 1376264 | tf_op jit(solution)/shard_map/ppermute | solution.py:35
  162.7 8.5 %collective-permute-start.15 = (bf16[128,1792]{1,0:T(8,128)(2,1)S(1)}, bf16[128,1792]{1,0:T(8,128)(2,1)S(1)}, u32[]{:S(2)}, u32[]{:S(2)}) collective-permute-start(bf16[128,1792]{1,0:T(8,128)(2,1)S(1)} %slice.363), channel_id=1, source_target_pairs={{0,2},{1,5},{2,0},{3,7},{4,6},{5,1},{6,4},{7,3},{8,10},{9,13},{10,... | collective-permute-start | bytes 1376264 | tf_op jit(solution)/shard_map/ppermute | solution.py:35
  172.5 12.0 %collective-permute-start.16 = (bf16[128,1792]{1,0:T(8,128)(2,1)S(1)}, bf16[128,1792]{1,0:T(8,128)(2,1)S(1)}, u32[]{:S(2)}, u32[]{:S(2)}) collective-permute-start(bf16[128,1792]{1,0:T(8,128)(2,1)S(1)} %get-tuple-element.153), channel_id=1, source_target_pairs={{0,2},{1,5},{2,0},{3,7},{4,6},{5,1},{6,4},{7,3},{8,10},{9,13},{10,... | collective-permute-start | bytes 1376264 | tf_op jit(solution)/shard_map/ppermute | solution.py:35
  174.0 12.3 %collective-permute-start.17 = (bf16[128,1792]{1,0:T(8,128)(2,1)S(1)}, bf16[128,1792]{1,0:T(8,128)(2,1)S(1)}, u32[]{:S(2)}, u32[]{:S(2)}) collective-permute-start(bf16[128,1792]{1,0:T(8,128)(2,1)S(1)} %get-tuple-element.153), channel_id=1, source_target_pairs={{0,4},{1,3},{2,6},{3,1},{4,0},{5,7},{6,2},{7,5},{8,12},{9,11},{10,... | collective-permute-start | bytes 1376264 | tf_op jit(solution)/shard_map/ppermute | solution.py:35
  176.1 17.7 %collective-permute-start.19 = (bf16[128,1792]{1,0:T(8,128)(2,1)S(1)}, bf16[128,1792]{1,0:T(8,128)(2,1)S(1)}, u32[]{:S(2)}, u32[]{:S(2)}) collective-permute-start(bf16[128,1792]{1,0:T(8,128)(2,1)S(1)} %get-tuple-element.153), channel_id=1, source_target_pairs={{0,1},{1,0},{2,3},{3,2},{4,5},{5,4},{6,7},{7,6},{8,9},{9,8},{10,11... | collective-permute-start | bytes 1376264 | tf_op jit(solution)/shard_map/ppermute | solution.py:35
  184.6 8.5 %collective-permute-start.18 = (bf16[128,1792]{1,0:T(8,128)(2,1)S(1)}, bf16[128,1792]{1,0:T(8,128)(2,1)S(1)}, u32[]{:S(2)}, u32[]{:S(2)}) collective-permute-start(bf16[128,1792]{1,0:T(8,128)(2,1)S(1)} %collective-permute-done.16), channel_id=1, source_target_pairs={{0,4},{1,3},{2,6},{3,1},{4,0},{5,7},{6,2},{7,5},{8,12},{9,11},{10,... | collective-permute-start | bytes 1376264 | tf_op jit(solution)/shard_map/ppermute | solution.py:35
  186.3 8.3 %collective-permute-start.20 = (bf16[128,1792]{1,0:T(8,128)(2,1)S(1)}, bf16[128,1792]{1,0:T(8,128)(2,1)S(1)}, u32[]{:S(2)}, u32[]{:S(2)}) collective-permute-start(bf16[128,1792]{1,0:T(8,128)(2,1)S(1)} %collective-permute-done.16), channel_id=1, source_target_pairs={{0,1},{1,0},{2,3},{3,2},{4,5},{5,4},{6,7},{7,6},{8,9},{9,8},{10,11... | collective-permute-start | bytes 1376264 | tf_op jit(solution)/shard_map/ppermute | solution.py:35
  186.3 9.1 %collective-permute-start.21 = (bf16[128,1792]{1,0:T(8,128)(2,1)S(1)}, bf16[128,1792]{1,0:T(8,128)(2,1)S(1)}, u32[]{:S(2)}, u32[]{:S(2)}) collective-permute-start(bf16[128,1792]{1,0:T(8,128)(2,1)S(1)} %collective-permute-done.17), channel_id=1, source_target_pairs={{0,1},{1,0},{2,3},{3,2},{4,5},{5,4},{6,7},{7,6},{8,9},{9,8},{10,11... | collective-permute-start | bytes 1376264 | tf_op jit(solution)/shard_map/ppermute | solution.py:35
  262.3 5.6 %collective-permute-start.30 = (bf16[512,1792]{1,0:T(8,128)(2,1)}, bf16[512,1792]{1,0:T(8,128)(2,1)}, u32[]{:S(2)}, u32[]{:S(2)}) collective-permute-start(bf16[512,1792]{1,0:T(8,128)(2,1)} %fusion.8), channel_id=1, source_target_pairs={{0,1},{1,0},{2,3},{3,2},{4,5},{5,4},{6,7},{7,6},{8,9},{9,8},{10,11... | collective-permute-start | bytes 5505032 | tf_op jit(solution)/shard_map/ppermute | solution.py:35
  262.3 190.8 %reduce-scatter.3.cloned.1.call-start = ((), (), s32[]{:S(2)}) async-start(), calls=%async_computation.5 | async-start | bytes 4587520 | tf_op jit(solution)/shard_map/reduce_scatter | solution.py:620
  270.0 13.5 %collective-permute-start.31 = (bf16[256,1792]{1,0:T(8,128)(2,1)S(1)}, bf16[256,1792]{1,0:T(8,128)(2,1)S(1)}, u32[]{:S(2)}, u32[]{:S(2)}) collective-permute-start(bf16[256,1792]{1,0:T(8,128)(2,1)S(1)} %get-tuple-element.93), channel_id=1, source_target_pairs={{0,4},{1,3},{2,6},{3,1},{4,0},{5,7},{6,2},{7,5},{8,12},{9,11},{10,... | collective-permute-start | bytes 2752520 | tf_op jit(solution)/shard_map/ppermute | solution.py:35
  283.6 10.3 %collective-permute-start.33 = (bf16[512,1792]{1,0:T(8,128)(2,1)S(1)}, bf16[512,1792]{1,0:T(8,128)(2,1)S(1)}, u32[]{:S(2)}, u32[]{:S(2)}) collective-permute-start(bf16[512,1792]{1,0:T(8,128)(2,1)S(1)} %convolution_convert_fusion.2), channel_id=1, source_target_pairs={{0,1},{1,0},{2,3},{3,2},{4,5},{5,4},{6,7},{7,6},{8,9},{9,8},{10,11... | collective-permute-start | bytes 5505032 | tf_op jit(solution)/shard_map/ppermute | solution.py:35
  283.7 8.5 %collective-permute-start.32 = (bf16[128,1792]{1,0:T(8,128)(2,1)S(1)}, bf16[128,1792]{1,0:T(8,128)(2,1)S(1)}, u32[]{:S(2)}, u32[]{:S(2)}) collective-permute-start(bf16[128,1792]{1,0:T(8,128)(2,1)S(1)} %get-tuple-element.101), channel_id=1, source_target_pairs={{0,2},{1,5},{2,0},{3,7},{4,6},{5,1},{6,4},{7,3},{8,10},{9,13},{10,... | collective-permute-start | bytes 1376264 | tf_op jit(solution)/shard_map/ppermute | solution.py:35
  295.7 13.3 %collective-permute-start.34 = (bf16[128,1792]{1,0:T(8,128)(2,1)S(1)}, bf16[128,1792]{1,0:T(8,128)(2,1)S(1)}, u32[]{:S(2)}, u32[]{:S(2)}) collective-permute-start(bf16[128,1792]{1,0:T(8,128)(2,1)S(1)} %get-tuple-element.105), channel_id=1, source_target_pairs={{0,2},{1,5},{2,0},{3,7},{4,6},{5,1},{6,4},{7,3},{8,10},{9,13},{10,... | collective-permute-start | bytes 1376264 | tf_op jit(solution)/shard_map/ppermute | solution.py:35
  297.3 11.7 %collective-permute-start.35 = (bf16[128,1792]{1,0:T(8,128)(2,1)S(1)}, bf16[128,1792]{1,0:T(8,128)(2,1)S(1)}, u32[]{:S(2)}, u32[]{:S(2)}) collective-permute-start(bf16[128,1792]{1,0:T(8,128)(2,1)S(1)} %get-tuple-element.105), channel_id=1, source_target_pairs={{0,4},{1,3},{2,6},{3,1},{4,0},{5,7},{6,2},{7,5},{8,12},{9,11},{10,... | collective-permute-start | bytes 1376264 | tf_op jit(solution)/shard_map/ppermute | solution.py:35
  309.1 8.5 %collective-permute-start.36 = (bf16[128,1792]{1,0:T(8,128)(2,1)S(1)}, bf16[128,1792]{1,0:T(8,128)(2,1)S(1)}, u32[]{:S(2)}, u32[]{:S(2)}) collective-permute-start(bf16[128,1792]{1,0:T(8,128)(2,1)S(1)} %collective-permute-done.34), channel_id=1, source_target_pairs={{0,4},{1,3},{2,6},{3,1},{4,0},{5,7},{6,2},{7,5},{8,12},{9,11},{10,... | collective-permute-start | bytes 1376264 | tf_op jit(solution)/shard_map/ppermute | solution.py:35
  309.6 8.0 %collective-permute-start.38 = (bf16[128,1792]{1,0:T(8,128)(2,1)S(1)}, bf16[128,1792]{1,0:T(8,128)(2,1)S(1)}, u32[]{:S(2)}, u32[]{:S(2)}) collective-permute-start(bf16[128,1792]{1,0:T(8,128)(2,1)S(1)} %collective-permute-done.34), channel_id=1, source_target_pairs={{0,1},{1,0},{2,3},{3,2},{4,5},{5,4},{6,7},{7,6},{8,9},{9,8},{10,11... | collective-permute-start | bytes 1376264 | tf_op jit(solution)/shard_map/ppermute | solution.py:35
  310.5 7.1 %collective-permute-start.37 = (bf16[128,1792]{1,0:T(8,128)(2,1)S(1)}, bf16[128,1792]{1,0:T(8,128)(2,1)S(1)}, u32[]{:S(2)}, u32[]{:S(2)}) collective-permute-start(bf16[128,1792]{1,0:T(8,128)(2,1)S(1)} %get-tuple-element.105), channel_id=1, source_target_pairs={{0,1},{1,0},{2,3},{3,2},{4,5},{5,4},{6,7},{7,6},{8,9},{9,8},{10,11... | collective-permute-start | bytes 1376264 | tf_op jit(solution)/shard_map/ppermute | solution.py:35
  310.5 7.2 %collective-permute-start.39 = (bf16[128,1792]{1,0:T(8,128)(2,1)S(1)}, bf16[128,1792]{1,0:T(8,128)(2,1)S(1)}, u32[]{:S(2)}, u32[]{:S(2)}) collective-permute-start(bf16[128,1792]{1,0:T(8,128)(2,1)S(1)} %collective-permute-done.35), channel_id=1, source_target_pairs={{0,1},{1,0},{2,3},{3,2},{4,5},{5,4},{6,7},{7,6},{8,9},{9,8},{10,11... | collective-permute-start | bytes 1376264 | tf_op jit(solution)/shard_map/ppermute | solution.py:35
  321.2 19.7 %collective-permute-start.41 = (bf16[256,1792]{1,0:T(8,128)(2,1)}, bf16[256,1792]{1,0:T(8,128)(2,1)}, u32[]{:S(2)}, u32[]{:S(2)}) collective-permute-start(bf16[256,1792]{1,0:T(8,128)(2,1)} %get-tuple-element.109), channel_id=1, source_target_pairs={{0,4},{1,3},{2,6},{3,1},{4,0},{5,7},{6,2},{7,5},{8,12},{9,11},{10,... | collective-permute-start | bytes 2752520 | tf_op jit(solution)/shard_map/ppermute | solution.py:35
  343.8 8.5 %collective-permute-start.42 = (bf16[128,1792]{1,0:T(8,128)(2,1)S(1)}, bf16[128,1792]{1,0:T(8,128)(2,1)S(1)}, u32[]{:S(2)}, u32[]{:S(2)}) collective-permute-start(bf16[128,1792]{1,0:T(8,128)(2,1)S(1)} %get-tuple-element.116), channel_id=1, source_target_pairs={{0,2},{1,5},{2,0},{3,7},{4,6},{5,1},{6,4},{7,3},{8,10},{9,13},{10,... | collective-permute-start | bytes 1376264 | tf_op jit(solution)/shard_map/ppermute | solution.py:35
  352.3 3.8 collective-permute-start.43
  358.0 13.7 %collective-permute-start.44 = (bf16[256,1792]{1,0:T(8,128)(2,1)}, bf16[256,1792]{1,0:T(8,128)(2,1)}, u32[]{:S(2)}, u32[]{:S(2)}) collective-permute-start(bf16[256,1792]{1,0:T(8,128)(2,1)} %get-tuple-element.122), channel_id=1, source_target_pairs={{0,4},{1,3},{2,6},{3,1},{4,0},{5,7},{6,2},{7,5},{8,12},{9,11},{10,... | collective-permute-start | bytes 2752520 | tf_op jit(solution)/shard_map/ppermute | solution.py:35
  372.9 8.5 %collective-permute-start.45 = (bf16[128,1792]{1,0:T(8,128)(2,1)S(1)}, bf16[128,1792]{1,0:T(8,128)(2,1)S(1)}, u32[]{:S(2)}, u32[]{:S(2)}) collective-permute-start(bf16[128,1792]{1,0:T(8,128)(2,1)S(1)} %add_convert_fusion.3), channel_id=1, source_target_pairs={{0,2},{1,5},{2,0},{3,7},{4,6},{5,1},{6,4},{7,3},{8,10},{9,13},{10,... | collective-permute-start | bytes 1376264 | tf_op jit(solution)/shard_map/ppermute | solution.py:35
  385.1 40.7 %collective-permute-start.46 = (bf16[448,1920]{1,0:T(8,128)(2,1)}, bf16[448,1920]{1,0:T(8,128)(2,1)}, u32[]{:S(2)}, u32[]{:S(2)}) collective-permute-start(bf16[448,1920]{1,0:T(8,128)(2,1)} %reduce-scatter.5.cloned.1.call-done.refs_0_), channel_id=1, source_target_pairs={{0,2},{1,5},{2,0},{3,7},{4,6},{5,1},{6,4},{7,3},{8,10},{9,13},{10,... | collective-permute-start | bytes 5160968 | tf_op jit(solution)/shard_map/ppermute | solution.py:35
  387.0 5.7 %collective-permute-start.49 = (f32[3,896]{1,0:T(4,128)S(1)}, f32[3,896]{1,0:T(4,128)S(1)}, u32[]{:S(2)}, u32[]{:S(2)}) collective-permute-start(f32[3,896]{1,0:T(4,128)S(1)} %select_n.259), channel_id=1, source_target_pairs={{0,8},{8,16},{16,24},{24,0},{1,9},{9,17},{17,25},{25,1},{2,10},{10... | collective-permute-start | bytes 32264 | tf_op jit(solution)/shard_map/ppermute | solution.py:72
  387.1 43.7 %collective-permute-start.47 = (bf16[448,1920]{1,0:T(8,128)(2,1)}, bf16[448,1920]{1,0:T(8,128)(2,1)}, u32[]{:S(2)}, u32[]{:S(2)}) collective-permute-start(bf16[448,1920]{1,0:T(8,128)(2,1)} %reduce-scatter.5.cloned.1.call-done.refs_0_), channel_id=1, source_target_pairs={{0,4},{1,3},{2,6},{3,1},{4,0},{5,7},{6,2},{7,5},{8,12},{9,11},{10,... | collective-permute-start | bytes 5160968 | tf_op jit(solution)/shard_map/ppermute | solution.py:35
  388.6 4.6 collective-permute-start.50
  389.2 8.1 %collective-permute-start.51 = (f32[3,896]{1,0:T(4,128)S(1)}, f32[3,896]{1,0:T(4,128)S(1)}, u32[]{:S(2)}, u32[]{:S(2)}) collective-permute-start(f32[3,896]{1,0:T(4,128)S(1)} %select_n.259), channel_id=1, source_target_pairs={{0,24},{8,0},{16,8},{24,16},{1,25},{9,1},{17,9},{25,17},{2,26},{10... | collective-permute-start | bytes 32264 | tf_op jit(solution)/shard_map/ppermute | solution.py:72
  425.8 22.2 %collective-permute-start.48 = (bf16[448,1920]{1,0:T(8,128)(2,1)}, bf16[448,1920]{1,0:T(8,128)(2,1)S(1)}, u32[]{:S(2)}, u32[]{:S(2)}) collective-permute-start(bf16[448,1920]{1,0:T(8,128)(2,1)} %collective-permute-done.46), channel_id=1, source_target_pairs={{0,4},{1,3},{2,6},{3,1},{4,0},{5,7},{6,2},{7,5},{8,12},{9,11},{10,... | collective-permute-start | bytes 5160968 | tf_op jit(solution)/shard_map/ppermute | solution.py:35
  453.2 25.9 %collective-permute-start.59 = (bf16[448,1024]{1,0:T(8,128)(2,1)}, bf16[448,1024]{1,0:T(8,128)(2,1)}, u32[]{:S(2)}, u32[]{:S(2)}) collective-permute-start(bf16[448,1024]{1,0:T(8,128)(2,1)} %reduce-scatter.3.cloned.1.call-done.refs_0_), channel_id=1, source_target_pairs={{0,2},{1,5},{2,0},{3,7},{4,6},{5,1},{6,4},{7,3},{8,10},{9,13},{10,... | collective-permute-start | bytes 2752520 | tf_op jit(solution)/shard_map/ppermute | solution.py:35
  454.8 24.4 %collective-permute-start.60 = (bf16[448,1024]{1,0:T(8,128)(2,1)}, bf16[448,1024]{1,0:T(8,128)(2,1)}, u32[]{:S(2)}, u32[]{:S(2)}) collective-permute-start(bf16[448,1024]{1,0:T(8,128)(2,1)} %reduce-scatter.3.cloned.1.call-done.refs_0_), channel_id=1, source_target_pairs={{0,4},{1,3},{2,6},{3,1},{4,0},{5,7},{6,2},{7,5},{8,12},{9,11},{10,... | collective-permute-start | bytes 2752520 | tf_op jit(solution)/shard_map/ppermute | solution.py:35
  456.1 8.8 %collective-permute-start.52 = (bf16[32,3584]{1,0:T(8,128)(2,1)S(1)}, bf16[32,3584]{1,0:T(8,128)(2,1)S(1)}, u32[]{:S(2)}, u32[]{:S(2)}) collective-permute-start(bf16[32,3584]{1,0:T(8,128)(2,1)S(1)} %get-tuple-element.181), channel_id=1, source_target_pairs={{0,24},{8,0},{16,8},{24,16},{1,25},{9,1},{17,9},{25,17},{2,26},{10... | collective-permute-start | bytes 688136 | tf_op jit(solution)/shard_map/ppermute | solution.py:72
  460.3 18.3 %collective-permute-start.53 = (bf16[32,3584]{1,0:T(8,128)(2,1)S(1)}, bf16[32,3584]{1,0:T(8,128)(2,1)S(1)}, u32[]{:S(2)}, u32[]{:S(2)}) collective-permute-start(bf16[32,3584]{1,0:T(8,128)(2,1)S(1)} %get-tuple-element.180), channel_id=1, source_target_pairs={{0,16},{8,24},{16,0},{24,8},{1,17},{9,25},{17,1},{25,9},{2,18},{10... | collective-permute-start | bytes 688136 | tf_op jit(solution)/shard_map/ppermute | solution.py:72
  461.4 17.2 %collective-permute-start.54 = (bf16[32,3584]{1,0:T(8,128)(2,1)S(1)}, bf16[32,3584]{1,0:T(8,128)(2,1)S(1)}, u32[]{:S(2)}, u32[]{:S(2)}) collective-permute-start(bf16[32,3584]{1,0:T(8,128)(2,1)S(1)} %get-tuple-element.179), channel_id=1, source_target_pairs={{0,8},{8,16},{16,24},{24,0},{1,9},{9,17},{17,25},{25,1},{2,10},{10... | collective-permute-start | bytes 688136 | tf_op jit(solution)/shard_map/ppermute | solution.py:72
  464.8 15.0 %collective-permute-start.55 = (bf16[32,3584]{1,0:T(8,128)(2,1)S(1)}, bf16[32,3584]{1,0:T(8,128)(2,1)S(1)}, u32[]{:S(2)}, u32[]{:S(2)}) collective-permute-start(bf16[32,3584]{1,0:T(8,128)(2,1)S(1)} %get-tuple-element.182.refs_0_), channel_id=1, source_target_pairs={{0,1},{1,0},{2,3},{3,2},{4,5},{5,4},{6,7},{7,6},{8,9},{9,8},{10,11... | collective-permute-start | bytes 688136 | tf_op jit(solution)/shard_map/ppermute | solution.py:35
  479.2 15.2 %collective-permute-start.62 = (bf16[448,1024]{1,0:T(8,128)(2,1)}, bf16[448,1024]{1,0:T(8,128)(2,1)}, u32[]{:S(2)}, u32[]{:S(2)}) collective-permute-start(bf16[448,1024]{1,0:T(8,128)(2,1)} %collective-permute-done.59), channel_id=1, source_target_pairs={{0,4},{1,3},{2,6},{3,1},{4,0},{5,7},{6,2},{7,5},{8,12},{9,11},{10,... | collective-permute-start | bytes 2752520 | tf_op jit(solution)/shard_map/ppermute | solution.py:35
  479.8 4.0 collective-permute-start.63
  483.8 9.2 %collective-permute-start.64 = (f32[3584]{0:T(1024)S(1)}, f32[3584]{0:T(1024)S(1)}, u32[]{:S(2)}, u32[]{:S(2)}) collective-permute-start(f32[3584]{0:T(1024)S(1)} %add.413), channel_id=1, source_target_pairs={{0,4},{1,3},{2,6},{3,1},{4,0},{5,7},{6,2},{7,5},{8,12},{9,11},{10,... | collective-permute-start | bytes 43016 | tf_op jit(solution)/shard_map/ppermute | solution.py:35
  (63 other events, 1299.2 us)
Sparse Core Ops, SparseCore 0:
  11.3 84.7 all-gather.2
  97.6 133.4 all-gather.4
  262.5 118.5 reduce-scatter.4
  383.9 69.2 reduce-scatter.2

commit v4 on v3

--- a/solution.py
+++ b/solution.py
@@ -70,6 +70,14 @@
 def z_shifted(value, sizes, steps):
     n = sizes[0]
     return lax.ppermute(value, "fsdp", [(i, (i + steps) % n) for i in range(n)])
+
+
+def packed(rest):
+    return jnp.concatenate(jnp.split(rest, 128 // rest.shape[1]), axis=1)
+
+
+def unpacked(full, width):
+    return jnp.concatenate(jnp.split(full, full.shape[1] // width, axis=1))
 
 
 def z_exchange(blocks, sizes):
@@ -234,30 +242,24 @@
         grad_conv_ref[lag : lag + 1, :] = conv_sums[lag]
 
 
-def weight_grad_kernel(turned, *refs):
+def weight_grad_kernel(*refs):
     out_ref = refs[-1]
     at = 0
-    for is_turned, left_ref, right_ref in zip(turned, refs[:-1:2], refs[1:-1:2]):
+    for left_ref, right_ref in zip(refs[:-1:2], refs[1:-1:2]):
         width = right_ref.shape[1]
-        dims = NN if is_turned else TN
-        out_ref[:, at : at + width] = product(left_ref[...], right_ref[...], dims, bf16)
+        out_ref[:, at : at + width] = product(left_ref[...], right_ref[...], TN, bf16)
         at += width
 
 
 def weight_grad(*pairs, step=256):
-    rows = pairs[0][1].shape[0]
-    turned = tuple(left.shape[1] == rows for left, _ in pairs)
-    d_model = pairs[0][0].shape[0 if turned[0] else 1]
+    rows, d_model = pairs[0][0].shape
     width = sum(right.shape[1] for _, right in pairs)
     specs = []
-    for is_turned, (left, right) in zip(turned, pairs):
-        if is_turned:
-            specs.append(pl.BlockSpec((step, rows), lambda i: (i, 0)))
-        else:
-            specs.append(pl.BlockSpec((rows, step), lambda i: (0, i)))
+    for left, right in pairs:
+        specs.append(pl.BlockSpec((rows, step), lambda i: (0, i)))
         specs.append(pl.BlockSpec((rows, right.shape[1]), lambda i: (0, 0)))
     return pl.pallas_call(
-        functools.partial(weight_grad_kernel, turned),
+        weight_grad_kernel,
         grid=(d_model // step,),
         out_shape=jax.ShapeDtypeStruct((d_model, width), bf16),
         in_specs=specs,
@@ -272,37 +274,95 @@
     )(*[operand for pair in pairs for operand in pair])
 
 
-def feed_forward_kernel(hidden_ref, grad_ref, weight_ref, inner_ref, pair_ref):
-    ff = inner_ref.shape[1]
-    both = product(hidden_ref[...], weight_ref[:, : 2 * ff], NN)
-    grad_inner = product(grad_ref[...], weight_ref[:, 2 * ff :], NN)
-    gate_act, upper = both[:, :ff], both[:, ff:]
+def mlp_grad_kernel(own_lanes, hidden_ref, grad_ref, pair_ref, inner_ref, out_ref, rest_ref):
+    lead = out_ref.shape[1] - pair_ref.shape[1]
+    pairs = product(hidden_ref[...], pair_ref[...], NN)
+    down = product(grad_ref[...], inner_ref[...], NN)
+    shared = down[:, lead : lead + 128]
+    lanes = lax.broadcasted_iota(jnp.int32, shared.shape, 1)
+    out_ref[:, :lead] = down[:, :lead].astype(bf16)
+    out_ref[:, lead : lead + 128] = jnp.where(lanes < own_lanes, shared, pairs[:, :128]).astype(bf16)
+    out_ref[:, lead + 128 :] = pairs[:, 128:].astype(bf16)
+    rest_ref[...] = shared.astype(bf16)
+
+
+def mlp_grad(hidden, grad, pair, inner, width, own_lanes, step=256):
+    d_model, rows = hidden.shape
+    return pl.pallas_call(
+        functools.partial(mlp_grad_kernel, own_lanes),
+        grid=(d_model // step,),
+        out_shape=(
+            jax.ShapeDtypeStruct((d_model, width), bf16),
+            jax.ShapeDtypeStruct((d_model, 128), bf16),
+        ),
+        in_specs=[
+            pl.BlockSpec((step, rows), lambda i: (i, 0)),
+            pl.BlockSpec((step, rows), lambda i: (i, 0)),
+            pl.BlockSpec(pair.shape, lambda i: (0, 0)),
+            pl.BlockSpec(inner.shape, lambda i: (0, 0)),
+        ],
+        out_specs=(
+            pl.BlockSpec((step, width), lambda i: (i, 0)),
+            pl.BlockSpec((step, 128), lambda i: (i, 0)),
+        ),
+        compiler_params=pltpu.CompilerParams(vmem_limit_bytes=40 * 1024 * 1024),
+        cost_estimate=pl.CostEstimate(
+            flops=2 * rows * d_model * width,
+            bytes_accessed=2 * (2 * rows * d_model + (rows + d_model) * width),
+            transcendentals=0,
+        ),
+        name="mlp_grad",
+    )(hidden, grad, pair, inner)
+
+
+def feed_forward_kernel(ff, hidden_ref, grad_ref, weight_ref, rest_ref, inner_ref, pair_ref):
+    own = weight_ref.shape[1] - 2 * ff
+    first = own // 128 * 128
+    lead = own - first
+    both = product(hidden_ref[...], weight_ref[:, first:], NN)
+    gate_act, upper = both[:, lead : lead + ff], both[:, lead + ff :]
+    grad = grad_ref[...]
+    grad_inner = jnp.concatenate(
+        [product(grad, weight_ref[:, :own], NN), product(grad, rest_ref[...], NN)], axis=1
+    )
     sigmoid = jax.nn.sigmoid(gate_act)
     silu = gate_act * sigmoid
-    inner_ref[...] = (silu * upper).astype(bf16)
+    rows, spare = inner_ref.shape[0], inner_ref.shape[1] - ff
+    inner_ref[...] = jnp.concatenate(
+        [(silu * upper).astype(bf16), jnp.zeros((rows, spare), bf16)], axis=1
+    )
     grad_gate = grad_inner * upper * (sigmoid * (1.0 + gate_act * (1.0 - sigmoid)))
-    pair_ref[:, :ff] = grad_gate.astype(bf16)
-    pair_ref[:, ff:] = (grad_inner * silu).astype(bf16)
-
-
-def feed_forward(hidden, grad, weight, step=256):
+    pair_ref[...] = jnp.concatenate(
+        [
+            jnp.zeros((rows, lead), bf16),
+            grad_gate.astype(bf16),
+            (grad_inner * silu).astype(bf16),
+        ],
+        axis=1,
+    )
+
+
+def feed_forward(hidden, grad, weight, rest, ff, step=256):
     rows, d_model = hidden.shape
-    ff = weight.shape[1] // 3
+    width = weight.shape[1]
+    first = (width - 2 * ff) // 128 * 128
+    padded = -(-ff // 128) * 128
     return pl.pallas_call(
-        feed_forward_kernel,
+        functools.partial(feed_forward_kernel, ff),
         grid=(rows // step,),
         out_shape=(
-            jax.ShapeDtypeStruct((rows, ff), bf16),
-            jax.ShapeDtypeStruct((rows, 2 * ff), bf16),
+            jax.ShapeDtypeStruct((rows, padded), bf16),
+            jax.ShapeDtypeStruct((rows, width - first), bf16),
         ),
         in_specs=[
             pl.BlockSpec((step, d_model), lambda i: (i, 0)),
             pl.BlockSpec((step, d_model), lambda i: (i, 0)),
-            pl.BlockSpec((d_model, 3 * ff), lambda i: (0, 0)),
+            pl.BlockSpec((d_model, width), lambda i: (0, 0)),
+            pl.BlockSpec(rest.shape, lambda i: (0, 0)),
         ],
         out_specs=(
-            pl.BlockSpec((step, ff), lambda i: (i, 0)),
-            pl.BlockSpec((step, 2 * ff), lambda i: (i, 0)),
+            pl.BlockSpec((step, padded), lambda i: (i, 0)),
+            pl.BlockSpec((step, width - first), lambda i: (i, 0)),
         ),
         compiler_params=pltpu.CompilerParams(vmem_limit_bytes=48 * 1024 * 1024),
         cost_estimate=pl.CostEstimate(
@@ -311,13 +371,62 @@
             transcendentals=rows * ff,
         ),
         name="feed_forward",
-    )(hidden, grad, weight)
+    )(hidden, grad, weight, rest)
+
+
+def mlp_placed_kernel(ff, index_ref, *refs):
+    mains, rests = refs[:4], refs[4:8]
+    pair_ref, down_ref, columns = refs[8:]
+    own = mains[0].shape[1] - 2 * ff
+    for k in range(4):
+        piece = index_ref[0] ^ k
+        columns[piece, :, :own] = mains[k][:, :own].astype(f32)
+        if rests[k].shape[1] == ff - own:
+            columns[piece, :, own:ff] = rests[k][...].astype(f32)
+        else:
+            for step in range(rests[k].shape[1] // (ff - own)):
+
+                @pl.when(pl.program_id(0) == step)
+                def _():
+                    at = step * (ff - own)
+                    columns[piece, :, own:ff] = rests[k][:, at : at + ff - own].astype(f32)
+        columns[piece, :, ff:] = mains[k][:, own:].astype(f32)
+    for out, at in ((pair_ref.at[0], ff), (pair_ref.at[1], 2 * ff), (down_ref.at[0], 0)):
+        out[...] = jnp.concatenate([columns[p, :, at : at + ff] for p in range(4)], axis=1)
+
+
+def mlp_placed(mains, rests, index, ff, steps):
+    rows, width = mains[0].shape
+    block, total = rows // steps, 4 * ff
+    if steps == 1:
+        rests = [unpacked(rest, ff - (width - 2 * ff)) for rest in rests]
+    return pl.pallas_call(
+        functools.partial(mlp_placed_kernel, ff),
+        grid=(steps,),
+        out_shape=[
+            jax.ShapeDtypeStruct((2, rows, total), f32),
+            jax.ShapeDtypeStruct((1, rows, total), f32),
+        ],
+        in_specs=[SMEM]
+        + [pl.BlockSpec((block, width), lambda i: (i, 0))] * 4
+        + [pl.BlockSpec(rests[0].shape, lambda i: (0, 0))] * 4,
+        out_specs=[
+            pl.BlockSpec((2, block, total), lambda i: (0, i, 0)),
+            pl.BlockSpec((1, block, total), lambda i: (0, i, 0)),
+        ],
+        scratch_shapes=[pltpu.VMEM((4, block, 3 * ff), f32)],
+        compiler_params=pltpu.CompilerParams(vmem_limit_bytes=40 * 1024 * 1024),
+        cost_estimate=pl.CostEstimate(
+            flops=0, bytes_accessed=20 * rows * total, transcendentals=0
+        ),
+        name="mlp_placed",
+    )(index.reshape(1).astype(jnp.int32), *mains, *rests)
 
 
 def placed_kernel(each, total, counts, index_ref, *refs):
     n_parts = len(refs) - len(counts)
     outs = refs[n_parts:]
-    for piece in range(n_parts):
+    for piece in range(total // each + (total % each > 0)):
         start = min(piece * each, total - each)
         shared = piece * each - start
         for k in range(n_parts):
@@ -350,6 +459,43 @@
         ),
         name="placed",
     )(index.reshape(1).astype(jnp.int32), *parts)
+
+
+def last_placed_kernel(count, place_ref, *refs):
+    *parts, _, _, first_ref, second_ref = refs
+    for i in range(count):
+        first_ref[i] = parts[i][...].astype(f32)
+    second_ref[0] = parts[count][...].astype(f32)
+
+
+def last_placed(part, index, each, total, first, second):
+    rows, count = part.shape[0], first.shape[0]
+    tiles, last = each // 128, total // 128 - 1
+
+    def source(i):
+        shift = tiles * (last // tiles + 1) - 1 - last
+        return lambda j, ref: (
+            0,
+            i * tiles + jnp.where(ref[0] == last // tiles, jnp.minimum(j + shift, tiles - 1), j),
+        )
+
+    def target(j, ref):
+        return (0, 0, jnp.minimum(ref[0] * tiles + j, last))
+
+    out_specs = [pl.BlockSpec((n, rows, 128), target) for n in (count, 1)]
+    return pl.pallas_call(
+        functools.partial(last_placed_kernel, count),
+        grid_spec=pltpu.PrefetchScalarGridSpec(
+            num_scalar_prefetch=1,
+            grid=(tiles,),
+            in_specs=[pl.BlockSpec((rows, 128), source(i)) for i in range(count + 1)]
+            + [pl.BlockSpec(memory_space=pl.ANY)] * 2,
+            out_specs=out_specs,
+        ),
+        out_shape=[jax.ShapeDtypeStruct(first.shape, f32), jax.ShapeDtypeStruct(second.shape, f32)],
+        input_output_aliases={count + 2: 0, count + 3: 1},
+        name="last_placed",
+    )(index.reshape(1).astype(jnp.int32), *[part] * (count + 1), first, second)
 
 
 def at_home_kernel(undo_ref, *refs):
@@ -446,7 +592,7 @@
     heads_all = attn_in.shape[2]
     width = HEADS_EACH * HEAD
     ff_all = gate_up.shape[2]
-    ff = -(-ff_all // (n_ctx * 128)) * 128
+    ff = ff_all // n_ctx
     from_each = tok_rows // n_fsdp
     half = from_each // n_tp
     group = n_ctx * tok_rows
@@ -457,14 +603,15 @@
     out_part = lax.dynamic_slice_in_dim(attn_out, start, width, 0)
     out_part = jnp.where(jnp.arange(width)[:, None] >= shared, out_part, jnp.zeros_like(out_part))
     attn_own = jnp.concatenate([sliced[0], sliced[1], sliced[2], out_part.T], axis=1)
-    ff_start, ff_shared = part_of(ff_all, ff, c)
-    sliced = lax.dynamic_slice_in_dim(gate_up, ff_start, ff, 2)
-    down_part = lax.dynamic_slice_in_dim(down_proj, ff_start, ff, 0)
-    down_part = jnp.where(jnp.arange(ff)[:, None] >= ff_shared, down_part, jnp.zeros_like(down_part))
-    mlp_own = jnp.concatenate([sliced[0], sliced[1], down_part.T], axis=1)
+    own_down = 3 * ff // 128 * 128 - 2 * ff
+    sliced = lax.dynamic_slice_in_dim(gate_up, c * ff, ff, 2)
+    down_own = lax.dynamic_slice_in_dim(down_proj, c * ff, ff, 0).T
+    mlp_own = jnp.concatenate([down_own[:, :own_down], sliced[0], sliced[1]], axis=1)
+    rest_own = down_own[:, own_down:]
+    rest_width = ff - own_down
     attn_w = lax.all_gather(attn_own, "fsdp", axis=0, tiled=True)
     mlp_w = lax.all_gather(after(mlp_own, attn_own), "fsdp", axis=0, tiled=True)
-    gate_w, down_w = mlp_w[:, : 2 * ff], mlp_w[:, 2 * ff :]
+    down_w, pair_w = mlp_w[:, :own_down], mlp_w[:, own_down // 128 * 128 :]
     qkv_w, out_w = attn_w[:, : 3 * width], attn_w[:, 3 * width :]
 
     small = jnp.concatenate(
@@ -540,7 +687,16 @@
     first_scale = lax.rsqrt(jnp.mean(own_x * own_x, axis=-1, keepdims=True) + epsilon)
     hidden = plane_gather((own_x * first_scale * gains[0]).astype(bf16), sizes)
     own_lengths = lengths[:, 0]
-    own_g = to_planes(after(cotangent, hidden))
+    hidden, given_g, rest_own = stage(hidden, cotangent, packed(rest_own))
+    own_g = to_planes(given_g)
+    if n_fsdp > 4:
+        rests = lax.all_gather(rest_own, "fsdp")
+        rest_w = jnp.concatenate([unpacked(rests[k], rest_width) for k in range(n_fsdp)])
+    else:
+        rest_w = jnp.zeros((d_model, rest_width), bf16)
+        for k in range(n_fsdp):
+            part = unpacked(z_shifted(rest_own, sizes, k) if k else rest_own, rest_width)
+            rest_w = lax.dynamic_update_slice_in_dim(rest_w, part, (f - k) % n_fsdp * d_own, 0)
     qkv = product(deal, product(hidden, qkv_w, NN, bf16), NN, bf16)
     grad_dealt = plane_gather(after(own_g, qkv), sizes)
     attended = product(deal, attend_forward(own_lengths, qkv, conv), TN, bf16)
@@ -556,24 +712,31 @@
     hidden_two = plane_gather((resid * second_scale * gains[1]).astype(bf16), sizes)
     hidden_two_turned, grad_dealt_turned = after((hidden_two.T, grad_dealt.T))
     inner, grad_pair = feed_forward(
-        after(hidden_two, hidden_two_turned, grad_dealt_turned), grad_dealt, mlp_w
-    )
-    grad_mlp_w = weight_grad((hidden_two_turned, grad_pair), (grad_dealt_turned, inner))
-    grad_mlp_w, grad_pair, inner = stage(grad_mlp_w, grad_pair, inner)
+        after(hidden_two, hidden_two_turned, grad_dealt_turned), grad_dealt, mlp_w, rest_w, ff
+    )
+    grad_mlp_w, grad_rest_w = mlp_grad(
+        hidden_two_turned, grad_dealt_turned, grad_pair, inner, mlp_w.shape[1], own_down % 128
+    )
+    grad_mlp_w, grad_rest_w, grad_pair, inner = stage(grad_mlp_w, grad_rest_w, grad_pair, inner)
     grad_mlp = lax.psum_scatter(grad_mlp_w, "fsdp", scatter_dimension=0, tiled=True)
-
-    sent = product(grad_pair[kept:], gate_w, NT, bf16)
+    grad_rest_w = grad_rest_w[:, own_down % 128 :][:, :rest_width]
+    rests = [
+        packed(lax.dynamic_slice_in_dim(grad_rest_w, (f + k) % n_fsdp * d_own, d_own, 0))
+        for k in range(n_fsdp)
+    ]
+
+    sent = product(grad_pair[kept:], pair_w, NT, bf16)
     sent, grad_pair = stage(sent, grad_pair)
 
     got = flipped(sent, sizes, 2)
-    part = product(grad_pair[:kept], gate_w, NT)
+    part = product(grad_pair[:kept], pair_w, NT)
     got, part = stage(got, part)
     part, sent = added(part, got)
     part, sent, inner = stage(part, sent, inner)
 
     got = flipped(sent, sizes, 1)
-    lift_sent = product(inner[kept:], down_w, NT, bf16)
-    lift = product(inner[:kept], down_w, NT)
+    lift = product(inner[:, :own_down], down_w, NT) + product(inner[:, own_down:ff], rest_w, NT)
+    lift, lift_sent = lift[:kept], lift[kept:].astype(bf16)
     got, part, lift_sent, lift = stage(got, part, lift_sent, lift)
     part, sent = added(part, got)
     part, sent, lift_sent, lift = stage(part, sent, lift_sent, lift)
@@ -620,7 +783,8 @@
     grad_attn = lax.psum_scatter(grad_attn_w, "fsdp", scatter_dimension=0, tiled=True)
     part, sent = added(part, got)
 
-    grad_hidden = part + flipped(sent, sizes, 0).astype(f32)
+    got_last = flipped(sent, sizes, 0)
+    grad_hidden = part + got_last.astype(f32)
     normed = own_x * first_scale
     scaled = grad_hidden * gains[0]
     grad_x = grad_resid + first_scale * (
@@ -628,14 +792,14 @@
     )
     grad_x = grad_x.astype(bf16)
 
-    spread = lax.dynamic_update_slice(jnp.zeros((CONV, heads_all), f32), grad_conv, (0, start))
-    taps = jnp.where(jnp.arange(heads_all)[None, :] >= start + shared, spread, 0.0)
-    if n_fsdp > 4:
-        taps = lax.psum(taps, "fsdp")
-    else:
-        taps = sum([z_shifted(taps, sizes, k) for k in range(1, n_fsdp)], taps)
-
-    steps = 4 if d_own % 64 == 0 else 1
+    taps = jnp.concatenate(jnp.split(grad_conv, width // 128, axis=1)).astype(bf16)
+    taps, grad_mlp, _, *rests = stage(taps, grad_mlp, got_last, *rests)
+    little = [jnp.concatenate([rest, taps]) for rest in rests]
+    little = sum(
+        [z_shifted(little[k], sizes, k).astype(f32) for k in range(1, n_fsdp)], little[0].astype(f32)
+    ).astype(bf16)
+
+    steps = 128 // rest_width if d_own * rest_width % (128 * 16) == 0 else 1
 
     def gain_part(own, grad, each, skipped):
         columns = own.shape[1]
@@ -643,12 +807,21 @@
         terms = own.astype(f32) * grad[:, :columns].astype(f32)
         return jnp.sum(jnp.where(counted[None, :], terms, 0.0), axis=1)
 
-    mlp_shares = ctx_shares(after(grad_mlp, grad_x), sizes, t)
-    gain_two = gain_part(mlp_own[:, : 2 * ff], grad_mlp, ff, ff_shared)
+    mlp_shares = ctx_shares(grad_mlp, sizes, t)
+    little_shares = ctx_shares(little, sizes, t)
+    rest_rows = d_own * rest_width // 128
+    rest_shares = [share[:rest_rows] for share in little_shares]
+    taps = [share[rest_rows:].astype(f32) for share in little_shares]
+    taps = [jnp.concatenate(jnp.split(tap, width // 128), axis=1) for tap in taps]
+    first_shared = n_ctx * width - heads_all
+    taps = jnp.stack(taps)
+    taps = [lax.dynamic_index_in_dim(taps, c ^ k, 0, False) for k in range(n_ctx)]
+    taps = jnp.concatenate(taps[:-1] + [taps[-1][:, first_shared:]], axis=1)
+    grad_conv = lax.dynamic_slice_in_dim(taps, f * (heads_all // n_fsdp), heads_all // n_fsdp, 1)
+    gain_two = gain_part(mlp_own[:, own_down:], grad_mlp[:, own_down:], ff, 0)
     rows_back = jnp.concatenate([result, grad_x], axis=1)
-    grad_gate_up, grad_down = placed(mlp_shares, c, ff, ff_all, (2, 1), steps)
-    grad_attn, rows_back, grad_gate_up, grad_down, gain_two, taps = stage(
-        grad_attn, rows_back, grad_gate_up, grad_down, gain_two, taps
+    grad_attn, rows_back, gain_two, grad_conv, rest_shares = stage(
+        grad_attn, rows_back, gain_two, grad_conv, rest_shares
     )
 
     near = near_shares(grad_attn, sizes)
@@ -656,24 +829,19 @@
     gain_one = gain_part(attn_own[:, : 3 * width], grad_attn, width, shared)
     gains_grad = jnp.stack([gain_one, gain_two])
     gains_grad = gains_grad + flipped(gains_grad, sizes, 2)
-    near, gains_grad = stage(near, gains_grad)
+    grad_gate_up, grad_down = mlp_placed(mlp_shares, rest_shares, c, ff, steps)
+    near, gains_grad, grad_gate_up, grad_down = stage(near, gains_grad, grad_gate_up, grad_down)
 
     attn_shares = ctx_shares(grad_attn, sizes, t, near)
-    small = jnp.concatenate([gains_grad.reshape(-1), taps.reshape(-1)])
+    grad_attn_in, grad_attn_out = placed(attn_shares[:3], c, width, heads_all, (3, 1), steps)
     for step in (0, 1):
-        small = small + flipped(small, sizes, step)
+        gains_grad = gains_grad + flipped(gains_grad, sizes, step)
     activations, input_grad = at_home(
         undo, home + [flipped(block, sizes, 2) for block in home], BATCHES, d_model
     )
-    grad_gains = small[: gains_grad.size].reshape(2, -1) / norm_gains.astype(f32)
-    grad_conv = lax.dynamic_slice_in_dim(
-        small[gains_grad.size :].reshape(CONV, heads_all),
-        f * (heads_all // n_fsdp),
-        heads_all // n_fsdp,
-        1,
-    )
-    grad_attn_in, grad_attn_out = placed(
-        attn_shares, c, width, heads_all, (3, 1), steps
+    grad_gains = gains_grad / norm_gains.astype(f32)
+    grad_attn_in, grad_attn_out = last_placed(
+        attn_shares[3], c ^ 3, width, heads_all, grad_attn_in, grad_attn_out
     )
     return (
         activations,

time: 511 us -> 499 us (0.977)
  waiting for transfers between devices: 240 us -> 200 us
  starting transfers between devices: 68.2 us -> 81.2 us
  Pallas kernels: 59.4 us -> 67.6 us
  local copies, waits for them, and re-layouts: 44 us -> 50.5 us
    ppermute x53 -> x56, waiting for transfers between devices: 147 us -> 124 us  [flipped(): return lax.ppermute(value, ('fsdp', 'ctx', 'tp'), pairs)]
    ppermute x12 -> x15, waiting for transfers between devices: 46 us -> 30.6 us  [z_shifted(): return lax.ppermute(value, 'fsdp', [(i, (i + steps) % n) for i in range(n)])]
    pallas_call x3 -> x5, Pallas kernels: 28 us -> 42.8 us  [the longest x1 13.6 us: feed_forward(): pl.pallas_call(functools.partial(feed_forward_kernel, ff), grid=(rows //...]
    reduce_scatter x1, waiting for transfers between devices: 0.01 us -> 12.1 us  [per_device(): lax.psum_scatter(grad_attn_w, 'fsdp', scatter_dimension=0, tiled=True)]
    ppermute x12 -> x15, starting transfers between devices: 18.1 us -> 29.6 us  [z_shifted(): return lax.ppermute(value, 'fsdp', [(i, (i + steps) % n) for i in range(n)])]
    all_gather x1, waiting for transfers between devices: 22.8 us -> 12.2 us  [per_device(): attn_w = lax.all_gather(attn_own, 'fsdp', axis=0, tiled=True)]
    pallas_call x2 -> x1, Pallas kernels: 9.79 us -> 3.17 us  [placed(): pl.pallas_call(functools.partial(placed_kernel, each, total, counts), gri...]
    ppermute x53 -> x56, starting transfers between devices: 41.5 us -> 43 us  [flipped(): return lax.ppermute(value, ('fsdp', 'ctx', 'tp'), pairs)]
  transfers between devices with their start and end apart: 70 -> 76, of which waited for: 33 -> 31; matrix products, arithmetic and copies ran while one was open for 21% -> 22% of each run, Pallas kernels for 6% -> 9%
where the time goes in v4:
time: 499 us; the launch traced here: 493 us
  waiting for transfers between devices  200 us (40%)
  starting transfers between devices  81.2 us (16%)
  Pallas kernels  67.6 us (14%)
  local copies, waits for them, and re-layouts  50.5 us (10%)
  matrix products  39.2 us (8%)
  other arithmetic  38.6 us (8%)
  between operations  15.9 us (3%)
    ppermute x56, waiting for transfers between devices, flipped(): return lax.ppermute(value, ('fsdp', 'ctx', 'tp'), pairs)  124 us
    ppermute x56, starting transfers between devices, flipped(): return lax.ppermute(value, ('fsdp', 'ctx', 'tp'), pairs)  43 us
    dot_general x14, matrix products, product(): lax.dot_general(left, right, (dims, ((), ())), preferred_element_type=f32)  39.2 us
    ppermute x15, waiting for transfers between devices, z_shifted(): return lax.ppermute(value, 'fsdp', [(i, (i + steps) % n) for i in range(n)])  30.6 us
    ppermute x15, starting transfers between devices, z_shifted(): return lax.ppermute(value, 'fsdp', [(i, (i + steps) % n) for i in range(n)])  29.6 us
    unnamed x197, local copies, waits for them, and re-layouts  24.5 us
    all_gather x1, waiting for transfers between devices, per_device(): mlp_w = lax.all_gather(after(mlp_own, attn_own), 'fsdp', axis=0, tiled=True)  18.6 us
    pallas_call x1, Pallas kernels, attend_backward(): pl.pallas_call(attend_backward_kernel, out_shape=(jax.ShapeDtypeStruct((r...  14.1 us
  transfers between devices with their start and end apart: 76, of which 31 were waited for; matrix products, arithmetic and copies ran while one was open for 22% of the time, Pallas kernels for 9%

profile of v4, /device:TPU:0, one launch (start us, length us, event | category | flops | bytes accessed | tf_op | source)
XLA Modules:
  0.0 492.9 jit_solution(3830789395281708124)
XLA Ops:
  12.9 8.2 %all-to-all-start = ((f32[16,1,1824]{2,1,0:T(1,128)}), f32[16,1,1824]{2,1,0:T(1,128)S(1)}, u32[]{:S(2)}, u32[]{:S(2)}) async-start(f32[16,1,1824]{2,1,0:T(1,128)} %broadcast_in_dim.54), calls=%async_computation | async-start | bytes 245760 | tf_op jit(solution)/shard_map/all_to_all | solution.py:625
  21.5 2.0 dynamic-slice_bitcast_fusion
  23.6 2.4 concatenate.106
  26.9 2.0 all-to-all-done
  30.8 3.9 collective-permute-start.1
  36.4 4.2 collective-permute-done
  40.6 6.8 %collective-permute-done.1 = bf16[32,1792]{1,0:T(8,128)(2,1)S(1)} collective-permute-done((bf16[32,1792]{1,0:T(8,128)(2,1)S(1)}, bf16[32,1792]{1,0:T(8,128)(2,1)S(1)}, u32[]{:S(2)}, u32[]{:S(2)}) %collective-permute-start.1) | collective-permute-done | bytes 114720 | tf_op jit(solution)/shard_map/ppermute | solution.py:72
  52.7 9.4 %collective-permute-done.3 = bf16[128,1792]{1,0:T(8,128)(2,1)S(1)} collective-permute-done((bf16[128,1792]{1,0:T(8,128)(2,1)}, bf16[128,1792]{1,0:T(8,128)(2,1)S(1)}, u32[]{:S(2)}, u32[]{:S(2)}) %collective-permute-start.3) | collective-permute-done | bytes 458784 | tf_op jit(solution)/shard_map/ppermute | solution.py:35
  65.1 5.4 %collective-permute-done.5 = bf16[128,1792]{1,0:T(8,128)(2,1)S(1)} collective-permute-done((bf16[128,1792]{1,0:T(8,128)(2,1)S(1)}, bf16[128,1792]{1,0:T(8,128)(2,1)S(1)}, u32[]{:S(2)}, u32[]{:S(2)}) %collective-permute-start.5) | collective-permute-done | bytes 458784 | tf_op jit(solution)/shard_map/ppermute | solution.py:35
  74.6 8.7 %collective-permute-start.30 = (bf16[112,128]{1,0:T(8,128)(2,1)S(1)}, bf16[112,128]{1,0:T(8,128)(2,1)S(1)}, u32[]{:S(2)}, u32[]{:S(2)}) collective-permute-start(bf16[112,128]{1,0:T(8,128)(2,1)S(1)} %pad_maximum_fusion.8), channel_id=1, source_target_pairs={{0,8},{8,16},{16,24},{24,0},{1,9},{9,17},{17,25},{25,1},{2,10},{10... | collective-permute-start | bytes 86024 | tf_op jit(solution)/shard_map/ppermute | solution.py:72
  83.3 3.3 collective-permute-start.31
  87.2 12.2 %all-gather.3.cloned.1.call-done = bf16[1792,1024]{1,0:T(8,128)(2,1)} async-done(((bf16[448,1024]{1,0:T(8,128)(2,1)}), bf16[1792,1024]{1,0:T(8,128)(2,1)}) %all-gather.3.cloned.1.call-update) | async-done | bytes 3670032 | tf_op jit(solution)/shard_map/all_gather | solution.py:612
  99.3 7.5 %fusion.25.qkv_ref = bf16[1024,768]{1,0:T(8,128)(2,1)S(1)} fusion(s32[1024]{0:T(1024)S(1)} %fusion.78, bf16[1024,1792]{1,0:T(8,128)(2,1)} %constant_dynamic-update-slice_fusion.refs_0_, bf16[1792,1024]{1,0:T(8,128)(2,1)} %all-gather.3.cloned.1.call-done), kind=kOutput, calls=%fused_computation.40 | convolution fusion | flops 4431806464 | bytes 7999488 | tf_op jit(solution)/shard_map/dot_general | solution.py:95
  106.9 5.8 %attend_forward.1 = bf16[1024,256]{1,0:T(8,128)(2,1)S(1)} custom-call(s32[2,3]{1,0:T(2,128)S(1)} %bitcast.98, bf16[1024,768]{1,0:T(8,128)(2,1)S(1)} %fusion.25.qkv_ref, f32[3,256]{1,0:T(4,128)S(1)} %constant_dynamic-slice_fusion.20.conv_ref), custom_call_target="tpu_custom_call" | custom-call | bytes 20000000 | tf_op jit(solution)/shard_map/attend_forward/pallas_call | solution.py:534
  117.0 2.8 collective-permute-start.12
  120.1 5.2 %collective-permute-done.10 = bf16[32,1792]{1,0:T(8,128)(2,1)S(1)} collective-permute-done((bf16[32,1792]{1,0:T(8,128)(2,1)S(1)}, bf16[32,1792]{1,0:T(8,128)(2,1)S(1)}, u32[]{:S(2)}, u32[]{:S(2)}) %collective-permute-start.10) | collective-permute-done | bytes 114720 | tf_op jit(solution)/shard_map/ppermute | solution.py:72
  125.3 8.6 %collective-permute-done.11 = bf16[32,1792]{1,0:T(8,128)(2,1)S(1)} collective-permute-done((bf16[32,1792]{1,0:T(8,128)(2,1)S(1)}, bf16[32,1792]{1,0:T(8,128)(2,1)S(1)}, u32[]{:S(2)}, u32[]{:S(2)}) %collective-permute-start.11) | collective-permute-done | bytes 114720 | tf_op jit(solution)/shard_map/ppermute | solution.py:72
  138.5 8.9 %collective-permute-done.23 = bf16[128,1792]{1,0:T(8,128)(2,1)S(1)} collective-permute-done((bf16[128,1792]{1,0:T(8,128)(2,1)S(1)}, bf16[128,1792]{1,0:T(8,128)(2,1)S(1)}, u32[]{:S(2)}, u32[]{:S(2)}) %collective-permute-start.23) | collective-permute-done | bytes 458784 | tf_op jit(solution)/shard_map/ppermute | solution.py:35
  149.6 11.1 %collective-permute-done.25 = bf16[128,1792]{1,0:T(8,128)(2,1)S(1)} collective-permute-done((bf16[128,1792]{1,0:T(8,128)(2,1)S(1)}, bf16[128,1792]{1,0:T(8,128)(2,1)S(1)}, u32[]{:S(2)}, u32[]{:S(2)}) %collective-permute-start.25) | collective-permute-done | bytes 458784 | tf_op jit(solution)/shard_map/ppermute | solution.py:35
  164.1 6.9 %collective-permute-done.15 = bf16[128,1792]{1,0:T(8,128)(2,1)S(1)} collective-permute-done((bf16[128,1792]{1,0:T(8,128)(2,1)S(1)}, bf16[128,1792]{1,0:T(8,128)(2,1)S(1)}, u32[]{:S(2)}, u32[]{:S(2)}) %collective-permute-start.15) | collective-permute-done | bytes 458784 | tf_op jit(solution)/shard_map/ppermute | solution.py:35
  174.6 9.8 %collective-permute-done.16 = bf16[128,1792]{1,0:T(8,128)(2,1)S(1)} collective-permute-done((bf16[128,1792]{1,0:T(8,128)(2,1)S(1)}, bf16[128,1792]{1,0:T(8,128)(2,1)S(1)}, u32[]{:S(2)}, u32[]{:S(2)}) %collective-permute-start.16) | collective-permute-done | bytes 458784 | tf_op jit(solution)/shard_map/ppermute | solution.py:35
  184.4 1.8 collective-permute-start.18
  188.2 4.6 collective-permute-done.18
  196.9 6.0 %copy.55.hidden_ref = bf16[1792,1024]{1,0:T(8,128)(2,1)} copy(bf16[1792,1024]{0,1:T(8,128)(2,1)} %bitcast.20) | data formatting | bytes 7340032 | tf_op jit(solution)/shard_map/optimization_barrier | solution.py:58
  202.8 5.9 %copy.56.grad_ref = bf16[1792,1024]{1,0:T(8,128)(2,1)} copy(bf16[1792,1024]{0,1:T(8,128)(2,1)} %bitcast.100) | data formatting | bytes 7340032 | tf_op jit(solution)/shard_map/optimization_barrier | solution.py:58
  208.8 18.6 %all-gather.5.cloned.1.call-done.weight_ref = bf16[1792,1792]{1,0:T(8,128)(2,1)} async-done(((bf16[448,1792]{1,0:T(8,128)(2,1)}), bf16[1792,1792]{1,0:T(8,128)(2,1)}) %all-gather.5.cloned.1.call-update) | async-done | bytes 6422544 | tf_op jit(solution)/shard_map/all_gather | solution.py:613
  227.4 13.6 %feed_forward.1 = (bf16[1024,640]{1,0:T(8,128)(2,1)S(1)}, bf16[1024,1280]{1,0:T(8,128)(2,1)S(1)}) custom-call(bf16[1024,1792]{1,0:T(8,128)(2,1)} %constant_dynamic-update-slice_fusion.8.hidden_ref, bf16[1024,1792]{1,0:T(8,128)(2,1)} %copy-done.22, bf16[1792,1792]{1,0:T(8,128)(2,1)} %all-gather.5.cloned.1.call-done.weight_ref, ...), custom_call_target="tpu_custom_call" | custom-call | flops 6694109184 | bytes 17612800 | tf_op jit(solution)/shard_map/feed_forward/pallas_call | solution.py:350
  241.1 9.9 %mlp_grad.1 = (bf16[1792,1792]{1,0:T(8,128)(2,1)}, bf16[1792,128]{1,0:T(8,128)(2,1)S(1)}) custom-call(bf16[1792,1024]{1,0:T(8,128)(2,1)S(1)} %copy-done.4, bf16[1792,1024]{1,0:T(8,128)(2,1)S(1)} %copy-done.5, bf16[1024,1280]{1,0:T(8,128)(2,1)S(1)} %get-tuple-element.109.pair_ref, bf16[1024,640]{1,0:T(8,128)(2,1)S(1)} %get-tuple-element.115.inner_ref), custom_call_target="tpu_custom_call" | custom-call | flops 6576668672 | bytes 17432576 | tf_op jit(solution)/shard_map/mlp_grad/pallas_call | solution.py:291
  250.9 6.5 %fusion.8 = bf16[512,1792]{1,0:T(8,128)(2,1)} fusion(bf16[1792,1792]{1,0:T(8,128)(2,1)} %all-gather.5.cloned.1.call-done.weight_ref, bf16[1024,1280]{1,0:T(8,128)(2,1)} %copy-done.11), kind=kOutput, calls=%fused_computation.13 | convolution fusion | flops 2349727744 | bytes 7733248 | tf_op jit(solution)/shard_map/dot_general | solution.py:95
  257.7 5.3 %fusion.4 = f32[512,1792]{1,0:T(8,128)S(1)} fusion(bf16[1792,1792]{1,0:T(8,128)(2,1)} %all-gather.5.cloned.1.call-done.weight_ref, bf16[1024,1280]{1,0:T(8,128)(2,1)} %copy-done.11), kind=kOutput, calls=%fused_computation.6 | convolution fusion | flops 2348810240 | bytes 9568256 | tf_op jit(solution)/shard_map/dot_general | solution.py:95
  263.0 2.0 add_convert_fusion.2
  265.1 1.7 collective-permute-start.34
  266.8 4.7 fusion.11
  272.6 3.0 copy-done.15
  275.9 2.6 collective-permute-done.34
  280.4 6.9 %collective-permute-done.35 = bf16[128,1792]{1,0:T(8,128)(2,1)S(1)} collective-permute-done((bf16[128,1792]{1,0:T(8,128)(2,1)S(1)}, bf16[128,1792]{1,0:T(8,128)(2,1)S(1)}, u32[]{:S(2)}, u32[]{:S(2)}) %collective-permute-start.35) | collective-permute-done | bytes 458784 | tf_op jit(solution)/shard_map/ppermute | solution.py:35
  289.0 1.9 add_convert_fusion.1
  293.9 10.3 %collective-permute-done.37 = bf16[128,1792]{1,0:T(8,128)(2,1)S(1)} collective-permute-done((bf16[128,1792]{1,0:T(8,128)(2,1)S(1)}, bf16[128,1792]{1,0:T(8,128)(2,1)S(1)}, u32[]{:S(2)}, u32[]{:S(2)}) %collective-permute-start.37) | collective-permute-done | bytes 458784 | tf_op jit(solution)/shard_map/ppermute | solution.py:35
  308.5 4.2 collective-permute-done.39
  317.2 4.9 fusion.31.grad_ref
  322.1 14.1 %attend_backward.1 = (bf16[1024,768]{1,0:T(8,128)(2,1)S(1)}, f32[3,256]{1,0:T(4,128)S(1)}) custom-call(s32[2,3]{1,0:T(2,128)S(1)} %bitcast.99, bf16[1024,768]{1,0:T(8,128)(2,1)S(1)} %fusion.25.qkv_ref, bf16[1024,256]{1,0:T(8,128)(2,1)S(1)} %fusion.31.grad_ref, f32[3,256]{1,0:T(4,128)S(1)} %constant_dynamic-slice_fusion.20.conv_ref), custom_call_target="tpu_custom_call" | custom-call | bytes 50000000 | tf_op jit(solution)/shard_map/attend_backward/pallas_call | solution.py:549
  336.2 2.8 add_convert_fusion.5
  340.6 2.4 fusion.26.refs_1_
  344.6 2.9 collective-permute-done.45
  349.7 1.8 collective-permute-done.46
  351.4 2.1 add_convert_fusion
  356.6 2.0 copy-done.7
  358.6 7.3 %weight_grad.1 = bf16[1792,1024]{1,0:T(8,128)(2,1)S(1)} custom-call(bf16[1024,1792]{1,0:T(8,128)(2,1)S(1)} %copy-done.7, bf16[1024,768]{1,0:T(8,128)(2,1)S(1)} %fusion.26.refs_1_, bf16[1024,1792]{1,0:T(8,128)(2,1)} %constant_dynamic-update-slice_fusion.24.refs_2_, bf16[1024,256]{1,0:T(8,128)(2,1)S(1)} %fusion.30.refs_3_), custom_call_target="tpu_custom_call" | custom-call | flops 3758096384 | bytes 13107200 | tf_op jit(solution)/shard_map/weight_grad/pallas_call | solution.py:261
  366.0 1.8 copy-done.3
  375.8 5.5 %collective-permute-done.48 = bf16[128,1792]{1,0:T(8,128)(2,1)S(1)} collective-permute-done((bf16[128,1792]{1,0:T(8,128)(2,1)S(1)}, bf16[128,1792]{1,0:T(8,128)(2,1)S(1)}, u32[]{:S(2)}, u32[]{:S(2)}) %collective-permute-start.48) | collective-permute-done | bytes 458784 | tf_op jit(solution)/shard_map/ppermute | solution.py:35
  389.4 2.7 collective-permute-start.51
  392.1 3.1 select_reduce_fusion
  400.2 23.1 %collective-permute-done.52 = bf16[118,128]{1,0:T(8,128)(2,1)S(1)} collective-permute-done((bf16[118,128]{1,0:T(8,128)(2,1)S(1)}, bf16[118,128]{1,0:T(8,128)(2,1)S(1)}, u32[]{:S(2)}, u32[]{:S(2)}) %collective-permute-start.52) | collective-permute-done | bytes 30240 | tf_op jit(solution)/shard_map/ppermute | solution.py:35
  424.0 3.3 collective-permute-done.54
  428.6 1.7 broadcast_select_fusion
  430.3 12.1 %reduce-scatter.3.cloned.1.call-done.refs_0_ = bf16[448,1024]{1,0:T(8,128)(2,1)} async-done(((bf16[1792,1024]{1,0:T(8,128)(2,1)}), bf16[448,1024]{1,0:T(8,128)(2,1)}) %reduce-scatter.3.cloned.1.call-update) | async-done | bytes 917520 | tf_op jit(solution)/shard_map/reduce_scatter | solution.py:783
  449.1 2.8 collective-permute-start.55
  453.3 9.8 %mlp_placed.1 = (f32[2,448,2432]{2,1,0:T(8,128)}, f32[1,448,2432]{2,1,0:T(8,128)}) custom-call(s32[1]{0:T(128)} %bitcast.35.index_ref, bf16[448,1792]{1,0:T(8,128)(2,1)S(1)} %copy-done.2, bf16[448,1792]{1,0:T(8,128)(2,1)S(1)} %get-tuple-element.201.refs_1_, bf16[448,1792]{1,0:T(8,128)(2,1)S(1)} %get-tuple-element.200.refs_2_, ...), custom_call_target="tpu_custom_call" | custom-call | bytes 21790720 | tf_op jit(solution)/shard_map/mlp_placed/pallas_call | solution.py:403
  463.8 2.1 collective-permute-done.62
  465.9 2.8 collective-permute-done.63
  469.3 4.1 collective-permute-done.56.refs_2_
  475.3 1.8 at_home.1
  478.4 3.2 placed.1
  483.7 2.2 last_placed.1
  (444 shorter events, 110.1 us)
Async XLA Ops:
  7.2 92.1 %all-gather.3.cloned.1.call-start = ((), (), s32[]{:S(2)}) async-start(), calls=%async_computation.3 | async-start | bytes 4587520 | tf_op jit(solution)/shard_map/all_gather | solution.py:612
  12.9 16.0 %all-to-all-start = ((f32[16,1,1824]{2,1,0:T(1,128)}), f32[16,1,1824]{2,1,0:T(1,128)S(1)}, u32[]{:S(2)}, u32[]{:S(2)}) async-start(f32[16,1,1824]{2,1,0:T(1,128)} %broadcast_in_dim.54), calls=%async_computation | async-start | bytes 245760 | tf_op jit(solution)/shard_map/all_to_all | solution.py:625
  21.2 206.3 %all-gather.5.cloned.1.call-start = ((), (), s32[]{:S(2)}) async-start(), calls=%async_computation.4 | async-start | bytes 8028160 | tf_op jit(solution)/shard_map/all_gather | solution.py:613
  26.0 359.2 %reduce-scatter.5.cloned.1.call-start = ((), (), s32[]{:S(2)}) async-start(), calls=%async_computation.6 | async-start | bytes 8028160 | tf_op jit(solution)/shard_map/reduce_scatter | solution.py:721
  30.0 10.5 %collective-permute-start = (bf16[32,1792]{1,0:T(8,128)(2,1)S(1)}, bf16[32,1792]{1,0:T(8,128)(2,1)S(1)}, u32[]{:S(2)}, u32[]{:S(2)}) collective-permute-start(bf16[32,1792]{1,0:T(8,128)(2,1)S(1)} %get-tuple-element.242), channel_id=1, source_target_pairs={{0,8},{8,16},{16,24},{24,0},{1,9},{9,17},{17,25},{25,1},{2,10},{10... | collective-permute-start | bytes 344072 | tf_op jit(solution)/shard_map/ppermute | solution.py:72
  30.8 16.6 %collective-permute-start.1 = (bf16[32,1792]{1,0:T(8,128)(2,1)S(1)}, bf16[32,1792]{1,0:T(8,128)(2,1)S(1)}, u32[]{:S(2)}, u32[]{:S(2)}) collective-permute-start(bf16[32,1792]{1,0:T(8,128)(2,1)S(1)} %get-tuple-element.241), channel_id=1, source_target_pairs={{0,16},{8,24},{16,0},{24,8},{1,17},{9,25},{17,1},{25,9},{2,18},{10... | collective-permute-start | bytes 344072 | tf_op jit(solution)/shard_map/ppermute | solution.py:72
  34.7 12.7 %collective-permute-start.2 = (bf16[32,1792]{1,0:T(8,128)(2,1)S(1)}, bf16[32,1792]{1,0:T(8,128)(2,1)S(1)}, u32[]{:S(2)}, u32[]{:S(2)}) collective-permute-start(bf16[32,1792]{1,0:T(8,128)(2,1)S(1)} %get-tuple-element.240), channel_id=1, source_target_pairs={{0,24},{8,0},{16,8},{24,16},{1,25},{9,1},{17,9},{25,17},{2,26},{10... | collective-permute-start | bytes 344072 | tf_op jit(solution)/shard_map/ppermute | solution.py:72
  48.6 13.4 %collective-permute-start.3 = (bf16[128,1792]{1,0:T(8,128)(2,1)}, bf16[128,1792]{1,0:T(8,128)(2,1)S(1)}, u32[]{:S(2)}, u32[]{:S(2)}) collective-permute-start(bf16[128,1792]{1,0:T(8,128)(2,1)} %get-tuple-element.189), channel_id=1, source_target_pairs={{0,2},{1,5},{2,0},{3,7},{4,6},{5,1},{6,4},{7,3},{8,10},{9,13},{10,... | collective-permute-start | bytes 1376264 | tf_op jit(solution)/shard_map/ppermute | solution.py:35
  50.1 13.0 %collective-permute-start.4 = (bf16[128,1792]{1,0:T(8,128)(2,1)}, bf16[128,1792]{1,0:T(8,128)(2,1)S(1)}, u32[]{:S(2)}, u32[]{:S(2)}) collective-permute-start(bf16[128,1792]{1,0:T(8,128)(2,1)} %get-tuple-element.189), channel_id=1, source_target_pairs={{0,4},{1,3},{2,6},{3,1},{4,0},{5,7},{6,2},{7,5},{8,12},{9,11},{10,... | collective-permute-start | bytes 1376264 | tf_op jit(solution)/shard_map/ppermute | solution.py:35
  52.6 18.8 %collective-permute-start.6 = (bf16[128,1792]{1,0:T(8,128)(2,1)}, bf16[128,1792]{1,0:T(8,128)(2,1)S(1)}, u32[]{:S(2)}, u32[]{:S(2)}) collective-permute-start(bf16[128,1792]{1,0:T(8,128)(2,1)} %get-tuple-element.189), channel_id=1, source_target_pairs={{0,1},{1,0},{2,3},{3,2},{4,5},{5,4},{6,7},{7,6},{8,9},{9,8},{10,11... | collective-permute-start | bytes 1376264 | tf_op jit(solution)/shard_map/ppermute | solution.py:35
  62.1 8.5 %collective-permute-start.5 = (bf16[128,1792]{1,0:T(8,128)(2,1)S(1)}, bf16[128,1792]{1,0:T(8,128)(2,1)S(1)}, u32[]{:S(2)}, u32[]{:S(2)}) collective-permute-start(bf16[128,1792]{1,0:T(8,128)(2,1)S(1)} %collective-permute-done.3), channel_id=1, source_target_pairs={{0,4},{1,3},{2,6},{3,1},{4,0},{5,7},{6,2},{7,5},{8,12},{9,11},{10,... | collective-permute-start | bytes 1376264 | tf_op jit(solution)/shard_map/ppermute | solution.py:35
  63.0 9.1 %collective-permute-start.7 = (bf16[128,1792]{1,0:T(8,128)(2,1)S(1)}, bf16[128,1792]{1,0:T(8,128)(2,1)S(1)}, u32[]{:S(2)}, u32[]{:S(2)}) collective-permute-start(bf16[128,1792]{1,0:T(8,128)(2,1)S(1)} %collective-permute-done.3), channel_id=1, source_target_pairs={{0,1},{1,0},{2,3},{3,2},{4,5},{5,4},{6,7},{7,6},{8,9},{9,8},{10,11... | collective-permute-start | bytes 1376264 | tf_op jit(solution)/shard_map/ppermute | solution.py:35
  63.0 9.9 %collective-permute-start.8 = (bf16[128,1792]{1,0:T(8,128)(2,1)S(1)}, bf16[128,1792]{1,0:T(8,128)(2,1)S(1)}, u32[]{:S(2)}, u32[]{:S(2)}) collective-permute-start(bf16[128,1792]{1,0:T(8,128)(2,1)S(1)} %collective-permute-done.4), channel_id=1, source_target_pairs={{0,1},{1,0},{2,3},{3,2},{4,5},{5,4},{6,7},{7,6},{8,9},{9,8},{10,11... | collective-permute-start | bytes 1376264 | tf_op jit(solution)/shard_map/ppermute | solution.py:35
  74.6 40.7 %collective-permute-start.30 = (bf16[112,128]{1,0:T(8,128)(2,1)S(1)}, bf16[112,128]{1,0:T(8,128)(2,1)S(1)}, u32[]{:S(2)}, u32[]{:S(2)}) collective-permute-start(bf16[112,128]{1,0:T(8,128)(2,1)S(1)} %pad_maximum_fusion.8), channel_id=1, source_target_pairs={{0,8},{8,16},{16,24},{24,0},{1,9},{9,17},{17,25},{25,1},{2,10},{10... | collective-permute-start | bytes 86024 | tf_op jit(solution)/shard_map/ppermute | solution.py:72
  83.3 33.7 %collective-permute-start.31 = (bf16[112,128]{1,0:T(8,128)(2,1)S(1)}, bf16[112,128]{1,0:T(8,128)(2,1)S(1)}, u32[]{:S(2)}, u32[]{:S(2)}) collective-permute-start(bf16[112,128]{1,0:T(8,128)(2,1)S(1)} %pad_maximum_fusion.8), channel_id=1, source_target_pairs={{0,16},{8,24},{16,0},{24,8},{1,17},{9,25},{17,1},{25,9},{2,18},{10... | collective-permute-start | bytes 86024 | tf_op jit(solution)/shard_map/ppermute | solution.py:72
  86.6 33.4 %collective-permute-start.32 = (bf16[112,128]{1,0:T(8,128)(2,1)S(1)}, bf16[112,128]{1,0:T(8,128)(2,1)S(1)}, u32[]{:S(2)}, u32[]{:S(2)}) collective-permute-start(bf16[112,128]{1,0:T(8,128)(2,1)S(1)} %pad_maximum_fusion.8), channel_id=1, source_target_pairs={{0,24},{8,0},{16,8},{24,16},{1,25},{9,1},{17,9},{25,17},{2,26},{10... | collective-permute-start | bytes 86024 | tf_op jit(solution)/shard_map/ppermute | solution.py:72
  114.9 22.1 %collective-permute-start.13 = (bf16[512,1792]{1,0:T(8,128)(2,1)S(1)}, bf16[512,1792]{1,0:T(8,128)(2,1)S(1)}, u32[]{:S(2)}, u32[]{:S(2)}) collective-permute-start(bf16[512,1792]{1,0:T(8,128)(2,1)S(1)} %convolution_convert_fusion), channel_id=1, source_target_pairs={{0,1},{1,0},{2,3},{3,2},{4,5},{5,4},{6,7},{7,6},{8,9},{9,8},{10,11... | collective-permute-start | bytes 5505032 | tf_op jit(solution)/shard_map/ppermute | solution.py:35
  115.0 10.3 %collective-permute-start.10 = (bf16[32,1792]{1,0:T(8,128)(2,1)S(1)}, bf16[32,1792]{1,0:T(8,128)(2,1)S(1)}, u32[]{:S(2)}, u32[]{:S(2)}) collective-permute-start(bf16[32,1792]{1,0:T(8,128)(2,1)S(1)} %get-tuple-element.238), channel_id=1, source_target_pairs={{0,8},{8,16},{16,24},{24,0},{1,9},{9,17},{17,25},{25,1},{2,10},{10... | collective-permute-start | bytes 344072 | tf_op jit(solution)/shard_map/ppermute | solution.py:72
  115.3 18.6 %collective-permute-start.11 = (bf16[32,1792]{1,0:T(8,128)(2,1)S(1)}, bf16[32,1792]{1,0:T(8,128)(2,1)S(1)}, u32[]{:S(2)}, u32[]{:S(2)}) collective-permute-start(bf16[32,1792]{1,0:T(8,128)(2,1)S(1)} %get-tuple-element.237), channel_id=1, source_target_pairs={{0,16},{8,24},{16,0},{24,8},{1,17},{9,25},{17,1},{25,9},{2,18},{10... | collective-permute-start | bytes 344072 | tf_op jit(solution)/shard_map/ppermute | solution.py:72
  117.0 16.9 %collective-permute-start.12 = (bf16[32,1792]{1,0:T(8,128)(2,1)S(1)}, bf16[32,1792]{1,0:T(8,128)(2,1)S(1)}, u32[]{:S(2)}, u32[]{:S(2)}) collective-permute-start(bf16[32,1792]{1,0:T(8,128)(2,1)S(1)} %get-tuple-element.236), channel_id=1, source_target_pairs={{0,24},{8,0},{16,8},{24,16},{1,25},{9,1},{17,9},{25,17},{2,26},{10... | collective-permute-start | bytes 344072 | tf_op jit(solution)/shard_map/ppermute | solution.py:72
  134.0 13.5 %collective-permute-start.23 = (bf16[128,1792]{1,0:T(8,128)(2,1)S(1)}, bf16[128,1792]{1,0:T(8,128)(2,1)S(1)}, u32[]{:S(2)}, u32[]{:S(2)}) collective-permute-start(bf16[128,1792]{1,0:T(8,128)(2,1)S(1)} %pad_maximum_fusion.3), channel_id=1, source_target_pairs={{0,2},{1,5},{2,0},{3,7},{4,6},{5,1},{6,4},{7,3},{8,10},{9,13},{10,... | collective-permute-start | bytes 1376264 | tf_op jit(solution)/shard_map/ppermute | solution.py:35
  135.5 13.5 %collective-permute-start.24 = (bf16[128,1792]{1,0:T(8,128)(2,1)S(1)}, bf16[128,1792]{1,0:T(8,128)(2,1)S(1)}, u32[]{:S(2)}, u32[]{:S(2)}) collective-permute-start(bf16[128,1792]{1,0:T(8,128)(2,1)S(1)} %pad_maximum_fusion.3), channel_id=1, source_target_pairs={{0,4},{1,3},{2,6},{3,1},{4,0},{5,7},{6,2},{7,5},{8,12},{9,11},{10,... | collective-permute-start | bytes 1376264 | tf_op jit(solution)/shard_map/ppermute | solution.py:35
  137.0 27.0 %collective-permute-start.26 = (bf16[128,1792]{1,0:T(8,128)(2,1)S(1)}, bf16[128,1792]{1,0:T(8,128)(2,1)S(1)}, u32[]{:S(2)}, u32[]{:S(2)}) collective-permute-start(bf16[128,1792]{1,0:T(8,128)(2,1)S(1)} %pad_maximum_fusion.3), channel_id=1, source_target_pairs={{0,1},{1,0},{2,3},{3,2},{4,5},{5,4},{6,7},{7,6},{8,9},{9,8},{10,11... | collective-permute-start | bytes 1376264 | tf_op jit(solution)/shard_map/ppermute | solution.py:35
  137.9 24.4 %collective-permute-start.14 = (bf16[256,1792]{1,0:T(8,128)(2,1)S(1)}, bf16[256,1792]{1,0:T(8,128)(2,1)S(1)}, u32[]{:S(2)}, u32[]{:S(2)}) collective-permute-start(bf16[256,1792]{1,0:T(8,128)(2,1)S(1)} %slice.405), channel_id=1, source_target_pairs={{0,4},{1,3},{2,6},{3,1},{4,0},{5,7},{6,2},{7,5},{8,12},{9,11},{10,... | collective-permute-start | bytes 2752520 | tf_op jit(solution)/shard_map/ppermute | solution.py:35
  147.4 13.2 %collective-permute-start.25 = (bf16[128,1792]{1,0:T(8,128)(2,1)S(1)}, bf16[128,1792]{1,0:T(8,128)(2,1)S(1)}, u32[]{:S(2)}, u32[]{:S(2)}) collective-permute-start(bf16[128,1792]{1,0:T(8,128)(2,1)S(1)} %collective-permute-done.23), channel_id=1, source_target_pairs={{0,4},{1,3},{2,6},{3,1},{4,0},{5,7},{6,2},{7,5},{8,12},{9,11},{10,... | collective-permute-start | bytes 1376264 | tf_op jit(solution)/shard_map/ppermute | solution.py:35
  149.0 15.1 %collective-permute-start.27 = (bf16[128,1792]{1,0:T(8,128)(2,1)S(1)}, bf16[128,1792]{1,0:T(8,128)(2,1)S(1)}, u32[]{:S(2)}, u32[]{:S(2)}) collective-permute-start(bf16[128,1792]{1,0:T(8,128)(2,1)S(1)} %collective-permute-done.23), channel_id=1, source_target_pairs={{0,1},{1,0},{2,3},{3,2},{4,5},{5,4},{6,7},{7,6},{8,9},{9,8},{10,11... | collective-permute-start | bytes 1376264 | tf_op jit(solution)/shard_map/ppermute | solution.py:35
  149.0 25.4 %collective-permute-start.28 = (bf16[128,1792]{1,0:T(8,128)(2,1)S(1)}, bf16[128,1792]{1,0:T(8,128)(2,1)S(1)}, u32[]{:S(2)}, u32[]{:S(2)}) collective-permute-start(bf16[128,1792]{1,0:T(8,128)(2,1)S(1)} %collective-permute-done.24), channel_id=1, source_target_pairs={{0,1},{1,0},{2,3},{3,2},{4,5},{5,4},{6,7},{7,6},{8,9},{9,8},{10,11... | collective-permute-start | bytes 1376264 | tf_op jit(solution)/shard_map/ppermute | solution.py:35
  160.6 13.8 %collective-permute-start.29 = (bf16[128,1792]{1,0:T(8,128)(2,1)S(1)}, bf16[128,1792]{1,0:T(8,128)(2,1)S(1)}, u32[]{:S(2)}, u32[]{:S(2)}) collective-permute-start(bf16[128,1792]{1,0:T(8,128)(2,1)S(1)} %collective-permute-done.25), channel_id=1, source_target_pairs={{0,1},{1,0},{2,3},{3,2},{4,5},{5,4},{6,7},{7,6},{8,9},{9,8},{10,11... | collective-permute-start | bytes 1376264 | tf_op jit(solution)/shard_map/ppermute | solution.py:35
  162.5 8.5 %collective-permute-start.15 = (bf16[128,1792]{1,0:T(8,128)(2,1)S(1)}, bf16[128,1792]{1,0:T(8,128)(2,1)S(1)}, u32[]{:S(2)}, u32[]{:S(2)}) collective-permute-start(bf16[128,1792]{1,0:T(8,128)(2,1)S(1)} %slice.406), channel_id=1, source_target_pairs={{0,2},{1,5},{2,0},{3,7},{4,6},{5,1},{6,4},{7,3},{8,10},{9,13},{10,... | collective-permute-start | bytes 1376264 | tf_op jit(solution)/shard_map/ppermute | solution.py:35
  172.4 12.0 %collective-permute-start.16 = (bf16[128,1792]{1,0:T(8,128)(2,1)S(1)}, bf16[128,1792]{1,0:T(8,128)(2,1)S(1)}, u32[]{:S(2)}, u32[]{:S(2)}) collective-permute-start(bf16[128,1792]{1,0:T(8,128)(2,1)S(1)} %get-tuple-element.185), channel_id=1, source_target_pairs={{0,2},{1,5},{2,0},{3,7},{4,6},{5,1},{6,4},{7,3},{8,10},{9,13},{10,... | collective-permute-start | bytes 1376264 | tf_op jit(solution)/shard_map/ppermute | solution.py:35
  173.9 12.3 %collective-permute-start.17 = (bf16[128,1792]{1,0:T(8,128)(2,1)S(1)}, bf16[128,1792]{1,0:T(8,128)(2,1)S(1)}, u32[]{:S(2)}, u32[]{:S(2)}) collective-permute-start(bf16[128,1792]{1,0:T(8,128)(2,1)S(1)} %get-tuple-element.185), channel_id=1, source_target_pairs={{0,4},{1,3},{2,6},{3,1},{4,0},{5,7},{6,2},{7,5},{8,12},{9,11},{10,... | collective-permute-start | bytes 1376264 | tf_op jit(solution)/shard_map/ppermute | solution.py:35
  174.5 19.2 %collective-permute-start.19 = (bf16[128,1792]{1,0:T(8,128)(2,1)S(1)}, bf16[128,1792]{1,0:T(8,128)(2,1)S(1)}, u32[]{:S(2)}, u32[]{:S(2)}) collective-permute-start(bf16[128,1792]{1,0:T(8,128)(2,1)S(1)} %get-tuple-element.185), channel_id=1, source_target_pairs={{0,1},{1,0},{2,3},{3,2},{4,5},{5,4},{6,7},{7,6},{8,9},{9,8},{10,11... | collective-permute-start | bytes 1376264 | tf_op jit(solution)/shard_map/ppermute | solution.py:35
  184.4 8.5 %collective-permute-start.18 = (bf16[128,1792]{1,0:T(8,128)(2,1)S(1)}, bf16[128,1792]{1,0:T(8,128)(2,1)S(1)}, u32[]{:S(2)}, u32[]{:S(2)}) collective-permute-start(bf16[128,1792]{1,0:T(8,128)(2,1)S(1)} %collective-permute-done.16), channel_id=1, source_target_pairs={{0,4},{1,3},{2,6},{3,1},{4,0},{5,7},{6,2},{7,5},{8,12},{9,11},{10,... | collective-permute-start | bytes 1376264 | tf_op jit(solution)/shard_map/ppermute | solution.py:35
  186.1 8.3 %collective-permute-start.20 = (bf16[128,1792]{1,0:T(8,128)(2,1)S(1)}, bf16[128,1792]{1,0:T(8,128)(2,1)S(1)}, u32[]{:S(2)}, u32[]{:S(2)}) collective-permute-start(bf16[128,1792]{1,0:T(8,128)(2,1)S(1)} %collective-permute-done.16), channel_id=1, source_target_pairs={{0,1},{1,0},{2,3},{3,2},{4,5},{5,4},{6,7},{7,6},{8,9},{9,8},{10,11... | collective-permute-start | bytes 1376264 | tf_op jit(solution)/shard_map/ppermute | solution.py:35
  186.1 9.2 %collective-permute-start.21 = (bf16[128,1792]{1,0:T(8,128)(2,1)S(1)}, bf16[128,1792]{1,0:T(8,128)(2,1)S(1)}, u32[]{:S(2)}, u32[]{:S(2)}) collective-permute-start(bf16[128,1792]{1,0:T(8,128)(2,1)S(1)} %collective-permute-done.17), channel_id=1, source_target_pairs={{0,1},{1,0},{2,3},{3,2},{4,5},{5,4},{6,7},{7,6},{8,9},{9,8},{10,11... | collective-permute-start | bytes 1376264 | tf_op jit(solution)/shard_map/ppermute | solution.py:35
  257.5 184.9 %reduce-scatter.3.cloned.1.call-start = ((), (), s32[]{:S(2)}) async-start(), calls=%async_computation.5 | async-start | bytes 4587520 | tf_op jit(solution)/shard_map/reduce_scatter | solution.py:783
  265.1 13.5 %collective-permute-start.34 = (bf16[256,1792]{1,0:T(8,128)(2,1)S(1)}, bf16[256,1792]{1,0:T(8,128)(2,1)S(1)}, u32[]{:S(2)}, u32[]{:S(2)}) collective-permute-start(bf16[256,1792]{1,0:T(8,128)(2,1)S(1)} %get-tuple-element.113), channel_id=1, source_target_pairs={{0,4},{1,3},{2,6},{3,1},{4,0},{5,7},{6,2},{7,5},{8,12},{9,11},{10,... | collective-permute-start | bytes 2752520 | tf_op jit(solution)/shard_map/ppermute | solution.py:35
  278.7 10.3 %collective-permute-start.36 = (bf16[512,1792]{1,0:T(8,128)(2,1)S(1)}, bf16[512,1792]{1,0:T(8,128)(2,1)S(1)}, u32[]{:S(2)}, u32[]{:S(2)}) collective-permute-start(bf16[512,1792]{1,0:T(8,128)(2,1)S(1)} %slice.404), channel_id=1, source_target_pairs={{0,1},{1,0},{2,3},{3,2},{4,5},{5,4},{6,7},{7,6},{8,9},{9,8},{10,11... | collective-permute-start | bytes 5505032 | tf_op jit(solution)/shard_map/ppermute | solution.py:35
  278.8 8.5 %collective-permute-start.35 = (bf16[128,1792]{1,0:T(8,128)(2,1)S(1)}, bf16[128,1792]{1,0:T(8,128)(2,1)S(1)}, u32[]{:S(2)}, u32[]{:S(2)}) collective-permute-start(bf16[128,1792]{1,0:T(8,128)(2,1)S(1)} %get-tuple-element.121), channel_id=1, source_target_pairs={{0,2},{1,5},{2,0},{3,7},{4,6},{5,1},{6,4},{7,3},{8,10},{9,13},{10,... | collective-permute-start | bytes 1376264 | tf_op jit(solution)/shard_map/ppermute | solution.py:35
  290.9 13.3 %collective-permute-start.37 = (bf16[128,1792]{1,0:T(8,128)(2,1)S(1)}, bf16[128,1792]{1,0:T(8,128)(2,1)S(1)}, u32[]{:S(2)}, u32[]{:S(2)}) collective-permute-start(bf16[128,1792]{1,0:T(8,128)(2,1)S(1)} %get-tuple-element.125), channel_id=1, source_target_pairs={{0,2},{1,5},{2,0},{3,7},{4,6},{5,1},{6,4},{7,3},{8,10},{9,13},{10,... | collective-permute-start | bytes 1376264 | tf_op jit(solution)/shard_map/ppermute | solution.py:35
  292.5 11.8 %collective-permute-start.38 = (bf16[128,1792]{1,0:T(8,128)(2,1)S(1)}, bf16[128,1792]{1,0:T(8,128)(2,1)S(1)}, u32[]{:S(2)}, u32[]{:S(2)}) collective-permute-start(bf16[128,1792]{1,0:T(8,128)(2,1)S(1)} %get-tuple-element.125), channel_id=1, source_target_pairs={{0,4},{1,3},{2,6},{3,1},{4,0},{5,7},{6,2},{7,5},{8,12},{9,11},{10,... | collective-permute-start | bytes 1376264 | tf_op jit(solution)/shard_map/ppermute | solution.py:35
  304.2 8.5 %collective-permute-start.39 = (bf16[128,1792]{1,0:T(8,128)(2,1)S(1)}, bf16[128,1792]{1,0:T(8,128)(2,1)S(1)}, u32[]{:S(2)}, u32[]{:S(2)}) collective-permute-start(bf16[128,1792]{1,0:T(8,128)(2,1)S(1)} %collective-permute-done.37), channel_id=1, source_target_pairs={{0,4},{1,3},{2,6},{3,1},{4,0},{5,7},{6,2},{7,5},{8,12},{9,11},{10,... | collective-permute-start | bytes 1376264 | tf_op jit(solution)/shard_map/ppermute | solution.py:35
  304.7 9.6 %collective-permute-start.41 = (bf16[128,1792]{1,0:T(8,128)(2,1)S(1)}, bf16[128,1792]{1,0:T(8,128)(2,1)S(1)}, u32[]{:S(2)}, u32[]{:S(2)}) collective-permute-start(bf16[128,1792]{1,0:T(8,128)(2,1)S(1)} %collective-permute-done.37), channel_id=1, source_target_pairs={{0,1},{1,0},{2,3},{3,2},{4,5},{5,4},{6,7},{7,6},{8,9},{9,8},{10,11... | collective-permute-start | bytes 1376264 | tf_op jit(solution)/shard_map/ppermute | solution.py:35
  305.6 7.9 %collective-permute-start.40 = (bf16[128,1792]{1,0:T(8,128)(2,1)S(1)}, bf16[128,1792]{1,0:T(8,128)(2,1)S(1)}, u32[]{:S(2)}, u32[]{:S(2)}) collective-permute-start(bf16[128,1792]{1,0:T(8,128)(2,1)S(1)} %get-tuple-element.125), channel_id=1, source_target_pairs={{0,1},{1,0},{2,3},{3,2},{4,5},{5,4},{6,7},{7,6},{8,9},{9,8},{10,11... | collective-permute-start | bytes 1376264 | tf_op jit(solution)/shard_map/ppermute | solution.py:35
  305.6 9.5 %collective-permute-start.42 = (bf16[128,1792]{1,0:T(8,128)(2,1)S(1)}, bf16[128,1792]{1,0:T(8,128)(2,1)S(1)}, u32[]{:S(2)}, u32[]{:S(2)}) collective-permute-start(bf16[128,1792]{1,0:T(8,128)(2,1)S(1)} %collective-permute-done.38), channel_id=1, source_target_pairs={{0,1},{1,0},{2,3},{3,2},{4,5},{5,4},{6,7},{7,6},{8,9},{9,8},{10,11... | collective-permute-start | bytes 1376264 | tf_op jit(solution)/shard_map/ppermute | solution.py:35
  316.7 19.5 %collective-permute-start.44 = (bf16[256,1792]{1,0:T(8,128)(2,1)}, bf16[256,1792]{1,0:T(8,128)(2,1)}, u32[]{:S(2)}, u32[]{:S(2)}) collective-permute-start(bf16[256,1792]{1,0:T(8,128)(2,1)} %get-tuple-element.129), channel_id=1, source_target_pairs={{0,4},{1,3},{2,6},{3,1},{4,0},{5,7},{6,2},{7,5},{8,12},{9,11},{10,... | collective-permute-start | bytes 2752520 | tf_op jit(solution)/shard_map/ppermute | solution.py:35
  339.0 8.5 %collective-permute-start.45 = (bf16[128,1792]{1,0:T(8,128)(2,1)S(1)}, bf16[128,1792]{1,0:T(8,128)(2,1)S(1)}, u32[]{:S(2)}, u32[]{:S(2)}) collective-permute-start(bf16[128,1792]{1,0:T(8,128)(2,1)S(1)} %get-tuple-element.136), channel_id=1, source_target_pairs={{0,2},{1,5},{2,0},{3,7},{4,6},{5,1},{6,4},{7,3},{8,10},{9,13},{10,... | collective-permute-start | bytes 1376264 | tf_op jit(solution)/shard_map/ppermute | solution.py:35
  353.5 14.4 %collective-permute-start.47 = (bf16[256,1792]{1,0:T(8,128)(2,1)}, bf16[256,1792]{1,0:T(8,128)(2,1)}, u32[]{:S(2)}, u32[]{:S(2)}) collective-permute-start(bf16[256,1792]{1,0:T(8,128)(2,1)} %get-tuple-element.142), channel_id=1, source_target_pairs={{0,4},{1,3},{2,6},{3,1},{4,0},{5,7},{6,2},{7,5},{8,12},{9,11},{10,... | collective-permute-start | bytes 2752520 | tf_op jit(solution)/shard_map/ppermute | solution.py:35
  372.7 8.5 %collective-permute-start.48 = (bf16[128,1792]{1,0:T(8,128)(2,1)S(1)}, bf16[128,1792]{1,0:T(8,128)(2,1)S(1)}, u32[]{:S(2)}, u32[]{:S(2)}) collective-permute-start(bf16[128,1792]{1,0:T(8,128)(2,1)S(1)} %add_convert_fusion.3), channel_id=1, source_target_pairs={{0,2},{1,5},{2,0},{3,7},{4,6},{5,1},{6,4},{7,3},{8,10},{9,13},{10,... | collective-permute-start | bytes 1376264 | tf_op jit(solution)/shard_map/ppermute | solution.py:35
  385.1 42.9 %collective-permute-start.65 = (bf16[448,1792]{1,0:T(8,128)(2,1)}, bf16[448,1792]{1,0:T(8,128)(2,1)}, u32[]{:S(2)}, u32[]{:S(2)}) collective-permute-start(bf16[448,1792]{1,0:T(8,128)(2,1)} %reduce-scatter.5.cloned.1.call-done.refs_0_), channel_id=1, source_target_pairs={{0,2},{1,5},{2,0},{3,7},{4,6},{5,1},{6,4},{7,3},{8,10},{9,13},{10,... | collective-permute-start | bytes 4816904 | tf_op jit(solution)/shard_map/ppermute | solution.py:35
  386.7 41.9 %collective-permute-start.66 = (bf16[448,1792]{1,0:T(8,128)(2,1)}, bf16[448,1792]{1,0:T(8,128)(2,1)S(1)}, u32[]{:S(2)}, u32[]{:S(2)}) collective-permute-start(bf16[448,1792]{1,0:T(8,128)(2,1)} %reduce-scatter.5.cloned.1.call-done.refs_0_), channel_id=1, source_target_pairs={{0,4},{1,3},{2,6},{3,1},{4,0},{5,7},{6,2},{7,5},{8,12},{9,11},{10,... | collective-permute-start | bytes 4816904 | tf_op jit(solution)/shard_map/ppermute | solution.py:35
  388.2 8.6 %collective-permute-start.50 = (bf16[118,128]{1,0:T(8,128)(2,1)S(1)}, bf16[118,128]{1,0:T(8,128)(2,1)S(1)}, u32[]{:S(2)}, u32[]{:S(2)}) collective-permute-start(bf16[118,128]{1,0:T(8,128)(2,1)S(1)} %get-tuple-element.274), channel_id=1, source_target_pairs={{0,16},{8,24},{16,0},{24,8},{1,17},{9,25},{17,1},{25,9},{2,18},{10... | collective-permute-start | bytes 90632 | tf_op jit(solution)/shard_map/ppermute | solution.py:72
  389.4 7.4 %collective-permute-start.51 = (bf16[118,128]{1,0:T(8,128)(2,1)S(1)}, bf16[118,128]{1,0:T(8,128)(2,1)S(1)}, u32[]{:S(2)}, u32[]{:S(2)}) collective-permute-start(bf16[118,128]{1,0:T(8,128)(2,1)S(1)} %get-tuple-element.275), channel_id=1, source_target_pairs={{0,24},{8,0},{16,8},{24,16},{1,25},{9,1},{17,9},{25,17},{2,26},{10... | collective-permute-start | bytes 90632 | tf_op jit(solution)/shard_map/ppermute | solution.py:72
  397.5 25.8 %collective-permute-start.52 = (bf16[118,128]{1,0:T(8,128)(2,1)S(1)}, bf16[118,128]{1,0:T(8,128)(2,1)S(1)}, u32[]{:S(2)}, u32[]{:S(2)}) collective-permute-start(bf16[118,128]{1,0:T(8,128)(2,1)S(1)} %add_convert_fusion.7), channel_id=1, source_target_pairs={{0,2},{1,5},{2,0},{3,7},{4,6},{5,1},{6,4},{7,3},{8,10},{9,13},{10,... | collective-permute-start | bytes 90632 | tf_op jit(solution)/shard_map/ppermute | solution.py:35
  398.7 24.6 %collective-permute-start.53 = (bf16[118,128]{1,0:T(8,128)(2,1)S(1)}, bf16[118,128]{1,0:T(8,128)(2,1)S(1)}, u32[]{:S(2)}, u32[]{:S(2)}) collective-permute-start(bf16[118,128]{1,0:T(8,128)(2,1)S(1)} %add_convert_fusion.7), channel_id=1, source_target_pairs={{0,4},{1,3},{2,6},{3,1},{4,0},{5,7},{6,2},{7,5},{8,12},{9,11},{10,... | collective-permute-start | bytes 90632 | tf_op jit(solution)/shard_map/ppermute | solution.py:35
  428.1 25.2 %collective-permute-start.67 = (bf16[448,1792]{1,0:T(8,128)(2,1)}, bf16[448,1792]{1,0:T(8,128)(2,1)}, u32[]{:S(2)}, u32[]{:S(2)}) collective-permute-start(bf16[448,1792]{1,0:T(8,128)(2,1)} %collective-permute-done.65), channel_id=1, source_target_pairs={{0,4},{1,3},{2,6},{3,1},{4,0},{5,7},{6,2},{7,5},{8,12},{9,11},{10,... | collective-permute-start | bytes 4816904 | tf_op jit(solution)/shard_map/ppermute | solution.py:35
  442.4 23.5 %collective-permute-start.62 = (bf16[448,1024]{1,0:T(8,128)(2,1)}, bf16[448,1024]{1,0:T(8,128)(2,1)S(1)}, u32[]{:S(2)}, u32[]{:S(2)}) collective-permute-start(bf16[448,1024]{1,0:T(8,128)(2,1)} %reduce-scatter.3.cloned.1.call-done.refs_0_), channel_id=1, source_target_pairs={{0,2},{1,5},{2,0},{3,7},{4,6},{5,1},{6,4},{7,3},{8,10},{9,13},{10,... | collective-permute-start | bytes 2752520 | tf_op jit(solution)/shard_map/ppermute | solution.py:35
  443.9 24.8 %collective-permute-start.63 = (bf16[448,1024]{1,0:T(8,128)(2,1)}, bf16[448,1024]{1,0:T(8,128)(2,1)S(1)}, u32[]{:S(2)}, u32[]{:S(2)}) collective-permute-start(bf16[448,1024]{1,0:T(8,128)(2,1)} %reduce-scatter.3.cloned.1.call-done.refs_0_), channel_id=1, source_target_pairs={{0,4},{1,3},{2,6},{3,1},{4,0},{5,7},{6,2},{7,5},{8,12},{9,11},{10,... | collective-permute-start | bytes 2752520 | tf_op jit(solution)/shard_map/ppermute | solution.py:35
  447.7 15.4 %collective-permute-start.64 = (f32[2,448]{1,0:T(2,128)S(1)}, f32[2,448]{1,0:T(2,128)S(1)}, u32[]{:S(2)}, u32[]{:S(2)}) collective-permute-start(f32[2,448]{1,0:T(2,128)S(1)} %pad_maximum_fusion.15), channel_id=1, source_target_pairs={{0,1},{1,0},{2,3},{3,2},{4,5},{5,4},{6,7},{7,6},{8,9},{9,8},{10,11... | collective-permute-start | bytes 10760 | tf_op jit(solution)/shard_map/ppermute | solution.py:35
  449.1 20.2 %collective-permute-start.55 = (bf16[32,3584]{1,0:T(8,128)(2,1)S(1)}, bf16[32,3584]{1,0:T(8,128)(2,1)S(1)}, u32[]{:S(2)}, u32[]{:S(2)}) collective-permute-start(bf16[32,3584]{1,0:T(8,128)(2,1)S(1)} %get-tuple-element.213), channel_id=1, source_target_pairs={{0,24},{8,0},{16,8},{24,16},{1,25},{9,1},{17,9},{25,17},{2,26},{10... | collective-permute-start | bytes 688136 | tf_op jit(solution)/shard_map/ppermute | solution.py:72
  453.3 20.1 %collective-permute-start.56 = (bf16[32,3584]{1,0:T(8,128)(2,1)S(1)}, bf16[32,3584]{1,0:T(8,128)(2,1)S(1)}, u32[]{:S(2)}, u32[]{:S(2)}) collective-permute-start(bf16[32,3584]{1,0:T(8,128)(2,1)S(1)} %get-tuple-element.212), channel_id=1, source_target_pairs={{0,16},{8,24},{16,0},{24,8},{1,17},{9,25},{17,1},{25,9},{2,18},{10... | collective-permute-start | bytes 688136 | tf_op jit(solution)/shard_map/ppermute | solution.py:72
  463.1 10.3 %collective-permute-start.57 = (bf16[32,3584]{1,0:T(8,128)(2,1)S(1)}, bf16[32,3584]{1,0:T(8,128)(2,1)S(1)}, u32[]{:S(2)}, u32[]{:S(2)}) collective-permute-start(bf16[32,3584]{1,0:T(8,128)(2,1)S(1)} %get-tuple-element.211), channel_id=1, source_target_pairs={{0,8},{8,16},{16,24},{24,0},{1,9},{9,17},{17,25},{25,1},{2,10},{10... | collective-permute-start | bytes 688136 | tf_op jit(solution)/shard_map/ppermute | solution.py:72
  465.9 8.0 %collective-permute-start.58 = (bf16[32,3584]{1,0:T(8,128)(2,1)S(1)}, bf16[32,3584]{1,0:T(8,128)(2,1)S(1)}, u32[]{:S(2)}, u32[]{:S(2)}) collective-permute-start(bf16[32,3584]{1,0:T(8,128)(2,1)S(1)} %get-tuple-element.214.refs_0_), channel_id=1, source_target_pairs={{0,1},{1,0},{2,3},{3,2},{4,5},{5,4},{6,7},{7,6},{8,9},{9,8},{10,11... | collective-permute-start | bytes 688136 | tf_op jit(solution)/shard_map/ppermute | solution.py:35
  468.7 14.1 %collective-permute-start.68 = (bf16[448,1024]{1,0:T(8,128)(2,1)S(1)}, bf16[448,1024]{1,0:T(8,128)(2,1)S(1)}, u32[]{:S(2)}, u32[]{:S(2)}) collective-permute-start(bf16[448,1024]{1,0:T(8,128)(2,1)S(1)} %collective-permute-done.62), channel_id=1, source_target_pairs={{0,4},{1,3},{2,6},{3,1},{4,0},{5,7},{6,2},{7,5},{8,12},{9,11},{10,... | collective-permute-start | bytes 2752520 | tf_op jit(solution)/shard_map/ppermute | solution.py:35
  (96 other events, 1295.7 us)
Sparse Core Ops, SparseCore 0:
  12.1 87.1 all-gather.2
  101.5 125.8 all-gather.4
  257.6 111.1 reduce-scatter.4
  371.5 70.8 reduce-scatter.2

commit v5 on v4

--- a/solution.py
+++ b/solution.py
@@ -286,7 +286,7 @@
     rest_ref[...] = shared.astype(bf16)
 
 
-def mlp_grad(hidden, grad, pair, inner, width, own_lanes, step=256):
+def mlp_grad(hidden, grad, pair, inner, width, own_lanes, step=448):
     d_model, rows = hidden.shape
     return pl.pallas_call(
         functools.partial(mlp_grad_kernel, own_lanes),
@@ -322,8 +322,15 @@
     both = product(hidden_ref[...], weight_ref[:, first:], NN)
     gate_act, upper = both[:, lead : lead + ff], both[:, lead + ff :]
     grad = grad_ref[...]
+    shared = weight_ref[:, first : first + 128]
+    lanes = lax.broadcasted_iota(jnp.int32, shared.shape, 1)
+    shared = jnp.where(lanes < lead, shared, rest_ref[...])
     grad_inner = jnp.concatenate(
-        [product(grad, weight_ref[:, :own], NN), product(grad, rest_ref[...], NN)], axis=1
+        [
+            product(grad, weight_ref[:, :first], NN),
+            product(grad, shared, NN)[:, : ff - first],
+        ],
+        axis=1,
     )
     sigmoid = jax.nn.sigmoid(gate_act)
     silu = gate_act * sigmoid
@@ -710,9 +717,12 @@
 
     second_scale = lax.rsqrt(jnp.mean(resid * resid, axis=-1, keepdims=True) + epsilon)
     hidden_two = plane_gather((resid * second_scale * gains[1]).astype(bf16), sizes)
-    hidden_two_turned, grad_dealt_turned = after((hidden_two.T, grad_dealt.T))
+    rest_tile = jnp.pad(rest_w, ((0, 0), (own_down % 128, 128 - own_down % 128 - rest_width)))
+    hidden_two_turned, grad_dealt_turned, rest_tile = after(
+        (hidden_two.T, grad_dealt.T, rest_tile)
+    )
     inner, grad_pair = feed_forward(
-        after(hidden_two, hidden_two_turned, grad_dealt_turned), grad_dealt, mlp_w, rest_w, ff
+        after(hidden_two, hidden_two_turned, grad_dealt_turned), grad_dealt, mlp_w, rest_tile, ff
     )
     grad_mlp_w, grad_rest_w = mlp_grad(
         hidden_two_turned, grad_dealt_turned, grad_pair, inner, mlp_w.shape[1], own_down % 128
@@ -750,11 +760,11 @@
         scaled - normed * jnp.mean(scaled * normed, axis=-1, keepdims=True)
     )
     grad_own = grad_resid.astype(bf16)
+    grad_own, lift, lift_got = stage(grad_own, lift, lift_got)
+
+    near = near_shares(grad_own, sizes)
     lift, lift_sent = added(lift, lift_got)
-    grad_own, lift, lift_sent = stage(grad_own, lift, lift_sent)
-
-    near = near_shares(grad_own, sizes)
-    grad_own, near = stage(grad_own, near)
+    grad_own, near, lift, lift_sent = stage(grad_own, near, lift, lift_sent)
     grad_branch = plane_gather(grad_own, sizes, near)
     grad_branch, lift_sent = stage(grad_branch, lift_sent)
 
@@ -762,28 +772,36 @@
     grad_attended = product(deal, product(grad_branch, out_w, NN, bf16), NN, bf16)
     grad_proj, grad_conv = attend_backward(own_lengths, qkv, grad_attended, conv)
     lift_got, lift, grad_proj = stage(lift_got, lift, grad_proj)
-    lift, lift_sent = added(lift, lift_got)
-    lift, lift_sent, grad_proj = stage(lift, lift_sent, grad_proj)
-
-    lift_got = flipped(lift_sent, sizes, 0)
+
     grad_proj = product(deal, grad_proj, TN, bf16)
     sent = product(grad_proj[kept:], qkv_w, NT, bf16)
-    lift_got, grad_proj, sent = stage(lift_got, grad_proj, sent)
-    result = (resid + (lift + lift_got.astype(f32))).astype(bf16)
+    lift_got, lift, grad_proj, sent = stage(lift_got, lift, grad_proj, sent)
 
     got = flipped(sent, sizes, 2)
     part = product(grad_proj[:kept], qkv_w, NT)
-    got, part = stage(got, part)
+    lift, lift_sent = added(lift, lift_got)
+    got, part, lift, lift_sent = stage(got, part, lift, lift_sent)
+    lift_got = flipped(lift_sent, sizes, 0)
     part, sent = added(part, got)
     part, sent, grad_proj = stage(part, sent, grad_proj)
 
     got = flipped(sent, sizes, 1)
     grad_attn_w = weight_grad((hidden, grad_proj), (grad_branch, attended))
-    got, part, grad_attn_w = stage(got, part, grad_attn_w)
+    got, part, grad_attn_w, lift_got = stage(got, part, grad_attn_w, lift_got)
+    result = (resid + (lift + lift_got.astype(f32))).astype(bf16)
     grad_attn = lax.psum_scatter(grad_attn_w, "fsdp", scatter_dimension=0, tiled=True)
     part, sent = added(part, got)
 
+    taps = jnp.concatenate(jnp.split(grad_conv, width // 128, axis=1)).astype(bf16)
+    grad_mlp, sent, taps, *rests = stage(grad_mlp, sent, taps, *rests)
     got_last = flipped(sent, sizes, 0)
+    mlp_near = near_shares(grad_mlp, sizes)
+    little = [jnp.concatenate([rest, taps]) for rest in rests]
+    little = sum(
+        [z_shifted(little[k], sizes, k).astype(f32) for k in range(1, n_fsdp)], little[0].astype(f32)
+    ).astype(bf16)
+    mlp_near, got_last, little = stage(mlp_near, got_last, little)
+
     grad_hidden = part + got_last.astype(f32)
     normed = own_x * first_scale
     scaled = grad_hidden * gains[0]
@@ -792,13 +810,6 @@
     )
     grad_x = grad_x.astype(bf16)
 
-    taps = jnp.concatenate(jnp.split(grad_conv, width // 128, axis=1)).astype(bf16)
-    taps, grad_mlp, _, *rests = stage(taps, grad_mlp, got_last, *rests)
-    little = [jnp.concatenate([rest, taps]) for rest in rests]
-    little = sum(
-        [z_shifted(little[k], sizes, k).astype(f32) for k in range(1, n_fsdp)], little[0].astype(f32)
-    ).astype(bf16)
-
     steps = 128 // rest_width if d_own * rest_width % (128 * 16) == 0 else 1
 
     def gain_part(own, grad, each, skipped):
@@ -807,7 +818,7 @@
         terms = own.astype(f32) * grad[:, :columns].astype(f32)
         return jnp.sum(jnp.where(counted[None, :], terms, 0.0), axis=1)
 
-    mlp_shares = ctx_shares(grad_mlp, sizes, t)
+    mlp_shares = ctx_shares(grad_mlp, sizes, t, mlp_near)
     little_shares = ctx_shares(little, sizes, t)
     rest_rows = d_own * rest_width // 128
     rest_shares = [share[:rest_rows] for share in little_shares]

time: 499 us -> 495 us (level)
  waiting for transfers between devices: 200 us -> 194 us
    reduce_scatter x1, waiting for transfers between devices: 12.1 us -> 3.5 us  [per_device(): lax.psum_scatter(grad_attn_w, 'fsdp', scatter_dimension=0, tiled=True)]
    unnamed x197 -> x163, local copies, waits for them, and re-layouts: 24.5 us -> 22.4 us
  transfers between devices with their start and end apart: 76 -> 76, of which waited for: 31 -> 29; matrix products, arithmetic and copies ran while one was open for 22% -> 24% of each run, Pallas kernels for 9% -> 9%
where the time goes in v5:
time: 495 us; the launch traced here: 489 us
  waiting for transfers between devices  194 us (39%)
  starting transfers between devices  79.5 us (16%)
  Pallas kernels  66.2 us (13%)
  local copies, waits for them, and re-layouts  49.5 us (10%)
  matrix products  43.5 us (9%)
  other arithmetic  41.2 us (8%)
  between operations  15.7 us (3%)
    ppermute x56, waiting for transfers between devices, flipped(): return lax.ppermute(value, ('fsdp', 'ctx', 'tp'), pairs)  129 us
    dot_general x14, matrix products, product(): lax.dot_general(left, right, (dims, ((), ())), preferred_element_type=f32)  43.5 us
    ppermute x56, starting transfers between devices, flipped(): return lax.ppermute(value, ('fsdp', 'ctx', 'tp'), pairs)  39.8 us
    ppermute x15, starting transfers between devices, z_shifted(): return lax.ppermute(value, 'fsdp', [(i, (i + steps) % n) for i in range(n)])  31.1 us
    ppermute x15, waiting for transfers between devices, z_shifted(): return lax.ppermute(value, 'fsdp', [(i, (i + steps) % n) for i in range(n)])  29.6 us
    unnamed x163, local copies, waits for them, and re-layouts  22.4 us
    all_gather x1, waiting for transfers between devices, per_device(): mlp_w = lax.all_gather(after(mlp_own, attn_own), 'fsdp', axis=0, tiled=True)  18.8 us
    pallas_call x1, Pallas kernels, attend_backward(): pl.pallas_call(attend_backward_kernel, out_shape=(jax.ShapeDtypeStruct((r...  14.1 us
  transfers between devices with their start and end apart: 76, of which 29 were waited for; matrix products, arithmetic and copies ran while one was open for 24% of the time, Pallas kernels for 9%

profile of v5, /device:TPU:0, one launch (start us, length us, event | category | flops | bytes accessed | tf_op | source)
XLA Modules:
  0.0 489.5 jit_solution(11485704785915939246)
XLA Ops:
  12.9 8.2 %all-to-all-start = ((f32[16,1,1824]{2,1,0:T(1,128)}), f32[16,1,1824]{2,1,0:T(1,128)S(1)}, u32[]{:S(2)}, u32[]{:S(2)}) async-start(f32[16,1,1824]{2,1,0:T(1,128)} %broadcast_in_dim.54), calls=%async_computation | async-start | bytes 245760 | tf_op jit(solution)/shard_map/all_to_all | solution.py:632
  21.5 2.0 dynamic-slice_bitcast_fusion
  23.5 2.4 concatenate.110
  26.9 2.1 all-to-all-done
  32.0 3.9 collective-permute-start.1
  37.5 4.2 collective-permute-done
  41.7 6.7 %collective-permute-done.1 = bf16[32,1792]{1,0:T(8,128)(2,1)S(1)} collective-permute-done((bf16[32,1792]{1,0:T(8,128)(2,1)S(1)}, bf16[32,1792]{1,0:T(8,128)(2,1)S(1)}, u32[]{:S(2)}, u32[]{:S(2)}) %collective-permute-start.1) | collective-permute-done | bytes 114720 | tf_op jit(solution)/shard_map/ppermute | solution.py:72
  52.9 10.4 %collective-permute-done.3 = bf16[128,1792]{1,0:T(8,128)(2,1)S(1)} collective-permute-done((bf16[128,1792]{1,0:T(8,128)(2,1)}, bf16[128,1792]{1,0:T(8,128)(2,1)S(1)}, u32[]{:S(2)}, u32[]{:S(2)}) %collective-permute-start.3) | collective-permute-done | bytes 458784 | tf_op jit(solution)/shard_map/ppermute | solution.py:35
  65.4 6.4 %collective-permute-done.5 = bf16[128,1792]{1,0:T(8,128)(2,1)S(1)} collective-permute-done((bf16[128,1792]{1,0:T(8,128)(2,1)S(1)}, bf16[128,1792]{1,0:T(8,128)(2,1)S(1)}, u32[]{:S(2)}, u32[]{:S(2)}) %collective-permute-start.5) | collective-permute-done | bytes 458784 | tf_op jit(solution)/shard_map/ppermute | solution.py:35
  75.8 10.1 %collective-permute-start.30 = (bf16[112,128]{1,0:T(8,128)(2,1)S(1)}, bf16[112,128]{1,0:T(8,128)(2,1)}, u32[]{:S(2)}, u32[]{:S(2)}) collective-permute-start(bf16[112,128]{1,0:T(8,128)(2,1)S(1)} %pad_maximum_fusion.8), channel_id=1, source_target_pairs={{0,8},{8,16},{16,24},{24,0},{1,9},{9,17},{17,25},{25,1},{2,10},{10... | collective-permute-start | bytes 86024 | tf_op jit(solution)/shard_map/ppermute | solution.py:72
  85.9 2.6 collective-permute-start.32
  88.8 10.5 %all-gather.3.cloned.1.call-done = bf16[1792,1024]{1,0:T(8,128)(2,1)} async-done(((bf16[448,1024]{1,0:T(8,128)(2,1)}), bf16[1792,1024]{1,0:T(8,128)(2,1)}) %all-gather.3.cloned.1.call-update) | async-done | bytes 3670032 | tf_op jit(solution)/shard_map/all_gather | solution.py:619
  99.3 7.5 %fusion.25.qkv_ref = bf16[1024,768]{1,0:T(8,128)(2,1)S(1)} fusion(s32[1024]{0:T(1024)S(1)} %fusion.78, bf16[1024,1792]{1,0:T(8,128)(2,1)} %constant_dynamic-update-slice_fusion.refs_0_, bf16[1792,1024]{1,0:T(8,128)(2,1)} %all-gather.3.cloned.1.call-done), kind=kOutput, calls=%fused_computation.40 | convolution fusion | flops 4431806464 | bytes 7999488 | tf_op jit(solution)/shard_map/dot_general | solution.py:95
  106.9 5.8 %attend_forward.1 = bf16[1024,256]{1,0:T(8,128)(2,1)S(1)} custom-call(s32[2,3]{1,0:T(2,128)S(1)} %bitcast.98, bf16[1024,768]{1,0:T(8,128)(2,1)S(1)} %fusion.25.qkv_ref, f32[3,256]{1,0:T(4,128)S(1)} %constant_dynamic-slice_fusion.20.conv_ref), custom_call_target="tpu_custom_call" | custom-call | bytes 20000000 | tf_op jit(solution)/shard_map/attend_forward/pallas_call | solution.py:541
  117.9 2.8 collective-permute-start.12
  122.1 3.2 collective-permute-done.10
  125.3 8.6 %collective-permute-done.11 = bf16[32,1792]{1,0:T(8,128)(2,1)S(1)} collective-permute-done((bf16[32,1792]{1,0:T(8,128)(2,1)S(1)}, bf16[32,1792]{1,0:T(8,128)(2,1)S(1)}, u32[]{:S(2)}, u32[]{:S(2)}) %collective-permute-start.11) | collective-permute-done | bytes 114720 | tf_op jit(solution)/shard_map/ppermute | solution.py:72
  138.5 8.9 %collective-permute-done.23 = bf16[128,1792]{1,0:T(8,128)(2,1)S(1)} collective-permute-done((bf16[128,1792]{1,0:T(8,128)(2,1)S(1)}, bf16[128,1792]{1,0:T(8,128)(2,1)S(1)}, u32[]{:S(2)}, u32[]{:S(2)}) %collective-permute-start.23) | collective-permute-done | bytes 458784 | tf_op jit(solution)/shard_map/ppermute | solution.py:35
  149.5 11.1 %collective-permute-done.25 = bf16[128,1792]{1,0:T(8,128)(2,1)S(1)} collective-permute-done((bf16[128,1792]{1,0:T(8,128)(2,1)S(1)}, bf16[128,1792]{1,0:T(8,128)(2,1)S(1)}, u32[]{:S(2)}, u32[]{:S(2)}) %collective-permute-start.25) | collective-permute-done | bytes 458784 | tf_op jit(solution)/shard_map/ppermute | solution.py:35
  164.0 6.9 %collective-permute-done.15 = bf16[128,1792]{1,0:T(8,128)(2,1)S(1)} collective-permute-done((bf16[128,1792]{1,0:T(8,128)(2,1)S(1)}, bf16[128,1792]{1,0:T(8,128)(2,1)S(1)}, u32[]{:S(2)}, u32[]{:S(2)}) %collective-permute-start.15) | collective-permute-done | bytes 458784 | tf_op jit(solution)/shard_map/ppermute | solution.py:35
  174.4 9.8 %collective-permute-done.16 = bf16[128,1792]{1,0:T(8,128)(2,1)S(1)} collective-permute-done((bf16[128,1792]{1,0:T(8,128)(2,1)S(1)}, bf16[128,1792]{1,0:T(8,128)(2,1)S(1)}, u32[]{:S(2)}, u32[]{:S(2)}) %collective-permute-start.16) | collective-permute-done | bytes 458784 | tf_op jit(solution)/shard_map/ppermute | solution.py:35
  184.2 1.8 collective-permute-start.18
  188.2 4.6 collective-permute-done.18
  196.7 5.9 %copy.55.hidden_ref = bf16[1792,1024]{1,0:T(8,128)(2,1)} copy(bf16[1792,1024]{0,1:T(8,128)(2,1)} %bitcast.20) | data formatting | bytes 7340032 | tf_op jit(solution)/shard_map/optimization_barrier | solution.py:58
  202.7 6.0 %copy.56.grad_ref = bf16[1792,1024]{1,0:T(8,128)(2,1)} copy(bf16[1792,1024]{0,1:T(8,128)(2,1)} %bitcast.100) | data formatting | bytes 7340032 | tf_op jit(solution)/shard_map/optimization_barrier | solution.py:58
  208.6 18.8 %all-gather.5.cloned.1.call-done.weight_ref = bf16[1792,1792]{1,0:T(8,128)(2,1)} async-done(((bf16[448,1792]{1,0:T(8,128)(2,1)}), bf16[1792,1792]{1,0:T(8,128)(2,1)}) %all-gather.5.cloned.1.call-update) | async-done | bytes 6422544 | tf_op jit(solution)/shard_map/all_gather | solution.py:620
  227.5 12.5 %feed_forward.1 = (bf16[1024,640]{1,0:T(8,128)(2,1)S(1)}, bf16[1024,1280]{1,0:T(8,128)(2,1)S(1)}) custom-call(bf16[1024,1792]{1,0:T(8,128)(2,1)} %constant_dynamic-update-slice_fusion.8.hidden_ref, bf16[1024,1792]{1,0:T(8,128)(2,1)} %copy-done.23, bf16[1792,1792]{1,0:T(8,128)(2,1)} %all-gather.5.cloned.1.call-done.weight_ref, bf16[1792,128]{1,0:T(8,128)(2,1)S(1)} %pad.4.rest_ref), custom_call_target="tpu_custom_call" | custom-call | flops 6694109184 | bytes 17612800 | tf_op jit(solution)/shard_map/feed_forward/pallas_call | solution.py:357
  240.0 9.6 %mlp_grad.1 = (bf16[1792,1792]{1,0:T(8,128)(2,1)}, bf16[1792,128]{1,0:T(8,128)(2,1)S(1)}) custom-call(bf16[1792,1024]{1,0:T(8,128)(2,1)S(1)} %copy-done.5, bf16[1792,1024]{1,0:T(8,128)(2,1)S(1)} %copy-done.6, bf16[1024,1280]{1,0:T(8,128)(2,1)S(1)} %get-tuple-element.119.pair_ref, bf16[1024,640]{1,0:T(8,128)(2,1)S(1)} %get-tuple-element.125.inner_ref), custom_call_target="tpu_custom_call" | custom-call | flops 6576668672 | bytes 17432576 | tf_op jit(solution)/shard_map/mlp_grad/pallas_call | solution.py:291
  249.6 6.5 %fusion.8 = bf16[512,1792]{1,0:T(8,128)(2,1)} fusion(bf16[1792,1792]{1,0:T(8,128)(2,1)} %all-gather.5.cloned.1.call-done.weight_ref, bf16[1024,1280]{1,0:T(8,128)(2,1)} %copy-done.12), kind=kOutput, calls=%fused_computation.13 | convolution fusion | flops 2349727744 | bytes 7733248 | tf_op jit(solution)/shard_map/dot_general | solution.py:95
  256.4 5.3 %fusion.4 = f32[512,1792]{1,0:T(8,128)S(1)} fusion(bf16[1792,1792]{1,0:T(8,128)(2,1)} %all-gather.5.cloned.1.call-done.weight_ref, bf16[1024,1280]{1,0:T(8,128)(2,1)} %copy-done.12), kind=kOutput, calls=%fused_computation.6 | convolution fusion | flops 2348810240 | bytes 9568256 | tf_op jit(solution)/shard_map/dot_general | solution.py:95
  261.7 2.0 add_convert_fusion.2
  265.4 4.7 fusion.11
  271.2 3.0 copy-done.16
  274.5 2.7 collective-permute-done.34
  277.4 1.7 collective-permute-start.35
  279.1 6.9 %collective-permute-done.35 = bf16[128,1792]{1,0:T(8,128)(2,1)S(1)} collective-permute-done((bf16[128,1792]{1,0:T(8,128)(2,1)S(1)}, bf16[128,1792]{1,0:T(8,128)(2,1)S(1)}, u32[]{:S(2)}, u32[]{:S(2)}) %collective-permute-start.35) | collective-permute-done | bytes 458784 | tf_op jit(solution)/shard_map/ppermute | solution.py:35
  290.7 1.9 add_convert_fusion.1
  292.5 8.5 %collective-permute-done.37 = bf16[128,1792]{1,0:T(8,128)(2,1)S(1)} collective-permute-done((bf16[128,1792]{1,0:T(8,128)(2,1)S(1)}, bf16[128,1792]{1,0:T(8,128)(2,1)S(1)}, u32[]{:S(2)}, u32[]{:S(2)}) %collective-permute-start.37) | collective-permute-done | bytes 458784 | tf_op jit(solution)/shard_map/ppermute | solution.py:35
  305.2 4.3 collective-permute-done.39
  314.0 4.9 %fusion.31.grad_ref = bf16[1024,256]{1,0:T(8,128)(2,1)S(1)} fusion(s32[1024]{0:T(1024)S(1)} %copy-done.62, bf16[1024,1792]{1,0:T(8,128)(2,1)} %constant_dynamic-update-slice_fusion.24.refs_2_, bf16[1792,1024]{1,0:T(8,128)(2,1)} %all-gather.3.cloned.1.call-done), kind=kOutput, calls=%fused_computation.52 | convolution fusion | flops 1477967872 | bytes 5115904 | tf_op jit(solution)/shard_map/dot_general | solution.py:95
  318.9 14.1 %attend_backward.1 = (bf16[1024,768]{1,0:T(8,128)(2,1)S(1)}, f32[3,256]{1,0:T(4,128)S(1)}) custom-call(s32[2,3]{1,0:T(2,128)S(1)} %bitcast.99, bf16[1024,768]{1,0:T(8,128)(2,1)S(1)} %fusion.25.qkv_ref, bf16[1024,256]{1,0:T(8,128)(2,1)S(1)} %fusion.31.grad_ref, f32[3,256]{1,0:T(4,128)S(1)} %constant_dynamic-slice_fusion.20.conv_ref), custom_call_target="tpu_custom_call" | custom-call | bytes 50000000 | tf_op jit(solution)/shard_map/attend_backward/pallas_call | solution.py:556
  333.0 2.4 fusion.26.refs_1_
  335.4 2.9 convolution_convert_fusion.1
  339.7 3.5 fusion.13
  343.2 2.4 add_convert_fusion.5
  345.7 3.7 add_convert_fusion
  354.7 7.3 %weight_grad.1 = bf16[1792,1024]{1,0:T(8,128)(2,1)S(1)} custom-call(bf16[1024,1792]{1,0:T(8,128)(2,1)S(1)} %copy-done.8, bf16[1024,768]{1,0:T(8,128)(2,1)S(1)} %fusion.26.refs_1_, bf16[1024,1792]{1,0:T(8,128)(2,1)} %constant_dynamic-update-slice_fusion.24.refs_2_, bf16[1024,256]{1,0:T(8,128)(2,1)S(1)} %fusion.30.refs_3_), custom_call_target="tpu_custom_call" | custom-call | flops 3758096384 | bytes 13107200 | tf_op jit(solution)/shard_map/weight_grad/pallas_call | solution.py:261
  362.0 1.8 copy-done.4
  363.8 2.1 collective-permute-done.47
  365.9 2.1 collective-permute-done.46
  368.6 2.1 add_convert_fusion.3
  376.7 2.8 collective-permute-start.53
  380.7 2.9 select_reduce_fusion
  384.3 28.3 %collective-permute-done.50 = bf16[128,1792]{1,0:T(8,128)(2,1)S(1)} collective-permute-done((bf16[128,1792]{1,0:T(8,128)(2,1)}, bf16[128,1792]{1,0:T(8,128)(2,1)S(1)}, u32[]{:S(2)}, u32[]{:S(2)}) %collective-permute-start.50) | collective-permute-done | bytes 458784 | tf_op jit(solution)/shard_map/ppermute | solution.py:35
  420.0 2.2 broadcast_select_fusion
  423.0 13.0 %collective-permute-done.56 = bf16[118,128]{1,0:T(8,128)(2,1)S(1)} collective-permute-done((bf16[118,128]{1,0:T(8,128)(2,1)S(1)}, bf16[118,128]{1,0:T(8,128)(2,1)S(1)}, u32[]{:S(2)}, u32[]{:S(2)}) %collective-permute-start.56) | collective-permute-done | bytes 30240 | tf_op jit(solution)/shard_map/ppermute | solution.py:35
  436.7 3.5 reduce-scatter.3.cloned.1.call-done.refs_0_
  446.6 2.8 collective-permute-start.57
  449.7 9.8 %mlp_placed.1 = (f32[2,448,2432]{2,1,0:T(8,128)}, f32[1,448,2432]{2,1,0:T(8,128)}) custom-call(s32[1]{0:T(128)} %bitcast.35.index_ref, bf16[448,1792]{1,0:T(8,128)(2,1)S(1)} %copy-done.3, bf16[448,1792]{1,0:T(8,128)(2,1)S(1)} %get-tuple-element.219.refs_1_, bf16[448,1792]{1,0:T(8,128)(2,1)S(1)} %get-tuple-element.218.refs_2_, ...), custom_call_target="tpu_custom_call" | custom-call | bytes 21790720 | tf_op jit(solution)/shard_map/mlp_placed/pallas_call | solution.py:410
  460.8 2.7 collective-permute-done.64
  465.0 5.5 %collective-permute-done.58.refs_2_ = bf16[32,3584]{1,0:T(8,128)(2,1)S(1)} collective-permute-done((bf16[32,3584]{1,0:T(8,128)(2,1)S(1)}, bf16[32,3584]{1,0:T(8,128)(2,1)S(1)}, u32[]{:S(2)}, u32[]{:S(2)}) %collective-permute-start.58) | collective-permute-done | bytes 229408 | tf_op jit(solution)/shard_map/ppermute | solution.py:72
  472.4 1.8 at_home.1
  475.6 3.2 placed.1
  480.3 2.2 last_placed.1
  (411 shorter events, 103.3 us)
Async XLA Ops:
  7.2 92.1 %all-gather.3.cloned.1.call-start = ((), (), s32[]{:S(2)}) async-start(), calls=%async_computation.3 | async-start | bytes 4587520 | tf_op jit(solution)/shard_map/all_gather | solution.py:619
  12.9 16.0 %all-to-all-start = ((f32[16,1,1824]{2,1,0:T(1,128)}), f32[16,1,1824]{2,1,0:T(1,128)S(1)}, u32[]{:S(2)}, u32[]{:S(2)}) async-start(f32[16,1,1824]{2,1,0:T(1,128)} %broadcast_in_dim.54), calls=%async_computation | async-start | bytes 245760 | tf_op jit(solution)/shard_map/all_to_all | solution.py:632
  21.2 206.3 %all-gather.5.cloned.1.call-start = ((), (), s32[]{:S(2)}) async-start(), calls=%async_computation.4 | async-start | bytes 8028160 | tf_op jit(solution)/shard_map/all_gather | solution.py:620
  25.9 344.9 %reduce-scatter.5.cloned.1.call-start = ((), (), s32[]{:S(2)}) async-start(), calls=%async_computation.6 | async-start | bytes 8028160 | tf_op jit(solution)/shard_map/reduce_scatter | solution.py:731
  31.2 10.5 %collective-permute-start = (bf16[32,1792]{1,0:T(8,128)(2,1)S(1)}, bf16[32,1792]{1,0:T(8,128)(2,1)S(1)}, u32[]{:S(2)}, u32[]{:S(2)}) collective-permute-start(bf16[32,1792]{1,0:T(8,128)(2,1)S(1)} %get-tuple-element.260), channel_id=1, source_target_pairs={{0,8},{8,16},{16,24},{24,0},{1,9},{9,17},{17,25},{25,1},{2,10},{10... | collective-permute-start | bytes 344072 | tf_op jit(solution)/shard_map/ppermute | solution.py:72
  32.0 16.5 %collective-permute-start.1 = (bf16[32,1792]{1,0:T(8,128)(2,1)S(1)}, bf16[32,1792]{1,0:T(8,128)(2,1)S(1)}, u32[]{:S(2)}, u32[]{:S(2)}) collective-permute-start(bf16[32,1792]{1,0:T(8,128)(2,1)S(1)} %get-tuple-element.259), channel_id=1, source_target_pairs={{0,16},{8,24},{16,0},{24,8},{1,17},{9,25},{17,1},{25,9},{2,18},{10... | collective-permute-start | bytes 344072 | tf_op jit(solution)/shard_map/ppermute | solution.py:72
  35.9 12.5 %collective-permute-start.2 = (bf16[32,1792]{1,0:T(8,128)(2,1)S(1)}, bf16[32,1792]{1,0:T(8,128)(2,1)S(1)}, u32[]{:S(2)}, u32[]{:S(2)}) collective-permute-start(bf16[32,1792]{1,0:T(8,128)(2,1)S(1)} %get-tuple-element.258), channel_id=1, source_target_pairs={{0,24},{8,0},{16,8},{24,16},{1,25},{9,1},{17,9},{25,17},{2,26},{10... | collective-permute-start | bytes 344072 | tf_op jit(solution)/shard_map/ppermute | solution.py:72
  49.7 13.6 %collective-permute-start.3 = (bf16[128,1792]{1,0:T(8,128)(2,1)}, bf16[128,1792]{1,0:T(8,128)(2,1)S(1)}, u32[]{:S(2)}, u32[]{:S(2)}) collective-permute-start(bf16[128,1792]{1,0:T(8,128)(2,1)} %get-tuple-element.207), channel_id=1, source_target_pairs={{0,2},{1,5},{2,0},{3,7},{4,6},{5,1},{6,4},{7,3},{8,10},{9,13},{10,... | collective-permute-start | bytes 1376264 | tf_op jit(solution)/shard_map/ppermute | solution.py:35
  50.5 12.8 %collective-permute-start.4 = (bf16[128,1792]{1,0:T(8,128)(2,1)}, bf16[128,1792]{1,0:T(8,128)(2,1)S(1)}, u32[]{:S(2)}, u32[]{:S(2)}) collective-permute-start(bf16[128,1792]{1,0:T(8,128)(2,1)} %get-tuple-element.207), channel_id=1, source_target_pairs={{0,4},{1,3},{2,6},{3,1},{4,0},{5,7},{6,2},{7,5},{8,12},{9,11},{10,... | collective-permute-start | bytes 1376264 | tf_op jit(solution)/shard_map/ppermute | solution.py:35
  52.8 19.8 %collective-permute-start.6 = (bf16[128,1792]{1,0:T(8,128)(2,1)}, bf16[128,1792]{1,0:T(8,128)(2,1)S(1)}, u32[]{:S(2)}, u32[]{:S(2)}) collective-permute-start(bf16[128,1792]{1,0:T(8,128)(2,1)} %get-tuple-element.207), channel_id=1, source_target_pairs={{0,1},{1,0},{2,3},{3,2},{4,5},{5,4},{6,7},{7,6},{8,9},{9,8},{10,11... | collective-permute-start | bytes 1376264 | tf_op jit(solution)/shard_map/ppermute | solution.py:35
  63.3 8.5 %collective-permute-start.5 = (bf16[128,1792]{1,0:T(8,128)(2,1)S(1)}, bf16[128,1792]{1,0:T(8,128)(2,1)S(1)}, u32[]{:S(2)}, u32[]{:S(2)}) collective-permute-start(bf16[128,1792]{1,0:T(8,128)(2,1)S(1)} %collective-permute-done.3), channel_id=1, source_target_pairs={{0,4},{1,3},{2,6},{3,1},{4,0},{5,7},{6,2},{7,5},{8,12},{9,11},{10,... | collective-permute-start | bytes 1376264 | tf_op jit(solution)/shard_map/ppermute | solution.py:35
  63.3 10.1 %collective-permute-start.7 = (bf16[128,1792]{1,0:T(8,128)(2,1)S(1)}, bf16[128,1792]{1,0:T(8,128)(2,1)S(1)}, u32[]{:S(2)}, u32[]{:S(2)}) collective-permute-start(bf16[128,1792]{1,0:T(8,128)(2,1)S(1)} %collective-permute-done.3), channel_id=1, source_target_pairs={{0,1},{1,0},{2,3},{3,2},{4,5},{5,4},{6,7},{7,6},{8,9},{9,8},{10,11... | collective-permute-start | bytes 1376264 | tf_op jit(solution)/shard_map/ppermute | solution.py:35
  63.3 10.9 %collective-permute-start.8 = (bf16[128,1792]{1,0:T(8,128)(2,1)S(1)}, bf16[128,1792]{1,0:T(8,128)(2,1)S(1)}, u32[]{:S(2)}, u32[]{:S(2)}) collective-permute-start(bf16[128,1792]{1,0:T(8,128)(2,1)S(1)} %collective-permute-done.4), channel_id=1, source_target_pairs={{0,1},{1,0},{2,3},{3,2},{4,5},{5,4},{6,7},{7,6},{8,9},{9,8},{10,11... | collective-permute-start | bytes 1376264 | tf_op jit(solution)/shard_map/ppermute | solution.py:35
  75.8 39.5 %collective-permute-start.30 = (bf16[112,128]{1,0:T(8,128)(2,1)S(1)}, bf16[112,128]{1,0:T(8,128)(2,1)}, u32[]{:S(2)}, u32[]{:S(2)}) collective-permute-start(bf16[112,128]{1,0:T(8,128)(2,1)S(1)} %pad_maximum_fusion.8), channel_id=1, source_target_pairs={{0,8},{8,16},{16,24},{24,0},{1,9},{9,17},{17,25},{25,1},{2,10},{10... | collective-permute-start | bytes 86024 | tf_op jit(solution)/shard_map/ppermute | solution.py:72
  85.9 31.9 %collective-permute-start.31 = (bf16[112,128]{1,0:T(8,128)(2,1)S(1)}, bf16[112,128]{1,0:T(8,128)(2,1)}, u32[]{:S(2)}, u32[]{:S(2)}) collective-permute-start(bf16[112,128]{1,0:T(8,128)(2,1)S(1)} %pad_maximum_fusion.8), channel_id=1, source_target_pairs={{0,16},{8,24},{16,0},{24,8},{1,17},{9,25},{17,1},{25,9},{2,18},{10... | collective-permute-start | bytes 86024 | tf_op jit(solution)/shard_map/ppermute | solution.py:72
  85.9 35.8 %collective-permute-start.32 = (bf16[112,128]{1,0:T(8,128)(2,1)S(1)}, bf16[112,128]{1,0:T(8,128)(2,1)S(1)}, u32[]{:S(2)}, u32[]{:S(2)}) collective-permute-start(bf16[112,128]{1,0:T(8,128)(2,1)S(1)} %pad_maximum_fusion.8), channel_id=1, source_target_pairs={{0,24},{8,0},{16,8},{24,16},{1,25},{9,1},{17,9},{25,17},{2,26},{10... | collective-permute-start | bytes 86024 | tf_op jit(solution)/shard_map/ppermute | solution.py:72
  114.9 22.2 %collective-permute-start.13 = (bf16[512,1792]{1,0:T(8,128)(2,1)S(1)}, bf16[512,1792]{1,0:T(8,128)(2,1)S(1)}, u32[]{:S(2)}, u32[]{:S(2)}) collective-permute-start(bf16[512,1792]{1,0:T(8,128)(2,1)S(1)} %convolution_convert_fusion), channel_id=1, source_target_pairs={{0,1},{1,0},{2,3},{3,2},{4,5},{5,4},{6,7},{7,6},{8,9},{9,8},{10,11... | collective-permute-start | bytes 5505032 | tf_op jit(solution)/shard_map/ppermute | solution.py:35
  115.0 10.3 %collective-permute-start.10 = (bf16[32,1792]{1,0:T(8,128)(2,1)S(1)}, bf16[32,1792]{1,0:T(8,128)(2,1)S(1)}, u32[]{:S(2)}, u32[]{:S(2)}) collective-permute-start(bf16[32,1792]{1,0:T(8,128)(2,1)S(1)} %get-tuple-element.256), channel_id=1, source_target_pairs={{0,8},{8,16},{16,24},{24,0},{1,9},{9,17},{17,25},{25,1},{2,10},{10... | collective-permute-start | bytes 344072 | tf_op jit(solution)/shard_map/ppermute | solution.py:72
  115.3 18.6 %collective-permute-start.11 = (bf16[32,1792]{1,0:T(8,128)(2,1)S(1)}, bf16[32,1792]{1,0:T(8,128)(2,1)S(1)}, u32[]{:S(2)}, u32[]{:S(2)}) collective-permute-start(bf16[32,1792]{1,0:T(8,128)(2,1)S(1)} %get-tuple-element.255), channel_id=1, source_target_pairs={{0,16},{8,24},{16,0},{24,8},{1,17},{9,25},{17,1},{25,9},{2,18},{10... | collective-permute-start | bytes 344072 | tf_op jit(solution)/shard_map/ppermute | solution.py:72
  117.9 16.0 %collective-permute-start.12 = (bf16[32,1792]{1,0:T(8,128)(2,1)S(1)}, bf16[32,1792]{1,0:T(8,128)(2,1)S(1)}, u32[]{:S(2)}, u32[]{:S(2)}) collective-permute-start(bf16[32,1792]{1,0:T(8,128)(2,1)S(1)} %get-tuple-element.254), channel_id=1, source_target_pairs={{0,24},{8,0},{16,8},{24,16},{1,25},{9,1},{17,9},{25,17},{2,26},{10... | collective-permute-start | bytes 344072 | tf_op jit(solution)/shard_map/ppermute | solution.py:72
  133.9 13.5 %collective-permute-start.23 = (bf16[128,1792]{1,0:T(8,128)(2,1)S(1)}, bf16[128,1792]{1,0:T(8,128)(2,1)S(1)}, u32[]{:S(2)}, u32[]{:S(2)}) collective-permute-start(bf16[128,1792]{1,0:T(8,128)(2,1)S(1)} %pad_maximum_fusion.3), channel_id=1, source_target_pairs={{0,2},{1,5},{2,0},{3,7},{4,6},{5,1},{6,4},{7,3},{8,10},{9,13},{10,... | collective-permute-start | bytes 1376264 | tf_op jit(solution)/shard_map/ppermute | solution.py:35
  135.5 13.4 %collective-permute-start.24 = (bf16[128,1792]{1,0:T(8,128)(2,1)S(1)}, bf16[128,1792]{1,0:T(8,128)(2,1)S(1)}, u32[]{:S(2)}, u32[]{:S(2)}) collective-permute-start(bf16[128,1792]{1,0:T(8,128)(2,1)S(1)} %pad_maximum_fusion.3), channel_id=1, source_target_pairs={{0,4},{1,3},{2,6},{3,1},{4,0},{5,7},{6,2},{7,5},{8,12},{9,11},{10,... | collective-permute-start | bytes 1376264 | tf_op jit(solution)/shard_map/ppermute | solution.py:35
  137.0 27.0 %collective-permute-start.26 = (bf16[128,1792]{1,0:T(8,128)(2,1)S(1)}, bf16[128,1792]{1,0:T(8,128)(2,1)S(1)}, u32[]{:S(2)}, u32[]{:S(2)}) collective-permute-start(bf16[128,1792]{1,0:T(8,128)(2,1)S(1)} %pad_maximum_fusion.3), channel_id=1, source_target_pairs={{0,1},{1,0},{2,3},{3,2},{4,5},{5,4},{6,7},{7,6},{8,9},{9,8},{10,11... | collective-permute-start | bytes 1376264 | tf_op jit(solution)/shard_map/ppermute | solution.py:35
  137.9 24.3 %collective-permute-start.14 = (bf16[256,1792]{1,0:T(8,128)(2,1)S(1)}, bf16[256,1792]{1,0:T(8,128)(2,1)S(1)}, u32[]{:S(2)}, u32[]{:S(2)}) collective-permute-start(bf16[256,1792]{1,0:T(8,128)(2,1)S(1)} %slice.401), channel_id=1, source_target_pairs={{0,4},{1,3},{2,6},{3,1},{4,0},{5,7},{6,2},{7,5},{8,12},{9,11},{10,... | collective-permute-start | bytes 2752520 | tf_op jit(solution)/shard_map/ppermute | solution.py:35
  147.4 13.2 %collective-permute-start.25 = (bf16[128,1792]{1,0:T(8,128)(2,1)S(1)}, bf16[128,1792]{1,0:T(8,128)(2,1)S(1)}, u32[]{:S(2)}, u32[]{:S(2)}) collective-permute-start(bf16[128,1792]{1,0:T(8,128)(2,1)S(1)} %collective-permute-done.23), channel_id=1, source_target_pairs={{0,4},{1,3},{2,6},{3,1},{4,0},{5,7},{6,2},{7,5},{8,12},{9,11},{10,... | collective-permute-start | bytes 1376264 | tf_op jit(solution)/shard_map/ppermute | solution.py:35
  148.9 15.1 %collective-permute-start.27 = (bf16[128,1792]{1,0:T(8,128)(2,1)S(1)}, bf16[128,1792]{1,0:T(8,128)(2,1)S(1)}, u32[]{:S(2)}, u32[]{:S(2)}) collective-permute-start(bf16[128,1792]{1,0:T(8,128)(2,1)S(1)} %collective-permute-done.23), channel_id=1, source_target_pairs={{0,1},{1,0},{2,3},{3,2},{4,5},{5,4},{6,7},{7,6},{8,9},{9,8},{10,11... | collective-permute-start | bytes 1376264 | tf_op jit(solution)/shard_map/ppermute | solution.py:35
  148.9 25.3 %collective-permute-start.28 = (bf16[128,1792]{1,0:T(8,128)(2,1)S(1)}, bf16[128,1792]{1,0:T(8,128)(2,1)S(1)}, u32[]{:S(2)}, u32[]{:S(2)}) collective-permute-start(bf16[128,1792]{1,0:T(8,128)(2,1)S(1)} %collective-permute-done.24), channel_id=1, source_target_pairs={{0,1},{1,0},{2,3},{3,2},{4,5},{5,4},{6,7},{7,6},{8,9},{9,8},{10,11... | collective-permute-start | bytes 1376264 | tf_op jit(solution)/shard_map/ppermute | solution.py:35
  160.6 13.7 %collective-permute-start.29 = (bf16[128,1792]{1,0:T(8,128)(2,1)S(1)}, bf16[128,1792]{1,0:T(8,128)(2,1)S(1)}, u32[]{:S(2)}, u32[]{:S(2)}) collective-permute-start(bf16[128,1792]{1,0:T(8,128)(2,1)S(1)} %collective-permute-done.25), channel_id=1, source_target_pairs={{0,1},{1,0},{2,3},{3,2},{4,5},{5,4},{6,7},{7,6},{8,9},{9,8},{10,11... | collective-permute-start | bytes 1376264 | tf_op jit(solution)/shard_map/ppermute | solution.py:35
  162.4 8.5 %collective-permute-start.15 = (bf16[128,1792]{1,0:T(8,128)(2,1)S(1)}, bf16[128,1792]{1,0:T(8,128)(2,1)S(1)}, u32[]{:S(2)}, u32[]{:S(2)}) collective-permute-start(bf16[128,1792]{1,0:T(8,128)(2,1)S(1)} %slice.402), channel_id=1, source_target_pairs={{0,2},{1,5},{2,0},{3,7},{4,6},{5,1},{6,4},{7,3},{8,10},{9,13},{10,... | collective-permute-start | bytes 1376264 | tf_op jit(solution)/shard_map/ppermute | solution.py:35
  172.3 12.0 %collective-permute-start.16 = (bf16[128,1792]{1,0:T(8,128)(2,1)S(1)}, bf16[128,1792]{1,0:T(8,128)(2,1)S(1)}, u32[]{:S(2)}, u32[]{:S(2)}) collective-permute-start(bf16[128,1792]{1,0:T(8,128)(2,1)S(1)} %get-tuple-element.203), channel_id=1, source_target_pairs={{0,2},{1,5},{2,0},{3,7},{4,6},{5,1},{6,4},{7,3},{8,10},{9,13},{10,... | collective-permute-start | bytes 1376264 | tf_op jit(solution)/shard_map/ppermute | solution.py:35
  173.8 12.3 %collective-permute-start.17 = (bf16[128,1792]{1,0:T(8,128)(2,1)S(1)}, bf16[128,1792]{1,0:T(8,128)(2,1)S(1)}, u32[]{:S(2)}, u32[]{:S(2)}) collective-permute-start(bf16[128,1792]{1,0:T(8,128)(2,1)S(1)} %get-tuple-element.203), channel_id=1, source_target_pairs={{0,4},{1,3},{2,6},{3,1},{4,0},{5,7},{6,2},{7,5},{8,12},{9,11},{10,... | collective-permute-start | bytes 1376264 | tf_op jit(solution)/shard_map/ppermute | solution.py:35
  174.3 19.2 %collective-permute-start.19 = (bf16[128,1792]{1,0:T(8,128)(2,1)S(1)}, bf16[128,1792]{1,0:T(8,128)(2,1)S(1)}, u32[]{:S(2)}, u32[]{:S(2)}) collective-permute-start(bf16[128,1792]{1,0:T(8,128)(2,1)S(1)} %get-tuple-element.203), channel_id=1, source_target_pairs={{0,1},{1,0},{2,3},{3,2},{4,5},{5,4},{6,7},{7,6},{8,9},{9,8},{10,11... | collective-permute-start | bytes 1376264 | tf_op jit(solution)/shard_map/ppermute | solution.py:35
  184.2 8.5 %collective-permute-start.18 = (bf16[128,1792]{1,0:T(8,128)(2,1)S(1)}, bf16[128,1792]{1,0:T(8,128)(2,1)S(1)}, u32[]{:S(2)}, u32[]{:S(2)}) collective-permute-start(bf16[128,1792]{1,0:T(8,128)(2,1)S(1)} %collective-permute-done.16), channel_id=1, source_target_pairs={{0,4},{1,3},{2,6},{3,1},{4,0},{5,7},{6,2},{7,5},{8,12},{9,11},{10,... | collective-permute-start | bytes 1376264 | tf_op jit(solution)/shard_map/ppermute | solution.py:35
  186.1 8.3 %collective-permute-start.20 = (bf16[128,1792]{1,0:T(8,128)(2,1)S(1)}, bf16[128,1792]{1,0:T(8,128)(2,1)S(1)}, u32[]{:S(2)}, u32[]{:S(2)}) collective-permute-start(bf16[128,1792]{1,0:T(8,128)(2,1)S(1)} %collective-permute-done.16), channel_id=1, source_target_pairs={{0,1},{1,0},{2,3},{3,2},{4,5},{5,4},{6,7},{7,6},{8,9},{9,8},{10,11... | collective-permute-start | bytes 1376264 | tf_op jit(solution)/shard_map/ppermute | solution.py:35
  186.1 9.1 %collective-permute-start.21 = (bf16[128,1792]{1,0:T(8,128)(2,1)S(1)}, bf16[128,1792]{1,0:T(8,128)(2,1)S(1)}, u32[]{:S(2)}, u32[]{:S(2)}) collective-permute-start(bf16[128,1792]{1,0:T(8,128)(2,1)S(1)} %collective-permute-done.17), channel_id=1, source_target_pairs={{0,1},{1,0},{2,3},{3,2},{4,5},{5,4},{6,7},{7,6},{8,9},{9,8},{10,11... | collective-permute-start | bytes 1376264 | tf_op jit(solution)/shard_map/ppermute | solution.py:35
  256.1 184.1 %reduce-scatter.3.cloned.1.call-start = ((), (), s32[]{:S(2)}) async-start(), calls=%async_computation.5 | async-start | bytes 4587520 | tf_op jit(solution)/shard_map/reduce_scatter | solution.py:792
  263.7 13.5 %collective-permute-start.34 = (bf16[256,1792]{1,0:T(8,128)(2,1)S(1)}, bf16[256,1792]{1,0:T(8,128)(2,1)S(1)}, u32[]{:S(2)}, u32[]{:S(2)}) collective-permute-start(bf16[256,1792]{1,0:T(8,128)(2,1)S(1)} %get-tuple-element.123), channel_id=1, source_target_pairs={{0,4},{1,3},{2,6},{3,1},{4,0},{5,7},{6,2},{7,5},{8,12},{9,11},{10,... | collective-permute-start | bytes 2752520 | tf_op jit(solution)/shard_map/ppermute | solution.py:35
  277.3 10.3 %collective-permute-start.36 = (bf16[512,1792]{1,0:T(8,128)(2,1)S(1)}, bf16[512,1792]{1,0:T(8,128)(2,1)S(1)}, u32[]{:S(2)}, u32[]{:S(2)}) collective-permute-start(bf16[512,1792]{1,0:T(8,128)(2,1)S(1)} %slice.400), channel_id=1, source_target_pairs={{0,1},{1,0},{2,3},{3,2},{4,5},{5,4},{6,7},{7,6},{8,9},{9,8},{10,11... | collective-permute-start | bytes 5505032 | tf_op jit(solution)/shard_map/ppermute | solution.py:35
  277.4 8.5 %collective-permute-start.35 = (bf16[128,1792]{1,0:T(8,128)(2,1)S(1)}, bf16[128,1792]{1,0:T(8,128)(2,1)S(1)}, u32[]{:S(2)}, u32[]{:S(2)}) collective-permute-start(bf16[128,1792]{1,0:T(8,128)(2,1)S(1)} %get-tuple-element.131), channel_id=1, source_target_pairs={{0,2},{1,5},{2,0},{3,7},{4,6},{5,1},{6,4},{7,3},{8,10},{9,13},{10,... | collective-permute-start | bytes 1376264 | tf_op jit(solution)/shard_map/ppermute | solution.py:35
  287.6 13.4 %collective-permute-start.37 = (bf16[128,1792]{1,0:T(8,128)(2,1)S(1)}, bf16[128,1792]{1,0:T(8,128)(2,1)S(1)}, u32[]{:S(2)}, u32[]{:S(2)}) collective-permute-start(bf16[128,1792]{1,0:T(8,128)(2,1)S(1)} %get-tuple-element.137), channel_id=1, source_target_pairs={{0,2},{1,5},{2,0},{3,7},{4,6},{5,1},{6,4},{7,3},{8,10},{9,13},{10,... | collective-permute-start | bytes 1376264 | tf_op jit(solution)/shard_map/ppermute | solution.py:35
  289.2 11.8 %collective-permute-start.38 = (bf16[128,1792]{1,0:T(8,128)(2,1)S(1)}, bf16[128,1792]{1,0:T(8,128)(2,1)S(1)}, u32[]{:S(2)}, u32[]{:S(2)}) collective-permute-start(bf16[128,1792]{1,0:T(8,128)(2,1)S(1)} %get-tuple-element.137), channel_id=1, source_target_pairs={{0,4},{1,3},{2,6},{3,1},{4,0},{5,7},{6,2},{7,5},{8,12},{9,11},{10,... | collective-permute-start | bytes 1376264 | tf_op jit(solution)/shard_map/ppermute | solution.py:35
  301.0 8.5 %collective-permute-start.39 = (bf16[128,1792]{1,0:T(8,128)(2,1)S(1)}, bf16[128,1792]{1,0:T(8,128)(2,1)S(1)}, u32[]{:S(2)}, u32[]{:S(2)}) collective-permute-start(bf16[128,1792]{1,0:T(8,128)(2,1)S(1)} %collective-permute-done.37), channel_id=1, source_target_pairs={{0,4},{1,3},{2,6},{3,1},{4,0},{5,7},{6,2},{7,5},{8,12},{9,11},{10,... | collective-permute-start | bytes 1376264 | tf_op jit(solution)/shard_map/ppermute | solution.py:35
  301.5 9.6 %collective-permute-start.41 = (bf16[128,1792]{1,0:T(8,128)(2,1)S(1)}, bf16[128,1792]{1,0:T(8,128)(2,1)S(1)}, u32[]{:S(2)}, u32[]{:S(2)}) collective-permute-start(bf16[128,1792]{1,0:T(8,128)(2,1)S(1)} %collective-permute-done.37), channel_id=1, source_target_pairs={{0,1},{1,0},{2,3},{3,2},{4,5},{5,4},{6,7},{7,6},{8,9},{9,8},{10,11... | collective-permute-start | bytes 1376264 | tf_op jit(solution)/shard_map/ppermute | solution.py:35
  302.3 8.0 %collective-permute-start.40 = (bf16[128,1792]{1,0:T(8,128)(2,1)S(1)}, bf16[128,1792]{1,0:T(8,128)(2,1)S(1)}, u32[]{:S(2)}, u32[]{:S(2)}) collective-permute-start(bf16[128,1792]{1,0:T(8,128)(2,1)S(1)} %get-tuple-element.137), channel_id=1, source_target_pairs={{0,1},{1,0},{2,3},{3,2},{4,5},{5,4},{6,7},{7,6},{8,9},{9,8},{10,11... | collective-permute-start | bytes 1376264 | tf_op jit(solution)/shard_map/ppermute | solution.py:35
  302.3 9.6 %collective-permute-start.42 = (bf16[128,1792]{1,0:T(8,128)(2,1)S(1)}, bf16[128,1792]{1,0:T(8,128)(2,1)S(1)}, u32[]{:S(2)}, u32[]{:S(2)}) collective-permute-start(bf16[128,1792]{1,0:T(8,128)(2,1)S(1)} %collective-permute-done.38), channel_id=1, source_target_pairs={{0,1},{1,0},{2,3},{3,2},{4,5},{5,4},{6,7},{7,6},{8,9},{9,8},{10,11... | collective-permute-start | bytes 1376264 | tf_op jit(solution)/shard_map/ppermute | solution.py:35
  313.5 19.5 %collective-permute-start.44 = (bf16[256,1792]{1,0:T(8,128)(2,1)}, bf16[256,1792]{1,0:T(8,128)(2,1)}, u32[]{:S(2)}, u32[]{:S(2)}) collective-permute-start(bf16[256,1792]{1,0:T(8,128)(2,1)} %get-tuple-element.141), channel_id=1, source_target_pairs={{0,4},{1,3},{2,6},{3,1},{4,0},{5,7},{6,2},{7,5},{8,12},{9,11},{10,... | collective-permute-start | bytes 2752520 | tf_op jit(solution)/shard_map/ppermute | solution.py:35
  349.4 18.6 %collective-permute-start.46 = (bf16[256,1792]{1,0:T(8,128)(2,1)}, bf16[256,1792]{1,0:T(8,128)(2,1)}, u32[]{:S(2)}, u32[]{:S(2)}) collective-permute-start(bf16[256,1792]{1,0:T(8,128)(2,1)} %get-tuple-element.154), channel_id=1, source_target_pairs={{0,4},{1,3},{2,6},{3,1},{4,0},{5,7},{6,2},{7,5},{8,12},{9,11},{10,... | collective-permute-start | bytes 2752520 | tf_op jit(solution)/shard_map/ppermute | solution.py:35
  352.1 13.8 %collective-permute-start.47 = (bf16[128,1792]{1,0:T(8,128)(2,1)}, bf16[128,1792]{1,0:T(8,128)(2,1)}, u32[]{:S(2)}, u32[]{:S(2)}) collective-permute-start(bf16[128,1792]{1,0:T(8,128)(2,1)} %get-tuple-element.157), channel_id=1, source_target_pairs={{0,2},{1,5},{2,0},{3,7},{4,6},{5,1},{6,4},{7,3},{8,10},{9,13},{10,... | collective-permute-start | bytes 1376264 | tf_op jit(solution)/shard_map/ppermute | solution.py:35
  370.8 41.8 %collective-permute-start.48 = (bf16[448,1792]{1,0:T(8,128)(2,1)}, bf16[448,1792]{1,0:T(8,128)(2,1)}, u32[]{:S(2)}, u32[]{:S(2)}) collective-permute-start(bf16[448,1792]{1,0:T(8,128)(2,1)} %reduce-scatter.5.cloned.1.call-done.refs_0_), channel_id=1, source_target_pairs={{0,2},{1,5},{2,0},{3,7},{4,6},{5,1},{6,4},{7,3},{8,10},{9,13},{10,... | collective-permute-start | bytes 4816904 | tf_op jit(solution)/shard_map/ppermute | solution.py:35
  371.3 41.3 %collective-permute-start.49 = (bf16[448,1792]{1,0:T(8,128)(2,1)}, bf16[448,1792]{1,0:T(8,128)(2,1)}, u32[]{:S(2)}, u32[]{:S(2)}) collective-permute-start(bf16[448,1792]{1,0:T(8,128)(2,1)} %reduce-scatter.5.cloned.1.call-done.refs_0_), channel_id=1, source_target_pairs={{0,4},{1,3},{2,6},{3,1},{4,0},{5,7},{6,2},{7,5},{8,12},{9,11},{10,... | collective-permute-start | bytes 4816904 | tf_op jit(solution)/shard_map/ppermute | solution.py:35
  375.6 8.3 %collective-permute-start.52 = (bf16[118,128]{1,0:T(8,128)(2,1)S(1)}, bf16[118,128]{1,0:T(8,128)(2,1)S(1)}, u32[]{:S(2)}, u32[]{:S(2)}) collective-permute-start(bf16[118,128]{1,0:T(8,128)(2,1)S(1)} %get-tuple-element.292), channel_id=1, source_target_pairs={{0,16},{8,24},{16,0},{24,8},{1,17},{9,25},{17,1},{25,9},{2,18},{10... | collective-permute-start | bytes 90632 | tf_op jit(solution)/shard_map/ppermute | solution.py:72
  380.2 32.4 %collective-permute-start.50 = (bf16[128,1792]{1,0:T(8,128)(2,1)}, bf16[128,1792]{1,0:T(8,128)(2,1)S(1)}, u32[]{:S(2)}, u32[]{:S(2)}) collective-permute-start(bf16[128,1792]{1,0:T(8,128)(2,1)} %add_convert_fusion.3), channel_id=1, source_target_pairs={{0,2},{1,5},{2,0},{3,7},{4,6},{5,1},{6,4},{7,3},{8,10},{9,13},{10,... | collective-permute-start | bytes 1376264 | tf_op jit(solution)/shard_map/ppermute | solution.py:35
  412.6 9.6 %collective-permute-start.54 = (bf16[118,128]{1,0:T(8,128)(2,1)S(1)}, bf16[118,128]{1,0:T(8,128)(2,1)S(1)}, u32[]{:S(2)}, u32[]{:S(2)}) collective-permute-start(bf16[118,128]{1,0:T(8,128)(2,1)S(1)} %add_convert_fusion.7), channel_id=1, source_target_pairs={{0,2},{1,5},{2,0},{3,7},{4,6},{5,1},{6,4},{7,3},{8,10},{9,13},{10,... | collective-permute-start | bytes 90632 | tf_op jit(solution)/shard_map/ppermute | solution.py:35
  414.1 8.8 %collective-permute-start.55 = (bf16[118,128]{1,0:T(8,128)(2,1)S(1)}, bf16[118,128]{1,0:T(8,128)(2,1)S(1)}, u32[]{:S(2)}, u32[]{:S(2)}) collective-permute-start(bf16[118,128]{1,0:T(8,128)(2,1)S(1)} %add_convert_fusion.7), channel_id=1, source_target_pairs={{0,4},{1,3},{2,6},{3,1},{4,0},{5,7},{6,2},{7,5},{8,12},{9,11},{10,... | collective-permute-start | bytes 90632 | tf_op jit(solution)/shard_map/ppermute | solution.py:35
  414.7 34.8 %collective-permute-start.67 = (bf16[448,1792]{1,0:T(8,128)(2,1)}, bf16[448,1792]{1,0:T(8,128)(2,1)}, u32[]{:S(2)}, u32[]{:S(2)}) collective-permute-start(bf16[448,1792]{1,0:T(8,128)(2,1)} %collective-permute-done.48), channel_id=1, source_target_pairs={{0,4},{1,3},{2,6},{3,1},{4,0},{5,7},{6,2},{7,5},{8,12},{9,11},{10,... | collective-permute-start | bytes 4816904 | tf_op jit(solution)/shard_map/ppermute | solution.py:35
  422.2 13.7 %collective-permute-start.56 = (bf16[118,128]{1,0:T(8,128)(2,1)S(1)}, bf16[118,128]{1,0:T(8,128)(2,1)S(1)}, u32[]{:S(2)}, u32[]{:S(2)}) collective-permute-start(bf16[118,128]{1,0:T(8,128)(2,1)S(1)} %collective-permute-done.54), channel_id=1, source_target_pairs={{0,4},{1,3},{2,6},{3,1},{4,0},{5,7},{6,2},{7,5},{8,12},{9,11},{10,... | collective-permute-start | bytes 90632 | tf_op jit(solution)/shard_map/ppermute | solution.py:35
  440.2 23.3 %collective-permute-start.64 = (bf16[448,1024]{1,0:T(8,128)(2,1)}, bf16[448,1024]{1,0:T(8,128)(2,1)S(1)}, u32[]{:S(2)}, u32[]{:S(2)}) collective-permute-start(bf16[448,1024]{1,0:T(8,128)(2,1)} %reduce-scatter.3.cloned.1.call-done.refs_0_), channel_id=1, source_target_pairs={{0,2},{1,5},{2,0},{3,7},{4,6},{5,1},{6,4},{7,3},{8,10},{9,13},{10,... | collective-permute-start | bytes 2752520 | tf_op jit(solution)/shard_map/ppermute | solution.py:35
  441.5 22.1 %collective-permute-start.65 = (bf16[448,1024]{1,0:T(8,128)(2,1)}, bf16[448,1024]{1,0:T(8,128)(2,1)S(1)}, u32[]{:S(2)}, u32[]{:S(2)}) collective-permute-start(bf16[448,1024]{1,0:T(8,128)(2,1)} %reduce-scatter.3.cloned.1.call-done.refs_0_), channel_id=1, source_target_pairs={{0,4},{1,3},{2,6},{3,1},{4,0},{5,7},{6,2},{7,5},{8,12},{9,11},{10,... | collective-permute-start | bytes 2752520 | tf_op jit(solution)/shard_map/ppermute | solution.py:35
  445.2 14.3 %collective-permute-start.66 = (f32[2,448]{1,0:T(2,128)S(1)}, f32[2,448]{1,0:T(2,128)S(1)}, u32[]{:S(2)}, u32[]{:S(2)}) collective-permute-start(f32[2,448]{1,0:T(2,128)S(1)} %pad_maximum_fusion.15), channel_id=1, source_target_pairs={{0,1},{1,0},{2,3},{3,2},{4,5},{5,4},{6,7},{7,6},{8,9},{9,8},{10,11... | collective-permute-start | bytes 10760 | tf_op jit(solution)/shard_map/ppermute | solution.py:35
  446.6 17.8 %collective-permute-start.57 = (bf16[32,3584]{1,0:T(8,128)(2,1)S(1)}, bf16[32,3584]{1,0:T(8,128)(2,1)S(1)}, u32[]{:S(2)}, u32[]{:S(2)}) collective-permute-start(bf16[32,3584]{1,0:T(8,128)(2,1)S(1)} %get-tuple-element.231), channel_id=1, source_target_pairs={{0,24},{8,0},{16,8},{24,16},{1,25},{9,1},{17,9},{25,17},{2,26},{10... | collective-permute-start | bytes 688136 | tf_op jit(solution)/shard_map/ppermute | solution.py:72
  449.4 21.0 %collective-permute-start.58 = (bf16[32,3584]{1,0:T(8,128)(2,1)S(1)}, bf16[32,3584]{1,0:T(8,128)(2,1)S(1)}, u32[]{:S(2)}, u32[]{:S(2)}) collective-permute-start(bf16[32,3584]{1,0:T(8,128)(2,1)S(1)} %get-tuple-element.230), channel_id=1, source_target_pairs={{0,16},{8,24},{16,0},{24,8},{1,17},{9,25},{17,1},{25,9},{2,18},{10... | collective-permute-start | bytes 688136 | tf_op jit(solution)/shard_map/ppermute | solution.py:72
  459.5 10.9 %collective-permute-start.59 = (bf16[32,3584]{1,0:T(8,128)(2,1)S(1)}, bf16[32,3584]{1,0:T(8,128)(2,1)S(1)}, u32[]{:S(2)}, u32[]{:S(2)}) collective-permute-start(bf16[32,3584]{1,0:T(8,128)(2,1)S(1)} %get-tuple-element.229), channel_id=1, source_target_pairs={{0,8},{8,16},{16,24},{24,0},{1,9},{9,17},{17,25},{25,1},{2,10},{10... | collective-permute-start | bytes 688136 | tf_op jit(solution)/shard_map/ppermute | solution.py:72
  463.6 15.7 %collective-permute-start.68 = (bf16[448,1024]{1,0:T(8,128)(2,1)S(1)}, bf16[448,1024]{1,0:T(8,128)(2,1)S(1)}, u32[]{:S(2)}, u32[]{:S(2)}) collective-permute-start(bf16[448,1024]{1,0:T(8,128)(2,1)S(1)} %collective-permute-done.64), channel_id=1, source_target_pairs={{0,4},{1,3},{2,6},{3,1},{4,0},{5,7},{6,2},{7,5},{8,12},{9,11},{10,... | collective-permute-start | bytes 2752520 | tf_op jit(solution)/shard_map/ppermute | solution.py:35
  464.5 7.9 %collective-permute-start.61 = (bf16[32,3584]{1,0:T(8,128)(2,1)S(1)}, bf16[32,3584]{1,0:T(8,128)(2,1)S(1)}, u32[]{:S(2)}, u32[]{:S(2)}) collective-permute-start(bf16[32,3584]{1,0:T(8,128)(2,1)S(1)} %collective-permute-done.57.refs_1_), channel_id=1, source_target_pairs={{0,1},{1,0},{2,3},{3,2},{4,5},{5,4},{6,7},{7,6},{8,9},{9,8},{10,11... | collective-permute-start | bytes 688136 | tf_op jit(solution)/shard_map/ppermute | solution.py:35
  (79 other events, 1062.2 us)
Sparse Core Ops, SparseCore 0:
  12.1 87.1 all-gather.2
  101.5 125.9 all-gather.4
  256.3 111.0 reduce-scatter.4
  370.1 70.0 reduce-scatter.2

commit v6 on v5

--- a/solution.py
+++ b/solution.py
@@ -572,6 +572,38 @@
     )(lengths, qkv, grad, conv)
 
 
+def attn_packed_kernel(tile_ref, in_ref, out_ref, packed_ref):
+    count = in_ref.shape[0]
+    tiles = packed_ref.shape[1] // (count + 1) // 128
+    for step in range(tiles):
+
+        @pl.when(pl.program_id(0) == step)
+        def _():
+            for i in range(count):
+                at = (i * tiles + step) * 128
+                packed_ref[:, at : at + 128] = in_ref[i]
+            at = (count * tiles + step) * 128
+            packed_ref[:, at : at + 128] = out_ref[...]
+
+
+def attn_packed(first, attn_in, attn_out, width):
+    count, rows, _ = attn_in.shape
+    return pl.pallas_call(
+        attn_packed_kernel,
+        grid_spec=pltpu.PrefetchScalarGridSpec(
+            num_scalar_prefetch=1,
+            grid=(width // 128,),
+            in_specs=[
+                pl.BlockSpec((count, rows, 128), lambda j, ref: (0, 0, ref[0] + j)),
+                pl.BlockSpec((rows, 128), lambda j, ref: (0, ref[0] + j)),
+            ],
+            out_specs=pl.BlockSpec((rows, (count + 1) * width), lambda j, ref: (0, 0)),
+        ),
+        out_shape=jax.ShapeDtypeStruct((rows, (count + 1) * width), bf16),
+        name="attn_packed",
+    )(first.reshape(1).astype(jnp.int32), attn_in, attn_out)
+
+
 def part_of(total, each, index):
     start = jnp.minimum(index * each, total - each)
     return start, index * each - start
@@ -606,10 +638,7 @@
     plane = BATCHES * group
 
     start, shared = part_of(heads_all, width, c)
-    sliced = lax.dynamic_slice_in_dim(attn_in, start, width, 2)
-    out_part = lax.dynamic_slice_in_dim(attn_out, start, width, 0)
-    out_part = jnp.where(jnp.arange(width)[:, None] >= shared, out_part, jnp.zeros_like(out_part))
-    attn_own = jnp.concatenate([sliced[0], sliced[1], sliced[2], out_part.T], axis=1)
+    attn_own = attn_packed(start // 128, attn_in, attn_out.T, width)
     own_down = 3 * ff // 128 * 128 - 2 * ff
     sliced = lax.dynamic_slice_in_dim(gate_up, c * ff, ff, 2)
     down_own = lax.dynamic_slice_in_dim(down_proj, c * ff, ff, 0).T
@@ -705,8 +734,11 @@
             part = unpacked(z_shifted(rest_own, sizes, k) if k else rest_own, rest_width)
             rest_w = lax.dynamic_update_slice_in_dim(rest_w, part, (f - k) % n_fsdp * d_own, 0)
     qkv = product(deal, product(hidden, qkv_w, NN, bf16), NN, bf16)
-    grad_dealt = plane_gather(after(own_g, qkv), sizes)
-    attended = product(deal, attend_forward(own_lengths, qkv, conv), TN, bf16)
+    counted = jnp.arange(width)[None, :] >= shared
+    attended = attend_forward(own_lengths, qkv, conv)
+    attended, own_g = stage(attended, own_g)
+    grad_dealt = plane_gather(own_g, sizes)
+    attended = jnp.where(counted, product(deal, attended, TN, bf16), jnp.zeros((), bf16))
     kept = plane // 2
     branch = plane_scatter(
         product(attended[:kept], out_w, NT),
@@ -770,6 +802,7 @@
 
     lift_got = flipped(lift_sent, sizes, 1)
     grad_attended = product(deal, product(grad_branch, out_w, NN, bf16), NN, bf16)
+    grad_attended = jnp.where(counted, grad_attended, jnp.zeros((), bf16))
     grad_proj, grad_conv = attend_backward(own_lengths, qkv, grad_attended, conv)
     lift_got, lift, grad_proj = stage(lift_got, lift, grad_proj)
 

time: 495 us -> 492 us (level)
    ppermute x15, waiting for transfers between devices: 29.6 us -> 37 us  [z_shifted(): return lax.ppermute(value, 'fsdp', [(i, (i + steps) % n) for i in range(n)])]
    unnamed x163 -> x153, local copies, waits for them, and re-layouts: 22.4 us -> 21.5 us
  transfers between devices with their start and end apart: 76 -> 76, of which waited for: 29 -> 31; matrix products, arithmetic and copies ran while one was open for 24% -> 24% of each run, Pallas kernels for 9% -> 9%
where the time goes in v6:
time: 492 us; the launch traced here: 487 us
  waiting for transfers between devices  194 us (39%)
  starting transfers between devices  77.4 us (16%)
  Pallas kernels  69.1 us (14%)
  matrix products  47.7 us (10%)
  local copies, waits for them, and re-layouts  45.4 us (9%)
  other arithmetic  37.3 us (8%)
  between operations  15.5 us (3%)
    ppermute x56, waiting for transfers between devices, flipped(): return lax.ppermute(value, ('fsdp', 'ctx', 'tp'), pairs)  128 us
    dot_general x14, matrix products, product(): lax.dot_general(left, right, (dims, ((), ())), preferred_element_type=f32)  47.7 us
    ppermute x56, starting transfers between devices, flipped(): return lax.ppermute(value, ('fsdp', 'ctx', 'tp'), pairs)  38.3 us
    ppermute x15, waiting for transfers between devices, z_shifted(): return lax.ppermute(value, 'fsdp', [(i, (i + steps) % n) for i in range(n)])  37 us
    ppermute x15, starting transfers between devices, z_shifted(): return lax.ppermute(value, 'fsdp', [(i, (i + steps) % n) for i in range(n)])  30.5 us
    unnamed x153, local copies, waits for them, and re-layouts  21.5 us
    all_gather x1, waiting for transfers between devices, per_device(): mlp_w = lax.all_gather(after(mlp_own, attn_own), 'fsdp', axis=0, tiled=True)  17.5 us
    pallas_call x1, Pallas kernels, attend_backward(): pl.pallas_call(attend_backward_kernel, out_shape=(jax.ShapeDtypeStruct((r...  14.1 us
  transfers between devices with their start and end apart: 76, of which 31 were waited for; matrix products, arithmetic and copies ran while one was open for 24% of the time, Pallas kernels for 9%

profile of v6, /device:TPU:0, one launch (start us, length us, event | category | flops | bytes accessed | tf_op | source)
XLA Modules:
  0.0 486.6 jit_solution(1100579302439114472)
XLA Ops:
  7.3 2.4 attn_packed.1
  10.6 8.3 %all-to-all-start = ((f32[16,1,1824]{2,1,0:T(1,128)}), f32[16,1,1824]{2,1,0:T(1,128)S(1)}, u32[]{:S(2)}, u32[]{:S(2)}) async-start(f32[16,1,1824]{2,1,0:T(1,128)} %broadcast_in_dim.62), calls=%async_computation | async-start | bytes 245760 | tf_op jit(solution)/shard_map/all_to_all | solution.py:661
  19.2 1.9 dynamic-slice_bitcast_fusion
  21.2 2.4 concatenate.103
  24.5 2.2 all-to-all-done
  29.7 2.5 collective-permute-start.1
  34.7 4.5 collective-permute-done
  39.2 6.4 %collective-permute-done.1 = bf16[32,1792]{1,0:T(8,128)(2,1)S(1)} collective-permute-done((bf16[32,1792]{1,0:T(8,128)(2,1)S(1)}, bf16[32,1792]{1,0:T(8,128)(2,1)S(1)}, u32[]{:S(2)}, u32[]{:S(2)}) %collective-permute-start.1) | collective-permute-done | bytes 114720 | tf_op jit(solution)/shard_map/ppermute | solution.py:72
  50.3 9.7 %collective-permute-done.3 = bf16[128,1792]{1,0:T(8,128)(2,1)S(1)} collective-permute-done((bf16[128,1792]{1,0:T(8,128)(2,1)S(1)}, bf16[128,1792]{1,0:T(8,128)(2,1)S(1)}, u32[]{:S(2)}, u32[]{:S(2)}) %collective-permute-start.3) | collective-permute-done | bytes 458784 | tf_op jit(solution)/shard_map/ppermute | solution.py:35
  62.9 5.6 %collective-permute-done.5 = bf16[128,1792]{1,0:T(8,128)(2,1)S(1)} collective-permute-done((bf16[128,1792]{1,0:T(8,128)(2,1)S(1)}, bf16[128,1792]{1,0:T(8,128)(2,1)S(1)}, u32[]{:S(2)}, u32[]{:S(2)}) %collective-permute-start.5) | collective-permute-done | bytes 458784 | tf_op jit(solution)/shard_map/ppermute | solution.py:35
  72.9 10.2 %collective-permute-start.10 = (bf16[32,1792]{1,0:T(8,128)(2,1)S(1)}, bf16[32,1792]{1,0:T(8,128)(2,1)S(1)}, u32[]{:S(2)}, u32[]{:S(2)}) collective-permute-start(bf16[32,1792]{1,0:T(8,128)(2,1)S(1)} %get-tuple-element.255), channel_id=1, source_target_pairs={{0,8},{8,16},{16,24},{24,0},{1,9},{9,17},{17,25},{25,1},{2,10},{10... | collective-permute-start | bytes 344072 | tf_op jit(solution)/shard_map/ppermute | solution.py:72
  83.1 2.0 collective-permute-start.11
  86.0 4.9 %collective-permute-done.10 = bf16[32,1792]{1,0:T(8,128)(2,1)S(1)} collective-permute-done((bf16[32,1792]{1,0:T(8,128)(2,1)S(1)}, bf16[32,1792]{1,0:T(8,128)(2,1)S(1)}, u32[]{:S(2)}, u32[]{:S(2)}) %collective-permute-start.10) | collective-permute-done | bytes 114720 | tf_op jit(solution)/shard_map/ppermute | solution.py:72
  90.9 8.0 %collective-permute-done.11 = bf16[32,1792]{1,0:T(8,128)(2,1)S(1)} collective-permute-done((bf16[32,1792]{1,0:T(8,128)(2,1)S(1)}, bf16[32,1792]{1,0:T(8,128)(2,1)S(1)}, u32[]{:S(2)}, u32[]{:S(2)}) %collective-permute-start.11) | collective-permute-done | bytes 114720 | tf_op jit(solution)/shard_map/ppermute | solution.py:72
  99.0 5.5 %all-gather.3.cloned.1.call-done = bf16[1792,1024]{1,0:T(8,128)(2,1)} async-done(((bf16[448,1024]{1,0:T(8,128)(2,1)}), bf16[1792,1024]{1,0:T(8,128)(2,1)}) %all-gather.3.cloned.1.call-update) | async-done | bytes 3670032 | tf_op jit(solution)/shard_map/all_gather | solution.py:648
  104.6 7.5 %fusion.25.qkv_ref = bf16[1024,768]{1,0:T(8,128)(2,1)S(1)} fusion(s32[1024]{0:T(1024)S(1)} %fusion.80, bf16[1024,1792]{1,0:T(8,128)(2,1)} %constant_dynamic-update-slice_fusion.refs_0_, bf16[1792,1024]{1,0:T(8,128)(2,1)} %all-gather.3.cloned.1.call-done), kind=kOutput, calls=%fused_computation.40 | convolution fusion | flops 4431806464 | bytes 7999488 | tf_op jit(solution)/shard_map/dot_general | solution.py:95
  112.1 5.8 %attend_forward.1 = bf16[1024,256]{1,0:T(8,128)(2,1)S(1)} custom-call(s32[2,3]{1,0:T(2,128)S(1)} %bitcast.92, bf16[1024,768]{1,0:T(8,128)(2,1)S(1)} %fusion.25.qkv_ref, f32[3,256]{1,0:T(4,128)S(1)} %constant_dynamic-slice_fusion.20.conv_ref), custom_call_target="tpu_custom_call" | custom-call | bytes 20000000 | tf_op jit(solution)/shard_map/attend_forward/pallas_call | solution.py:541
  119.4 3.1 convolution_convert_fusion
  124.1 2.7 collective-permute-start.32
  127.0 2.1 collective-permute-done.30
  129.3 4.5 collective-permute-done.31
  137.5 2.5 convert_add_fusion
  140.5 6.5 %collective-permute-done.23 = bf16[128,1792]{1,0:T(8,128)(2,1)S(1)} collective-permute-done((bf16[128,1792]{1,0:T(8,128)(2,1)S(1)}, bf16[128,1792]{1,0:T(8,128)(2,1)S(1)}, u32[]{:S(2)}, u32[]{:S(2)}) %collective-permute-start.23) | collective-permute-done | bytes 458784 | tf_op jit(solution)/shard_map/ppermute | solution.py:35
  148.1 10.9 %collective-permute-done.25 = bf16[128,1792]{1,0:T(8,128)(2,1)S(1)} collective-permute-done((bf16[128,1792]{1,0:T(8,128)(2,1)S(1)}, bf16[128,1792]{1,0:T(8,128)(2,1)S(1)}, u32[]{:S(2)}, u32[]{:S(2)}) %collective-permute-start.25) | collective-permute-done | bytes 458784 | tf_op jit(solution)/shard_map/ppermute | solution.py:35
  162.1 6.9 %collective-permute-done.15 = bf16[128,1792]{1,0:T(8,128)(2,1)S(1)} collective-permute-done((bf16[128,1792]{1,0:T(8,128)(2,1)S(1)}, bf16[128,1792]{1,0:T(8,128)(2,1)S(1)}, u32[]{:S(2)}, u32[]{:S(2)}) %collective-permute-start.15) | collective-permute-done | bytes 458784 | tf_op jit(solution)/shard_map/ppermute | solution.py:35
  172.4 11.0 %collective-permute-done.16 = bf16[128,1792]{1,0:T(8,128)(2,1)S(1)} collective-permute-done((bf16[128,1792]{1,0:T(8,128)(2,1)S(1)}, bf16[128,1792]{1,0:T(8,128)(2,1)S(1)}, u32[]{:S(2)}, u32[]{:S(2)}) %collective-permute-start.16) | collective-permute-done | bytes 458784 | tf_op jit(solution)/shard_map/ppermute | solution.py:35
  186.2 5.6 %collective-permute-done.18 = bf16[128,1792]{1,0:T(8,128)(2,1)S(1)} collective-permute-done((bf16[128,1792]{1,0:T(8,128)(2,1)S(1)}, bf16[128,1792]{1,0:T(8,128)(2,1)S(1)}, u32[]{:S(2)}, u32[]{:S(2)}) %collective-permute-start.18) | collective-permute-done | bytes 458784 | tf_op jit(solution)/shard_map/ppermute | solution.py:35
  195.9 6.0 %copy.55.hidden_ref = bf16[1792,1024]{1,0:T(8,128)(2,1)} copy(bf16[1792,1024]{0,1:T(8,128)(2,1)} %bitcast.18) | data formatting | bytes 7340032 | tf_op jit(solution)/shard_map/optimization_barrier | solution.py:58
  201.9 6.0 %copy.56.grad_ref = bf16[1792,1024]{1,0:T(8,128)(2,1)} copy(bf16[1792,1024]{0,1:T(8,128)(2,1)} %bitcast.94) | data formatting | bytes 7340032 | tf_op jit(solution)/shard_map/optimization_barrier | solution.py:58
  207.8 17.5 %all-gather.5.cloned.1.call-done.weight_ref = bf16[1792,1792]{1,0:T(8,128)(2,1)} async-done(((bf16[448,1792]{1,0:T(8,128)(2,1)}), bf16[1792,1792]{1,0:T(8,128)(2,1)}) %all-gather.5.cloned.1.call-update) | async-done | bytes 6422544 | tf_op jit(solution)/shard_map/all_gather | solution.py:649
  225.3 12.5 %feed_forward.1 = (bf16[1024,640]{1,0:T(8,128)(2,1)S(1)}, bf16[1024,1280]{1,0:T(8,128)(2,1)S(1)}) custom-call(bf16[1024,1792]{1,0:T(8,128)(2,1)} %constant_dynamic-update-slice_fusion.8.hidden_ref, bf16[1024,1792]{1,0:T(8,128)(2,1)} %copy-done.22, bf16[1792,1792]{1,0:T(8,128)(2,1)} %all-gather.5.cloned.1.call-done.weight_ref, bf16[1792,128]{1,0:T(8,128)(2,1)S(1)} %pad.4.rest_ref), custom_call_target="tpu_custom_call" | custom-call | flops 6694109184 | bytes 17612800 | tf_op jit(solution)/shard_map/feed_forward/pallas_call | solution.py:357
  237.8 9.6 %mlp_grad.1 = (bf16[1792,1792]{1,0:T(8,128)(2,1)}, bf16[1792,128]{1,0:T(8,128)(2,1)S(1)}) custom-call(bf16[1792,1024]{1,0:T(8,128)(2,1)S(1)} %copy-done.5, bf16[1792,1024]{1,0:T(8,128)(2,1)S(1)} %copy-done.6, bf16[1024,1280]{1,0:T(8,128)(2,1)S(1)} %get-tuple-element.121.pair_ref, bf16[1024,640]{1,0:T(8,128)(2,1)S(1)} %get-tuple-element.127.inner_ref), custom_call_target="tpu_custom_call" | custom-call | flops 6576668672 | bytes 17432576 | tf_op jit(solution)/shard_map/mlp_grad/pallas_call | solution.py:291
  247.4 6.5 %fusion.8 = bf16[512,1792]{1,0:T(8,128)(2,1)} fusion(bf16[1792,1792]{1,0:T(8,128)(2,1)} %all-gather.5.cloned.1.call-done.weight_ref, bf16[1024,1280]{1,0:T(8,128)(2,1)} %copy-done.11), kind=kOutput, calls=%fused_computation.13 | convolution fusion | flops 2349727744 | bytes 7733248 | tf_op jit(solution)/shard_map/dot_general | solution.py:95
  254.2 5.3 %fusion.4 = f32[512,1792]{1,0:T(8,128)S(1)} fusion(bf16[1792,1792]{1,0:T(8,128)(2,1)} %all-gather.5.cloned.1.call-done.weight_ref, bf16[1024,1280]{1,0:T(8,128)(2,1)} %copy-done.11), kind=kOutput, calls=%fused_computation.6 | convolution fusion | flops 2348810240 | bytes 9568256 | tf_op jit(solution)/shard_map/dot_general | solution.py:95
  259.5 2.0 add_convert_fusion.2
  263.2 4.7 fusion.11
  269.1 3.0 copy-done.15
  272.3 2.7 collective-permute-done.34
  276.9 6.9 %collective-permute-done.35 = bf16[128,1792]{1,0:T(8,128)(2,1)S(1)} collective-permute-done((bf16[128,1792]{1,0:T(8,128)(2,1)S(1)}, bf16[128,1792]{1,0:T(8,128)(2,1)S(1)}, u32[]{:S(2)}, u32[]{:S(2)}) %collective-permute-start.35) | collective-permute-done | bytes 458784 | tf_op jit(solution)/shard_map/ppermute | solution.py:35
  288.5 1.9 add_convert_fusion.1
  290.4 8.4 %collective-permute-done.37 = bf16[128,1792]{1,0:T(8,128)(2,1)S(1)} collective-permute-done((bf16[128,1792]{1,0:T(8,128)(2,1)S(1)}, bf16[128,1792]{1,0:T(8,128)(2,1)S(1)}, u32[]{:S(2)}, u32[]{:S(2)}) %collective-permute-start.37) | collective-permute-done | bytes 458784 | tf_op jit(solution)/shard_map/ppermute | solution.py:35
  303.1 4.2 collective-permute-done.39
  311.8 4.9 %fusion.35.grad_ref = bf16[1024,256]{1,0:T(8,128)(2,1)S(1)} fusion(s32[1024]{0:T(1024)S(1)} %copy-done.54, bf16[1024,1792]{1,0:T(8,128)(2,1)} %constant_dynamic-update-slice_fusion.24.refs_2_, bf16[1792,1024]{1,0:T(8,128)(2,1)} %all-gather.3.cloned.1.call-done, pred[256]{0:T(512)(128)(4,1)S(1)} %copy-done.60), kind=kOutput, calls=%fused_computation.57 | convolution fusion | flops 1478230016 | bytes 5116160 | tf_op jit(solution)/shard_map/dot_general | solution.py:95
  316.8 14.1 %attend_backward.1 = (bf16[1024,768]{1,0:T(8,128)(2,1)S(1)}, f32[3,256]{1,0:T(4,128)S(1)}) custom-call(s32[2,3]{1,0:T(2,128)S(1)} %bitcast.93, bf16[1024,768]{1,0:T(8,128)(2,1)S(1)} %fusion.25.qkv_ref, bf16[1024,256]{1,0:T(8,128)(2,1)S(1)} %fusion.35.grad_ref, f32[3,256]{1,0:T(4,128)S(1)} %constant_dynamic-slice_fusion.20.conv_ref), custom_call_target="tpu_custom_call" | custom-call | bytes 50000000 | tf_op jit(solution)/shard_map/attend_backward/pallas_call | solution.py:556
  330.9 2.4 fusion.26.refs_1_
  333.2 2.9 convolution_convert_fusion.1
  337.6 3.5 fusion.13
  341.1 2.5 add_convert_fusion.5
  343.6 3.6 add_convert_fusion
  352.4 7.9 %weight_grad.1 = bf16[1792,1024]{1,0:T(8,128)(2,1)S(1)} custom-call(bf16[1024,1792]{1,0:T(8,128)(2,1)} %constant_dynamic-update-slice_fusion.refs_0_, bf16[1024,768]{1,0:T(8,128)(2,1)S(1)} %fusion.26.refs_1_, bf16[1024,1792]{1,0:T(8,128)(2,1)} %constant_dynamic-update-slice_fusion.24.refs_2_, bf16[1024,256]{1,0:T(8,128)(2,1)S(1)} %fusion.36.refs_3_), custom_call_target="tpu_custom_call" | custom-call | flops 3758096384 | bytes 13107200 | tf_op jit(solution)/shard_map/weight_grad/pallas_call | solution.py:261
  363.6 2.2 collective-permute-done.46
  366.4 2.1 add_convert_fusion.3
  374.6 2.7 collective-permute-start.53
  378.5 2.9 select_reduce_fusion
  382.2 28.2 %collective-permute-done.50 = bf16[128,1792]{1,0:T(8,128)(2,1)S(1)} collective-permute-done((bf16[128,1792]{1,0:T(8,128)(2,1)}, bf16[128,1792]{1,0:T(8,128)(2,1)S(1)}, u32[]{:S(2)}, u32[]{:S(2)}) %collective-permute-start.50) | collective-permute-done | bytes 458784 | tf_op jit(solution)/shard_map/ppermute | solution.py:35
  417.9 2.1 broadcast_select_fusion
  420.8 13.0 %collective-permute-done.56 = bf16[118,128]{1,0:T(8,128)(2,1)S(1)} collective-permute-done((bf16[118,128]{1,0:T(8,128)(2,1)S(1)}, bf16[118,128]{1,0:T(8,128)(2,1)S(1)}, u32[]{:S(2)}, u32[]{:S(2)}) %collective-permute-start.56) | collective-permute-done | bytes 30240 | tf_op jit(solution)/shard_map/ppermute | solution.py:35
  433.9 4.2 reduce-scatter.3.cloned.1.call-done.refs_0_
  443.8 2.8 collective-permute-start.57
  446.9 9.8 %mlp_placed.1 = (f32[2,448,2432]{2,1,0:T(8,128)}, f32[1,448,2432]{2,1,0:T(8,128)}) custom-call(s32[1]{0:T(128)} %bitcast.33.index_ref, bf16[448,1792]{1,0:T(8,128)(2,1)S(1)} %copy-done.3, bf16[448,1792]{1,0:T(8,128)(2,1)S(1)} %get-tuple-element.221.refs_1_, bf16[448,1792]{1,0:T(8,128)(2,1)S(1)} %get-tuple-element.220.refs_2_, ...), custom_call_target="tpu_custom_call" | custom-call | bytes 21790720 | tf_op jit(solution)/shard_map/mlp_placed/pallas_call | solution.py:410
  458.0 3.6 collective-permute-done.64
  462.7 5.0 %collective-permute-done.58.refs_2_ = bf16[32,3584]{1,0:T(8,128)(2,1)S(1)} collective-permute-done((bf16[32,3584]{1,0:T(8,128)(2,1)S(1)}, bf16[32,3584]{1,0:T(8,128)(2,1)S(1)}, u32[]{:S(2)}, u32[]{:S(2)}) %collective-permute-start.58) | collective-permute-done | bytes 229408 | tf_op jit(solution)/shard_map/ppermute | solution.py:72
  472.7 3.2 placed.1
  477.4 2.2 last_placed.1
  (399 shorter events, 102.5 us)
Async XLA Ops:
  7.2 97.4 %all-gather.3.cloned.1.call-start = ((), (), s32[]{:S(2)}) async-start(), calls=%async_computation.3 | async-start | bytes 4587520 | tf_op jit(solution)/shard_map/all_gather | solution.py:648
  10.6 16.1 %all-to-all-start = ((f32[16,1,1824]{2,1,0:T(1,128)}), f32[16,1,1824]{2,1,0:T(1,128)S(1)}, u32[]{:S(2)}, u32[]{:S(2)}) async-start(f32[16,1,1824]{2,1,0:T(1,128)} %broadcast_in_dim.62), calls=%async_computation | async-start | bytes 245760 | tf_op jit(solution)/shard_map/all_to_all | solution.py:661
  18.9 206.4 %all-gather.5.cloned.1.call-start = ((), (), s32[]{:S(2)}) async-start(), calls=%async_computation.4 | async-start | bytes 8028160 | tf_op jit(solution)/shard_map/all_gather | solution.py:649
  23.6 345.0 %reduce-scatter.5.cloned.1.call-start = ((), (), s32[]{:S(2)}) async-start(), calls=%async_computation.6 | async-start | bytes 8028160 | tf_op jit(solution)/shard_map/reduce_scatter | solution.py:763
  28.9 10.3 %collective-permute-start = (bf16[32,1792]{1,0:T(8,128)(2,1)S(1)}, bf16[32,1792]{1,0:T(8,128)(2,1)S(1)}, u32[]{:S(2)}, u32[]{:S(2)}) collective-permute-start(bf16[32,1792]{1,0:T(8,128)(2,1)S(1)} %get-tuple-element.259), channel_id=1, source_target_pairs={{0,8},{8,16},{16,24},{24,0},{1,9},{9,17},{17,25},{25,1},{2,10},{10... | collective-permute-start | bytes 344072 | tf_op jit(solution)/shard_map/ppermute | solution.py:72
  29.7 15.9 %collective-permute-start.1 = (bf16[32,1792]{1,0:T(8,128)(2,1)S(1)}, bf16[32,1792]{1,0:T(8,128)(2,1)S(1)}, u32[]{:S(2)}, u32[]{:S(2)}) collective-permute-start(bf16[32,1792]{1,0:T(8,128)(2,1)S(1)} %get-tuple-element.258), channel_id=1, source_target_pairs={{0,16},{8,24},{16,0},{24,8},{1,17},{9,25},{17,1},{25,9},{2,18},{10... | collective-permute-start | bytes 344072 | tf_op jit(solution)/shard_map/ppermute | solution.py:72
  32.2 13.4 %collective-permute-start.2 = (bf16[32,1792]{1,0:T(8,128)(2,1)S(1)}, bf16[32,1792]{1,0:T(8,128)(2,1)S(1)}, u32[]{:S(2)}, u32[]{:S(2)}) collective-permute-start(bf16[32,1792]{1,0:T(8,128)(2,1)S(1)} %get-tuple-element.257), channel_id=1, source_target_pairs={{0,24},{8,0},{16,8},{24,16},{1,25},{9,1},{17,9},{25,17},{2,26},{10... | collective-permute-start | bytes 344072 | tf_op jit(solution)/shard_map/ppermute | solution.py:72
  46.8 13.2 %collective-permute-start.3 = (bf16[128,1792]{1,0:T(8,128)(2,1)S(1)}, bf16[128,1792]{1,0:T(8,128)(2,1)S(1)}, u32[]{:S(2)}, u32[]{:S(2)}) collective-permute-start(bf16[128,1792]{1,0:T(8,128)(2,1)S(1)} %get-tuple-element.209), channel_id=1, source_target_pairs={{0,2},{1,5},{2,0},{3,7},{4,6},{5,1},{6,4},{7,3},{8,10},{9,13},{10,... | collective-permute-start | bytes 1376264 | tf_op jit(solution)/shard_map/ppermute | solution.py:35
  48.0 12.8 %collective-permute-start.4 = (bf16[128,1792]{1,0:T(8,128)(2,1)S(1)}, bf16[128,1792]{1,0:T(8,128)(2,1)S(1)}, u32[]{:S(2)}, u32[]{:S(2)}) collective-permute-start(bf16[128,1792]{1,0:T(8,128)(2,1)S(1)} %get-tuple-element.209), channel_id=1, source_target_pairs={{0,4},{1,3},{2,6},{3,1},{4,0},{5,7},{6,2},{7,5},{8,12},{9,11},{10,... | collective-permute-start | bytes 1376264 | tf_op jit(solution)/shard_map/ppermute | solution.py:35
  50.3 19.0 %collective-permute-start.6 = (bf16[128,1792]{1,0:T(8,128)(2,1)S(1)}, bf16[128,1792]{1,0:T(8,128)(2,1)S(1)}, u32[]{:S(2)}, u32[]{:S(2)}) collective-permute-start(bf16[128,1792]{1,0:T(8,128)(2,1)S(1)} %get-tuple-element.209), channel_id=1, source_target_pairs={{0,1},{1,0},{2,3},{3,2},{4,5},{5,4},{6,7},{7,6},{8,9},{9,8},{10,11... | collective-permute-start | bytes 1376264 | tf_op jit(solution)/shard_map/ppermute | solution.py:35
  60.0 8.5 %collective-permute-start.5 = (bf16[128,1792]{1,0:T(8,128)(2,1)S(1)}, bf16[128,1792]{1,0:T(8,128)(2,1)S(1)}, u32[]{:S(2)}, u32[]{:S(2)}) collective-permute-start(bf16[128,1792]{1,0:T(8,128)(2,1)S(1)} %collective-permute-done.3), channel_id=1, source_target_pairs={{0,4},{1,3},{2,6},{3,1},{4,0},{5,7},{6,2},{7,5},{8,12},{9,11},{10,... | collective-permute-start | bytes 1376264 | tf_op jit(solution)/shard_map/ppermute | solution.py:35
  60.8 9.3 %collective-permute-start.7 = (bf16[128,1792]{1,0:T(8,128)(2,1)S(1)}, bf16[128,1792]{1,0:T(8,128)(2,1)S(1)}, u32[]{:S(2)}, u32[]{:S(2)}) collective-permute-start(bf16[128,1792]{1,0:T(8,128)(2,1)S(1)} %collective-permute-done.3), channel_id=1, source_target_pairs={{0,1},{1,0},{2,3},{3,2},{4,5},{5,4},{6,7},{7,6},{8,9},{9,8},{10,11... | collective-permute-start | bytes 1376264 | tf_op jit(solution)/shard_map/ppermute | solution.py:35
  60.8 10.1 %collective-permute-start.8 = (bf16[128,1792]{1,0:T(8,128)(2,1)S(1)}, bf16[128,1792]{1,0:T(8,128)(2,1)S(1)}, u32[]{:S(2)}, u32[]{:S(2)}) collective-permute-start(bf16[128,1792]{1,0:T(8,128)(2,1)S(1)} %collective-permute-done.4), channel_id=1, source_target_pairs={{0,1},{1,0},{2,3},{3,2},{4,5},{5,4},{6,7},{7,6},{8,9},{9,8},{10,11... | collective-permute-start | bytes 1376264 | tf_op jit(solution)/shard_map/ppermute | solution.py:35
  72.9 18.1 %collective-permute-start.10 = (bf16[32,1792]{1,0:T(8,128)(2,1)S(1)}, bf16[32,1792]{1,0:T(8,128)(2,1)S(1)}, u32[]{:S(2)}, u32[]{:S(2)}) collective-permute-start(bf16[32,1792]{1,0:T(8,128)(2,1)S(1)} %get-tuple-element.255), channel_id=1, source_target_pairs={{0,8},{8,16},{16,24},{24,0},{1,9},{9,17},{17,25},{25,1},{2,10},{10... | collective-permute-start | bytes 344072 | tf_op jit(solution)/shard_map/ppermute | solution.py:72
  83.1 15.9 %collective-permute-start.11 = (bf16[32,1792]{1,0:T(8,128)(2,1)S(1)}, bf16[32,1792]{1,0:T(8,128)(2,1)S(1)}, u32[]{:S(2)}, u32[]{:S(2)}) collective-permute-start(bf16[32,1792]{1,0:T(8,128)(2,1)S(1)} %get-tuple-element.254), channel_id=1, source_target_pairs={{0,16},{8,24},{16,0},{24,8},{1,17},{9,25},{17,1},{25,9},{2,18},{10... | collective-permute-start | bytes 344072 | tf_op jit(solution)/shard_map/ppermute | solution.py:72
  85.1 13.9 %collective-permute-start.12 = (bf16[32,1792]{1,0:T(8,128)(2,1)S(1)}, bf16[32,1792]{1,0:T(8,128)(2,1)S(1)}, u32[]{:S(2)}, u32[]{:S(2)}) collective-permute-start(bf16[32,1792]{1,0:T(8,128)(2,1)S(1)} %get-tuple-element.253), channel_id=1, source_target_pairs={{0,24},{8,0},{16,8},{24,16},{1,25},{9,1},{17,9},{25,17},{2,26},{10... | collective-permute-start | bytes 344072 | tf_op jit(solution)/shard_map/ppermute | solution.py:72
  122.5 15.1 %collective-permute-start.13 = (bf16[512,1792]{1,0:T(8,128)(2,1)}, bf16[512,1792]{1,0:T(8,128)(2,1)}, u32[]{:S(2)}, u32[]{:S(2)}) collective-permute-start(bf16[512,1792]{1,0:T(8,128)(2,1)} %convolution_convert_fusion), channel_id=1, source_target_pairs={{0,1},{1,0},{2,3},{3,2},{4,5},{5,4},{6,7},{7,6},{8,9},{9,8},{10,11... | collective-permute-start | bytes 5505032 | tf_op jit(solution)/shard_map/ppermute | solution.py:35
  122.6 11.2 %collective-permute-start.31 = (bf16[112,128]{1,0:T(8,128)(2,1)S(1)}, bf16[112,128]{1,0:T(8,128)(2,1)S(1)}, u32[]{:S(2)}, u32[]{:S(2)}) collective-permute-start(bf16[112,128]{1,0:T(8,128)(2,1)S(1)} %pad_maximum_fusion.7), channel_id=1, source_target_pairs={{0,16},{8,24},{16,0},{24,8},{1,17},{9,25},{17,1},{25,9},{2,18},{10... | collective-permute-start | bytes 86024 | tf_op jit(solution)/shard_map/ppermute | solution.py:72
  124.1 9.8 %collective-permute-start.32 = (bf16[112,128]{1,0:T(8,128)(2,1)S(1)}, bf16[112,128]{1,0:T(8,128)(2,1)S(1)}, u32[]{:S(2)}, u32[]{:S(2)}) collective-permute-start(bf16[112,128]{1,0:T(8,128)(2,1)S(1)} %pad_maximum_fusion.7), channel_id=1, source_target_pairs={{0,24},{8,0},{16,8},{24,16},{1,25},{9,1},{17,9},{25,17},{2,26},{10... | collective-permute-start | bytes 86024 | tf_op jit(solution)/shard_map/ppermute | solution.py:72
  134.2 12.8 %collective-permute-start.23 = (bf16[128,1792]{1,0:T(8,128)(2,1)S(1)}, bf16[128,1792]{1,0:T(8,128)(2,1)S(1)}, u32[]{:S(2)}, u32[]{:S(2)}) collective-permute-start(bf16[128,1792]{1,0:T(8,128)(2,1)S(1)} %pad_maximum_fusion.2), channel_id=1, source_target_pairs={{0,2},{1,5},{2,0},{3,7},{4,6},{5,1},{6,4},{7,3},{8,10},{9,13},{10,... | collective-permute-start | bytes 1376264 | tf_op jit(solution)/shard_map/ppermute | solution.py:35
  135.8 11.7 %collective-permute-start.24 = (bf16[128,1792]{1,0:T(8,128)(2,1)S(1)}, bf16[128,1792]{1,0:T(8,128)(2,1)S(1)}, u32[]{:S(2)}, u32[]{:S(2)}) collective-permute-start(bf16[128,1792]{1,0:T(8,128)(2,1)S(1)} %pad_maximum_fusion.2), channel_id=1, source_target_pairs={{0,4},{1,3},{2,6},{3,1},{4,0},{5,7},{6,2},{7,5},{8,12},{9,11},{10,... | collective-permute-start | bytes 1376264 | tf_op jit(solution)/shard_map/ppermute | solution.py:35
  137.5 24.4 %collective-permute-start.26 = (bf16[128,1792]{1,0:T(8,128)(2,1)S(1)}, bf16[128,1792]{1,0:T(8,128)(2,1)S(1)}, u32[]{:S(2)}, u32[]{:S(2)}) collective-permute-start(bf16[128,1792]{1,0:T(8,128)(2,1)S(1)} %pad_maximum_fusion.2), channel_id=1, source_target_pairs={{0,1},{1,0},{2,3},{3,2},{4,5},{5,4},{6,7},{7,6},{8,9},{9,8},{10,11... | collective-permute-start | bytes 1376264 | tf_op jit(solution)/shard_map/ppermute | solution.py:35
  140.1 20.1 %collective-permute-start.14 = (bf16[256,1792]{1,0:T(8,128)(2,1)S(1)}, bf16[256,1792]{1,0:T(8,128)(2,1)S(1)}, u32[]{:S(2)}, u32[]{:S(2)}) collective-permute-start(bf16[256,1792]{1,0:T(8,128)(2,1)S(1)} %slice.393), channel_id=1, source_target_pairs={{0,4},{1,3},{2,6},{3,1},{4,0},{5,7},{6,2},{7,5},{8,12},{9,11},{10,... | collective-permute-start | bytes 2752520 | tf_op jit(solution)/shard_map/ppermute | solution.py:35
  147.1 12.0 %collective-permute-start.25 = (bf16[128,1792]{1,0:T(8,128)(2,1)S(1)}, bf16[128,1792]{1,0:T(8,128)(2,1)S(1)}, u32[]{:S(2)}, u32[]{:S(2)}) collective-permute-start(bf16[128,1792]{1,0:T(8,128)(2,1)S(1)} %collective-permute-done.23), channel_id=1, source_target_pairs={{0,4},{1,3},{2,6},{3,1},{4,0},{5,7},{6,2},{7,5},{8,12},{9,11},{10,... | collective-permute-start | bytes 1376264 | tf_op jit(solution)/shard_map/ppermute | solution.py:35
  147.5 14.5 %collective-permute-start.27 = (bf16[128,1792]{1,0:T(8,128)(2,1)S(1)}, bf16[128,1792]{1,0:T(8,128)(2,1)S(1)}, u32[]{:S(2)}, u32[]{:S(2)}) collective-permute-start(bf16[128,1792]{1,0:T(8,128)(2,1)S(1)} %collective-permute-done.23), channel_id=1, source_target_pairs={{0,1},{1,0},{2,3},{3,2},{4,5},{5,4},{6,7},{7,6},{8,9},{9,8},{10,11... | collective-permute-start | bytes 1376264 | tf_op jit(solution)/shard_map/ppermute | solution.py:35
  147.5 24.7 %collective-permute-start.28 = (bf16[128,1792]{1,0:T(8,128)(2,1)S(1)}, bf16[128,1792]{1,0:T(8,128)(2,1)S(1)}, u32[]{:S(2)}, u32[]{:S(2)}) collective-permute-start(bf16[128,1792]{1,0:T(8,128)(2,1)S(1)} %collective-permute-done.24), channel_id=1, source_target_pairs={{0,1},{1,0},{2,3},{3,2},{4,5},{5,4},{6,7},{7,6},{8,9},{9,8},{10,11... | collective-permute-start | bytes 1376264 | tf_op jit(solution)/shard_map/ppermute | solution.py:35
  159.0 13.2 %collective-permute-start.29 = (bf16[128,1792]{1,0:T(8,128)(2,1)S(1)}, bf16[128,1792]{1,0:T(8,128)(2,1)S(1)}, u32[]{:S(2)}, u32[]{:S(2)}) collective-permute-start(bf16[128,1792]{1,0:T(8,128)(2,1)S(1)} %collective-permute-done.25), channel_id=1, source_target_pairs={{0,1},{1,0},{2,3},{3,2},{4,5},{5,4},{6,7},{7,6},{8,9},{9,8},{10,11... | collective-permute-start | bytes 1376264 | tf_op jit(solution)/shard_map/ppermute | solution.py:35
  160.4 8.5 %collective-permute-start.15 = (bf16[128,1792]{1,0:T(8,128)(2,1)S(1)}, bf16[128,1792]{1,0:T(8,128)(2,1)S(1)}, u32[]{:S(2)}, u32[]{:S(2)}) collective-permute-start(bf16[128,1792]{1,0:T(8,128)(2,1)S(1)} %slice.394), channel_id=1, source_target_pairs={{0,2},{1,5},{2,0},{3,7},{4,6},{5,1},{6,4},{7,3},{8,10},{9,13},{10,... | collective-permute-start | bytes 1376264 | tf_op jit(solution)/shard_map/ppermute | solution.py:35
  170.4 13.0 %collective-permute-start.16 = (bf16[128,1792]{1,0:T(8,128)(2,1)S(1)}, bf16[128,1792]{1,0:T(8,128)(2,1)S(1)}, u32[]{:S(2)}, u32[]{:S(2)}) collective-permute-start(bf16[128,1792]{1,0:T(8,128)(2,1)S(1)} %get-tuple-element.205), channel_id=1, source_target_pairs={{0,2},{1,5},{2,0},{3,7},{4,6},{5,1},{6,4},{7,3},{8,10},{9,13},{10,... | collective-permute-start | bytes 1376264 | tf_op jit(solution)/shard_map/ppermute | solution.py:35
  171.8 12.3 %collective-permute-start.17 = (bf16[128,1792]{1,0:T(8,128)(2,1)S(1)}, bf16[128,1792]{1,0:T(8,128)(2,1)S(1)}, u32[]{:S(2)}, u32[]{:S(2)}) collective-permute-start(bf16[128,1792]{1,0:T(8,128)(2,1)S(1)} %get-tuple-element.205), channel_id=1, source_target_pairs={{0,4},{1,3},{2,6},{3,1},{4,0},{5,7},{6,2},{7,5},{8,12},{9,11},{10,... | collective-permute-start | bytes 1376264 | tf_op jit(solution)/shard_map/ppermute | solution.py:35
  172.3 20.4 %collective-permute-start.19 = (bf16[128,1792]{1,0:T(8,128)(2,1)S(1)}, bf16[128,1792]{1,0:T(8,128)(2,1)S(1)}, u32[]{:S(2)}, u32[]{:S(2)}) collective-permute-start(bf16[128,1792]{1,0:T(8,128)(2,1)S(1)} %get-tuple-element.205), channel_id=1, source_target_pairs={{0,1},{1,0},{2,3},{3,2},{4,5},{5,4},{6,7},{7,6},{8,9},{9,8},{10,11... | collective-permute-start | bytes 1376264 | tf_op jit(solution)/shard_map/ppermute | solution.py:35
  183.4 8.5 %collective-permute-start.18 = (bf16[128,1792]{1,0:T(8,128)(2,1)S(1)}, bf16[128,1792]{1,0:T(8,128)(2,1)S(1)}, u32[]{:S(2)}, u32[]{:S(2)}) collective-permute-start(bf16[128,1792]{1,0:T(8,128)(2,1)S(1)} %collective-permute-done.16), channel_id=1, source_target_pairs={{0,4},{1,3},{2,6},{3,1},{4,0},{5,7},{6,2},{7,5},{8,12},{9,11},{10,... | collective-permute-start | bytes 1376264 | tf_op jit(solution)/shard_map/ppermute | solution.py:35
  184.1 9.3 %collective-permute-start.20 = (bf16[128,1792]{1,0:T(8,128)(2,1)S(1)}, bf16[128,1792]{1,0:T(8,128)(2,1)S(1)}, u32[]{:S(2)}, u32[]{:S(2)}) collective-permute-start(bf16[128,1792]{1,0:T(8,128)(2,1)S(1)} %collective-permute-done.16), channel_id=1, source_target_pairs={{0,1},{1,0},{2,3},{3,2},{4,5},{5,4},{6,7},{7,6},{8,9},{9,8},{10,11... | collective-permute-start | bytes 1376264 | tf_op jit(solution)/shard_map/ppermute | solution.py:35
  184.1 10.2 %collective-permute-start.21 = (bf16[128,1792]{1,0:T(8,128)(2,1)S(1)}, bf16[128,1792]{1,0:T(8,128)(2,1)S(1)}, u32[]{:S(2)}, u32[]{:S(2)}) collective-permute-start(bf16[128,1792]{1,0:T(8,128)(2,1)S(1)} %collective-permute-done.17), channel_id=1, source_target_pairs={{0,1},{1,0},{2,3},{3,2},{4,5},{5,4},{6,7},{7,6},{8,9},{9,8},{10,11... | collective-permute-start | bytes 1376264 | tf_op jit(solution)/shard_map/ppermute | solution.py:35
  254.0 184.2 %reduce-scatter.3.cloned.1.call-start = ((), (), s32[]{:S(2)}) async-start(), calls=%async_computation.5 | async-start | bytes 4587520 | tf_op jit(solution)/shard_map/reduce_scatter | solution.py:825
  261.6 13.5 %collective-permute-start.34 = (bf16[256,1792]{1,0:T(8,128)(2,1)S(1)}, bf16[256,1792]{1,0:T(8,128)(2,1)S(1)}, u32[]{:S(2)}, u32[]{:S(2)}) collective-permute-start(bf16[256,1792]{1,0:T(8,128)(2,1)S(1)} %get-tuple-element.125), channel_id=1, source_target_pairs={{0,4},{1,3},{2,6},{3,1},{4,0},{5,7},{6,2},{7,5},{8,12},{9,11},{10,... | collective-permute-start | bytes 2752520 | tf_op jit(solution)/shard_map/ppermute | solution.py:35
  275.2 10.2 %collective-permute-start.36 = (bf16[512,1792]{1,0:T(8,128)(2,1)S(1)}, bf16[512,1792]{1,0:T(8,128)(2,1)S(1)}, u32[]{:S(2)}, u32[]{:S(2)}) collective-permute-start(bf16[512,1792]{1,0:T(8,128)(2,1)S(1)} %slice.392), channel_id=1, source_target_pairs={{0,1},{1,0},{2,3},{3,2},{4,5},{5,4},{6,7},{7,6},{8,9},{9,8},{10,11... | collective-permute-start | bytes 5505032 | tf_op jit(solution)/shard_map/ppermute | solution.py:35
  275.3 8.5 %collective-permute-start.35 = (bf16[128,1792]{1,0:T(8,128)(2,1)S(1)}, bf16[128,1792]{1,0:T(8,128)(2,1)S(1)}, u32[]{:S(2)}, u32[]{:S(2)}) collective-permute-start(bf16[128,1792]{1,0:T(8,128)(2,1)S(1)} %get-tuple-element.133), channel_id=1, source_target_pairs={{0,2},{1,5},{2,0},{3,7},{4,6},{5,1},{6,4},{7,3},{8,10},{9,13},{10,... | collective-permute-start | bytes 1376264 | tf_op jit(solution)/shard_map/ppermute | solution.py:35
  285.4 13.4 %collective-permute-start.37 = (bf16[128,1792]{1,0:T(8,128)(2,1)S(1)}, bf16[128,1792]{1,0:T(8,128)(2,1)S(1)}, u32[]{:S(2)}, u32[]{:S(2)}) collective-permute-start(bf16[128,1792]{1,0:T(8,128)(2,1)S(1)} %get-tuple-element.139), channel_id=1, source_target_pairs={{0,2},{1,5},{2,0},{3,7},{4,6},{5,1},{6,4},{7,3},{8,10},{9,13},{10,... | collective-permute-start | bytes 1376264 | tf_op jit(solution)/shard_map/ppermute | solution.py:35
  287.0 11.8 %collective-permute-start.38 = (bf16[128,1792]{1,0:T(8,128)(2,1)S(1)}, bf16[128,1792]{1,0:T(8,128)(2,1)S(1)}, u32[]{:S(2)}, u32[]{:S(2)}) collective-permute-start(bf16[128,1792]{1,0:T(8,128)(2,1)S(1)} %get-tuple-element.139), channel_id=1, source_target_pairs={{0,4},{1,3},{2,6},{3,1},{4,0},{5,7},{6,2},{7,5},{8,12},{9,11},{10,... | collective-permute-start | bytes 1376264 | tf_op jit(solution)/shard_map/ppermute | solution.py:35
  298.8 8.5 %collective-permute-start.39 = (bf16[128,1792]{1,0:T(8,128)(2,1)S(1)}, bf16[128,1792]{1,0:T(8,128)(2,1)S(1)}, u32[]{:S(2)}, u32[]{:S(2)}) collective-permute-start(bf16[128,1792]{1,0:T(8,128)(2,1)S(1)} %collective-permute-done.37), channel_id=1, source_target_pairs={{0,4},{1,3},{2,6},{3,1},{4,0},{5,7},{6,2},{7,5},{8,12},{9,11},{10,... | collective-permute-start | bytes 1376264 | tf_op jit(solution)/shard_map/ppermute | solution.py:35
  299.3 9.6 %collective-permute-start.41 = (bf16[128,1792]{1,0:T(8,128)(2,1)S(1)}, bf16[128,1792]{1,0:T(8,128)(2,1)S(1)}, u32[]{:S(2)}, u32[]{:S(2)}) collective-permute-start(bf16[128,1792]{1,0:T(8,128)(2,1)S(1)} %collective-permute-done.37), channel_id=1, source_target_pairs={{0,1},{1,0},{2,3},{3,2},{4,5},{5,4},{6,7},{7,6},{8,9},{9,8},{10,11... | collective-permute-start | bytes 1376264 | tf_op jit(solution)/shard_map/ppermute | solution.py:35
  300.2 7.9 %collective-permute-start.40 = (bf16[128,1792]{1,0:T(8,128)(2,1)S(1)}, bf16[128,1792]{1,0:T(8,128)(2,1)S(1)}, u32[]{:S(2)}, u32[]{:S(2)}) collective-permute-start(bf16[128,1792]{1,0:T(8,128)(2,1)S(1)} %get-tuple-element.139), channel_id=1, source_target_pairs={{0,1},{1,0},{2,3},{3,2},{4,5},{5,4},{6,7},{7,6},{8,9},{9,8},{10,11... | collective-permute-start | bytes 1376264 | tf_op jit(solution)/shard_map/ppermute | solution.py:35
  300.2 9.5 %collective-permute-start.42 = (bf16[128,1792]{1,0:T(8,128)(2,1)S(1)}, bf16[128,1792]{1,0:T(8,128)(2,1)S(1)}, u32[]{:S(2)}, u32[]{:S(2)}) collective-permute-start(bf16[128,1792]{1,0:T(8,128)(2,1)S(1)} %collective-permute-done.38), channel_id=1, source_target_pairs={{0,1},{1,0},{2,3},{3,2},{4,5},{5,4},{6,7},{7,6},{8,9},{9,8},{10,11... | collective-permute-start | bytes 1376264 | tf_op jit(solution)/shard_map/ppermute | solution.py:35
  311.3 19.5 %collective-permute-start.44 = (bf16[256,1792]{1,0:T(8,128)(2,1)}, bf16[256,1792]{1,0:T(8,128)(2,1)}, u32[]{:S(2)}, u32[]{:S(2)}) collective-permute-start(bf16[256,1792]{1,0:T(8,128)(2,1)} %get-tuple-element.143), channel_id=1, source_target_pairs={{0,4},{1,3},{2,6},{3,1},{4,0},{5,7},{6,2},{7,5},{8,12},{9,11},{10,... | collective-permute-start | bytes 2752520 | tf_op jit(solution)/shard_map/ppermute | solution.py:35
  336.1 7.5 %collective-permute-start.45 = (bf16[512,1792]{1,0:T(8,128)(2,1)}, bf16[512,1792]{1,0:T(8,128)(2,1)}, u32[]{:S(2)}, u32[]{:S(2)}) collective-permute-start(bf16[512,1792]{1,0:T(8,128)(2,1)} %convolution_convert_fusion.1), channel_id=1, source_target_pairs={{0,1},{1,0},{2,3},{3,2},{4,5},{5,4},{6,7},{7,6},{8,9},{9,8},{10,11... | collective-permute-start | bytes 5505032 | tf_op jit(solution)/shard_map/ppermute | solution.py:35
  347.1 18.6 %collective-permute-start.46 = (bf16[256,1792]{1,0:T(8,128)(2,1)}, bf16[256,1792]{1,0:T(8,128)(2,1)}, u32[]{:S(2)}, u32[]{:S(2)}) collective-permute-start(bf16[256,1792]{1,0:T(8,128)(2,1)} %get-tuple-element.156), channel_id=1, source_target_pairs={{0,4},{1,3},{2,6},{3,1},{4,0},{5,7},{6,2},{7,5},{8,12},{9,11},{10,... | collective-permute-start | bytes 2752520 | tf_op jit(solution)/shard_map/ppermute | solution.py:35
  349.9 13.7 %collective-permute-start.47 = (bf16[128,1792]{1,0:T(8,128)(2,1)}, bf16[128,1792]{1,0:T(8,128)(2,1)S(1)}, u32[]{:S(2)}, u32[]{:S(2)}) collective-permute-start(bf16[128,1792]{1,0:T(8,128)(2,1)} %get-tuple-element.159), channel_id=1, source_target_pairs={{0,2},{1,5},{2,0},{3,7},{4,6},{5,1},{6,4},{7,3},{8,10},{9,13},{10,... | collective-permute-start | bytes 1376264 | tf_op jit(solution)/shard_map/ppermute | solution.py:35
  368.6 41.8 %collective-permute-start.48 = (bf16[448,1792]{1,0:T(8,128)(2,1)}, bf16[448,1792]{1,0:T(8,128)(2,1)}, u32[]{:S(2)}, u32[]{:S(2)}) collective-permute-start(bf16[448,1792]{1,0:T(8,128)(2,1)} %reduce-scatter.5.cloned.1.call-done.refs_0_), channel_id=1, source_target_pairs={{0,2},{1,5},{2,0},{3,7},{4,6},{5,1},{6,4},{7,3},{8,10},{9,13},{10,... | collective-permute-start | bytes 4816904 | tf_op jit(solution)/shard_map/ppermute | solution.py:35
  369.1 41.3 %collective-permute-start.49 = (bf16[448,1792]{1,0:T(8,128)(2,1)}, bf16[448,1792]{1,0:T(8,128)(2,1)}, u32[]{:S(2)}, u32[]{:S(2)}) collective-permute-start(bf16[448,1792]{1,0:T(8,128)(2,1)} %reduce-scatter.5.cloned.1.call-done.refs_0_), channel_id=1, source_target_pairs={{0,4},{1,3},{2,6},{3,1},{4,0},{5,7},{6,2},{7,5},{8,12},{9,11},{10,... | collective-permute-start | bytes 4816904 | tf_op jit(solution)/shard_map/ppermute | solution.py:35
  373.4 8.4 %collective-permute-start.52 = (bf16[118,128]{1,0:T(8,128)(2,1)S(1)}, bf16[118,128]{1,0:T(8,128)(2,1)S(1)}, u32[]{:S(2)}, u32[]{:S(2)}) collective-permute-start(bf16[118,128]{1,0:T(8,128)(2,1)S(1)} %get-tuple-element.291), channel_id=1, source_target_pairs={{0,16},{8,24},{16,0},{24,8},{1,17},{9,25},{17,1},{25,9},{2,18},{10... | collective-permute-start | bytes 90632 | tf_op jit(solution)/shard_map/ppermute | solution.py:72
  374.6 7.6 %collective-permute-start.53 = (bf16[118,128]{1,0:T(8,128)(2,1)S(1)}, bf16[118,128]{1,0:T(8,128)(2,1)S(1)}, u32[]{:S(2)}, u32[]{:S(2)}) collective-permute-start(bf16[118,128]{1,0:T(8,128)(2,1)S(1)} %get-tuple-element.292), channel_id=1, source_target_pairs={{0,24},{8,0},{16,8},{24,16},{1,25},{9,1},{17,9},{25,17},{2,26},{10... | collective-permute-start | bytes 90632 | tf_op jit(solution)/shard_map/ppermute | solution.py:72
  378.0 32.3 %collective-permute-start.50 = (bf16[128,1792]{1,0:T(8,128)(2,1)}, bf16[128,1792]{1,0:T(8,128)(2,1)S(1)}, u32[]{:S(2)}, u32[]{:S(2)}) collective-permute-start(bf16[128,1792]{1,0:T(8,128)(2,1)} %add_convert_fusion.3), channel_id=1, source_target_pairs={{0,2},{1,5},{2,0},{3,7},{4,6},{5,1},{6,4},{7,3},{8,10},{9,13},{10,... | collective-permute-start | bytes 1376264 | tf_op jit(solution)/shard_map/ppermute | solution.py:35
  410.4 9.7 %collective-permute-start.54 = (bf16[118,128]{1,0:T(8,128)(2,1)S(1)}, bf16[118,128]{1,0:T(8,128)(2,1)S(1)}, u32[]{:S(2)}, u32[]{:S(2)}) collective-permute-start(bf16[118,128]{1,0:T(8,128)(2,1)S(1)} %add_convert_fusion.7), channel_id=1, source_target_pairs={{0,2},{1,5},{2,0},{3,7},{4,6},{5,1},{6,4},{7,3},{8,10},{9,13},{10,... | collective-permute-start | bytes 90632 | tf_op jit(solution)/shard_map/ppermute | solution.py:35
  411.9 8.7 %collective-permute-start.55 = (bf16[118,128]{1,0:T(8,128)(2,1)S(1)}, bf16[118,128]{1,0:T(8,128)(2,1)S(1)}, u32[]{:S(2)}, u32[]{:S(2)}) collective-permute-start(bf16[118,128]{1,0:T(8,128)(2,1)S(1)} %add_convert_fusion.7), channel_id=1, source_target_pairs={{0,4},{1,3},{2,6},{3,1},{4,0},{5,7},{6,2},{7,5},{8,12},{9,11},{10,... | collective-permute-start | bytes 90632 | tf_op jit(solution)/shard_map/ppermute | solution.py:35
  412.4 34.2 %collective-permute-start.67 = (bf16[448,1792]{1,0:T(8,128)(2,1)}, bf16[448,1792]{1,0:T(8,128)(2,1)}, u32[]{:S(2)}, u32[]{:S(2)}) collective-permute-start(bf16[448,1792]{1,0:T(8,128)(2,1)} %collective-permute-done.48), channel_id=1, source_target_pairs={{0,4},{1,3},{2,6},{3,1},{4,0},{5,7},{6,2},{7,5},{8,12},{9,11},{10,... | collective-permute-start | bytes 4816904 | tf_op jit(solution)/shard_map/ppermute | solution.py:35
  420.1 13.7 %collective-permute-start.56 = (bf16[118,128]{1,0:T(8,128)(2,1)S(1)}, bf16[118,128]{1,0:T(8,128)(2,1)S(1)}, u32[]{:S(2)}, u32[]{:S(2)}) collective-permute-start(bf16[118,128]{1,0:T(8,128)(2,1)S(1)} %collective-permute-done.54), channel_id=1, source_target_pairs={{0,4},{1,3},{2,6},{3,1},{4,0},{5,7},{6,2},{7,5},{8,12},{9,11},{10,... | collective-permute-start | bytes 90632 | tf_op jit(solution)/shard_map/ppermute | solution.py:35
  438.1 23.4 %collective-permute-start.64 = (bf16[448,1024]{1,0:T(8,128)(2,1)}, bf16[448,1024]{1,0:T(8,128)(2,1)S(1)}, u32[]{:S(2)}, u32[]{:S(2)}) collective-permute-start(bf16[448,1024]{1,0:T(8,128)(2,1)} %reduce-scatter.3.cloned.1.call-done.refs_0_), channel_id=1, source_target_pairs={{0,2},{1,5},{2,0},{3,7},{4,6},{5,1},{6,4},{7,3},{8,10},{9,13},{10,... | collective-permute-start | bytes 2752520 | tf_op jit(solution)/shard_map/ppermute | solution.py:35
  439.3 22.3 %collective-permute-start.65 = (bf16[448,1024]{1,0:T(8,128)(2,1)}, bf16[448,1024]{1,0:T(8,128)(2,1)S(1)}, u32[]{:S(2)}, u32[]{:S(2)}) collective-permute-start(bf16[448,1024]{1,0:T(8,128)(2,1)} %reduce-scatter.3.cloned.1.call-done.refs_0_), channel_id=1, source_target_pairs={{0,4},{1,3},{2,6},{3,1},{4,0},{5,7},{6,2},{7,5},{8,12},{9,11},{10,... | collective-permute-start | bytes 2752520 | tf_op jit(solution)/shard_map/ppermute | solution.py:35
  442.4 14.3 %collective-permute-start.66 = (f32[2,448]{1,0:T(2,128)S(1)}, f32[2,448]{1,0:T(2,128)S(1)}, u32[]{:S(2)}, u32[]{:S(2)}) collective-permute-start(f32[2,448]{1,0:T(2,128)S(1)} %pad_maximum_fusion.14), channel_id=1, source_target_pairs={{0,1},{1,0},{2,3},{3,2},{4,5},{5,4},{6,7},{7,6},{8,9},{9,8},{10,11... | collective-permute-start | bytes 10760 | tf_op jit(solution)/shard_map/ppermute | solution.py:35
  443.8 18.5 %collective-permute-start.57 = (bf16[32,3584]{1,0:T(8,128)(2,1)S(1)}, bf16[32,3584]{1,0:T(8,128)(2,1)S(1)}, u32[]{:S(2)}, u32[]{:S(2)}) collective-permute-start(bf16[32,3584]{1,0:T(8,128)(2,1)S(1)} %get-tuple-element.230), channel_id=1, source_target_pairs={{0,24},{8,0},{16,8},{24,16},{1,25},{9,1},{17,9},{25,17},{2,26},{10... | collective-permute-start | bytes 688136 | tf_op jit(solution)/shard_map/ppermute | solution.py:72
  446.7 21.0 %collective-permute-start.58 = (bf16[32,3584]{1,0:T(8,128)(2,1)S(1)}, bf16[32,3584]{1,0:T(8,128)(2,1)S(1)}, u32[]{:S(2)}, u32[]{:S(2)}) collective-permute-start(bf16[32,3584]{1,0:T(8,128)(2,1)S(1)} %get-tuple-element.229), channel_id=1, source_target_pairs={{0,16},{8,24},{16,0},{24,8},{1,17},{9,25},{17,1},{25,9},{2,18},{10... | collective-permute-start | bytes 688136 | tf_op jit(solution)/shard_map/ppermute | solution.py:72
  456.7 10.9 %collective-permute-start.59 = (bf16[32,3584]{1,0:T(8,128)(2,1)S(1)}, bf16[32,3584]{1,0:T(8,128)(2,1)S(1)}, u32[]{:S(2)}, u32[]{:S(2)}) collective-permute-start(bf16[32,3584]{1,0:T(8,128)(2,1)S(1)} %get-tuple-element.228), channel_id=1, source_target_pairs={{0,8},{8,16},{16,24},{24,0},{1,9},{9,17},{17,25},{25,1},{2,10},{10... | collective-permute-start | bytes 688136 | tf_op jit(solution)/shard_map/ppermute | solution.py:72
  461.6 14.9 %collective-permute-start.68 = (bf16[448,1024]{1,0:T(8,128)(2,1)S(1)}, bf16[448,1024]{1,0:T(8,128)(2,1)S(1)}, u32[]{:S(2)}, u32[]{:S(2)}) collective-permute-start(bf16[448,1024]{1,0:T(8,128)(2,1)S(1)} %collective-permute-done.64), channel_id=1, source_target_pairs={{0,4},{1,3},{2,6},{3,1},{4,0},{5,7},{6,2},{7,5},{8,12},{9,11},{10,... | collective-permute-start | bytes 2752520 | tf_op jit(solution)/shard_map/ppermute | solution.py:35
  (74 other events, 1643.2 us)
Sparse Core Ops, SparseCore 0:
  10.2 94.3 all-gather.2
  106.7 118.5 all-gather.4
  254.1 111.1 reduce-scatter.4
  368.0 70.0 reduce-scatter.2
